TPU v7x, 32 devices: a whole 2x2x4 slice. The times are simulated.
32 devices in a mesh: seq: 8 (over z, y), head: 4 (over x, core).
Axes of the slice: x: 2, y: 2, z: 4, core: 2. Of those that a mesh axis runs over, the one named last changes fastest.
Arguments:
- tokens: bfloat16 [1024, 2560], P('seq'), may hold values from -51 to 51
- raw_keys: bfloat16 [32768, 768], P(('seq', 'head')), may hold values from -6 to 6
- raw_values: bfloat16 [32768, 512], P(('seq', 'head')), may hold values from -6 to 6
- query_weight: bfloat16 [2560, 12288], P('seq', 'head'), may hold values from -0.125 to 0.125
- output_weight: bfloat16 [8192, 2560], P('head', 'seq'), may hold values from -0.09375 to 0.09375
- key_expand: bfloat16 [192, 768], replicated, may hold values from -0.4375 to 0.4375
- key_mix: float32 [32, 768], replicated, may hold values from -1 to 1
- key_reduce: bfloat16 [768, 192], replicated, may hold values from -1.6953125 to 1.6953125
- value_expand: bfloat16 [128, 768], replicated, may hold values from -0.5 to 0.5
- value_mix: float32 [32, 768], replicated, may hold values from -1 to 1
- value_reduce: bfloat16 [768, 128], replicated, may hold values from -0.65625 to 0.65625
Outputs:
- branch_output: bfloat16 [1024, 2560], P('seq', 'head')
All inputs are finite; a program needn't handle non-finite values.
Results may differ from a plain program's by a relative error of at most 0.008.
The roundings to bfloat16 on the way count: a program that leaves them out, or rounds other values in their place, can miss the bound.
Values may be sent and summed in bfloat16 or wider, within the bound.
No kernel may reach another device: no remote copies, remote signals or barrier semaphores. Data moves between devices by JAX's collectives and lax.ppermute only.
A program may use at most 128 MiB of HBM per device.

v0:
```python
import jax
import jax.numpy as jnp
from jax import lax
from jax.sharding import PartitionSpec as P

G = 4
BLK = 32
STRIDE = 16
CTX_DEV = 3968


def shifted(block, axis, distance):
    devices = range(lax.axis_size(axis))
    route = [(i - distance, i) for i in devices if i - distance in devices]
    return lax.ppermute(block, axis, route)


def project(raw, expand, groups):
    width_in = expand.shape[0]
    shaped = raw.reshape(raw.shape[0], groups, width_in)
    return jnp.einsum("tgc,ch->tgh", shaped, expand, preferred_element_type=jnp.float32)


def half_sums(projected, mix_half):
    shaped = projected.reshape(-1, STRIDE, projected.shape[1], projected.shape[2])
    return jnp.sum(shaped * mix_half[None, :, None, :], axis=1)


def finish(hidden, reduce_weight):
    activated = jax.nn.gelu(hidden, approximate=False).astype(jnp.bfloat16)
    return jnp.einsum(
        "bgh,hc->gcb", activated, reduce_weight, preferred_element_type=jnp.float32
    ).astype(jnp.bfloat16)


def attend_blocks(query_block, packed_keys, packed_values, block_ids, positions, key_span):
    key_width = packed_keys.shape[0]
    value_width = packed_values.shape[0]
    step_count = packed_keys.shape[1] // key_span
    score_scale = key_width ** (-0.5)
    rows_here = query_block.shape[0]

    def add_block(step_index, running):
        old_max, row_total, weighted = running
        key_block = lax.dynamic_slice_in_dim(packed_keys, step_index * key_span, key_span, 1)
        ids_block = lax.dynamic_slice_in_dim(block_ids, step_index * key_span, key_span, 0)
        value_block = lax.dynamic_slice_in_dim(packed_values, step_index * key_span, key_span, 1)
        scores = jnp.dot(query_block, key_block, preferred_element_type=jnp.float32) * score_scale
        visible = (STRIDE * ids_block + BLK - 1)[None, :] <= positions[:, None]
        scores = jnp.where(visible, scores, -jnp.inf)
        new_max = jnp.maximum(old_max, jnp.max(scores, axis=1))
        safe_max = jnp.where(jnp.isfinite(new_max), new_max, 0.0)
        rescale = jnp.exp(old_max - safe_max)
        exponent = jnp.exp(scores - safe_max[:, None])
        product = lax.dot_general(
            exponent.astype(jnp.bfloat16),
            value_block,
            (((1,), (1,)), ((), ())),
            preferred_element_type=jnp.float32,
        )
        return (
            new_max,
            row_total * rescale + jnp.sum(exponent, axis=1),
            weighted * rescale[:, None] + product,
        )

    start_state = (
        jnp.full((rows_here,), -jnp.inf, jnp.float32),
        jnp.zeros((rows_here,), jnp.float32),
        jnp.zeros((rows_here, value_width), jnp.float32),
    )
    return lax.fori_loop(0, step_count, add_block, start_state)


def shards(
    tokens,
    raw_keys,
    raw_values,
    query_weight,
    output_weight,
    key_expand,
    key_mix,
    key_reduce,
    value_expand,
    value_mix,
    value_reduce,
):
    groups = G
    head_count = lax.axis_size("head")
    seq_count = lax.axis_size("seq")
    key_width = key_expand.shape[0]
    value_width = value_expand.shape[0]
    local_tokens = raw_keys.shape[0]
    local_blocks = local_tokens // STRIDE
    row_count = tokens.shape[0]
    edge_keys, edge_values = shifted((raw_keys[:STRIDE], raw_values[:STRIDE]), ("seq", "head"), -1)
    key_proj = project(jnp.concatenate([raw_keys, edge_keys], axis=0), key_expand, groups)
    value_proj = project(jnp.concatenate([raw_values, edge_values], axis=0), value_expand, groups)
    hidden_keys = half_sums(key_proj[:-STRIDE], key_mix[:STRIDE]) + half_sums(
        key_proj[STRIDE:], key_mix[STRIDE:]
    )
    hidden_values = half_sums(value_proj[:-STRIDE], value_mix[:STRIDE]) + half_sums(
        value_proj[STRIDE:], value_mix[STRIDE:]
    )
    stacked = jnp.concatenate(
        [finish(hidden_keys, key_reduce), finish(hidden_values, value_reduce)], axis=1
    )
    queries = jnp.dot(
        tokens,
        lax.all_gather(query_weight, "seq", axis=0, tiled=True),
        preferred_element_type=jnp.float32,
    ).astype(jnp.bfloat16)
    heads_local = query_weight.shape[1] // key_width
    positions = (
        CTX_DEV * seq_count
        + lax.axis_index("seq") * row_count
        + jnp.arange(4 * row_count, dtype=jnp.int32) % row_count
    )
    wide = lax.all_gather(stacked, "seq", axis=2, tiled=True)
    columns = jnp.arange(wide.shape[2], dtype=jnp.int32)
    block_ids = (
        columns // local_blocks * head_count + lax.axis_index("head")
    ) * local_blocks + columns % local_blocks
    every_query = lax.all_gather(queries, "head", axis=1, tiled=True)
    heads_all = every_query.shape[1] // key_width
    every_set = (
        every_query.reshape(row_count, heads_all, key_width)
        .transpose(1, 0, 2)
        .reshape(heads_all // 4, 4 * row_count, key_width)
    )
    heads_group = heads_all // groups

    def per_set(inputs):
        query_block, set_index = inputs
        group_blocks = lax.dynamic_index_in_dim(
            wide, set_index * 4 // heads_group, 0, keepdims=False
        )
        return attend_blocks(
            query_block,
            group_blocks[:key_width],
            group_blocks[key_width:],
            block_ids,
            positions,
            local_blocks * 8,
        )

    part_max, part_total, part_sum = lax.map(
        per_set, (every_set, jnp.arange(heads_all // 4, dtype=jnp.int32))
    )
    part_max = part_max.reshape(heads_all, 1, row_count)
    part_total = part_total.reshape(heads_all, 1, row_count)
    part_sum = part_sum.reshape(heads_all, 1, row_count, value_width)
    got_sum, got_max, got_total = (
        lax.all_to_all(part_sum, "head", split_axis=0, concat_axis=1, tiled=True),
        lax.all_to_all(part_max, "head", split_axis=0, concat_axis=1, tiled=True),
        lax.all_to_all(part_total, "head", split_axis=0, concat_axis=1, tiled=True),
    )
    top = jnp.max(got_max, axis=1, keepdims=True)
    factor = jnp.exp(got_max - top)
    row_total = jnp.sum(got_total * factor, axis=1)
    weighted = jnp.sum(got_sum * factor[..., None], axis=1)
    attended = (weighted / row_total[..., None]).astype(jnp.bfloat16)
    attended = attended.transpose(1, 0, 2).reshape(row_count, heads_local * value_width)
    partial_out = jnp.dot(
        attended,
        lax.all_gather(output_weight, "seq", axis=1, tiled=True),
        preferred_element_type=jnp.float32,
    )
    return lax.psum_scatter(partial_out, "head", scatter_dimension=1, tiled=True).astype(
        jnp.bfloat16
    )


def solution(mesh):
    in_specs = (
        P("seq", None),
        P(("seq", "head"), None),
        P(("seq", "head"), None),
        P("seq", "head"),
        P("head", "seq"),
        P(),
        P(),
        P(),
        P(),
        P(),
        P(),
    )
    out_specs = P("seq", "head")
    return jax.shard_map(shards, mesh=mesh, in_specs=in_specs, out_specs=out_specs, check_vma=False)
```

profile of v0, /device:TPU:2, one launch (start us, length us, event | category | flops | bytes accessed | tf_op | source)
XLA Modules:
  0.0 492.7 jit_solution(7417791110379844152)
XLA Ops:
  8.0 1.9 collective-permute-start
  10.7 1.9 collective-permute-start.1
  14.3 3.0 fusion.38
  17.3 10.0 %fusion.131 = (f32[1024,4,768]{2,0,1:T(8,128)}, f32[1024,4,768]{2,0,1:T(8,128)}) fusion(f32[1040,4,768]{2,0,1:T(8,128)S(1)} %fusion.38), kind=kLoop, calls=%fused_computation.172 | loop fusion | bytes 50331648 | tf_op jit(solution)/shard_map/slice | solution.py:103
  27.3 11.6 %multiply_reduce_fusion = (f32[64,4,768]{2,0,1:T(8,128)S(1)}, f32[64,4,768]{2,0,1:T(8,128)S(1)}) fusion(f32[16,768]{1,0:T(8,128)S(1)} %get-tuple-element.337, f32[1024,4,768]{2,0,1:T(8,128)} %get-tuple-element.333, f32[16,768]{1,0:T(8,128)S(1)} %get-tuple-element.338, f32[1024,4,768]{2,0,1:T(8,128)} %get-tuple-element.334), kind=kLoop, calls=%fused_computation.47 | loop fusion | flops 12189696 | bytes 26836992 | tf_op jit(solution)/shard_map/reduce_sum | solution.py:26
  38.9 1.8 fusion.37
  40.8 1.3 pad_maximum_fusion
  42.0 2.7 copy.27
  44.8 1.9 fusion.65
  46.7 9.0 %fusion.130 = (f32[1024,4,768]{2,0,1:T(8,128)}, f32[1024,4,768]{2,0,1:T(8,128)}) fusion(f32[1040,4,768]{2,0,1:T(8,128)S(1)} %fusion.65), kind=kLoop, calls=%fused_computation.171 | loop fusion | bytes 50331648 | tf_op jit(solution)/shard_map/slice | solution.py:100
  55.7 11.8 %multiply_reduce_fusion.2 = (f32[64,4,768]{2,0,1:T(8,128)S(1)}, f32[64,4,768]{2,0,1:T(8,128)S(1)}) fusion(f32[16,768]{1,0:T(8,128)S(1)} %get-tuple-element.335, f32[1024,4,768]{2,0,1:T(8,128)} %get-tuple-element.331, f32[16,768]{1,0:T(8,128)S(1)} %get-tuple-element.336, f32[1024,4,768]{2,0,1:T(8,128)} %get-tuple-element.332), kind=kLoop, calls=%fused_computation.49 | loop fusion | flops 12189696 | bytes 26836992 | tf_op jit(solution)/shard_map/reduce_sum | solution.py:26
  67.5 1.8 fusion.36
  70.2 155.4 %all-gather.5.cloned.1.call-done = bf16[2560,3072]{1,0:T(8,128)(2,1)} async-done(((bf16[320,3072]{1,0:T(8,128)(2,1)}), bf16[2560,3072]{1,0:T(8,128)(2,1)}) %all-gather.5.cloned.1.call-update) | async-done | bytes 15728656 | tf_op jit(solution)/shard_map/all_gather | solution.py:110
  225.6 8.6 %convolution_convert_fusion = bf16[128,3072]{1,0:T(8,128)(2,1)} fusion(bf16[128,2560]{1,0:T(8,128)(2,1)S(1)} %copy-done, bf16[2560,3072]{1,0:T(8,128)(2,1)} %all-gather.5.cloned.1.call-done), kind=kOutput, calls=%fused_computation.52 | convolution fusion | flops 2013659136 | bytes 17170432 | tf_op jit(solution)/shard_map/dot_general | solution.py:108
  234.8 35.4 %all-gather.9.cloned.1.call-done = bf16[4,320,512]{1,2,0:T(8,128)(2,1)} async-done(((bf16[4,320,64]{1,2,0:T(8,128)(2,1)}), bf16[4,320,512]{1,2,0:T(8,128)(2,1)}) %all-gather.9.cloned.1.call-update) | async-done | bytes 1310736 | tf_op jit(solution)/shard_map/all_gather | solution.py:119
  270.2 1.7 copy.30
  271.9 26.1 %all-gather.7.cloned.1.call-done = bf16[128,12288]{1,0:T(8,128)(2,1)} async-done(((bf16[128,3072]{1,0:T(8,128)(2,1)}), bf16[128,12288]{1,0:T(8,128)(2,1)}) %all-gather.7.cloned.1.call-update) | async-done | bytes 3145744 | tf_op jit(solution)/shard_map/all_gather | solution.py:124
  298.0 4.6 copy.25
  302.6 5.9 %copy.32 = bf16[64,128,192]{2,1,0:T(8,128)(2,1)} copy(bf16[64,128,192]{1,2,0:T(8,128)(2,1)} %bitcast.97) | data formatting | bytes 6291456
  308.5 66.8 %while.27 = (s32[]{:T(128)}, f32[16,512]{1,0:T(8,128)S(1)}, f32[16,512]{1,0:T(8,128)S(1)}, f32[16,512,128]{2,1,0:T(8,128)}, bf16[16,512,192]{2,1,0:T(8,128)(2,1)...) while((s32[]{:T(128)}, f32[16,512]{1,0:T(8,128)S(1)}, ...), condition=%wide.region_7.8_spmd.clone, body=%wide.region_4.7_spmd.clone.sunk | while | flops 169951248 | bytes 4038029 | solution.py:147
  309.9 1.4 fusion.148
  311.3 1.1 fusion.151
  314.1 1.4 fusion.148
  318.3 1.4 fusion.148
  322.4 1.4 fusion.148
  326.6 1.4 fusion.148
  330.8 1.4 fusion.148
  335.0 1.4 fusion.148
  339.1 1.4 fusion.148
  340.5 1.1 fusion.151
  343.3 1.4 fusion.148
  347.5 1.4 fusion.148
  351.7 1.4 fusion.148
  355.8 1.4 fusion.148
  360.0 1.4 fusion.148
  364.2 1.4 fusion.148
  368.4 1.4 fusion.148
  372.5 1.4 fusion.148
  376.0 5.1 %all-to-all-start.1 = ((f32[64,1,128]{2,1,0:T(1,128)}), f32[64,1,128]{2,1,0:T(1,128)S(1)}, u32[]{:S(2)}, u32[]{:S(2)}) async-start(f32[64,1,128]{2,1,0:T(1,128)} %reshape.132), calls=%async_computation.1 | async-start | bytes 65536 | tf_op jit(solution)/shard_map/all_to_all | solution.py:155
  381.1 1.9 all-to-all-done.1
  383.0 6.3 %all_to_all.54 = f32[64,1,128]{2,1,0:T(1,128)S(1)} all-to-all(f32[64,1,128]{2,1,0:T(1,128)S(1)} %reshape.133), channel_id=1, replica_groups=mesh['seq'=8,'head'=4] {'head'}, dimensions={0} | all-to-all | bytes 65536 | tf_op jit(solution)/shard_map/all_to_all | solution.py:156
  389.3 6.8 %all-to-all-start = ((f32[64,1,128,128]{3,2,1,0:T(8,128)}), f32[64,1,128,128]{3,2,1,0:T(8,128)}, u32[]{:S(2)}, u32[]{:S(2)}) async-start(f32[64,1,128,128]{3,2,1,0:T(8,128)} %bitcast.100), calls=%async_computation | async-start | bytes 8388608 | tf_op jit(solution)/shard_map/all_to_all | solution.py:154
  396.2 46.6 %all-to-all-done = f32[64,1,128,128]{3,2,1,0:T(8,128)} async-done(((f32[64,1,128,128]{3,2,1,0:T(8,128)}), f32[64,1,128,128]{3,2,1,0:T(8,128)}, u32[]{:S(2)}, u32[]{:S(2)}) %all-to-all-start) | async-done | bytes 4194336 | tf_op jit(solution)/shard_map/all_to_all | solution.py:154
  442.7 2.9 multiply_reduce_fusion.4
  446.3 5.8 %all-gather.11.cloned.1.call-done = bf16[2048,2560]{0,1:T(8,128)(2,1)} async-done(((bf16[2048,320]{0,1:T(8,128)(2,1)}), bf16[2048,2560]{0,1:T(8,128)(2,1)}) %all-gather.11.cloned.1.call-update) | async-done | bytes 10485776 | tf_op jit(solution)/shard_map/all_gather | solution.py:166
  452.1 8.7 %fusion.134 = f32[128,2560]{1,0:T(8,128)} fusion(bf16[128,2048]{0,1:T(8,128)(2,1)S(1)} %bitcast.101, bf16[2048,2560]{0,1:T(8,128)(2,1)} %all-gather.11.cloned.1.call-done), kind=kOutput, calls=%fused_computation.175 | convolution fusion | flops 1342177280 | bytes 12320768 | tf_op jit(solution)/shard_map/dot_general | solution.py:164
  460.8 23.7 %reduce-scatter.2.cloned.1.call-done = f32[128,640]{1,0:T(8,128)} async-done(((f32[128,2560]{1,0:T(8,128)}), f32[128,640]{1,0:T(8,128)}) %reduce-scatter.2.cloned.1.call-update) | async-done | bytes 327696 | tf_op jit(solution)/shard_map/reduce_scatter | solution.py:169
  484.5 1.7 convert_element_type.47
  (163 shorter events, 37.5 us)
Async XLA Ops:
  6.5 219.1 %copy-start = (bf16[128,2560]{1,0:T(8,128)(2,1)S(1)}, bf16[128,2560]{1,0:T(8,128)(2,1)}, u32[]{:S(2)}) copy-start(bf16[128,2560]{1,0:T(8,128)(2,1)} %param.13) | copy-start | bytes 1966084
  6.5 219.1 %all-gather.5.cloned.1.call-start = ((), (), s32[]{:S(2)}) async-start(), calls=%async_computation.4 | async-start | bytes 17694720 | tf_op jit(solution)/shard_map/all_gather | solution.py:110
  7.3 262.9 %all-gather.9.cloned.1.call-start = ((), (), s32[]{:S(2)}) async-start(), calls=%async_computation.6 | async-start | bytes 1769472 | tf_op jit(solution)/shard_map/all_gather | solution.py:119
  8.0 32.7 %collective-permute-start = (bf16[16,768]{1,0:T(8,128)(2,1)S(1)}, bf16[16,768]{1,0:T(8,128)(2,1)S(1)}, u32[]{:S(2)}, u32[]{:S(2)}) collective-permute-start(bf16[16,768]{1,0:T(8,128)(2,1)S(1)} %slice.56), channel_id=1, source_target_pairs={{1,0},{2,1},{3,2},{4,3},{5,4},{6,5},{7,6},{8,7},{9,8},{10,9},{11,1... | collective-permute-start | bytes 73736 | tf_op jit(solution)/shard_map/ppermute | solution.py:15
  10.7 3.6 collective-permute-start.1
  27.3 11.6 %copy-start.4 = (bf16[768,128]{1,0:T(8,128)(2,1)S(1)}, bf16[768,128]{1,0:T(8,128)(2,1)}, u32[]{:S(2)}) copy-start(bf16[768,128]{1,0:T(8,128)(2,1)} %param.23) | copy-start | bytes 589828
  38.9 1.8 copy-start.1
  40.8 4.0 copy-start.2
  55.7 11.8 %copy-start.3 = (bf16[768,192]{0,1:T(8,128)(2,1)S(1)}, bf16[768,192]{0,1:T(8,128)(2,1)}, u32[]{:S(2)}) copy-start(bf16[768,192]{0,1:T(8,128)(2,1)} %param.20) | copy-start | bytes 884740
  70.1 227.9 %all-gather.7.cloned.1.call-start = ((), (), s32[]{:S(2)}) async-start(), calls=%async_computation.5 | async-start | bytes 3932160 | tf_op jit(solution)/shard_map/all_gather | solution.py:124
  234.2 217.9 %all-gather.11.cloned.1.call-start = ((), (), s32[]{:S(2)}) async-start(), calls=%async_computation.7 | async-start | bytes 11796480 | tf_op jit(solution)/shard_map/all_gather | solution.py:166
  376.0 7.1 %all-to-all-start.1 = ((f32[64,1,128]{2,1,0:T(1,128)}), f32[64,1,128]{2,1,0:T(1,128)S(1)}, u32[]{:S(2)}, u32[]{:S(2)}) async-start(f32[64,1,128]{2,1,0:T(1,128)} %reshape.132), calls=%async_computation.1 | async-start | bytes 65536 | tf_op jit(solution)/shard_map/all_to_all | solution.py:155
  389.3 53.4 %all-to-all-start = ((f32[64,1,128,128]{3,2,1,0:T(8,128)}), f32[64,1,128,128]{3,2,1,0:T(8,128)}, u32[]{:S(2)}, u32[]{:S(2)}) async-start(f32[64,1,128,128]{3,2,1,0:T(8,128)} %bitcast.100), calls=%async_computation | async-start | bytes 8388608 | tf_op jit(solution)/shard_map/all_to_all | solution.py:154
  396.1 88.4 %reduce-scatter.2.cloned.1.call-start = ((), (), s32[]{:S(2)}) async-start(), calls=%async_computation.8 | async-start | bytes 1638400 | tf_op jit(solution)/shard_map/reduce_scatter | solution.py:169
Sparse Core Ops, SparseCore 0:
  9.5 216.0 all-gather.4
  227.8 42.3 all-gather.8
  271.8 26.1 all-gather.6
  300.0 151.9 all-gather.10
  460.9 23.5 reduce-scatter.1
where the time goes:
time: 497 us; the launch traced here: 493 us
  waiting for transfers between devices  296 us (60%)
  matrix products  64.5 us (13%)
  local copies, waits for them, and re-layouts  50.5 us (10%)
  other arithmetic  34 us (7%)
  starting transfers between devices  15.9 us (3%)
  between operations  13.3 us (3%)
  loops' own time  12 us (2%)
  blocking collectives  6.29 us (1%)
    all_gather x1, waiting for transfers between devices, shards(): lax.all_gather(query_weight, 'seq', axis=0, tiled=True)  155 us
    all_to_all x1, waiting for transfers between devices, shards(): lax.all_to_all(part_sum, 'head', split_axis=0, concat_axis=1, tiled=True)  46.6 us
    all_gather x1, waiting for transfers between devices, shards(): wide = lax.all_gather(stacked, 'seq', axis=2, tiled=True)  35.4 us
    all_gather x1, waiting for transfers between devices, shards(): every_query = lax.all_gather(queries, 'head', axis=1, tiled=True)  26.1 us
    reduce_scatter x1, waiting for transfers between devices, shards(): lax.psum_scatter(partial_out, 'head', scatter_dimension=1, tiled=True)  23.7 us
    reduce_sum x2, other arithmetic, half_sums(): return jnp.sum(shaped * mix_half[None, :, None, :], axis=1)  23.3 us
    dot_general x16, matrix products, add_block(): jnp.dot(query_block, key_block, preferred_element_type=jnp.float32)  21.8 us
    dot_general x16, matrix products, add_block(): lax.dot_general(exponent.astype(jnp.bfloat16), value_block, (((1,), (1,))...  16.8 us
  transfers between devices with their start and end apart: 9, of which 7 were waited for; matrix products, arithmetic and copies ran while one was open for 28% of the time, Pallas kernels for 0%

commit v1 on v0

v1 whole, which is shorter than its diff:
```python
import jax
import jax.numpy as jnp
import numpy as np
from jax import lax
from jax.experimental import pallas as pl
from jax.experimental.pallas import tpu as pltpu
from jax.sharding import Mesh
from jax.sharding import PartitionSpec as P

G = 4
BLK = 32
STRIDE = 16
LANES = 128
OUTER = 4
VMEM_LIMIT = 56 * 1024 * 1024


def round_up(value, unit):
    return -(-value // unit) * unit


def swap(block, axis, bit):
    return lax.ppermute(block, axis, [(i, i ^ bit) for i in range(lax.axis_size(axis))])


def window_of(group, width):
    low = group * width // LANES * LANES
    return low, round_up((group + 1) * width, LANES) - low, group * width - low


def compress_one(raw_ref, edge_ref, expand_ref, mix_ref, reduce_ref, sorted_ref, hidden_ref, groups):
    width, units = expand_ref.shape
    tokens = raw_ref.shape[0]
    rows = 8 * STRIDE
    chunks = tokens // rows
    blocks = tokens // STRIDE
    to = lax.broadcasted_iota(jnp.int32, (rows, rows), 0)
    come = lax.broadcasted_iota(jnp.int32, (rows, rows), 1)
    order = (come == (to % 8) * STRIDE + to // 8).astype(jnp.bfloat16)
    for chunk in range(chunks):
        piece = slice(chunk * rows, (chunk + 1) * rows)
        sorted_ref[piece, :] = jnp.dot(
            order, raw_ref[piece, :], preferred_element_type=jnp.float32
        ).astype(jnp.bfloat16)
    tile = 256 if units % 256 == 0 else units
    for group in range(groups):
        low, span, offset = window_of(group, width)
        parts = []
        if offset:
            parts.append(jnp.zeros((offset, units), jnp.bfloat16))
        parts.append(expand_ref[...])
        if span - offset - width:
            parts.append(jnp.zeros((span - offset - width, units), jnp.bfloat16))
        expand = jnp.concatenate(parts, axis=0) if len(parts) > 1 else parts[0]
        for start in range(0, units, tile):
            lanes = slice(start, start + tile)
            weight = expand[:, lanes]
            projected = jnp.dot(
                sorted_ref[:, low : low + span], weight, preferred_element_type=jnp.float32
            ).reshape(chunks, STRIDE, 8, tile)
            mix_low = mix_ref[:STRIDE, lanes][None, :, None, :]
            mix_high = mix_ref[STRIDE:, lanes]
            first = jnp.sum(projected * mix_low, axis=1).reshape(blocks, tile)
            second = jnp.sum(projected * mix_high[None, :, None, :], axis=1).reshape(blocks, tile)
            edge = jnp.dot(edge_ref[:, low : low + span], weight, preferred_element_type=jnp.float32)
            edge = jnp.sum(edge * mix_high, axis=0, keepdims=True)
            hidden = first + jnp.concatenate([second[1:], edge], axis=0)
            half = 0.5 * hidden
            activated = half + half * lax.erf(hidden * np.float32(2.0**-0.5))
            hidden_ref[group * blocks : (group + 1) * blocks, lanes] = activated.astype(jnp.bfloat16)
    return jnp.dot(hidden_ref[...], reduce_ref[...], preferred_element_type=jnp.float32).astype(
        jnp.bfloat16
    )


def compress_kernel(
    raw_keys, raw_values, edge_keys, edge_values, key_expand, key_mix, key_reduce,
    value_expand, value_mix, value_reduce, packed, sorted_keys, sorted_values, hidden,
):
    groups, blocks, _ = packed.shape
    key_width = key_expand.shape[0]
    value_start = round_up(key_width, LANES)
    keys = compress_one(
        raw_keys, edge_keys, key_expand, key_mix, key_reduce, sorted_keys, hidden, groups
    )
    values = compress_one(
        raw_values, edge_values, value_expand, value_mix, value_reduce, sorted_values, hidden, groups
    )
    for group in range(groups):
        rows = slice(group * blocks, (group + 1) * blocks)
        packed[group, :, :key_width] = keys[rows]
        packed[group, :, key_width:value_start] = jnp.zeros(
            (blocks, value_start - key_width), jnp.bfloat16
        )
        packed[group, :, value_start:] = values[rows]


def compress(raw_keys, raw_values, edge_keys, edge_values, *weights):
    key_expand, _, _, value_expand, _, _ = weights
    units = key_expand.shape[1]
    tokens = raw_keys.shape[0]
    blocks = tokens // STRIDE
    width = round_up(key_expand.shape[0], LANES) + value_expand.shape[0]
    flops = 2 * tokens * units * (raw_keys.shape[1] + raw_values.shape[1])
    return pl.pallas_call(
        compress_kernel,
        out_shape=jax.ShapeDtypeStruct((G, blocks, width), jnp.bfloat16),
        scratch_shapes=[
            pltpu.VMEM(raw_keys.shape, jnp.bfloat16),
            pltpu.VMEM(raw_values.shape, jnp.bfloat16),
            pltpu.VMEM((G * blocks, units), jnp.bfloat16),
        ],
        compiler_params=pltpu.CompilerParams(vmem_limit_bytes=VMEM_LIMIT),
        cost_estimate=pl.CostEstimate(
            flops=flops * 6, bytes_accessed=4 * raw_keys.size, transcendentals=0
        ),
        name="compress",
    )(raw_keys, raw_values, edge_keys, edge_values, *weights)


def attend(own, other, weight_own, weight_other, packed, limits, places, key_width, masked):
    rows = own.shape[0]
    heads = weight_own.shape[1] // key_width
    value_start = round_up(key_width, LANES)
    value_width = packed.shape[1] - value_start
    columns = packed.shape[0]
    factor = np.float32(key_width**-0.5 * np.log2(np.e))
    tile = min(256, rows)

    def kernel(own_ref, other_ref, wown_ref, wother_ref, kv_ref, limit_ref, place_ref, out_ref, query_ref):
        query_ref[...] = jnp.dot(
            own_ref[...], wown_ref[...], preferred_element_type=jnp.float32
        ) + jnp.dot(other_ref[...], wother_ref[...], preferred_element_type=jnp.float32)
        keys = kv_ref[:, :key_width]
        values = kv_ref[:, value_start:]
        for head in range(heads):
            for start in range(0, rows, tile):
                query = query_ref[
                    start : start + tile, head * key_width : (head + 1) * key_width
                ].astype(jnp.bfloat16)
                scores = lax.dot_general(
                    query, keys, (((1,), (1,)), ((), ())), preferred_element_type=jnp.float32
                )
                pieces = []
                for low, high, hide in masked:
                    piece = scores[:, low:high]
                    if hide:
                        visible = limit_ref[:, low:high] <= place_ref[start : start + tile, :]
                        piece = jnp.where(visible, piece, -jnp.inf)
                    pieces.append(piece)
                scores = jnp.concatenate(pieces, axis=1) if len(pieces) > 1 else pieces[0]
                top = jnp.max(scores, axis=1, keepdims=True)
                exponent = jnp.exp2((scores - top) * factor)
                total = jnp.sum(exponent, axis=1, keepdims=True)
                numerator = jnp.dot(
                    exponent.astype(jnp.bfloat16), values, preferred_element_type=jnp.float32
                )
                out_ref[
                    start : start + tile, head * value_width : (head + 1) * value_width
                ] = (numerator / total).astype(jnp.bfloat16)

    flops = 2 * rows * heads * (columns * (key_width + value_width) + own.shape[1] * 2 * key_width)
    return pl.pallas_call(
        kernel,
        out_shape=jax.ShapeDtypeStruct((rows, heads * value_width), jnp.bfloat16),
        scratch_shapes=[pltpu.VMEM((rows, heads * key_width), jnp.float32)],
        compiler_params=pltpu.CompilerParams(vmem_limit_bytes=VMEM_LIMIT),
        cost_estimate=pl.CostEstimate(
            flops=flops * 3,
            bytes_accessed=2 * (own.size * 2 + weight_own.size * 2 + packed.size),
            transcendentals=rows * heads * columns,
        ),
        name="attend",
    )(own, other, weight_own, weight_other, packed, limits, places)


def gather_line(block, axis, dim):
    count = lax.axis_size(axis)
    if count != 4:
        return lax.all_gather(block, axis, axis=dim, tiled=True)
    me = lax.axis_index(axis)
    far = swap(block, axis, 2)
    up = lax.ppermute(block, axis, [(i, i + 1) for i in range(3)])
    down = lax.ppermute(block, axis, [(i + 1, i) for i in range(3)])
    passed = lax.ppermute(far, axis, [(1, 0), (2, 3)])
    lower = jnp.where(me == 0, passed, up)
    upper = jnp.where(me == 3, passed, down)
    size = block.shape[dim]
    shape = list(block.shape)
    shape[dim] = count * size
    out = jnp.zeros(shape, block.dtype)
    for piece, place in ((block, me), (lower, (me + 3) % 4), (upper, (me + 1) % 4), (far, me ^ 2)):
        out = lax.dynamic_update_slice_in_dim(out, piece, place * size, dim)
    return out


def gather_pair(block, axis):
    if lax.axis_size(axis) != 2:
        return lax.all_gather(block, axis, axis=0)
    other = swap(block, axis, 1)
    first = lax.axis_index(axis) == 0
    return jnp.stack([jnp.where(first, block, other), jnp.where(first, other, block)])


def shards(
    tokens, raw_keys, raw_values, query_weight, output_weight,
    key_expand, key_mix, key_reduce, value_expand, value_mix, value_reduce,
):
    outer, inner, heads_axis = (lax.axis_size(name) for name in ("outer", "inner", "head"))
    z, y, h = (lax.axis_index(name) for name in ("outer", "inner", "head"))
    key_width, value_width = key_expand.shape[0], value_expand.shape[0]
    row_count, model = tokens.shape
    devices = outer * inner * heads_axis
    blocks = raw_keys.shape[0] // STRIDE
    context = raw_keys.shape[0] * devices - row_count * outer * inner
    part = query_weight.shape[0]
    heads_here = query_weight.shape[1] // key_width // outer
    chunk_count = 2 if heads_here % 2 == 0 else 1
    heads_chunk = heads_here // chunk_count
    fast = inner == 2 and outer == 4 and heads_axis == 4

    split = query_weight.reshape(part, chunk_count, outer, heads_chunk * key_width)
    weights = []
    for chunk in range(chunk_count):
        sent = split[:, chunk].transpose(1, 0, 2)
        weights.append(lax.all_to_all(sent, "outer", split_axis=0, concat_axis=0, tiled=True))

    edge = jnp.concatenate([raw_keys[:STRIDE], raw_values[:STRIDE]], axis=1)
    edge = lax.ppermute(
        edge, ("outer", "inner", "head"), [(i + 1, i) for i in range(devices - 1)]
    )
    edge_keys, edge_values = edge[:, : raw_keys.shape[1]], edge[:, raw_keys.shape[1] :]

    quarter = row_count // heads_axis if fast else row_count
    mine = lax.dynamic_slice_in_dim(tokens, h * quarter, quarter, 0) if fast else tokens
    mine = mine.reshape(quarter, outer, inner, part)
    if inner == 2:
        ordered = [lax.dynamic_index_in_dim(mine, y ^ step, 2, False) for step in range(2)]
    else:
        ordered = [mine[:, :, step] for step in range(inner)]
    mine = jnp.concatenate([piece.reshape(quarter, outer * part) for piece in ordered], axis=1)
    gathered = gather_line(mine, "outer", 0)
    if fast:
        across = swap(gathered, "head", 2)
        rows = outer * quarter
        every = jnp.zeros((heads_axis * rows, model), tokens.dtype)
        pair_here = jnp.concatenate([gathered, across], axis=0)
        pair_there = swap(pair_here, "head", 1)
        for piece, place in (
            (pair_here[:rows], h), (pair_here[rows:], h ^ 2),
            (pair_there[:rows], h ^ 1), (pair_there[rows:], h ^ 3),
        ):
            every = lax.dynamic_update_slice(every, piece, (place * rows, 0))
    else:
        every = gathered
    shape = (every.shape[0] // (outer * quarter), outer, quarter)
    places = (
        context
        + (lax.broadcasted_iota(jnp.int32, shape, 1) * inner + y) * row_count
        + lax.broadcasted_iota(jnp.int32, shape, 0) * quarter
        + lax.broadcasted_iota(jnp.int32, shape, 2)
    ).reshape(-1, 1)

    packed = compress(
        raw_keys, raw_values, edge_keys, edge_values,
        key_expand, key_mix, key_reduce, value_expand, value_mix, value_reduce,
    )
    if heads_axis != G:
        packed = jnp.broadcast_to(packed[:, None], (G, heads_axis // G, *packed.shape[1:]))
        packed = packed.reshape(heads_axis, blocks, -1)
    packed = lax.all_to_all(packed, "head", split_axis=0, concat_axis=0, tiled=True)
    packed = gather_line(packed.reshape(heads_axis * blocks, -1), "outer", 0)
    packed = gather_pair(packed, "inner").reshape(devices * blocks, -1)
    ids = np.arange(devices * blocks).reshape(outer, inner, heads_axis, blocks)
    ids = ids.transpose(1, 0, 2, 3).reshape(-1)
    limits = STRIDE * ids + BLK - 1
    hidden = [bool((limits[i : i + LANES] > context).any()) for i in range(0, len(ids), LANES)]
    masked, start = [], 0
    for i in range(1, len(hidden) + 1):
        if i == len(hidden) or hidden[i] != hidden[start]:
            masked.append((start * LANES, min(i * LANES, len(ids)), hidden[start]))
            start = i
    limits = jnp.asarray(limits[None, :], jnp.int32)

    if inner == 2:
        out_weights = [output_weight, swap(output_weight, "inner", 1)]
    else:
        out_weights = [lax.all_gather(output_weight, "inner", axis=1, tiled=True)]

    total = None
    for chunk in range(chunk_count):
        weight = weights[chunk].reshape(outer * part, heads_chunk * key_width)
        if inner == 2:
            weight_own, weight_other = weight, swap(weight, "inner", 1)
            split_at = outer * part
        else:
            weight = lax.all_gather(weight, "inner", axis=0, tiled=True)
            split_at = inner // 2 * outer * part
            weight_own, weight_other = weight[:split_at], weight[split_at:]
        attended = attend(
            every[:, :split_at], every[:, split_at:], weight_own, weight_other,
            packed, limits, places, key_width, masked,
        )
        attended = gather_line(attended, "outer", 1)
        width = attended.shape[1]
        product = jnp.concatenate(
            [
                jnp.dot(
                    attended, weight[chunk * width : (chunk + 1) * width],
                    preferred_element_type=jnp.float32,
                )
                for weight in out_weights
            ],
            axis=1,
        )
        total = product if total is None else total + product

    columns = total.shape[1]
    if fast:
        x, c = h // 2, h % 2
        total = total.reshape(heads_axis, 2, 2, quarter, columns)
        keep = lax.dynamic_index_in_dim(total, c, 2, False)
        send = lax.dynamic_index_in_dim(total, 1 - c, 2, False).astype(jnp.bfloat16)
        total = keep + swap(send, "head", 1).astype(jnp.float32)
        keep = lax.dynamic_index_in_dim(total, x, 1, False)
        send = lax.dynamic_index_in_dim(total, 1 - x, 1, False).astype(jnp.bfloat16)
        total = keep + swap(send, "head", 2).astype(jnp.float32)
        result = total.astype(jnp.bfloat16).reshape(row_count, columns)
        first, second = result[:, : columns // 2], result[:, columns // 2 :]
        result = jnp.concatenate(
            [jnp.where(y == 0, first, second), jnp.where(y == 0, second, first)], axis=1
        )
        route = [
            ((a * inner + b) * heads_axis + k, (k * inner + b) * heads_axis + a)
            for a in range(outer) for b in range(inner) for k in range(heads_axis)
        ]
        return lax.ppermute(result, ("outer", "inner", "head"), route)
    total = lax.psum_scatter(total, "head", scatter_dimension=0, tiled=True).astype(jnp.bfloat16)
    total = lax.all_gather(total, "head", axis=0, tiled=True)
    total = lax.all_to_all(
        total.reshape(outer, row_count, columns), "outer", split_axis=0, concat_axis=0, tiled=True
    )
    total = total.transpose(1, 0, 2).reshape(row_count, model)
    return lax.dynamic_slice_in_dim(total, h * (model // heads_axis), model // heads_axis, 1)


def solution(mesh):
    seq_count, head_count = mesh.shape["seq"], mesh.shape["head"]
    inner = seq_count // OUTER
    finer = Mesh(
        mesh.devices.reshape(OUTER, inner, head_count), ("outer", "inner", "head")
    )
    seq = ("outer", "inner")
    in_specs = (
        P(seq, None),
        P((*seq, "head"), None),
        P((*seq, "head"), None),
        P(seq, "head"),
        P("head", seq),
        P(), P(), P(), P(), P(), P(),
    )
    return jax.shard_map(
        shards, mesh=finer, in_specs=in_specs, out_specs=P(seq, "head"), check_vma=False
    )
```

time: 497 us -> 224 us (0.45)
  waiting for transfers between devices: 296 us -> 98.5 us
  matrix products: 64.5 us -> 5.07 us
  starting transfers between devices: 15.9 us -> 55.7 us
  Pallas kernels: 0 us -> 25.4 us
  other arithmetic: 34 us -> 8.63 us
  local copies, waits for them, and re-layouts: 50.5 us -> 28.6 us
  between operations: 13.3 us -> 0.59 us
  loops' own time: 12 us -> 0 us
  blocking collectives: 6.29 us -> 0 us
    all_gather x4 -> x0, waiting for transfers between devices: 223 us -> none  [the longest x1 155 us: shards(): lax.all_gather(query_weight, 'seq', axis=0, tiled=True)]
    ppermute x2 -> x26, waiting for transfers between devices: 0.01 us -> 92.3 us  [the longest x12 63.9 us: swap(): lax.ppermute(block, axis, [(i, i ^ bit) for i in range(lax.axis_size(axis...]
    dot_general x38 -> x4, matrix products: 64.5 us -> 5.07 us  [shards(): jnp.dot(attended, weight[chunk * width:(chunk + 1) * width], preferred_el...]
    all_to_all x2 -> x3, waiting for transfers between devices: 48.5 us -> 6.18 us  [the longest x2 6.15 us: shards(): lax.all_to_all(sent, 'outer', split_axis=0, concat_axis=0, tiled=True)]
    ppermute x2 -> x26, starting transfers between devices: 3.82 us -> 40.6 us  [the longest x4 14.5 us: gather_line(): up = lax.ppermute(block, axis, [(i, i + 1) for i in range(3)])]
    reduce_sum x20 -> x0, other arithmetic: 29.4 us -> none  [the longest x2 23.3 us: half_sums(): return jnp.sum(shaped * mix_half[None, :, None, :], axis=1)]
    pallas_call x0 -> x3, Pallas kernels: none -> 25.4 us  [the longest x2 16.8 us: attend(): pl.pallas_call(kernel, out_shape=jax.ShapeDtypeStruct((rows, heads * valu...]
    reduce_scatter x1 -> x0, waiting for transfers between devices: 23.7 us -> none  [shards(): lax.psum_scatter(partial_out, 'head', scatter_dimension=1, tiled=True)]
  transfers between devices with their start and end apart: 9 -> 29, of which waited for: 7 -> 14; matrix products, arithmetic and copies ran while one was open for 28% -> 14% of each run, Pallas kernels for 0% -> 11%
where the time goes in v1:
time: 224 us; the launch traced here: 222 us
  waiting for transfers between devices  98.5 us (44%)
  starting transfers between devices  55.7 us (25%)
  local copies, waits for them, and re-layouts  28.6 us (13%)
  Pallas kernels  25.4 us (11%)
  other arithmetic  8.63 us (4%)
  matrix products  5.07 us (2%)
    ppermute x12, waiting for transfers between devices, swap(): lax.ppermute(block, axis, [(i, i ^ bit) for i in range(lax.axis_size(axis...  63.9 us
    pallas_call x2, Pallas kernels, attend(): pl.pallas_call(kernel, out_shape=jax.ShapeDtypeStruct((rows, heads * valu...  16.8 us
    ppermute x4, starting transfers between devices, gather_line(): up = lax.ppermute(block, axis, [(i, i + 1) for i in range(3)])  14.5 us
    all_to_all x2, starting transfers between devices, shards(): lax.all_to_all(sent, 'outer', split_axis=0, concat_axis=0, tiled=True)  11.5 us
    ppermute x12, starting transfers between devices, swap(): lax.ppermute(block, axis, [(i, i ^ bit) for i in range(lax.axis_size(axis...  10.3 us
    ppermute x4, waiting for transfers between devices, gather_line(): passed = lax.ppermute(far, axis, [(1, 0), (2, 3)])  10.1 us
    ppermute x1, waiting for transfers between devices, shards(): return lax.ppermute(result, ('outer', 'inner', 'head'), route)  9.61 us
    unnamed x27, local copies, waits for them, and re-layouts  9.41 us
  transfers between devices with their start and end apart: 29, of which 14 were waited for; matrix products, arithmetic and copies ran while one was open for 14% of the time, Pallas kernels for 11%

profile of v1, /device:TPU:2, one launch (start us, length us, event | category | flops | bytes accessed | tf_op | source)
XLA Modules:
  0.0 222.5 jit_solution(10712531093884662113)
XLA Ops:
  1.3 1.3 dynamic-slice_reduce_fusion
  4.1 2.6 %collective-permute-start = (bf16[32,2560]{1,0:T(8,128)(2,1)}, bf16[32,2560]{1,0:T(8,128)(2,1)}, u32[]{:S(2)}, u32[]{:S(2)}) collective-permute-start(bf16[32,2560]{1,0:T(8,128)(2,1)} %constant_dynamic-update-slice_fusion.10), channel_id=1, source_target_pairs={{0,16},{8,24},{16,0},{24,8},{1,17},{9,25},{17,1},{25,9},{2,18},{10... | collective-permute-start | bytes 491528 | tf_op jit(solution)/shard_map/ppermute | solution.py:23
  6.7 4.1 %collective-permute-start.2 = (bf16[32,2560]{1,0:T(8,128)(2,1)}, bf16[32,2560]{1,0:T(8,128)(2,1)}, u32[]{:S(2)}, u32[]{:S(2)}) collective-permute-start(bf16[32,2560]{1,0:T(8,128)(2,1)} %constant_dynamic-update-slice_fusion.10), channel_id=1, source_target_pairs={{0,8},{8,16},{16,24},{1,9},{9,17},{17,25},{2,10},{10,18},{18,26},{... | collective-permute-start | bytes 491528 | tf_op jit(solution)/shard_map/ppermute | solution.py:183
  10.9 1.3 collective-permute-start.3
  12.2 1.9 collective-permute-start.7
  14.1 3.7 %reshape.89 = bf16[320,2,4,384]{3,2,1,0:T(4,128)(2,1)S(1)} reshape(bf16[320,3072]{1,0:T(8,128)(2,1)} %param.15) | data formatting | bytes 3932160 | tf_op jit(solution)/shard_map/reshape | solution.py:222
  18.8 2.0 fusion.12
  20.8 1.9 copy.27.key_reduce
  23.9 8.5 %compress.1 = bf16[4,64,384]{2,1,0:T(8,128)(2,1)} custom-call(bf16[1024,768]{1,0:T(8,128)(2,1)} %raw_keys.1, bf16[1024,512]{1,0:T(8,128)(2,1)} %raw_values.1, bf16[16,768]{1,0:T(8,128)(2,1)} %slice.71.edge_keys, bf16[16,512]{1,0:T(8,128)(2,1)} %slice.72.edge_values, bf16[192,768]{1,0:T(8,128)(2,1)} %key_expand.1, f32[32,768]{1,0:T(8,128)} %key_mix.1, ...), custom_call_target="tpu_custom_call" | custom-call | flops 12079595520 | bytes 3145728 | tf_op jit(solution)/shard_map/compress/pallas_call | solution.py:105
  32.4 3.5 %all-to-all-start.1 = ((bf16[4,64,384]{2,1,0:T(8,128)(2,1)}), bf16[4,64,384]{2,1,0:T(8,128)(2,1)S(1)}, u32[]{:S(2)}, u32[]{:S(2)}) async-start(bf16[4,64,384]{2,1,0:T(8,128)(2,1)} %compress.1), calls=%async_computation.1 | async-start | bytes 393216 | tf_op jit(solution)/shard_map/all_to_all | solution.py:271
  36.0 1.3 collective-permute-start.1
  39.5 7.1 %all-to-all-start = ((bf16[4,320,384]{2,1,0:T(8,128)(2,1)}), bf16[4,320,384]{2,1,0:T(8,128)(2,1)}, u32[]{:S(2)}, u32[]{:S(2)}) async-start(bf16[4,320,384]{2,1,0:T(8,128)(2,1)} %bitcast.36), calls=%async_computation | async-start | bytes 1966080 | tf_op jit(solution)/shard_map/all_to_all | solution.py:226
  46.7 3.0 %collective-permute-start.8 = (bf16[256,384]{1,0:T(8,128)(2,1)S(1)}, bf16[256,384]{1,0:T(8,128)(2,1)S(1)}, u32[]{:S(2)}, u32[]{:S(2)}) collective-permute-start(bf16[256,384]{1,0:T(8,128)(2,1)S(1)} %bitcast.40), channel_id=1, source_target_pairs={{0,16},{8,24},{16,0},{24,8},{1,17},{9,25},{17,1},{25,9},{2,18},{10... | collective-permute-start | bytes 589832 | tf_op jit(solution)/shard_map/ppermute | solution.py:23
  49.7 3.2 %collective-permute-start.10 = (bf16[256,384]{1,0:T(8,128)(2,1)S(1)}, bf16[256,384]{1,0:T(8,128)(2,1)S(1)}, u32[]{:S(2)}, u32[]{:S(2)}) collective-permute-start(bf16[256,384]{1,0:T(8,128)(2,1)S(1)} %bitcast.41), channel_id=1, source_target_pairs={{0,8},{8,16},{16,24},{1,9},{9,17},{17,25},{2,10},{10,18},{18,26},{... | collective-permute-start | bytes 589832 | tf_op jit(solution)/shard_map/ppermute | solution.py:183
  53.0 1.3 collective-permute-start.11
  56.2 24.2 %collective-permute-done.8 = bf16[256,384]{1,0:T(8,128)(2,1)S(1)} collective-permute-done((bf16[256,384]{1,0:T(8,128)(2,1)S(1)}, bf16[256,384]{1,0:T(8,128)(2,1)S(1)}, u32[]{:S(2)}, u32[]{:S(2)}) %collective-permute-start.8) | collective-permute-done | bytes 196640 | tf_op jit(solution)/shard_map/ppermute | solution.py:23
  80.4 1.3 collective-permute-start.9
  85.1 3.4 %collective-permute-done.9 = bf16[256,384]{1,0:T(8,128)(2,1)S(1)} collective-permute-done((bf16[256,384]{1,0:T(8,128)(2,1)S(1)}, bf16[256,384]{1,0:T(8,128)(2,1)S(1)}, u32[]{:S(2)}, u32[]{:S(2)}) %collective-permute-start.9) | collective-permute-done | bytes 196640 | tf_op jit(solution)/shard_map/ppermute | solution.py:185
  90.9 4.4 %all-to-all-start.2 = ((bf16[4,320,384]{2,1,0:T(8,128)(2,1)}), bf16[4,320,384]{2,1,0:T(8,128)(2,1)}, u32[]{:S(2)}, u32[]{:S(2)}) async-start(bf16[4,320,384]{2,1,0:T(8,128)(2,1)} %bitcast.35), calls=%async_computation.2 | async-start | bytes 1966080 | tf_op jit(solution)/shard_map/all_to_all | solution.py:226
  95.3 3.4 %collective-permute-done.4 = bf16[128,2560]{1,0:T(8,128)(2,1)S(1)} collective-permute-done((bf16[128,2560]{1,0:T(8,128)(2,1)S(1)}, bf16[128,2560]{1,0:T(8,128)(2,1)S(1)}, u32[]{:S(2)}, u32[]{:S(2)}) %collective-permute-start.4) | collective-permute-done | bytes 655392 | tf_op jit(solution)/shard_map/ppermute | solution.py:23
  98.7 1.2 pad_maximum_fusion.1
  103.3 5.6 %collective-permute-done.12 = bf16[1024,384]{1,0:T(8,128)(2,1)} collective-permute-done((bf16[1024,384]{1,0:T(8,128)(2,1)}, bf16[1024,384]{1,0:T(8,128)(2,1)}, u32[]{:S(2)}, u32[]{:S(2)}) %collective-permute-start.12) | collective-permute-done | bytes 786464 | tf_op jit(solution)/shard_map/ppermute | solution.py:23
  108.8 1.5 select_bitcast_fusion.1
  110.4 1.4 pad_maximum_fusion
  112.0 6.1 %all-to-all-done.2 = bf16[4,320,384]{2,1,0:T(8,128)(2,1)} async-done(((bf16[4,320,384]{2,1,0:T(8,128)(2,1)}), bf16[4,320,384]{2,1,0:T(8,128)(2,1)}, u32[]{:S(2)}, u32[]{:S(2)}) %all-to-all-start.2) | async-done | bytes 983072 | tf_op jit(solution)/shard_map/all_to_all | solution.py:226
  118.2 1.7 collective-permute-start.18
  121.0 1.1 slice_dynamic-update-slice_fusion
  122.2 1.7 fusion.11
  123.9 12.8 %collective-permute-done.6.wother_ref = bf16[1280,384]{1,0:T(8,128)(2,1)} collective-permute-done((bf16[1280,384]{1,0:T(8,128)(2,1)}, bf16[1280,384]{1,0:T(8,128)(2,1)}, u32[]{:S(2)}, u32[]{:S(2)}) %collective-permute-start.6) | collective-permute-done | bytes 983072 | tf_op jit(solution)/shard_map/ppermute | solution.py:23
  136.7 8.4 %attend.2 = bf16[512,256]{1,0:T(8,128)(2,1)} custom-call(bf16[512,1280]{1,0:T(8,128)(2,1)} %get-tuple-element.8.own_ref, bf16[512,1280]{1,0:T(8,128)(2,1)} %get-tuple-element.7.other_ref, bf16[1280,384]{1,0:T(8,128)(2,1)} %bitcast.2.wown_ref, bf16[1280,384]{1,0:T(8,128)(2,1)} %collective-permute-done.6.wother_ref, bf16[2048,384]{1,0:T(8,128)(2,1)} %bitcast.37, ...), custom_call_target="tpu_custom_call" | custom-call | flops 7046430720 | bytes 6160384 | tf_op jit(solution)/shard_map/attend/pallas_call | solution.py:163
  145.2 9.0 %collective-permute-done.18.wother_ref = bf16[1280,384]{1,0:T(8,128)(2,1)S(1)} collective-permute-done((bf16[1280,384]{1,0:T(8,128)(2,1)}, bf16[1280,384]{1,0:T(8,128)(2,1)S(1)}, u32[]{:S(2)}, u32[]{:S(2)}) %collective-permute-start.18) | collective-permute-done | bytes 983072 | tf_op jit(solution)/shard_map/ppermute | solution.py:23
  155.2 8.4 %attend.3 = bf16[512,256]{1,0:T(8,128)(2,1)} custom-call(bf16[512,1280]{1,0:T(8,128)(2,1)} %get-tuple-element.8.own_ref, bf16[512,1280]{1,0:T(8,128)(2,1)} %get-tuple-element.7.other_ref, bf16[1280,384]{1,0:T(8,128)(2,1)} %bitcast.11.wown_ref, bf16[1280,384]{1,0:T(8,128)(2,1)} %copy-done.10, bf16[2048,384]{1,0:T(8,128)(2,1)} %bitcast.38, ...), custom_call_target="tpu_custom_call" | custom-call | flops 7046430720 | bytes 6160384 | tf_op jit(solution)/shard_map/attend/pallas_call | solution.py:163
  163.6 1.7 collective-permute-start.15
  165.3 1.3 collective-permute-start.14
  167.3 5.4 %collective-permute-start.21 = (bf16[512,256]{1,0:T(8,128)(2,1)}, bf16[512,256]{1,0:T(8,128)(2,1)S(1)}, u32[]{:S(2)}, u32[]{:S(2)}) collective-permute-start(bf16[512,256]{1,0:T(8,128)(2,1)} %attend.3), channel_id=1, source_target_pairs={{0,8},{8,16},{16,24},{1,9},{9,17},{17,25},{2,10},{10,18},{18,26},{... | collective-permute-start | bytes 786440 | tf_op jit(solution)/shard_map/ppermute | solution.py:183
  172.9 1.8 collective-permute-done.19
  174.7 1.3 collective-permute-start.20
  176.2 1.3 collective-permute-start.16
  177.5 1.5 collective-permute-start.22
  179.1 6.7 %collective-permute-done.20 = bf16[512,256]{1,0:T(8,128)(2,1)S(1)} collective-permute-done((bf16[512,256]{1,0:T(8,128)(2,1)S(1)}, bf16[512,256]{1,0:T(8,128)(2,1)S(1)}, u32[]{:S(2)}, u32[]{:S(2)}) %collective-permute-start.20) | collective-permute-done | bytes 262176 | tf_op jit(solution)/shard_map/ppermute | solution.py:185
  185.9 5.5 %collective-permute-done.16 = bf16[512,256]{1,0:T(8,128)(2,1)S(1)} collective-permute-done((bf16[512,256]{1,0:T(8,128)(2,1)S(1)}, bf16[512,256]{1,0:T(8,128)(2,1)S(1)}, u32[]{:S(2)}, u32[]{:S(2)}) %collective-permute-start.16) | collective-permute-done | bytes 262176 | tf_op jit(solution)/shard_map/ppermute | solution.py:184
  191.5 3.1 %collective-permute-done.22 = bf16[512,256]{1,0:T(8,128)(2,1)S(1)} collective-permute-done((bf16[512,256]{1,0:T(8,128)(2,1)S(1)}, bf16[512,256]{1,0:T(8,128)(2,1)S(1)}, u32[]{:S(2)}, u32[]{:S(2)}) %collective-permute-start.22) | collective-permute-done | bytes 262176 | tf_op jit(solution)/shard_map/ppermute | solution.py:184
  196.3 1.8 fusion
  198.1 1.8 fusion.2
  200.6 1.6 collective-permute-done.23
  203.1 5.5 %collective-permute-done.24 = bf16[4,32,640]{2,1,0:T(8,128)(2,1)S(1)} collective-permute-done((bf16[4,32,640]{2,1,0:T(8,128)(2,1)S(1)}, bf16[4,32,640]{2,1,0:T(8,128)(2,1)S(1)}, u32[]{:S(2)}, u32[]{:S(2)}) %collective-permute-start.24) | collective-permute-done | bytes 163872 | tf_op jit(solution)/shard_map/ppermute | solution.py:23
  208.8 3.4 %collective-permute-start.25 = (bf16[128,640]{1,0:T(8,128)(2,1)S(1)}, bf16[128,640]{1,0:T(8,128)(2,1)S(1)}, u32[]{:S(2)}, u32[]{:S(2)}) collective-permute-start(bf16[128,640]{1,0:T(8,128)(2,1)S(1)} %pad_maximum_fusion.2), channel_id=1, source_target_pairs={{0,0},{1,8},{2,16},{3,24},{4,4},{5,12},{6,20},{7,28},{8,1},{9,9},{... | collective-permute-start | bytes 491528 | tf_op jit(solution)/shard_map/ppermute | solution.py:337
  212.2 9.6 %collective-permute-done.25 = bf16[128,640]{1,0:T(8,128)(2,1)S(1)} collective-permute-done((bf16[128,640]{1,0:T(8,128)(2,1)S(1)}, bf16[128,640]{1,0:T(8,128)(2,1)S(1)}, u32[]{:S(2)}, u32[]{:S(2)}) %collective-permute-start.25) | collective-permute-done | bytes 163872 | tf_op jit(solution)/shard_map/ppermute | solution.py:337
  (98 shorter events, 25.8 us)
Async XLA Ops:
  0.0 1.1 copy-start
  0.0 12.2 %slice-start = ((bf16[1024,768]{1,0:T(8,128)(2,1)}), bf16[16,768]{1,0:T(8,128)(2,1)S(1)}, s32[]{:S(2)}) async-start(bf16[1024,768]{1,0:T(8,128)(2,1)} %raw_keys.1), calls=%async_computation.3 | async-start | bytes 49152 | tf_op jit(solution)/shard_map/slice | solution.py:228
  0.0 12.2 %slice-start.1 = ((bf16[1024,512]{1,0:T(8,128)(2,1)}), bf16[16,512]{1,0:T(8,128)(2,1)S(1)}, s32[]{:S(2)}) async-start(bf16[1024,512]{1,0:T(8,128)(2,1)} %raw_values.1), calls=%async_computation.4 | async-start | bytes 32768 | tf_op jit(solution)/shard_map/slice | solution.py:228
  4.1 31.8 %collective-permute-start = (bf16[32,2560]{1,0:T(8,128)(2,1)}, bf16[32,2560]{1,0:T(8,128)(2,1)}, u32[]{:S(2)}, u32[]{:S(2)}) collective-permute-start(bf16[32,2560]{1,0:T(8,128)(2,1)} %constant_dynamic-update-slice_fusion.10), channel_id=1, source_target_pairs={{0,16},{8,24},{16,0},{24,8},{1,17},{9,25},{17,1},{25,9},{2,18},{10... | collective-permute-start | bytes 491528 | tf_op jit(solution)/shard_map/ppermute | solution.py:23
  6.7 46.2 %collective-permute-start.2 = (bf16[32,2560]{1,0:T(8,128)(2,1)}, bf16[32,2560]{1,0:T(8,128)(2,1)}, u32[]{:S(2)}, u32[]{:S(2)}) collective-permute-start(bf16[32,2560]{1,0:T(8,128)(2,1)} %constant_dynamic-update-slice_fusion.10), channel_id=1, source_target_pairs={{0,8},{8,16},{16,24},{1,9},{9,17},{17,25},{2,10},{10,18},{18,26},{... | collective-permute-start | bytes 491528 | tf_op jit(solution)/shard_map/ppermute | solution.py:183
  10.9 44.4 %collective-permute-start.3 = (bf16[32,2560]{1,0:T(8,128)(2,1)}, bf16[32,2560]{1,0:T(8,128)(2,1)}, u32[]{:S(2)}, u32[]{:S(2)}) collective-permute-start(bf16[32,2560]{1,0:T(8,128)(2,1)} %constant_dynamic-update-slice_fusion.10), channel_id=1, source_target_pairs={{8,0},{16,8},{24,16},{9,1},{17,9},{25,17},{10,2},{18,10},{26,18},{... | collective-permute-start | bytes 491528 | tf_op jit(solution)/shard_map/ppermute | solution.py:184
  12.2 10.5 %collective-permute-start.7 = (bf16[16,1280]{1,0:T(8,128)(2,1)S(1)}, bf16[16,1280]{1,0:T(8,128)(2,1)S(1)}, u32[]{:S(2)}, u32[]{:S(2)}) collective-permute-start(bf16[16,1280]{1,0:T(8,128)(2,1)S(1)} %pad_maximum_fusion.3), channel_id=1, source_target_pairs={{1,0},{2,1},{3,2},{4,3},{5,4},{6,5},{7,6},{8,7},{9,8},{10,9},{11,1... | collective-permute-start | bytes 122888 | tf_op jit(solution)/shard_map/ppermute | solution.py:229
  23.9 13.4 %copy-start.4 = (bf16[320,1,4,384]{3,2,1,0:T(4,128)(2,1)S(1)}, bf16[320,1,4,384]{3,2,1,0:T(4,128)(2,1)}, u32[]{:S(2)}) copy-start(bf16[320,1,4,384]{3,2,1,0:T(4,128)(2,1)} %get-tuple-element.10) | copy-start | bytes 2949124
  32.4 6.0 %copy-start.3 = (bf16[320,1,4,384]{3,2,1,0:T(4,128)(2,1)S(1)}, bf16[320,1,4,384]{3,2,1,0:T(4,128)(2,1)}, u32[]{:S(2)}) copy-start(bf16[320,1,4,384]{3,2,1,0:T(4,128)(2,1)} %get-tuple-element.9) | copy-start | bytes 2949124
  32.4 7.1 %all-to-all-start.1 = ((bf16[4,64,384]{2,1,0:T(8,128)(2,1)}), bf16[4,64,384]{2,1,0:T(8,128)(2,1)S(1)}, u32[]{:S(2)}, u32[]{:S(2)}) async-start(bf16[4,64,384]{2,1,0:T(8,128)(2,1)} %compress.1), calls=%async_computation.1 | async-start | bytes 393216 | tf_op jit(solution)/shard_map/all_to_all | solution.py:271
  36.0 18.3 %collective-permute-start.1 = (bf16[32,2560]{1,0:T(8,128)(2,1)}, bf16[32,2560]{1,0:T(8,128)(2,1)}, u32[]{:S(2)}, u32[]{:S(2)}) collective-permute-start(bf16[32,2560]{1,0:T(8,128)(2,1)} %collective-permute-done), channel_id=1, source_target_pairs={{8,0},{16,24},{9,1},{17,25},{10,2},{18,26},{11,3},{19,27},{12,4},{... | collective-permute-start | bytes 491528 | tf_op jit(solution)/shard_map/ppermute | solution.py:185
  39.5 51.4 %all-to-all-start = ((bf16[4,320,384]{2,1,0:T(8,128)(2,1)}), bf16[4,320,384]{2,1,0:T(8,128)(2,1)}, u32[]{:S(2)}, u32[]{:S(2)}) async-start(bf16[4,320,384]{2,1,0:T(8,128)(2,1)} %bitcast.36), calls=%async_computation | async-start | bytes 1966080 | tf_op jit(solution)/shard_map/all_to_all | solution.py:226
  46.7 33.8 %collective-permute-start.8 = (bf16[256,384]{1,0:T(8,128)(2,1)S(1)}, bf16[256,384]{1,0:T(8,128)(2,1)S(1)}, u32[]{:S(2)}, u32[]{:S(2)}) collective-permute-start(bf16[256,384]{1,0:T(8,128)(2,1)S(1)} %bitcast.40), channel_id=1, source_target_pairs={{0,16},{8,24},{16,0},{24,8},{1,17},{9,25},{17,1},{25,9},{2,18},{10... | collective-permute-start | bytes 589832 | tf_op jit(solution)/shard_map/ppermute | solution.py:23
  49.7 35.4 %collective-permute-start.10 = (bf16[256,384]{1,0:T(8,128)(2,1)S(1)}, bf16[256,384]{1,0:T(8,128)(2,1)S(1)}, u32[]{:S(2)}, u32[]{:S(2)}) collective-permute-start(bf16[256,384]{1,0:T(8,128)(2,1)S(1)} %bitcast.41), channel_id=1, source_target_pairs={{0,8},{8,16},{16,24},{1,9},{9,17},{17,25},{2,10},{10,18},{18,26},{... | collective-permute-start | bytes 589832 | tf_op jit(solution)/shard_map/ppermute | solution.py:183
  53.0 36.2 %collective-permute-start.11 = (bf16[256,384]{1,0:T(8,128)(2,1)S(1)}, bf16[256,384]{1,0:T(8,128)(2,1)S(1)}, u32[]{:S(2)}, u32[]{:S(2)}) collective-permute-start(bf16[256,384]{1,0:T(8,128)(2,1)S(1)} %bitcast.42), channel_id=1, source_target_pairs={{8,0},{16,8},{24,16},{9,1},{17,9},{25,17},{10,2},{18,10},{26,18},{... | collective-permute-start | bytes 589832 | tf_op jit(solution)/shard_map/ppermute | solution.py:184
  80.4 8.1 %collective-permute-start.9 = (bf16[256,384]{1,0:T(8,128)(2,1)S(1)}, bf16[256,384]{1,0:T(8,128)(2,1)S(1)}, u32[]{:S(2)}, u32[]{:S(2)}) collective-permute-start(bf16[256,384]{1,0:T(8,128)(2,1)S(1)} %collective-permute-done.8), channel_id=1, source_target_pairs={{8,0},{16,24},{9,1},{17,25},{10,2},{18,26},{11,3},{19,27},{12,4},{... | collective-permute-start | bytes 589832 | tf_op jit(solution)/shard_map/ppermute | solution.py:185
  82.7 16.1 %copy-start.1 = (bf16[128,2560]{1,0:T(8,128)(2,1)}, bf16[128,2560]{1,0:T(8,128)(2,1)S(1)}, u32[]{:S(2)}) copy-start(bf16[128,2560]{1,0:T(8,128)(2,1)S(1)} %constant_dynamic-update-slice_fusion.8) | copy-start | bytes 1966084
  82.7 16.1 %collective-permute-start.4 = (bf16[128,2560]{1,0:T(8,128)(2,1)S(1)}, bf16[128,2560]{1,0:T(8,128)(2,1)S(1)}, u32[]{:S(2)}, u32[]{:S(2)}) collective-permute-start(bf16[128,2560]{1,0:T(8,128)(2,1)S(1)} %constant_dynamic-update-slice_fusion.8), channel_id=1, source_target_pairs={{0,2},{1,3},{2,0},{3,1},{4,6},{5,7},{6,4},{7,5},{8,10},{9,11},{10,... | collective-permute-start | bytes 1966088 | tf_op jit(solution)/shard_map/ppermute | solution.py:23
  90.6 18.2 %collective-permute-start.12 = (bf16[1024,384]{1,0:T(8,128)(2,1)}, bf16[1024,384]{1,0:T(8,128)(2,1)}, u32[]{:S(2)}, u32[]{:S(2)}) collective-permute-start(bf16[1024,384]{1,0:T(8,128)(2,1)} %constant_dynamic-update-slice_fusion.4), channel_id=1, source_target_pairs={{0,4},{4,0},{1,5},{5,1},{2,6},{6,2},{3,7},{7,3},{8,12},{12,8},{9,1... | collective-permute-start | bytes 2359304 | tf_op jit(solution)/shard_map/ppermute | solution.py:23
  90.9 27.3 %all-to-all-start.2 = ((bf16[4,320,384]{2,1,0:T(8,128)(2,1)}), bf16[4,320,384]{2,1,0:T(8,128)(2,1)}, u32[]{:S(2)}, u32[]{:S(2)}) async-start(bf16[4,320,384]{2,1,0:T(8,128)(2,1)} %bitcast.35), calls=%async_computation.2 | async-start | bytes 1966080 | tf_op jit(solution)/shard_map/all_to_all | solution.py:226
  98.7 1.3 copy-start.5
  100.0 19.9 %collective-permute-start.5 = (bf16[256,2560]{1,0:T(8,128)(2,1)}, bf16[256,2560]{1,0:T(8,128)(2,1)}, u32[]{:S(2)}, u32[]{:S(2)}) collective-permute-start(bf16[256,2560]{1,0:T(8,128)(2,1)} %pad_maximum_fusion.1), channel_id=1, source_target_pairs={{0,1},{1,0},{2,3},{3,2},{4,5},{5,4},{6,7},{7,6},{8,9},{9,8},{10,11... | collective-permute-start | bytes 3932168 | tf_op jit(solution)/shard_map/ppermute | solution.py:23
  101.1 1.1 copy-start.2
  102.2 1.1 copy-start.6
  111.7 25.0 %collective-permute-start.6 = (bf16[1280,384]{1,0:T(8,128)(2,1)}, bf16[1280,384]{1,0:T(8,128)(2,1)}, u32[]{:S(2)}, u32[]{:S(2)}) collective-permute-start(bf16[1280,384]{1,0:T(8,128)(2,1)} %bitcast.2.wown_ref), channel_id=1, source_target_pairs={{0,4},{4,0},{1,5},{5,1},{2,6},{6,2},{3,7},{7,3},{8,12},{12,8},{9,1... | collective-permute-start | bytes 2949128 | tf_op jit(solution)/shard_map/ppermute | solution.py:23
  118.2 36.0 %collective-permute-start.18 = (bf16[1280,384]{1,0:T(8,128)(2,1)}, bf16[1280,384]{1,0:T(8,128)(2,1)S(1)}, u32[]{:S(2)}, u32[]{:S(2)}) collective-permute-start(bf16[1280,384]{1,0:T(8,128)(2,1)} %bitcast.11.wown_ref), channel_id=1, source_target_pairs={{0,4},{4,0},{1,5},{5,1},{2,6},{6,2},{3,7},{7,3},{8,12},{12,8},{9,1... | collective-permute-start | bytes 2949128 | tf_op jit(solution)/shard_map/ppermute | solution.py:23
  145.1 18.4 %copy-start.7 = (bf16[512,256]{1,0:T(8,128)(2,1)S(1)}, bf16[512,256]{1,0:T(8,128)(2,1)}, u32[]{:S(2)}) copy-start(bf16[512,256]{1,0:T(8,128)(2,1)} %attend.2) | copy-start | bytes 786436
  145.1 21.5 %copy-start.9 = (bf16[2048,320]{0,1:T(8,128)(2,1)S(1)}, bf16[2048,320]{0,1:T(8,128)(2,1)}, u32[]{:S(2)}) copy-start(bf16[2048,320]{0,1:T(8,128)(2,1)} %param.16) | copy-start | bytes 3932164
  145.2 20.2 %collective-permute-start.13 = (bf16[512,256]{1,0:T(8,128)(2,1)}, bf16[512,256]{1,0:T(8,128)(2,1)S(1)}, u32[]{:S(2)}, u32[]{:S(2)}) collective-permute-start(bf16[512,256]{1,0:T(8,128)(2,1)} %attend.2), channel_id=1, source_target_pairs={{0,16},{8,24},{16,0},{24,8},{1,17},{9,25},{17,1},{25,9},{2,18},{10... | collective-permute-start | bytes 786440 | tf_op jit(solution)/shard_map/ppermute | solution.py:23
  154.2 1.0 copy-start.10
  163.6 11.1 %collective-permute-start.19 = (bf16[512,256]{1,0:T(8,128)(2,1)}, bf16[512,256]{1,0:T(8,128)(2,1)S(1)}, u32[]{:S(2)}, u32[]{:S(2)}) collective-permute-start(bf16[512,256]{1,0:T(8,128)(2,1)} %attend.3), channel_id=1, source_target_pairs={{0,16},{8,24},{16,0},{24,8},{1,17},{9,25},{17,1},{25,9},{2,18},{10... | collective-permute-start | bytes 786440 | tf_op jit(solution)/shard_map/ppermute | solution.py:23
  163.6 12.6 %collective-permute-start.15 = (bf16[512,256]{1,0:T(8,128)(2,1)S(1)}, bf16[512,256]{1,0:T(8,128)(2,1)S(1)}, u32[]{:S(2)}, u32[]{:S(2)}) collective-permute-start(bf16[512,256]{1,0:T(8,128)(2,1)S(1)} %copy-done.7), channel_id=1, source_target_pairs={{0,8},{8,16},{16,24},{1,9},{9,17},{17,25},{2,10},{10,18},{18,26},{... | collective-permute-start | bytes 786440 | tf_op jit(solution)/shard_map/ppermute | solution.py:183
  165.3 12.2 %collective-permute-start.14 = (bf16[512,256]{1,0:T(8,128)(2,1)S(1)}, bf16[512,256]{1,0:T(8,128)(2,1)S(1)}, u32[]{:S(2)}, u32[]{:S(2)}) collective-permute-start(bf16[512,256]{1,0:T(8,128)(2,1)S(1)} %collective-permute-done.13), channel_id=1, source_target_pairs={{8,0},{16,24},{9,1},{17,25},{10,2},{18,26},{11,3},{19,27},{12,4},{... | collective-permute-start | bytes 786440 | tf_op jit(solution)/shard_map/ppermute | solution.py:185
  166.7 29.6 %collective-permute-start.17 = (bf16[2048,320]{0,1:T(8,128)(2,1)S(1)}, bf16[2048,320]{0,1:T(8,128)(2,1)}, u32[]{:S(2)}, u32[]{:S(2)}) collective-permute-start(bf16[2048,320]{0,1:T(8,128)(2,1)S(1)} %copy-done.9), channel_id=1, source_target_pairs={{0,4},{4,0},{1,5},{5,1},{2,6},{6,2},{3,7},{7,3},{8,12},{12,8},{9,1... | collective-permute-start | bytes 3932168 | tf_op jit(solution)/shard_map/ppermute | solution.py:23
  167.3 8.8 %copy-start.8 = (bf16[512,256]{1,0:T(8,128)(2,1)S(1)}, bf16[512,256]{1,0:T(8,128)(2,1)}, u32[]{:S(2)}) copy-start(bf16[512,256]{1,0:T(8,128)(2,1)} %attend.3) | copy-start | bytes 786436
  167.3 11.8 %collective-permute-start.21 = (bf16[512,256]{1,0:T(8,128)(2,1)}, bf16[512,256]{1,0:T(8,128)(2,1)S(1)}, u32[]{:S(2)}, u32[]{:S(2)}) collective-permute-start(bf16[512,256]{1,0:T(8,128)(2,1)} %attend.3), channel_id=1, source_target_pairs={{0,8},{8,16},{16,24},{1,9},{9,17},{17,25},{2,10},{10,18},{18,26},{... | collective-permute-start | bytes 786440 | tf_op jit(solution)/shard_map/ppermute | solution.py:183
  174.7 11.1 %collective-permute-start.20 = (bf16[512,256]{1,0:T(8,128)(2,1)S(1)}, bf16[512,256]{1,0:T(8,128)(2,1)S(1)}, u32[]{:S(2)}, u32[]{:S(2)}) collective-permute-start(bf16[512,256]{1,0:T(8,128)(2,1)S(1)} %collective-permute-done.19), channel_id=1, source_target_pairs={{8,0},{16,24},{9,1},{17,25},{10,2},{18,26},{11,3},{19,27},{12,4},{... | collective-permute-start | bytes 786440 | tf_op jit(solution)/shard_map/ppermute | solution.py:185
  176.2 15.3 %collective-permute-start.16 = (bf16[512,256]{1,0:T(8,128)(2,1)S(1)}, bf16[512,256]{1,0:T(8,128)(2,1)S(1)}, u32[]{:S(2)}, u32[]{:S(2)}) collective-permute-start(bf16[512,256]{1,0:T(8,128)(2,1)S(1)} %copy-done.7), channel_id=1, source_target_pairs={{8,0},{16,8},{24,16},{9,1},{17,9},{25,17},{10,2},{18,10},{26,18},{... | collective-permute-start | bytes 786440 | tf_op jit(solution)/shard_map/ppermute | solution.py:184
  177.5 17.1 %collective-permute-start.22 = (bf16[512,256]{1,0:T(8,128)(2,1)S(1)}, bf16[512,256]{1,0:T(8,128)(2,1)S(1)}, u32[]{:S(2)}, u32[]{:S(2)}) collective-permute-start(bf16[512,256]{1,0:T(8,128)(2,1)S(1)} %copy-done.8), channel_id=1, source_target_pairs={{8,0},{16,8},{24,16},{9,1},{17,9},{25,17},{10,2},{18,10},{26,18},{... | collective-permute-start | bytes 786440 | tf_op jit(solution)/shard_map/ppermute | solution.py:184
  200.5 1.7 collective-permute-start.23
  202.3 6.3 %collective-permute-start.24 = (bf16[4,32,640]{2,1,0:T(8,128)(2,1)S(1)}, bf16[4,32,640]{2,1,0:T(8,128)(2,1)S(1)}, u32[]{:S(2)}, u32[]{:S(2)}) collective-permute-start(bf16[4,32,640]{2,1,0:T(8,128)(2,1)S(1)} %fusion.10), channel_id=1, source_target_pairs={{0,2},{1,3},{2,0},{3,1},{4,6},{5,7},{6,4},{7,5},{8,10},{9,11},{10,... | collective-permute-start | bytes 491528 | tf_op jit(solution)/shard_map/ppermute | solution.py:23
  208.8 13.0 %collective-permute-start.25 = (bf16[128,640]{1,0:T(8,128)(2,1)S(1)}, bf16[128,640]{1,0:T(8,128)(2,1)S(1)}, u32[]{:S(2)}, u32[]{:S(2)}) collective-permute-start(bf16[128,640]{1,0:T(8,128)(2,1)S(1)} %pad_maximum_fusion.2), channel_id=1, source_target_pairs={{0,0},{1,8},{2,16},{3,24},{4,4},{5,12},{6,20},{7,28},{8,1},{9,9},{... | collective-permute-start | bytes 491528 | tf_op jit(solution)/shard_map/ppermute | solution.py:337

commit v2 on v1

--- a/solution.py
+++ b/solution.py
@@ -118,60 +118,160 @@
     )(raw_keys, raw_values, edge_keys, edge_values, *weights)
 
 
-def attend(own, other, weight_own, weight_other, packed, limits, places, key_width, masked):
-    rows = own.shape[0]
-    heads = weight_own.shape[1] // key_width
+def project(pieces, weights):
+    part, depth = pieces[0].shape
+    rows = part * len(pieces)
+    shares, share, columns = weights[0].shape
+
+    def kernel(*refs):
+        piece_refs = refs[: len(pieces)]
+        weight_refs = refs[len(pieces) : -2]
+        out_ref, all_ref = refs[-2:]
+        for index, weight_ref in enumerate(weight_refs):
+            for owner in range(shares):
+                start = (owner * len(weights) + index) * share
+                all_ref[start : start + share, :] = weight_ref[owner]
+        for index, piece in enumerate(piece_refs):
+            out_ref[index * part : (index + 1) * part, :] = jnp.dot(
+                piece[...], all_ref[...], preferred_element_type=jnp.float32
+            ).astype(jnp.bfloat16)
+
+    return pl.pallas_call(
+        kernel,
+        out_shape=jax.ShapeDtypeStruct((rows, columns), jnp.bfloat16),
+        scratch_shapes=[pltpu.VMEM((depth, columns), jnp.bfloat16)],
+        compiler_params=pltpu.CompilerParams(vmem_limit_bytes=VMEM_LIMIT),
+        cost_estimate=pl.CostEstimate(
+            flops=2 * rows * depth * columns, bytes_accessed=2 * rows * depth, transcendentals=0
+        ),
+        name="project",
+    )(*pieces, *weights)
+
+
+def attend(here, queries, head, packed, limits, places, key_width, masked, layout):
+    rows_each = queries[0].shape[0]
+    rows = rows_each * len(queries)
     value_start = round_up(key_width, LANES)
     value_width = packed.shape[1] - value_start
     columns = packed.shape[0]
     factor = np.float32(key_width**-0.5 * np.log2(np.e))
-    tile = min(256, rows)
-
-    def kernel(own_ref, other_ref, wown_ref, wother_ref, kv_ref, limit_ref, place_ref, out_ref, query_ref):
-        query_ref[...] = jnp.dot(
-            own_ref[...], wown_ref[...], preferred_element_type=jnp.float32
-        ) + jnp.dot(other_ref[...], wother_ref[...], preferred_element_type=jnp.float32)
+    tile = min(256, rows_each)
+    unit, outputs, sends = layout
+
+    def kernel(here_ref, *refs):
+        query_refs = refs[: len(queries)]
+        kv_ref, limit_ref, place_ref = refs[len(queries) : len(queries) + 3]
+        out_refs = refs[len(queries) + 3 :]
         keys = kv_ref[:, :key_width]
         values = kv_ref[:, value_start:]
-        for head in range(heads):
-            for start in range(0, rows, tile):
-                query = query_ref[
-                    start : start + tile, head * key_width : (head + 1) * key_width
-                ].astype(jnp.bfloat16)
-                scores = lax.dot_general(
-                    query, keys, (((1,), (1,)), ((), ())), preferred_element_type=jnp.float32
-                )
-                pieces = []
-                for low, high, hide in masked:
-                    piece = scores[:, low:high]
-                    if hide:
-                        visible = limit_ref[:, low:high] <= place_ref[start : start + tile, :]
-                        piece = jnp.where(visible, piece, -jnp.inf)
-                    pieces.append(piece)
-                scores = jnp.concatenate(pieces, axis=1) if len(pieces) > 1 else pieces[0]
-                top = jnp.max(scores, axis=1, keepdims=True)
-                exponent = jnp.exp2((scores - top) * factor)
-                total = jnp.sum(exponent, axis=1, keepdims=True)
-                numerator = jnp.dot(
-                    exponent.astype(jnp.bfloat16), values, preferred_element_type=jnp.float32
-                )
-                out_ref[
-                    start : start + tile, head * value_width : (head + 1) * value_width
-                ] = (numerator / total).astype(jnp.bfloat16)
-
-    flops = 2 * rows * heads * (columns * (key_width + value_width) + own.shape[1] * 2 * key_width)
+        for start in range(0, rows, tile):
+            from_ref, at = query_refs[start // rows_each], start % rows_each
+            query = from_ref[at : at + tile, head * key_width : (head + 1) * key_width]
+            scores = lax.dot_general(
+                query, keys, (((1,), (1,)), ((), ())), preferred_element_type=jnp.float32
+            )
+            pieces = []
+            for low, high, hide in masked:
+                piece = scores[:, low:high]
+                if hide:
+                    visible = limit_ref[:, low:high] <= place_ref[start : start + tile, :]
+                    piece = jnp.where(visible, piece, -jnp.inf)
+                pieces.append(piece)
+            scores = jnp.concatenate(pieces, axis=1) if len(pieces) > 1 else pieces[0]
+            top = jnp.max(scores, axis=1, keepdims=True)
+            exponent = jnp.exp2((scores - top) * factor)
+            total = jnp.sum(exponent, axis=1, keepdims=True)
+            numerator = jnp.dot(
+                exponent.astype(jnp.bfloat16), values, preferred_element_type=jnp.float32
+            )
+            done = (numerator / total).astype(jnp.bfloat16)
+            for low in range(0, tile, unit):
+                which, where = sends((start + low) // unit, here_ref[0], here_ref[1])
+                if not isinstance(where, int):
+                    where = pl.multiple_of(where, unit)
+                out_refs[which][pl.ds(where, unit), :] = done[low : low + unit]
+
+    shape = jax.ShapeDtypeStruct((rows // outputs, value_width), jnp.bfloat16)
     return pl.pallas_call(
         kernel,
-        out_shape=jax.ShapeDtypeStruct((rows, heads * value_width), jnp.bfloat16),
-        scratch_shapes=[pltpu.VMEM((rows, heads * key_width), jnp.float32)],
+        out_shape=(shape,) * outputs,
+        in_specs=[pl.BlockSpec(memory_space=pltpu.SMEM)]
+        + [pl.BlockSpec(memory_space=pltpu.VMEM)] * (len(queries) + 3),
         compiler_params=pltpu.CompilerParams(vmem_limit_bytes=VMEM_LIMIT),
         cost_estimate=pl.CostEstimate(
-            flops=flops * 3,
-            bytes_accessed=2 * (own.size * 2 + weight_own.size * 2 + packed.size),
-            transcendentals=rows * heads * columns,
+            flops=2 * rows * columns * (key_width + value_width),
+            bytes_accessed=2 * packed.size,
+            transcendentals=0,
         ),
         name="attend",
-    )(own, other, weight_own, weight_other, packed, limits, places)
+    )(here, *queries, packed, limits, places)
+
+
+def expel(place, pieces, weights, before, chunk, chunks, shape):
+    rows, width = pieces[0].shape
+    depth, step, single = 4 * width, weights[0].shape[0], width // 2
+    last = shape is not None
+
+    def kernel(place_ref, *refs):
+        own, up, down, passed, far = refs[:5]
+        weight_refs = refs[5 : 5 + len(weights)]
+        rest = refs[5 + len(weights) :]
+        before_refs, outs = rest[: len(before)], rest[len(before) :]
+        z, core, y = place_ref[0], place_ref[1] & 1, place_ref[2]
+        lower = jnp.where(z == 0, passed[...], up[...])
+        upper = jnp.where(z == 3, passed[...], down[...])
+        for side, weight in enumerate(weight_refs):
+            lanes = slice(side * step, (side + 1) * step)
+            total = before_refs[0][:, lanes] if before else None
+            for block, at in (
+                (own[...], z), (lower, (z + 3) & 3), (upper, (z + 1) & 3), (far[...], z ^ 2)
+            ):
+                starts = [((at * 2 + inner) * chunks + chunk) * single for inner in (y, 1 - y)]
+                both = [weight[:, pl.ds(pl.multiple_of(start, single), single)] for start in starts]
+                product = lax.dot_general(
+                    block, jnp.concatenate(both, axis=1), (((1,), (1,)), ((), ())),
+                    preferred_element_type=jnp.float32,
+                )
+                total = product if total is None else total + product
+            if not last:
+                outs[0][:, lanes] = total
+                continue
+            keep_ref, send_ref, hold_ref = outs
+            hold_ref[...] = total.reshape(hold_ref.shape)
+            keep_ref[:, :, :, lanes] = hold_ref[:, :, pl.ds(core, 1)][:, :, 0]
+            send_ref[:, :, :, lanes] = hold_ref[:, :, pl.ds(1 - core, 1)][:, :, 0].astype(jnp.bfloat16)
+
+    columns = step * len(weights)
+    if last:
+        groups, quarter = shape
+        out_shape = (
+            jax.ShapeDtypeStruct((groups, 2, quarter, columns), jnp.float32),
+            jax.ShapeDtypeStruct((groups, 2, quarter, columns), jnp.bfloat16),
+        )
+        scratch = [pltpu.VMEM((groups, 2, 2, quarter, step), jnp.float32)]
+    else:
+        out_shape, scratch = jax.ShapeDtypeStruct((rows, columns), jnp.float32), []
+    count = len(pieces) + len(weights) + len(before)
+    return pl.pallas_call(
+        kernel,
+        out_shape=out_shape,
+        in_specs=[pl.BlockSpec(memory_space=pltpu.SMEM)]
+        + [pl.BlockSpec(memory_space=pltpu.VMEM)] * count,
+        scratch_shapes=scratch,
+        compiler_params=pltpu.CompilerParams(vmem_limit_bytes=VMEM_LIMIT),
+        cost_estimate=pl.CostEstimate(
+            flops=2 * rows * depth * columns, bytes_accessed=2 * depth * columns, transcendentals=0
+        ),
+        name="expel",
+    )(place, *pieces, *weights, *before)
+
+
+def line_pieces(block, axis):
+    far = swap(block, axis, 2)
+    up = lax.ppermute(block, axis, [(i, i + 1) for i in range(3)])
+    down = lax.ppermute(block, axis, [(i + 1, i) for i in range(3)])
+    passed = lax.ppermute(far, axis, [(1, 0), (2, 3)])
+    return block, up, down, passed, far
 
 
 def gather_line(block, axis, dim):
@@ -179,10 +279,7 @@
     if count != 4:
         return lax.all_gather(block, axis, axis=dim, tiled=True)
     me = lax.axis_index(axis)
-    far = swap(block, axis, 2)
-    up = lax.ppermute(block, axis, [(i, i + 1) for i in range(3)])
-    down = lax.ppermute(block, axis, [(i + 1, i) for i in range(3)])
-    passed = lax.ppermute(far, axis, [(1, 0), (2, 3)])
+    block, up, down, passed, far = line_pieces(block, axis)
     lower = jnp.where(me == 0, passed, up)
     upper = jnp.where(me == 3, passed, down)
     size = block.shape[dim]
@@ -214,16 +311,20 @@
     blocks = raw_keys.shape[0] // STRIDE
     context = raw_keys.shape[0] * devices - row_count * outer * inner
     part = query_weight.shape[0]
-    heads_here = query_weight.shape[1] // key_width // outer
-    chunk_count = 2 if heads_here % 2 == 0 else 1
-    heads_chunk = heads_here // chunk_count
     fast = inner == 2 and outer == 4 and heads_axis == 4
 
-    split = query_weight.reshape(part, chunk_count, outer, heads_chunk * key_width)
-    weights = []
-    for chunk in range(chunk_count):
-        sent = split[:, chunk].transpose(1, 0, 2)
-        weights.append(lax.all_to_all(sent, "outer", split_axis=0, concat_axis=0, tiled=True))
+    seq_axes = ("outer", "inner") if fast else "outer"
+    shares = outer * inner if fast else outer
+    share = query_weight.shape[1] // shares
+    halves = 2 if fast and part % 32 == 0 else 1
+    weight = []
+    for half in range(halves):
+        rows = slice(half * part // halves, (half + 1) * part // halves)
+        sent = jnp.stack([query_weight[rows, i * share : (i + 1) * share] for i in range(shares)])
+        weight.append(lax.all_to_all(sent, seq_axes, split_axis=0, concat_axis=0, tiled=True))
+    if not fast:
+        weight = lax.all_gather(weight[0], "inner", axis=1).reshape(model, share)
+    heads_here = share // key_width
 
     edge = jnp.concatenate([raw_keys[:STRIDE], raw_values[:STRIDE]], axis=1)
     edge = lax.ppermute(
@@ -231,97 +332,109 @@
     )
     edge_keys, edge_values = edge[:, : raw_keys.shape[1]], edge[:, raw_keys.shape[1] :]
 
-    quarter = row_count // heads_axis if fast else row_count
-    mine = lax.dynamic_slice_in_dim(tokens, h * quarter, quarter, 0) if fast else tokens
-    mine = mine.reshape(quarter, outer, inner, part)
-    if inner == 2:
-        ordered = [lax.dynamic_index_in_dim(mine, y ^ step, 2, False) for step in range(2)]
+    if fast:
+        quarter = row_count // heads_axis
+        mine = lax.dynamic_slice_in_dim(tokens, h * quarter, quarter, 0)
+        mine, up, down, passed, far = line_pieces(mine, "outer")
+        first = jnp.concatenate([mine, far], axis=0)
+        second = jnp.concatenate([jnp.where(z == 0, passed, up), jnp.where(z == 3, passed, down)], axis=0)
+        first = jnp.concatenate([first, swap(first, "inner", 1)], axis=0)
+        second = jnp.concatenate([second, swap(second, "head", 2)], axis=0)
+        pieces = [first, second, swap(first, "head", 2), swap(second, "inner", 1)]
+        steps = [
+            (0, 0, 0), (3, 0, 0), (0, 1, 0), (3, 1, 0), (1, 0, 0), (2, 0, 0), (1, 0, 2), (2, 0, 2),
+            (0, 0, 2), (3, 0, 2), (0, 1, 2), (3, 1, 2), (1, 1, 0), (2, 1, 0), (1, 1, 2), (2, 1, 2),
+        ]
+        steps = steps + [(a, b, k ^ 1) for a, b, k in steps]
+        queries = [
+            project(pieces, weight),
+            project([swap(piece, "head", 1) for piece in pieces], weight),
+        ]
+
+        def of_block(block, z, h):
+            line, side, turn = steps[block]
+            there = (z, (z + 3) & 3, (z + 1) & 3, z ^ 2)[line]
+            return side, ((h ^ turn) * outer + there) * quarter
+
+        bases = []
+        for block, (_, side, _) in enumerate(steps):
+            where = of_block(block, z, h)[1] // quarter
+            bases.append((where % outer * inner + (y ^ side)) * row_count + where // outer * quarter)
+        bases = jnp.stack(bases)[:, None] + jnp.arange(quarter)[None, :]
+        layout = (quarter, inner, of_block)
     else:
-        ordered = [mine[:, :, step] for step in range(inner)]
-    mine = jnp.concatenate([piece.reshape(quarter, outer * part) for piece in ordered], axis=1)
-    gathered = gather_line(mine, "outer", 0)
-    if fast:
-        across = swap(gathered, "head", 2)
-        rows = outer * quarter
-        every = jnp.zeros((heads_axis * rows, model), tokens.dtype)
-        pair_here = jnp.concatenate([gathered, across], axis=0)
-        pair_there = swap(pair_here, "head", 1)
-        for piece, place in (
-            (pair_here[:rows], h), (pair_here[rows:], h ^ 2),
-            (pair_there[:rows], h ^ 1), (pair_there[rows:], h ^ 3),
-        ):
-            every = lax.dynamic_update_slice(every, piece, (place * rows, 0))
-    else:
-        every = gathered
-    shape = (every.shape[0] // (outer * quarter), outer, quarter)
-    places = (
-        context
-        + (lax.broadcasted_iota(jnp.int32, shape, 1) * inner + y) * row_count
-        + lax.broadcasted_iota(jnp.int32, shape, 0) * quarter
-        + lax.broadcasted_iota(jnp.int32, shape, 2)
-    ).reshape(-1, 1)
+        every = gather_line(tokens, "outer", 0)
+        queries = [jnp.dot(every, weight, preferred_element_type=jnp.float32).astype(jnp.bfloat16)]
+        bases = (jnp.arange(outer) * inner + y)[:, None] * row_count + jnp.arange(row_count)[None, :]
+        layout = (row_count, 1, lambda block, z, h: (0, block * row_count))
+    places = (context + bases).astype(jnp.int32).reshape(-1, 1)
+    here = jnp.stack([z, h, y]).astype(jnp.int32)
 
     packed = compress(
         raw_keys, raw_values, edge_keys, edge_values,
         key_expand, key_mix, key_reduce, value_expand, value_mix, value_reduce,
     )
-    if heads_axis != G:
+    ids = np.arange(devices * blocks).reshape(outer, inner, heads_axis, blocks)
+    if fast:
+        stay = lax.dynamic_index_in_dim(packed, h, 0, False)
+        away = [lax.dynamic_index_in_dim(packed, h ^ step, 0, False) for step in (1, 2, 3)]
+        came = [swap(piece, "head", step) for step, piece in zip((1, 2, 3), away)]
+        packed = jnp.concatenate([stay, *came], axis=0)
+        bound = np.broadcast_to(ids.max(axis=(2, 3), keepdims=True), ids.shape)
+    else:
         packed = jnp.broadcast_to(packed[:, None], (G, heads_axis // G, *packed.shape[1:]))
         packed = packed.reshape(heads_axis, blocks, -1)
-    packed = lax.all_to_all(packed, "head", split_axis=0, concat_axis=0, tiled=True)
-    packed = gather_line(packed.reshape(heads_axis * blocks, -1), "outer", 0)
+        packed = lax.all_to_all(packed, "head", split_axis=0, concat_axis=0, tiled=True)
+        packed = packed.reshape(heads_axis * blocks, -1)
+        bound = ids
+    packed = gather_line(packed, "outer", 0)
     packed = gather_pair(packed, "inner").reshape(devices * blocks, -1)
-    ids = np.arange(devices * blocks).reshape(outer, inner, heads_axis, blocks)
-    ids = ids.transpose(1, 0, 2, 3).reshape(-1)
-    limits = STRIDE * ids + BLK - 1
-    hidden = [bool((limits[i : i + LANES] > context).any()) for i in range(0, len(ids), LANES)]
+    bound = (STRIDE * bound + BLK - 1).transpose(1, 0, 2, 3).reshape(-1)
+    hidden = [bool((bound[i : i + LANES] > context).any()) for i in range(0, len(bound), LANES)]
     masked, start = [], 0
     for i in range(1, len(hidden) + 1):
         if i == len(hidden) or hidden[i] != hidden[start]:
-            masked.append((start * LANES, min(i * LANES, len(ids)), hidden[start]))
+            masked.append((start * LANES, min(i * LANES, len(bound)), hidden[start]))
             start = i
-    limits = jnp.asarray(limits[None, :], jnp.int32)
-
-    if inner == 2:
-        out_weights = [output_weight, swap(output_weight, "inner", 1)]
+    if fast:
+        column = np.arange(heads_axis)[None, None, :, None]
+        ids = ids[:, :, :1] + (column ^ h) * blocks
+        limits = (STRIDE * ids + BLK - 1).transpose(1, 0, 2, 3).reshape(1, -1).astype(jnp.int32)
     else:
-        out_weights = [lax.all_gather(output_weight, "inner", axis=1, tiled=True)]
+        limits = (STRIDE * ids + BLK - 1).transpose(1, 0, 2, 3).reshape(1, -1)
+        limits = jnp.asarray(limits, jnp.int32)
+
+    if fast:
+        turned = output_weight.T
+        out_weights = [turned, swap(turned, "inner", 1)]
+    else:
+        out_weights = lax.all_gather(output_weight, "inner", axis=1, tiled=True)
 
     total = None
-    for chunk in range(chunk_count):
-        weight = weights[chunk].reshape(outer * part, heads_chunk * key_width)
-        if inner == 2:
-            weight_own, weight_other = weight, swap(weight, "inner", 1)
-            split_at = outer * part
+    for head in range(heads_here):
+        attended = attend(
+            here, queries, head, packed, limits, places, key_width, masked, layout
+        )
+        if fast:
+            last = head == heads_here - 1
+            block = jnp.concatenate([attended[0], swap(attended[1], "inner", 1)], axis=1)
+            total = expel(
+                here, line_pieces(block, "outer"), out_weights, [] if total is None else [total],
+                head, heads_here, (heads_axis, quarter) if last else None,
+            )
         else:
-            weight = lax.all_gather(weight, "inner", axis=0, tiled=True)
-            split_at = inner // 2 * outer * part
-            weight_own, weight_other = weight[:split_at], weight[split_at:]
-        attended = attend(
-            every[:, :split_at], every[:, split_at:], weight_own, weight_other,
-            packed, limits, places, key_width, masked,
-        )
-        attended = gather_line(attended, "outer", 1)
-        width = attended.shape[1]
-        product = jnp.concatenate(
-            [
-                jnp.dot(
-                    attended, weight[chunk * width : (chunk + 1) * width],
-                    preferred_element_type=jnp.float32,
-                )
-                for weight in out_weights
-            ],
-            axis=1,
-        )
-        total = product if total is None else total + product
-
-    columns = total.shape[1]
+            attended = gather_line(attended[0], "outer", 1)
+            rows = out_weights.reshape(outer, heads_here, value_width, -1)[:, head]
+            product = jnp.dot(
+                attended, rows.reshape(outer * value_width, -1), preferred_element_type=jnp.float32
+            )
+            total = product if total is None else total + product
+
     if fast:
-        x, c = h // 2, h % 2
-        total = total.reshape(heads_axis, 2, 2, quarter, columns)
-        keep = lax.dynamic_index_in_dim(total, c, 2, False)
-        send = lax.dynamic_index_in_dim(total, 1 - c, 2, False).astype(jnp.bfloat16)
+        keep, send = total
+        columns = keep.shape[-1]
         total = keep + swap(send, "head", 1).astype(jnp.float32)
+        x = h // 2
         keep = lax.dynamic_index_in_dim(total, x, 1, False)
         send = lax.dynamic_index_in_dim(total, 1 - x, 1, False).astype(jnp.bfloat16)
         total = keep + swap(send, "head", 2).astype(jnp.float32)
@@ -335,6 +448,7 @@
             for a in range(outer) for b in range(inner) for k in range(heads_axis)
         ]
         return lax.ppermute(result, ("outer", "inner", "head"), route)
+    columns = total.shape[1]
     total = lax.psum_scatter(total, "head", scatter_dimension=0, tiled=True).astype(jnp.bfloat16)
     total = lax.all_gather(total, "head", axis=0, tiled=True)
     total = lax.all_to_all(

time: 224 us -> 235 us (1.049)
  Pallas kernels: 25.4 us -> 40 us
  waiting for transfers between devices: 98.5 us -> 105 us
  local copies, waits for them, and re-layouts: 28.6 us -> 22.2 us
  matrix products: 5.07 us -> 0 us
    pallas_call x2 -> x6, Pallas kernels: 16.8 us -> 31.5 us  [the longest x2 12 us: attend(): pl.pallas_call(kernel, out_shape=(shape,) * outputs, in_specs=[pl.BlockSp...]
    ppermute x12 -> x21, starting transfers between devices: 10.3 us -> 20.8 us  [swap(): lax.ppermute(block, axis, [(i, i ^ bit) for i in range(lax.axis_size(axis...]
    ppermute x12 -> x21, waiting for transfers between devices: 63.9 us -> 73 us  [swap(): lax.ppermute(block, axis, [(i, i ^ bit) for i in range(lax.axis_size(axis...]
    all_to_all x3 -> x2, starting transfers between devices: 15 us -> 7.29 us  [shards(): lax.all_to_all(sent, seq_axes, split_axis=0, concat_axis=0, tiled=True)]
    all_to_all x3 -> x2, waiting for transfers between devices: 6.18 us -> 0.01 us  [shards(): lax.all_to_all(sent, seq_axes, split_axis=0, concat_axis=0, tiled=True)]
    unnamed x27 -> x57, local copies, waits for them, and re-layouts: 9.41 us -> 14.7 us
    dot_general x4 -> x0, matrix products: 5.07 us -> none  [shards(): jnp.dot(attended, weight[chunk * width:(chunk + 1) * width], preferred_el...]
    concatenate x1 -> x5, other arithmetic: 1.24 us -> 5.67 us  [the longest x1 2.05 us: shards(): second = jnp.concatenate([second, swap(second, 'head', 2)], axis=0)]
  transfers between devices with their start and end apart: 29 -> 37, of which waited for: 14 -> 15; matrix products, arithmetic and copies ran while one was open for 14% -> 11% of each run, Pallas kernels for 11% -> 15%
where the time goes in v2:
time: 235 us; the launch traced here: 234 us
  waiting for transfers between devices  105 us (45%)
  starting transfers between devices  55 us (23%)
  Pallas kernels  40 us (17%)
  local copies, waits for them, and re-layouts  22.2 us (9%)
  other arithmetic  10.6 us (5%)
    ppermute x21, waiting for transfers between devices, swap(): lax.ppermute(block, axis, [(i, i ^ bit) for i in range(lax.axis_size(axis...  73 us
    ppermute x21, starting transfers between devices, swap(): lax.ppermute(block, axis, [(i, i ^ bit) for i in range(lax.axis_size(axis...  20.8 us
    ppermute x4, waiting for transfers between devices, line_pieces(): passed = lax.ppermute(far, axis, [(1, 0), (2, 3)])  14.7 us
    unnamed x57, local copies, waits for them, and re-layouts  14.7 us
    ppermute x4, starting transfers between devices, line_pieces(): up = lax.ppermute(block, axis, [(i, i + 1) for i in range(3)])  12.7 us
    pallas_call x2, Pallas kernels, attend(): pl.pallas_call(kernel, out_shape=(shape,) * outputs, in_specs=[pl.BlockSp...  12 us
    pallas_call x2, Pallas kernels, expel(): pl.pallas_call(kernel, out_shape=out_shape, in_specs=[pl.BlockSpec(memory...  10.3 us
    ppermute x1, waiting for transfers between devices, shards(): return lax.ppermute(result, ('outer', 'inner', 'head'), route)  9.67 us
  transfers between devices with their start and end apart: 37, of which 15 were waited for; matrix products, arithmetic and copies ran while one was open for 11% of the time, Pallas kernels for 15%

profile of v2, /device:TPU:2, one launch (start us, length us, event | category | flops | bytes accessed | tf_op | source)
XLA Modules:
  0.0 233.7 jit_solution(15904418615035052868)
XLA Ops:
  1.1 2.7 %collective-permute-start = (bf16[32,2560]{1,0:T(8,128)(2,1)S(1)}, bf16[32,2560]{1,0:T(8,128)(2,1)S(1)}, u32[]{:S(2)}, u32[]{:S(2)}) collective-permute-start(bf16[32,2560]{1,0:T(8,128)(2,1)S(1)} %constant_dynamic-slice_fusion), channel_id=1, source_target_pairs={{0,16},{8,24},{16,0},{24,8},{1,17},{9,25},{17,1},{25,9},{2,18},{10... | collective-permute-start | bytes 491528 | tf_op jit(solution)/shard_map/ppermute | solution.py:23
  3.8 3.5 %collective-permute-start.3 = (bf16[32,2560]{1,0:T(8,128)(2,1)S(1)}, bf16[32,2560]{1,0:T(8,128)(2,1)S(1)}, u32[]{:S(2)}, u32[]{:S(2)}) collective-permute-start(bf16[32,2560]{1,0:T(8,128)(2,1)S(1)} %constant_dynamic-slice_fusion), channel_id=1, source_target_pairs={{0,8},{8,16},{16,24},{1,9},{9,17},{17,25},{2,10},{10,18},{18,26},{... | collective-permute-start | bytes 491528 | tf_op jit(solution)/shard_map/ppermute | solution.py:271
  8.7 1.9 collective-permute-start.12
  10.6 1.6 bitcast_dynamic-update-slice_fusion.7
  12.3 1.7 bitcast_dynamic-update-slice_fusion.6
  14.0 1.6 bitcast_dynamic-update-slice_fusion.5
  20.5 8.4 %compress.1 = bf16[4,64,384]{2,1,0:T(8,128)(2,1)} custom-call(bf16[1024,768]{1,0:T(8,128)(2,1)} %raw_keys.1, bf16[1024,512]{1,0:T(8,128)(2,1)} %raw_values.1, bf16[16,768]{1,0:T(8,128)(2,1)} %slice.88.edge_keys, bf16[16,512]{1,0:T(8,128)(2,1)} %slice.89.edge_values, bf16[192,768]{1,0:T(8,128)(2,1)} %key_expand.1, f32[32,768]{1,0:T(8,128)} %key_mix.1, ...), custom_call_target="tpu_custom_call" | custom-call | flops 12079595520 | bytes 3145728 | tf_op jit(solution)/shard_map/compress/pallas_call | solution.py:105
  30.5 1.5 collective-permute-start.14
  32.0 1.7 bitcast_dynamic-update-slice_fusion
  34.6 3.6 %all-to-all-start = ((bf16[8,160,384]{2,1,0:T(8,128)(2,1)}), bf16[8,160,384]{2,1,0:T(8,128)(2,1)S(1)}, u32[]{:S(2)}, u32[]{:S(2)}) async-start(bf16[8,160,384]{2,1,0:T(8,128)(2,1)} %get-tuple-element.18), calls=%async_computation | async-start | bytes 1966080 | tf_op jit(solution)/shard_map/all_to_all | solution.py:324
  38.9 1.3 collective-permute-start.4
  40.4 3.4 %collective-permute-start.16 = (bf16[256,384]{1,0:T(8,128)(2,1)S(1)}, bf16[256,384]{1,0:T(8,128)(2,1)S(1)}, u32[]{:S(2)}, u32[]{:S(2)}) collective-permute-start(bf16[256,384]{1,0:T(8,128)(2,1)S(1)} %get-tuple-element.35), channel_id=1, source_target_pairs={{0,16},{8,24},{16,0},{24,8},{1,17},{9,25},{17,1},{25,9},{2,18},{10... | collective-permute-start | bytes 589832 | tf_op jit(solution)/shard_map/ppermute | solution.py:23
  43.8 3.3 %collective-permute-start.18 = (bf16[256,384]{1,0:T(8,128)(2,1)S(1)}, bf16[256,384]{1,0:T(8,128)(2,1)S(1)}, u32[]{:S(2)}, u32[]{:S(2)}) collective-permute-start(bf16[256,384]{1,0:T(8,128)(2,1)S(1)} %get-tuple-element.35), channel_id=1, source_target_pairs={{0,8},{8,16},{16,24},{1,9},{9,17},{17,25},{2,10},{10,18},{18,26},{... | collective-permute-start | bytes 589832 | tf_op jit(solution)/shard_map/ppermute | solution.py:271
  47.1 1.3 collective-permute-start.2
  50.4 6.5 %collective-permute-done.4 = bf16[32,2560]{1,0:T(8,128)(2,1)S(1)} collective-permute-done((bf16[32,2560]{1,0:T(8,128)(2,1)S(1)}, bf16[32,2560]{1,0:T(8,128)(2,1)S(1)}, u32[]{:S(2)}, u32[]{:S(2)}) %collective-permute-start.4) | collective-permute-done | bytes 163872 | tf_op jit(solution)/shard_map/ppermute | solution.py:272
  56.9 3.0 %collective-permute-start.1 = (bf16[64,2560]{1,0:T(8,128)(2,1)}, bf16[64,2560]{1,0:T(8,128)(2,1)}, u32[]{:S(2)}, u32[]{:S(2)}) collective-permute-start(bf16[64,2560]{1,0:T(8,128)(2,1)} %pad_maximum_fusion.3), channel_id=1, source_target_pairs={{0,4},{4,0},{1,5},{5,1},{2,6},{6,2},{3,7},{7,3},{8,12},{12,8},{9,1... | collective-permute-start | bytes 983048 | tf_op jit(solution)/shard_map/ppermute | solution.py:23
  59.9 15.9 %collective-permute-done.16 = bf16[256,384]{1,0:T(8,128)(2,1)S(1)} collective-permute-done((bf16[256,384]{1,0:T(8,128)(2,1)S(1)}, bf16[256,384]{1,0:T(8,128)(2,1)S(1)}, u32[]{:S(2)}, u32[]{:S(2)}) %collective-permute-start.16) | collective-permute-done | bytes 196640 | tf_op jit(solution)/shard_map/ppermute | solution.py:23
  78.8 5.0 %collective-permute-done.17 = bf16[256,384]{1,0:T(8,128)(2,1)S(1)} collective-permute-done((bf16[256,384]{1,0:T(8,128)(2,1)S(1)}, bf16[256,384]{1,0:T(8,128)(2,1)S(1)}, u32[]{:S(2)}, u32[]{:S(2)}) %collective-permute-start.17) | collective-permute-done | bytes 196640 | tf_op jit(solution)/shard_map/ppermute | solution.py:273
  84.0 1.4 collective-permute-start.20
  85.5 3.7 %all-to-all-start.1 = ((bf16[8,160,384]{2,1,0:T(8,128)(2,1)}), bf16[8,160,384]{2,1,0:T(8,128)(2,1)S(1)}, u32[]{:S(2)}, u32[]{:S(2)}) async-start(bf16[8,160,384]{2,1,0:T(8,128)(2,1)} %copy-done.7), calls=%async_computation.1 | async-start | bytes 1966080 | tf_op jit(solution)/shard_map/all_to_all | solution.py:324
  89.3 2.0 pad_maximum_fusion.1.refs_0_
  91.6 2.1 pad_maximum_fusion.2.refs_1_
  93.6 1.7 collective-permute-start.7
  96.3 1.3 add.630.refs_4_
  98.2 8.3 %collective-permute-done.6.refs_2_ = bf16[128,2560]{1,0:T(8,128)(2,1)} collective-permute-done((bf16[128,2560]{1,0:T(8,128)(2,1)}, bf16[128,2560]{1,0:T(8,128)(2,1)}, u32[]{:S(2)}, u32[]{:S(2)}) %collective-permute-start.6) | collective-permute-done | bytes 655392 | tf_op jit(solution)/shard_map/ppermute | solution.py:23
  106.5 20.3 %collective-permute-done.7.refs_3_ = bf16[128,2560]{1,0:T(8,128)(2,1)} collective-permute-done((bf16[128,2560]{1,0:T(8,128)(2,1)}, bf16[128,2560]{1,0:T(8,128)(2,1)}, u32[]{:S(2)}, u32[]{:S(2)}) %collective-permute-start.7) | collective-permute-done | bytes 655392 | tf_op jit(solution)/shard_map/ppermute | solution.py:23
  127.4 1.4 collective-permute-start.26
  130.1 1.4 pad_maximum_fusion
  132.4 4.6 %project.2.refs_0_ = bf16[512,384]{1,0:T(8,128)(2,1)} custom-call(bf16[128,2560]{1,0:T(8,128)(2,1)} %pad_maximum_fusion.1.refs_0_, bf16[128,2560]{1,0:T(8,128)(2,1)} %pad_maximum_fusion.2.refs_1_, bf16[128,2560]{1,0:T(8,128)(2,1)} %collective-permute-done.6.refs_2_, bf16[128,2560]{1,0:T(8,128)(2,1)} %collective-permute-done.7.refs_3_, ...), custom_call_target="tpu_custom_call" | custom-call | flops 1006632960 | bytes 2621440 | tf_op jit(solution)/shard_map/project/pallas_call | solution.py:139
  137.0 4.6 %project.3.refs_1_ = bf16[512,384]{1,0:T(8,128)(2,1)} custom-call(bf16[128,2560]{1,0:T(8,128)(2,1)} %collective-permute-done.8.refs_0_, bf16[128,2560]{1,0:T(8,128)(2,1)} %collective-permute-done.9.refs_1_, bf16[128,2560]{1,0:T(8,128)(2,1)} %collective-permute-done.10.refs_2_, bf16[128,2560]{1,0:T(8,128)(2,1)} %collective-permute-done.11.refs_3_, ...), custom_call_target="tpu_custom_call" | custom-call | flops 1006632960 | bytes 2621440 | tf_op jit(solution)/shard_map/project/pallas_call | solution.py:139
  141.6 6.0 %attend.3 = (bf16[512,128]{1,0:T(8,128)(2,1)}, bf16[512,128]{1,0:T(8,128)(2,1)}) custom-call(s32[3]{0:T(128)} %pad_add_fusion.here_ref.place_ref, bf16[512,384]{1,0:T(8,128)(2,1)} %project.2.refs_0_, bf16[512,384]{1,0:T(8,128)(2,1)} %project.3.refs_1_, bf16[2048,384]{1,0:T(8,128)(2,1)} %bitcast.93, s32[1,2048]{1,0:T(1,128)} %sub.145.refs_3_, ...), custom_call_target="tpu_custom_call" | custom-call | flops 1342177280 | bytes 1572864 | tf_op jit(solution)/shard_map/attend/pallas_call | solution.py:195
  148.2 6.0 %attend.2 = (bf16[512,128]{1,0:T(8,128)(2,1)}, bf16[512,128]{1,0:T(8,128)(2,1)}) custom-call(s32[3]{0:T(128)} %pad_add_fusion.here_ref.place_ref, bf16[512,384]{1,0:T(8,128)(2,1)} %project.2.refs_0_, bf16[512,384]{1,0:T(8,128)(2,1)} %project.3.refs_1_, bf16[2048,384]{1,0:T(8,128)(2,1)} %bitcast.94, s32[1,2048]{1,0:T(1,128)} %sub.145.refs_3_, ...), custom_call_target="tpu_custom_call" | custom-call | flops 1342177280 | bytes 1572864 | tf_op jit(solution)/shard_map/attend/pallas_call | solution.py:195
  155.2 1.4 collective-permute-start.21
  156.6 5.3 %collective-permute-done.27 = bf16[512,128]{1,0:T(8,128)(2,1)S(1)} collective-permute-done((bf16[512,128]{1,0:T(8,128)(2,1)}, bf16[512,128]{1,0:T(8,128)(2,1)S(1)}, u32[]{:S(2)}, u32[]{:S(2)}) %collective-permute-start.27) | collective-permute-done | bytes 131104 | tf_op jit(solution)/shard_map/ppermute | solution.py:23
  162.3 2.1 collective-permute-done.21
  165.4 1.4 collective-permute-start.28
  166.8 1.3 collective-permute-start.29
  168.1 13.0 %collective-permute-done.30.refs_4_ = bf16[512,256]{1,0:T(8,128)(2,1)S(1)} collective-permute-done((bf16[512,256]{1,0:T(8,128)(2,1)S(1)}, bf16[512,256]{1,0:T(8,128)(2,1)S(1)}, u32[]{:S(2)}, u32[]{:S(2)}) %collective-permute-start.30) | collective-permute-done | bytes 262176 | tf_op jit(solution)/shard_map/ppermute | solution.py:23
  182.4 4.6 %collective-permute-start.22 = (bf16[512,256]{1,0:T(8,128)(2,1)S(1)}, bf16[512,256]{1,0:T(8,128)(2,1)S(1)}, u32[]{:S(2)}, u32[]{:S(2)}) collective-permute-start(bf16[512,256]{1,0:T(8,128)(2,1)S(1)} %constant_dynamic-update-slice_fusion.refs_0_), channel_id=1, source_target_pairs={{0,8},{8,16},{16,24},{1,9},{9,17},{17,25},{2,10},{10,18},{18,26},{... | collective-permute-start | bytes 786440 | tf_op jit(solution)/shard_map/ppermute | solution.py:271
  188.3 1.3 collective-permute-start.25
  190.2 5.6 %collective-permute-done.31.refs_3_ = bf16[512,256]{1,0:T(8,128)(2,1)S(1)} collective-permute-done((bf16[512,256]{1,0:T(8,128)(2,1)S(1)}, bf16[512,256]{1,0:T(8,128)(2,1)S(1)}, u32[]{:S(2)}, u32[]{:S(2)}) %collective-permute-start.31) | collective-permute-done | bytes 262176 | tf_op jit(solution)/shard_map/ppermute | solution.py:273
  196.5 4.6 %expel.2.refs_7_ = f32[512,640]{1,0:T(8,128)} custom-call(s32[3]{0:T(128)} %pad_add_fusion.here_ref.place_ref, bf16[512,256]{1,0:T(8,128)(2,1)} %copy-done.10, bf16[512,256]{1,0:T(8,128)(2,1)} %copy-done.15, bf16[512,256]{1,0:T(8,128)(2,1)} %copy-done.16, bf16[512,256]{1,0:T(8,128)(2,1)} %copy-done.18, bf16[512,256]{1,0:T(8,128)(2,1)} %copy-done.13, ...), custom_call_target="tpu_custom_call" | custom-call | flops 671088640 | bytes 1310720 | tf_op jit(solution)/shard_map/expel/pallas_call | solution.py:255
  201.4 4.0 %collective-permute-done.25.refs_3_ = bf16[512,256]{1,0:T(8,128)(2,1)S(1)} collective-permute-done((bf16[512,256]{1,0:T(8,128)(2,1)S(1)}, bf16[512,256]{1,0:T(8,128)(2,1)S(1)}, u32[]{:S(2)}, u32[]{:S(2)}) %collective-permute-start.25) | collective-permute-done | bytes 262176 | tf_op jit(solution)/shard_map/ppermute | solution.py:273
  206.1 5.7 %expel.3 = (f32[4,2,32,640]{3,2,1,0:T(8,128)}, bf16[4,2,32,640]{3,2,1,0:T(8,128)(2,1)}) custom-call(s32[3]{0:T(128)} %pad_add_fusion.here_ref.place_ref, bf16[512,256]{1,0:T(8,128)(2,1)} %copy-done.9, bf16[512,256]{1,0:T(8,128)(2,1)} %copy-done.14, bf16[512,256]{1,0:T(8,128)(2,1)} %copy-done.17, bf16[512,256]{1,0:T(8,128)(2,1)} %copy-done.19, ...), custom_call_target="tpu_custom_call" | custom-call | flops 671088640 | bytes 1310720 | tf_op jit(solution)/shard_map/expel/pallas_call | solution.py:255
  211.9 1.8 collective-permute-done.32
  215.0 6.2 %collective-permute-done.33 = bf16[4,32,640]{2,1,0:T(8,128)(2,1)S(1)} collective-permute-done((bf16[4,32,640]{2,1,0:T(8,128)(2,1)S(1)}, bf16[4,32,640]{2,1,0:T(8,128)(2,1)S(1)}, u32[]{:S(2)}, u32[]{:S(2)}) %collective-permute-start.33) | collective-permute-done | bytes 163872 | tf_op jit(solution)/shard_map/ppermute | solution.py:23
  221.4 1.9 collective-permute-start.34
  223.4 9.7 %collective-permute-done.34 = bf16[128,640]{1,0:T(8,128)(2,1)S(1)} collective-permute-done((bf16[128,640]{1,0:T(8,128)(2,1)S(1)}, bf16[128,640]{1,0:T(8,128)(2,1)S(1)}, u32[]{:S(2)}, u32[]{:S(2)}) %collective-permute-start.34) | collective-permute-done | bytes 163872 | tf_op jit(solution)/shard_map/ppermute | solution.py:450
  (124 shorter events, 29.8 us)
Async XLA Ops:
  1.1 14.5 %copy-start.3 = (bf16[320,3072]{1,0:T(8,128)(2,1)S(1)}, bf16[320,3072]{1,0:T(8,128)(2,1)}, u32[]{:S(2)}) copy-start(bf16[320,3072]{1,0:T(8,128)(2,1)} %param.16) | copy-start | bytes 5898244
  1.1 47.3 %copy-start.4 = (bf16[32,2560]{1,0:T(8,128)(2,1)}, bf16[32,2560]{1,0:T(8,128)(2,1)S(1)}, u32[]{:S(2)}) copy-start(bf16[32,2560]{1,0:T(8,128)(2,1)S(1)} %constant_dynamic-slice_fusion) | copy-start | bytes 491524
  1.1 45.9 %collective-permute-start = (bf16[32,2560]{1,0:T(8,128)(2,1)S(1)}, bf16[32,2560]{1,0:T(8,128)(2,1)S(1)}, u32[]{:S(2)}, u32[]{:S(2)}) collective-permute-start(bf16[32,2560]{1,0:T(8,128)(2,1)S(1)} %constant_dynamic-slice_fusion), channel_id=1, source_target_pairs={{0,16},{8,24},{16,0},{24,8},{1,17},{9,25},{17,1},{25,9},{2,18},{10... | collective-permute-start | bytes 491528 | tf_op jit(solution)/shard_map/ppermute | solution.py:23
  3.8 45.4 %collective-permute-start.3 = (bf16[32,2560]{1,0:T(8,128)(2,1)S(1)}, bf16[32,2560]{1,0:T(8,128)(2,1)S(1)}, u32[]{:S(2)}, u32[]{:S(2)}) collective-permute-start(bf16[32,2560]{1,0:T(8,128)(2,1)S(1)} %constant_dynamic-slice_fusion), channel_id=1, source_target_pairs={{0,8},{8,16},{16,24},{1,9},{9,17},{17,25},{2,10},{10,18},{18,26},{... | collective-permute-start | bytes 491528 | tf_op jit(solution)/shard_map/ppermute | solution.py:271
  8.7 10.5 %collective-permute-start.12 = (bf16[16,1280]{1,0:T(8,128)(2,1)S(1)}, bf16[16,1280]{1,0:T(8,128)(2,1)S(1)}, u32[]{:S(2)}, u32[]{:S(2)}) collective-permute-start(bf16[16,1280]{1,0:T(8,128)(2,1)S(1)} %pad_maximum_fusion.7), channel_id=1, source_target_pairs={{1,0},{2,1},{3,2},{4,3},{5,4},{6,5},{7,6},{8,7},{9,8},{10,9},{11,1... | collective-permute-start | bytes 122888 | tf_op jit(solution)/shard_map/ppermute | solution.py:330
  29.8 9.2 %collective-permute-start.15 = (bf16[64,384]{1,0:T(8,128)(2,1)S(1)}, bf16[64,384]{1,0:T(8,128)(2,1)S(1)}, u32[]{:S(2)}, u32[]{:S(2)}) collective-permute-start(bf16[64,384]{1,0:T(8,128)(2,1)S(1)} %get-tuple-element.38), channel_id=1, source_target_pairs={{0,3},{1,2},{2,1},{3,0},{4,7},{5,6},{6,5},{7,4},{8,11},{9,10},{10,... | collective-permute-start | bytes 147464 | tf_op jit(solution)/shard_map/ppermute | solution.py:23
  30.5 9.8 %collective-permute-start.14 = (bf16[64,384]{1,0:T(8,128)(2,1)S(1)}, bf16[64,384]{1,0:T(8,128)(2,1)S(1)}, u32[]{:S(2)}, u32[]{:S(2)}) collective-permute-start(bf16[64,384]{1,0:T(8,128)(2,1)S(1)} %get-tuple-element.39), channel_id=1, source_target_pairs={{0,2},{1,3},{2,0},{3,1},{4,6},{5,7},{6,4},{7,5},{8,10},{9,11},{10,... | collective-permute-start | bytes 147464 | tf_op jit(solution)/shard_map/ppermute | solution.py:23
  32.0 8.3 %collective-permute-start.13 = (bf16[64,384]{1,0:T(8,128)(2,1)S(1)}, bf16[64,384]{1,0:T(8,128)(2,1)S(1)}, u32[]{:S(2)}, u32[]{:S(2)}) collective-permute-start(bf16[64,384]{1,0:T(8,128)(2,1)S(1)} %get-tuple-element.40), channel_id=1, source_target_pairs={{0,1},{1,0},{2,3},{3,2},{4,5},{5,4},{6,7},{7,6},{8,9},{9,8},{10,11... | collective-permute-start | bytes 147464 | tf_op jit(solution)/shard_map/ppermute | solution.py:23
  34.6 50.9 %all-to-all-start = ((bf16[8,160,384]{2,1,0:T(8,128)(2,1)}), bf16[8,160,384]{2,1,0:T(8,128)(2,1)S(1)}, u32[]{:S(2)}, u32[]{:S(2)}) async-start(bf16[8,160,384]{2,1,0:T(8,128)(2,1)} %get-tuple-element.18), calls=%async_computation | async-start | bytes 1966080 | tf_op jit(solution)/shard_map/all_to_all | solution.py:324
  38.9 18.0 %collective-permute-start.4 = (bf16[32,2560]{1,0:T(8,128)(2,1)S(1)}, bf16[32,2560]{1,0:T(8,128)(2,1)S(1)}, u32[]{:S(2)}, u32[]{:S(2)}) collective-permute-start(bf16[32,2560]{1,0:T(8,128)(2,1)S(1)} %constant_dynamic-slice_fusion), channel_id=1, source_target_pairs={{8,0},{16,8},{24,16},{9,1},{17,9},{25,17},{10,2},{18,10},{26,18},{... | collective-permute-start | bytes 491528 | tf_op jit(solution)/shard_map/ppermute | solution.py:272
  40.4 35.4 %collective-permute-start.16 = (bf16[256,384]{1,0:T(8,128)(2,1)S(1)}, bf16[256,384]{1,0:T(8,128)(2,1)S(1)}, u32[]{:S(2)}, u32[]{:S(2)}) collective-permute-start(bf16[256,384]{1,0:T(8,128)(2,1)S(1)} %get-tuple-element.35), channel_id=1, source_target_pairs={{0,16},{8,24},{16,0},{24,8},{1,17},{9,25},{17,1},{25,9},{2,18},{10... | collective-permute-start | bytes 589832 | tf_op jit(solution)/shard_map/ppermute | solution.py:23
  43.8 35.0 %collective-permute-start.18 = (bf16[256,384]{1,0:T(8,128)(2,1)S(1)}, bf16[256,384]{1,0:T(8,128)(2,1)S(1)}, u32[]{:S(2)}, u32[]{:S(2)}) collective-permute-start(bf16[256,384]{1,0:T(8,128)(2,1)S(1)} %get-tuple-element.35), channel_id=1, source_target_pairs={{0,8},{8,16},{16,24},{1,9},{9,17},{17,25},{2,10},{10,18},{18,26},{... | collective-permute-start | bytes 589832 | tf_op jit(solution)/shard_map/ppermute | solution.py:271
  47.1 36.9 %copy-start.8 = (bf16[32,2560]{1,0:T(8,128)(2,1)}, bf16[32,2560]{1,0:T(8,128)(2,1)S(1)}, u32[]{:S(2)}) copy-start(bf16[32,2560]{1,0:T(8,128)(2,1)S(1)} %collective-permute-done) | copy-start | bytes 491524
  47.1 30.0 %collective-permute-start.2 = (bf16[32,2560]{1,0:T(8,128)(2,1)S(1)}, bf16[32,2560]{1,0:T(8,128)(2,1)S(1)}, u32[]{:S(2)}, u32[]{:S(2)}) collective-permute-start(bf16[32,2560]{1,0:T(8,128)(2,1)S(1)} %collective-permute-done), channel_id=1, source_target_pairs={{8,0},{16,24},{9,1},{17,25},{10,2},{18,26},{11,3},{19,27},{12,4},{... | collective-permute-start | bytes 491528 | tf_op jit(solution)/shard_map/ppermute | solution.py:273
  49.1 34.7 %collective-permute-start.19 = (bf16[256,384]{1,0:T(8,128)(2,1)S(1)}, bf16[256,384]{1,0:T(8,128)(2,1)S(1)}, u32[]{:S(2)}, u32[]{:S(2)}) collective-permute-start(bf16[256,384]{1,0:T(8,128)(2,1)S(1)} %get-tuple-element.35), channel_id=1, source_target_pairs={{8,0},{16,8},{24,16},{9,1},{17,9},{25,17},{10,2},{18,10},{26,18},{... | collective-permute-start | bytes 589832 | tf_op jit(solution)/shard_map/ppermute | solution.py:272
  56.9 32.4 %collective-permute-start.1 = (bf16[64,2560]{1,0:T(8,128)(2,1)}, bf16[64,2560]{1,0:T(8,128)(2,1)}, u32[]{:S(2)}, u32[]{:S(2)}) collective-permute-start(bf16[64,2560]{1,0:T(8,128)(2,1)} %pad_maximum_fusion.3), channel_id=1, source_target_pairs={{0,4},{4,0},{1,5},{5,1},{2,6},{6,2},{3,7},{7,3},{8,12},{12,8},{9,1... | collective-permute-start | bytes 983048 | tf_op jit(solution)/shard_map/ppermute | solution.py:23
  75.8 8.0 %collective-permute-start.17 = (bf16[256,384]{1,0:T(8,128)(2,1)S(1)}, bf16[256,384]{1,0:T(8,128)(2,1)S(1)}, u32[]{:S(2)}, u32[]{:S(2)}) collective-permute-start(bf16[256,384]{1,0:T(8,128)(2,1)S(1)} %collective-permute-done.16), channel_id=1, source_target_pairs={{8,0},{16,24},{9,1},{17,25},{10,2},{18,26},{11,3},{19,27},{12,4},{... | collective-permute-start | bytes 589832 | tf_op jit(solution)/shard_map/ppermute | solution.py:273
  77.1 6.9 %copy-start.5 = (bf16[32,2560]{1,0:T(8,128)(2,1)}, bf16[32,2560]{1,0:T(8,128)(2,1)S(1)}, u32[]{:S(2)}) copy-start(bf16[32,2560]{1,0:T(8,128)(2,1)S(1)} %get-tuple-element.43) | copy-start | bytes 491524
  77.1 6.9 %copy-start.6 = (bf16[32,2560]{1,0:T(8,128)(2,1)}, bf16[32,2560]{1,0:T(8,128)(2,1)S(1)}, u32[]{:S(2)}) copy-start(bf16[32,2560]{1,0:T(8,128)(2,1)S(1)} %get-tuple-element.44) | copy-start | bytes 491524
  78.0 13.6 %collective-permute-start.5 = (bf16[64,2560]{1,0:T(8,128)(2,1)}, bf16[64,2560]{1,0:T(8,128)(2,1)}, u32[]{:S(2)}, u32[]{:S(2)}) collective-permute-start(bf16[64,2560]{1,0:T(8,128)(2,1)} %pad_maximum_fusion.4), channel_id=1, source_target_pairs={{0,2},{1,3},{2,0},{3,1},{4,6},{5,7},{6,4},{7,5},{8,10},{9,11},{10,... | collective-permute-start | bytes 983048 | tf_op jit(solution)/shard_map/ppermute | solution.py:23
  84.0 43.3 %collective-permute-start.20 = (bf16[1024,384]{1,0:T(8,128)(2,1)S(1)}, bf16[1024,384]{1,0:T(8,128)(2,1)}, u32[]{:S(2)}, u32[]{:S(2)}) collective-permute-start(bf16[1024,384]{1,0:T(8,128)(2,1)S(1)} %constant_dynamic-update-slice_fusion.4), channel_id=1, source_target_pairs={{0,4},{4,0},{1,5},{5,1},{2,6},{6,2},{3,7},{7,3},{8,12},{12,8},{9,1... | collective-permute-start | bytes 2359304 | tf_op jit(solution)/shard_map/ppermute | solution.py:23
  85.5 45.9 %all-to-all-start.1 = ((bf16[8,160,384]{2,1,0:T(8,128)(2,1)}), bf16[8,160,384]{2,1,0:T(8,128)(2,1)S(1)}, u32[]{:S(2)}, u32[]{:S(2)}) async-start(bf16[8,160,384]{2,1,0:T(8,128)(2,1)} %copy-done.7), calls=%async_computation.1 | async-start | bytes 1966080 | tf_op jit(solution)/shard_map/all_to_all | solution.py:324
  91.3 15.2 %collective-permute-start.6 = (bf16[128,2560]{1,0:T(8,128)(2,1)}, bf16[128,2560]{1,0:T(8,128)(2,1)}, u32[]{:S(2)}, u32[]{:S(2)}) collective-permute-start(bf16[128,2560]{1,0:T(8,128)(2,1)} %pad_maximum_fusion.1.refs_0_), channel_id=1, source_target_pairs={{0,2},{1,3},{2,0},{3,1},{4,6},{5,7},{6,4},{7,5},{8,10},{9,11},{10,... | collective-permute-start | bytes 1966088 | tf_op jit(solution)/shard_map/ppermute | solution.py:23
  93.6 33.1 %collective-permute-start.7 = (bf16[128,2560]{1,0:T(8,128)(2,1)}, bf16[128,2560]{1,0:T(8,128)(2,1)}, u32[]{:S(2)}, u32[]{:S(2)}) collective-permute-start(bf16[128,2560]{1,0:T(8,128)(2,1)} %pad_maximum_fusion.2.refs_1_), channel_id=1, source_target_pairs={{0,4},{4,0},{1,5},{5,1},{2,6},{6,2},{3,7},{7,3},{8,12},{12,8},{9,1... | collective-permute-start | bytes 1966088 | tf_op jit(solution)/shard_map/ppermute | solution.py:23
  97.7 39.3 %collective-permute-start.8 = (bf16[128,2560]{1,0:T(8,128)(2,1)}, bf16[128,2560]{1,0:T(8,128)(2,1)}, u32[]{:S(2)}, u32[]{:S(2)}) collective-permute-start(bf16[128,2560]{1,0:T(8,128)(2,1)} %pad_maximum_fusion.1.refs_0_), channel_id=1, source_target_pairs={{0,1},{1,0},{2,3},{3,2},{4,5},{5,4},{6,7},{7,6},{8,9},{9,8},{10,11... | collective-permute-start | bytes 1966088 | tf_op jit(solution)/shard_map/ppermute | solution.py:23
  97.7 39.3 %collective-permute-start.9 = (bf16[128,2560]{1,0:T(8,128)(2,1)}, bf16[128,2560]{1,0:T(8,128)(2,1)}, u32[]{:S(2)}, u32[]{:S(2)}) collective-permute-start(bf16[128,2560]{1,0:T(8,128)(2,1)} %pad_maximum_fusion.2.refs_1_), channel_id=1, source_target_pairs={{0,1},{1,0},{2,3},{3,2},{4,5},{5,4},{6,7},{7,6},{8,9},{9,8},{10,11... | collective-permute-start | bytes 1966088 | tf_op jit(solution)/shard_map/ppermute | solution.py:23
  106.5 30.5 %collective-permute-start.10 = (bf16[128,2560]{1,0:T(8,128)(2,1)}, bf16[128,2560]{1,0:T(8,128)(2,1)}, u32[]{:S(2)}, u32[]{:S(2)}) collective-permute-start(bf16[128,2560]{1,0:T(8,128)(2,1)} %collective-permute-done.6.refs_2_), channel_id=1, source_target_pairs={{0,1},{1,0},{2,3},{3,2},{4,5},{5,4},{6,7},{7,6},{8,9},{9,8},{10,11... | collective-permute-start | bytes 1966088 | tf_op jit(solution)/shard_map/ppermute | solution.py:23
  126.8 10.2 %collective-permute-start.11 = (bf16[128,2560]{1,0:T(8,128)(2,1)}, bf16[128,2560]{1,0:T(8,128)(2,1)}, u32[]{:S(2)}, u32[]{:S(2)}) collective-permute-start(bf16[128,2560]{1,0:T(8,128)(2,1)} %collective-permute-done.7.refs_3_), channel_id=1, source_target_pairs={{0,1},{1,0},{2,3},{3,2},{4,5},{5,4},{6,7},{7,6},{8,9},{9,8},{10,11... | collective-permute-start | bytes 1966088 | tf_op jit(solution)/shard_map/ppermute | solution.py:23
  127.4 55.0 %collective-permute-start.26 = (bf16[320,2048]{1,0:T(8,128)(2,1)}, bf16[320,2048]{1,0:T(8,128)(2,1)}, u32[]{:S(2)}, u32[]{:S(2)}) collective-permute-start(bf16[320,2048]{1,0:T(8,128)(2,1)} %bitcast.90), channel_id=1, source_target_pairs={{0,4},{4,0},{1,5},{5,1},{2,6},{6,2},{3,7},{7,3},{8,12},{12,8},{9,1... | collective-permute-start | bytes 3932168 | tf_op jit(solution)/shard_map/ppermute | solution.py:23
  147.6 9.0 %copy-start.20 = (bf16[512,128]{1,0:T(8,128)(2,1)S(1)}, bf16[512,128]{1,0:T(8,128)(2,1)}, u32[]{:S(2)}) copy-start(bf16[512,128]{1,0:T(8,128)(2,1)} %get-tuple-element.13) | copy-start | bytes 393220
  147.6 14.4 %collective-permute-start.27 = (bf16[512,128]{1,0:T(8,128)(2,1)}, bf16[512,128]{1,0:T(8,128)(2,1)S(1)}, u32[]{:S(2)}, u32[]{:S(2)}) collective-permute-start(bf16[512,128]{1,0:T(8,128)(2,1)} %get-tuple-element.14), channel_id=1, source_target_pairs={{0,4},{4,0},{1,5},{5,1},{2,6},{6,2},{3,7},{7,3},{8,12},{12,8},{9,1... | collective-permute-start | bytes 393224 | tf_op jit(solution)/shard_map/ppermute | solution.py:23
  155.2 9.2 %collective-permute-start.21 = (bf16[512,128]{1,0:T(8,128)(2,1)}, bf16[512,128]{1,0:T(8,128)(2,1)S(1)}, u32[]{:S(2)}, u32[]{:S(2)}) collective-permute-start(bf16[512,128]{1,0:T(8,128)(2,1)} %get-tuple-element.12), channel_id=1, source_target_pairs={{0,4},{4,0},{1,5},{5,1},{2,6},{6,2},{3,7},{7,3},{8,12},{12,8},{9,1... | collective-permute-start | bytes 393224 | tf_op jit(solution)/shard_map/ppermute | solution.py:23
  162.0 33.8 %copy-start.10 = (bf16[512,256]{1,0:T(8,128)(2,1)}, bf16[512,256]{1,0:T(8,128)(2,1)S(1)}, u32[]{:S(2)}) copy-start(bf16[512,256]{1,0:T(8,128)(2,1)S(1)} %constant_dynamic-update-slice_fusion.2.refs_0_) | copy-start | bytes 786436
  162.0 19.0 %collective-permute-start.30 = (bf16[512,256]{1,0:T(8,128)(2,1)S(1)}, bf16[512,256]{1,0:T(8,128)(2,1)S(1)}, u32[]{:S(2)}, u32[]{:S(2)}) collective-permute-start(bf16[512,256]{1,0:T(8,128)(2,1)S(1)} %constant_dynamic-update-slice_fusion.2.refs_0_), channel_id=1, source_target_pairs={{0,16},{8,24},{16,0},{24,8},{1,17},{9,25},{17,1},{25,9},{2,18},{10... | collective-permute-start | bytes 786440 | tf_op jit(solution)/shard_map/ppermute | solution.py:23
  164.4 36.7 %copy-start.9 = (bf16[512,256]{1,0:T(8,128)(2,1)}, bf16[512,256]{1,0:T(8,128)(2,1)S(1)}, u32[]{:S(2)}) copy-start(bf16[512,256]{1,0:T(8,128)(2,1)S(1)} %constant_dynamic-update-slice_fusion.refs_0_) | copy-start | bytes 786436
  164.4 22.5 %collective-permute-start.24 = (bf16[512,256]{1,0:T(8,128)(2,1)S(1)}, bf16[512,256]{1,0:T(8,128)(2,1)S(1)}, u32[]{:S(2)}, u32[]{:S(2)}) collective-permute-start(bf16[512,256]{1,0:T(8,128)(2,1)S(1)} %constant_dynamic-update-slice_fusion.refs_0_), channel_id=1, source_target_pairs={{0,16},{8,24},{16,0},{24,8},{1,17},{9,25},{17,1},{25,9},{2,18},{10... | collective-permute-start | bytes 786440 | tf_op jit(solution)/shard_map/ppermute | solution.py:23
  165.4 22.9 %collective-permute-start.28 = (bf16[512,256]{1,0:T(8,128)(2,1)S(1)}, bf16[512,256]{1,0:T(8,128)(2,1)S(1)}, u32[]{:S(2)}, u32[]{:S(2)}) collective-permute-start(bf16[512,256]{1,0:T(8,128)(2,1)S(1)} %constant_dynamic-update-slice_fusion.2.refs_0_), channel_id=1, source_target_pairs={{0,8},{8,16},{16,24},{1,9},{9,17},{17,25},{2,10},{10,18},{18,26},{... | collective-permute-start | bytes 786440 | tf_op jit(solution)/shard_map/ppermute | solution.py:271
  166.8 23.4 %collective-permute-start.29 = (bf16[512,256]{1,0:T(8,128)(2,1)S(1)}, bf16[512,256]{1,0:T(8,128)(2,1)S(1)}, u32[]{:S(2)}, u32[]{:S(2)}) collective-permute-start(bf16[512,256]{1,0:T(8,128)(2,1)S(1)} %constant_dynamic-update-slice_fusion.2.refs_0_), channel_id=1, source_target_pairs={{8,0},{16,8},{24,16},{9,1},{17,9},{25,17},{10,2},{18,10},{26,18},{... | collective-permute-start | bytes 786440 | tf_op jit(solution)/shard_map/ppermute | solution.py:272
  181.1 14.7 %copy-start.13 = (bf16[512,256]{1,0:T(8,128)(2,1)}, bf16[512,256]{1,0:T(8,128)(2,1)S(1)}, u32[]{:S(2)}) copy-start(bf16[512,256]{1,0:T(8,128)(2,1)S(1)} %collective-permute-done.30.refs_4_) | copy-start | bytes 786436
  181.1 14.7 %collective-permute-start.31 = (bf16[512,256]{1,0:T(8,128)(2,1)S(1)}, bf16[512,256]{1,0:T(8,128)(2,1)S(1)}, u32[]{:S(2)}, u32[]{:S(2)}) collective-permute-start(bf16[512,256]{1,0:T(8,128)(2,1)S(1)} %collective-permute-done.30.refs_4_), channel_id=1, source_target_pairs={{8,0},{16,24},{9,1},{17,25},{10,2},{18,26},{11,3},{19,27},{12,4},{... | collective-permute-start | bytes 786440 | tf_op jit(solution)/shard_map/ppermute | solution.py:273
  182.4 18.8 %collective-permute-start.22 = (bf16[512,256]{1,0:T(8,128)(2,1)S(1)}, bf16[512,256]{1,0:T(8,128)(2,1)S(1)}, u32[]{:S(2)}, u32[]{:S(2)}) collective-permute-start(bf16[512,256]{1,0:T(8,128)(2,1)S(1)} %constant_dynamic-update-slice_fusion.refs_0_), channel_id=1, source_target_pairs={{0,8},{8,16},{16,24},{1,9},{9,17},{17,25},{2,10},{10,18},{18,26},{... | collective-permute-start | bytes 786440 | tf_op jit(solution)/shard_map/ppermute | solution.py:271
  187.0 14.2 %copy-start.12 = (bf16[512,256]{1,0:T(8,128)(2,1)}, bf16[512,256]{1,0:T(8,128)(2,1)S(1)}, u32[]{:S(2)}) copy-start(bf16[512,256]{1,0:T(8,128)(2,1)S(1)} %collective-permute-done.24.refs_4_) | copy-start | bytes 786436
  187.0 14.4 %collective-permute-start.23 = (bf16[512,256]{1,0:T(8,128)(2,1)S(1)}, bf16[512,256]{1,0:T(8,128)(2,1)S(1)}, u32[]{:S(2)}, u32[]{:S(2)}) collective-permute-start(bf16[512,256]{1,0:T(8,128)(2,1)S(1)} %constant_dynamic-update-slice_fusion.refs_0_), channel_id=1, source_target_pairs={{8,0},{16,8},{24,16},{9,1},{17,9},{25,17},{10,2},{18,10},{26,18},{... | collective-permute-start | bytes 786440 | tf_op jit(solution)/shard_map/ppermute | solution.py:272
  188.3 7.5 %copy-start.15 = (bf16[512,256]{1,0:T(8,128)(2,1)}, bf16[512,256]{1,0:T(8,128)(2,1)S(1)}, u32[]{:S(2)}) copy-start(bf16[512,256]{1,0:T(8,128)(2,1)S(1)} %collective-permute-done.28.refs_1_) | copy-start | bytes 786436
  188.3 17.1 %collective-permute-start.25 = (bf16[512,256]{1,0:T(8,128)(2,1)S(1)}, bf16[512,256]{1,0:T(8,128)(2,1)S(1)}, u32[]{:S(2)}, u32[]{:S(2)}) collective-permute-start(bf16[512,256]{1,0:T(8,128)(2,1)S(1)} %collective-permute-done.24.refs_4_), channel_id=1, source_target_pairs={{8,0},{16,24},{9,1},{17,25},{10,2},{18,26},{11,3},{19,27},{12,4},{... | collective-permute-start | bytes 786440 | tf_op jit(solution)/shard_map/ppermute | solution.py:273
  211.9 1.8 collective-permute-start.32
  214.9 6.3 %collective-permute-start.33 = (bf16[4,32,640]{2,1,0:T(8,128)(2,1)S(1)}, bf16[4,32,640]{2,1,0:T(8,128)(2,1)S(1)}, u32[]{:S(2)}, u32[]{:S(2)}) collective-permute-start(bf16[4,32,640]{2,1,0:T(8,128)(2,1)S(1)} %fusion.1), channel_id=1, source_target_pairs={{0,2},{1,3},{2,0},{3,1},{4,6},{5,7},{6,4},{7,5},{8,10},{9,11},{10,... | collective-permute-start | bytes 491528 | tf_op jit(solution)/shard_map/ppermute | solution.py:23
  221.4 11.6 %collective-permute-start.34 = (bf16[128,640]{1,0:T(8,128)(2,1)S(1)}, bf16[128,640]{1,0:T(8,128)(2,1)S(1)}, u32[]{:S(2)}, u32[]{:S(2)}) collective-permute-start(bf16[128,640]{1,0:T(8,128)(2,1)S(1)} %pad_maximum_fusion.6), channel_id=1, source_target_pairs={{0,0},{1,8},{2,16},{3,24},{4,4},{5,12},{6,20},{7,28},{8,1},{9,9},{... | collective-permute-start | bytes 491528 | tf_op jit(solution)/shard_map/ppermute | solution.py:450
  (12 other events, 42.4 us)

commit v3 on v2

--- a/solution.py
+++ b/solution.py
@@ -13,6 +13,7 @@
 LANES = 128
 OUTER = 4
 VMEM_LIMIT = 56 * 1024 * 1024
+PROJECT_WEIGHT = 20
 
 
 def round_up(value, unit):
@@ -112,40 +113,74 @@
         ],
         compiler_params=pltpu.CompilerParams(vmem_limit_bytes=VMEM_LIMIT),
         cost_estimate=pl.CostEstimate(
-            flops=flops * 6, bytes_accessed=4 * raw_keys.size, transcendentals=0
+            flops=flops, bytes_accessed=2 * raw_keys.size, transcendentals=0
         ),
         name="compress",
     )(raw_keys, raw_values, edge_keys, edge_values, *weights)
 
 
-def project(pieces, weights):
+def cut(weight, shares):
+    rows, columns = weight.shape
+    share = columns // shares
+
+    def kernel(in_ref, out_ref):
+        out_ref[0] = in_ref[...]
+
+    return pl.pallas_call(
+        kernel,
+        out_shape=jax.ShapeDtypeStruct((shares, rows, share), weight.dtype),
+        grid=(shares,),
+        in_specs=[pl.BlockSpec((rows, share), lambda i: (0, i))],
+        out_specs=pl.BlockSpec((1, rows, share), lambda i: (i, 0, 0)),
+        cost_estimate=pl.CostEstimate(flops=0, bytes_accessed=0, transcendentals=0),
+        name="cut",
+    )(weight)
+
+
+def project(pieces, weight):
     part, depth = pieces[0].shape
     rows = part * len(pieces)
-    shares, share, columns = weights[0].shape
+    columns = weight.shape[1]
+    group = len(pieces) // 2
 
     def kernel(*refs):
-        piece_refs = refs[: len(pieces)]
-        weight_refs = refs[len(pieces) : -2]
-        out_ref, all_ref = refs[-2:]
-        for index, weight_ref in enumerate(weight_refs):
-            for owner in range(shares):
-                start = (owner * len(weights) + index) * share
-                all_ref[start : start + share, :] = weight_ref[owner]
-        for index, piece in enumerate(piece_refs):
-            out_ref[index * part : (index + 1) * part, :] = jnp.dot(
-                piece[...], all_ref[...], preferred_element_type=jnp.float32
+        piece_refs, weight_hbm = refs[: len(pieces)], refs[len(pieces)]
+        out_ref, rows_ref, weight_ref, sems = refs[len(pieces) + 1 :]
+        copies = [
+            pltpu.make_async_copy(
+                piece, rows_ref.at[index * part : (index + 1) * part], sems.at[index]
+            )
+            for index, piece in enumerate(piece_refs)
+        ]
+        bring = pltpu.make_async_copy(weight_hbm, weight_ref, sems.at[len(pieces)])
+        bring.start()
+        for copy in copies:
+            copy.start()
+        bring.wait()
+        for start in range(0, len(pieces), group):
+            for copy in copies[start : start + group]:
+                copy.wait()
+            place = slice(start * part, (start + group) * part)
+            out_ref[place, :] = jnp.dot(
+                rows_ref[place, :], weight_ref[...], preferred_element_type=jnp.float32
             ).astype(jnp.bfloat16)
 
     return pl.pallas_call(
         kernel,
         out_shape=jax.ShapeDtypeStruct((rows, columns), jnp.bfloat16),
-        scratch_shapes=[pltpu.VMEM((depth, columns), jnp.bfloat16)],
+        in_specs=[pl.BlockSpec(memory_space=pl.ANY)] * (len(pieces) + 1),
+        scratch_shapes=[
+            pltpu.VMEM((rows, depth), jnp.bfloat16),
+            pltpu.VMEM((depth, columns), jnp.bfloat16),
+            pltpu.SemaphoreType.DMA((len(pieces) + 1,)),
+        ],
         compiler_params=pltpu.CompilerParams(vmem_limit_bytes=VMEM_LIMIT),
         cost_estimate=pl.CostEstimate(
-            flops=2 * rows * depth * columns, bytes_accessed=2 * rows * depth, transcendentals=0
+            flops=PROJECT_WEIGHT * 2 * rows * depth * columns,
+            bytes_accessed=2 * rows * depth, transcendentals=0,
         ),
         name="project",
-    )(*pieces, *weights)
+    )(*pieces, weight)
 
 
 def attend(here, queries, head, packed, limits, places, key_width, masked, layout):
@@ -209,7 +244,7 @@
 
 def expel(place, pieces, weights, before, chunk, chunks, shape):
     rows, width = pieces[0].shape
-    depth, step, single = 4 * width, weights[0].shape[0], width // 2
+    depth, step, single = 4 * width, weights[0].shape[1], width // 2
     last = shape is not None
 
     def kernel(place_ref, *refs):
@@ -227,10 +262,9 @@
                 (own[...], z), (lower, (z + 3) & 3), (upper, (z + 1) & 3), (far[...], z ^ 2)
             ):
                 starts = [((at * 2 + inner) * chunks + chunk) * single for inner in (y, 1 - y)]
-                both = [weight[:, pl.ds(pl.multiple_of(start, single), single)] for start in starts]
-                product = lax.dot_general(
-                    block, jnp.concatenate(both, axis=1), (((1,), (1,)), ((), ())),
-                    preferred_element_type=jnp.float32,
+                both = [weight[pl.ds(pl.multiple_of(start, single), single), :] for start in starts]
+                product = jnp.dot(
+                    block, jnp.concatenate(both, axis=0), preferred_element_type=jnp.float32
                 )
                 total = product if total is None else total + product
             if not last:
@@ -274,19 +308,23 @@
     return block, up, down, passed, far
 
 
+def ring_pieces(block, axis):
+    before = lax.ppermute(block, axis, [(i, (i + 1) % 4) for i in range(4)])
+    after = lax.ppermute(block, axis, [((i + 1) % 4, i) for i in range(4)])
+    return block, before, after, swap(block, axis, 2)
+
+
 def gather_line(block, axis, dim):
     count = lax.axis_size(axis)
     if count != 4:
         return lax.all_gather(block, axis, axis=dim, tiled=True)
     me = lax.axis_index(axis)
-    block, up, down, passed, far = line_pieces(block, axis)
-    lower = jnp.where(me == 0, passed, up)
-    upper = jnp.where(me == 3, passed, down)
+    block, before, after, far = ring_pieces(block, axis)
     size = block.shape[dim]
     shape = list(block.shape)
     shape[dim] = count * size
     out = jnp.zeros(shape, block.dtype)
-    for piece, place in ((block, me), (lower, (me + 3) % 4), (upper, (me + 1) % 4), (far, me ^ 2)):
+    for piece, place in ((block, me), (before, (me + 3) % 4), (after, (me + 1) % 4), (far, me ^ 2)):
         out = lax.dynamic_update_slice_in_dim(out, piece, place * size, dim)
     return out
 
@@ -316,14 +354,14 @@
     seq_axes = ("outer", "inner") if fast else "outer"
     shares = outer * inner if fast else outer
     share = query_weight.shape[1] // shares
-    halves = 2 if fast and part % 32 == 0 else 1
-    weight = []
-    for half in range(halves):
-        rows = slice(half * part // halves, (half + 1) * part // halves)
-        sent = jnp.stack([query_weight[rows, i * share : (i + 1) * share] for i in range(shares)])
-        weight.append(lax.all_to_all(sent, seq_axes, split_axis=0, concat_axis=0, tiled=True))
+    if fast:
+        sent = cut(query_weight, shares)
+    else:
+        sent = jnp.stack([query_weight[:, i * share : (i + 1) * share] for i in range(shares)])
+    weight = lax.all_to_all(sent, seq_axes, split_axis=0, concat_axis=0, tiled=True)
     if not fast:
-        weight = lax.all_gather(weight[0], "inner", axis=1).reshape(model, share)
+        weight = lax.all_gather(weight, "inner", axis=1)
+    weight = weight.reshape(model, share)
     heads_here = share // key_width
 
     edge = jnp.concatenate([raw_keys[:STRIDE], raw_values[:STRIDE]], axis=1)
@@ -335,9 +373,9 @@
     if fast:
         quarter = row_count // heads_axis
         mine = lax.dynamic_slice_in_dim(tokens, h * quarter, quarter, 0)
-        mine, up, down, passed, far = line_pieces(mine, "outer")
+        mine, before, after, far = ring_pieces(mine, "outer")
         first = jnp.concatenate([mine, far], axis=0)
-        second = jnp.concatenate([jnp.where(z == 0, passed, up), jnp.where(z == 3, passed, down)], axis=0)
+        second = jnp.concatenate([before, after], axis=0)
         first = jnp.concatenate([first, swap(first, "inner", 1)], axis=0)
         second = jnp.concatenate([second, swap(second, "head", 2)], axis=0)
         pieces = [first, second, swap(first, "head", 2), swap(second, "inner", 1)]
@@ -346,10 +384,9 @@
             (0, 0, 2), (3, 0, 2), (0, 1, 2), (3, 1, 2), (1, 1, 0), (2, 1, 0), (1, 1, 2), (2, 1, 2),
         ]
         steps = steps + [(a, b, k ^ 1) for a, b, k in steps]
-        queries = [
-            project(pieces, weight),
-            project([swap(piece, "head", 1) for piece in pieces], weight),
-        ]
+        weight, late = lax.optimization_barrier((weight, pieces[3]))
+        partners = [swap(piece, "head", 1) for piece in (*pieces[:3], late)]
+        queries = [project([*pieces, *partners], weight)]
 
         def of_block(block, z, h):
             line, side, turn = steps[block]
@@ -405,8 +442,7 @@
         limits = jnp.asarray(limits, jnp.int32)
 
     if fast:
-        turned = output_weight.T
-        out_weights = [turned, swap(turned, "inner", 1)]
+        out_weights = [output_weight, swap(output_weight, "inner", 1)]
     else:
         out_weights = lax.all_gather(output_weight, "inner", axis=1, tiled=True)
 

time: 235 us -> 230 us (0.979)
  waiting for transfers between devices: 105 us -> 99.2 us
  local copies, waits for them, and re-layouts: 22.2 us -> 16.5 us
  starting transfers between devices: 55 us -> 60.2 us
  Pallas kernels: 40 us -> 43.2 us
    ppermute x21, waiting for transfers between devices: 73 us -> 86.1 us  [swap(): lax.ppermute(block, axis, [(i, i ^ bit) for i in range(lax.axis_size(axis...]
    ppermute x4 -> x2, waiting for transfers between devices: 14.7 us -> 4.41 us  [line_pieces(): passed = lax.ppermute(far, axis, [(1, 0), (2, 3)])]
    unnamed x57 -> x31, local copies, waits for them, and re-layouts: 14.7 us -> 6.43 us
    ppermute x0 -> x4, starting transfers between devices: none -> 7.69 us  [the longest x2 6.18 us: ring_pieces(): after = lax.ppermute(block, axis, [((i + 1) % 4, i) for i in range(4)])]
    ppermute x21, starting transfers between devices: 20.8 us -> 28.2 us  [swap(): lax.ppermute(block, axis, [(i, i ^ bit) for i in range(lax.axis_size(axis...]
    ppermute x4 -> x2, waiting for transfers between devices: 7.27 us -> 0.86 us  [line_pieces(): down = lax.ppermute(block, axis, [(i + 1, i) for i in range(3)])]
    pallas_call x0 -> x1, Pallas kernels: none -> 5.63 us  [cut(): pl.pallas_call(kernel, out_shape=jax.ShapeDtypeStruct((shares, rows, shar...]
    ppermute x4 -> x2, starting transfers between devices: 12.7 us -> 7.38 us  [line_pieces(): up = lax.ppermute(block, axis, [(i, i + 1) for i in range(3)])]
  transfers between devices with their start and end apart: 37 -> 34, of which waited for: 15 -> 15; matrix products, arithmetic and copies ran while one was open for 11% -> 10% of each run, Pallas kernels for 15% -> 16%
where the time goes in v3:
time: 230 us; the launch traced here: 229 us
  waiting for transfers between devices  99.2 us (43%)
  starting transfers between devices  60.2 us (26%)
  Pallas kernels  43.2 us (19%)
  local copies, waits for them, and re-layouts  16.5 us (7%)
  other arithmetic  9.49 us (4%)
    ppermute x21, waiting for transfers between devices, swap(): lax.ppermute(block, axis, [(i, i ^ bit) for i in range(lax.axis_size(axis...  86.1 us
    ppermute x21, starting transfers between devices, swap(): lax.ppermute(block, axis, [(i, i ^ bit) for i in range(lax.axis_size(axis...  28.2 us
    pallas_call x2, Pallas kernels, attend(): pl.pallas_call(kernel, out_shape=(shape,) * outputs, in_specs=[pl.BlockSp...  12.2 us
    pallas_call x2, Pallas kernels, expel(): pl.pallas_call(kernel, out_shape=out_shape, in_specs=[pl.BlockSpec(memory...  10.7 us
    pallas_call x1, Pallas kernels, compress(): pl.pallas_call(compress_kernel, out_shape=jax.ShapeDtypeStruct((G, blocks...  8.44 us
    ppermute x1, waiting for transfers between devices, shards(): return lax.ppermute(result, ('outer', 'inner', 'head'), route)  7.83 us
    ppermute x2, starting transfers between devices, line_pieces(): up = lax.ppermute(block, axis, [(i, i + 1) for i in range(3)])  7.38 us
    unnamed x31, local copies, waits for them, and re-layouts  6.43 us
  transfers between devices with their start and end apart: 34, of which 15 were waited for; matrix products, arithmetic and copies ran while one was open for 10% of the time, Pallas kernels for 16%

profile of v3, /device:TPU:2, one launch (start us, length us, event | category | flops | bytes accessed | tf_op | source)
XLA Modules:
  0.0 229.0 jit_solution(14702420451095714558)
XLA Ops:
  1.5 1.9 collective-permute-start.11
  3.5 5.6 %cut.1 = bf16[8,320,384]{2,1,0:T(8,128)(2,1)} custom-call(bf16[320,3072]{1,0:T(8,128)(2,1)} %in_ref.1), custom_call_target="tpu_custom_call" | custom-call | tf_op jit(solution)/shard_map/cut/pallas_call | solution.py:129
  9.1 6.0 %all-to-all-start = ((bf16[8,320,384]{2,1,0:T(8,128)(2,1)}), bf16[8,320,384]{2,1,0:T(8,128)(2,1)S(1)}, u32[]{:S(2)}, u32[]{:S(2)}) async-start(bf16[8,320,384]{2,1,0:T(8,128)(2,1)} %cut.1), calls=%async_computation | async-start | bytes 3932160 | tf_op jit(solution)/shard_map/all_to_all | solution.py:361
  17.2 8.4 %compress.1 = bf16[4,64,384]{2,1,0:T(8,128)(2,1)} custom-call(bf16[1024,768]{1,0:T(8,128)(2,1)} %raw_keys.1, bf16[1024,512]{1,0:T(8,128)(2,1)} %raw_values.1, bf16[16,768]{1,0:T(8,128)(2,1)} %slice.24.edge_keys, bf16[16,512]{1,0:T(8,128)(2,1)} %slice.25.edge_values, bf16[192,768]{1,0:T(8,128)(2,1)} %key_expand.1, f32[32,768]{1,0:T(8,128)} %key_mix.1, ...), custom_call_target="tpu_custom_call" | custom-call | flops 2013265920 | bytes 1572864 | tf_op jit(solution)/shard_map/compress/pallas_call | solution.py:106
  26.9 1.5 collective-permute-start.13
  29.1 2.9 %collective-permute-start = (bf16[32,2560]{1,0:T(8,128)(2,1)}, bf16[32,2560]{1,0:T(8,128)(2,1)}, u32[]{:S(2)}, u32[]{:S(2)}) collective-permute-start(bf16[32,2560]{1,0:T(8,128)(2,1)} %constant_dynamic-slice_fusion), channel_id=1, source_target_pairs={{0,16},{8,24},{16,0},{24,8},{1,17},{9,25},{17,1},{25,9},{2,18},{10... | collective-permute-start | bytes 491528 | tf_op jit(solution)/shard_map/ppermute | solution.py:24
  32.0 1.5 collective-permute-start.2
  33.5 2.4 %collective-permute-start.3 = (bf16[32,2560]{1,0:T(8,128)(2,1)}, bf16[32,2560]{1,0:T(8,128)(2,1)S(1)}, u32[]{:S(2)}, u32[]{:S(2)}) collective-permute-start(bf16[32,2560]{1,0:T(8,128)(2,1)} %constant_dynamic-slice_fusion), channel_id=1, source_target_pairs={{8,0},{16,8},{24,16},{0,24},{9,1},{17,9},{25,17},{1,25},{10,2},{18... | collective-permute-start | bytes 491528 | tf_op jit(solution)/shard_map/ppermute | solution.py:313
  36.9 3.8 %collective-permute-start.16 = (bf16[256,384]{1,0:T(8,128)(2,1)S(1)}, bf16[256,384]{1,0:T(8,128)(2,1)S(1)}, u32[]{:S(2)}, u32[]{:S(2)}) collective-permute-start(bf16[256,384]{1,0:T(8,128)(2,1)S(1)} %get-tuple-element.23), channel_id=1, source_target_pairs={{8,0},{16,8},{24,16},{0,24},{9,1},{17,9},{25,17},{1,25},{10,2},{18... | collective-permute-start | bytes 589832 | tf_op jit(solution)/shard_map/ppermute | solution.py:313
  40.7 36.1 %collective-permute-done = bf16[32,2560]{1,0:T(8,128)(2,1)} collective-permute-done((bf16[32,2560]{1,0:T(8,128)(2,1)}, bf16[32,2560]{1,0:T(8,128)(2,1)}, u32[]{:S(2)}, u32[]{:S(2)}) %collective-permute-start) | collective-permute-done | bytes 163872 | tf_op jit(solution)/shard_map/ppermute | solution.py:24
  77.8 1.5 collective-permute-start.1
  81.2 1.6 constant_dynamic-update-slice_fusion.2
  83.5 2.7 %collective-permute-done.1 = bf16[64,2560]{1,0:T(8,128)(2,1)S(1)} collective-permute-done((bf16[64,2560]{1,0:T(8,128)(2,1)S(1)}, bf16[64,2560]{1,0:T(8,128)(2,1)S(1)}, u32[]{:S(2)}, u32[]{:S(2)}) %collective-permute-start.1) | collective-permute-done | bytes 327712 | tf_op jit(solution)/shard_map/ppermute | solution.py:24
  86.1 1.9 pad_maximum_fusion.1.refs_0_
  89.0 1.3 collective-permute-start.6
  90.4 1.7 collective-permute-done.17
  92.1 1.5 collective-permute-start.18
  94.3 8.4 %collective-permute-done.5.refs_2_ = bf16[128,2560]{1,0:T(8,128)(2,1)} collective-permute-done((bf16[128,2560]{1,0:T(8,128)(2,1)}, bf16[128,2560]{1,0:T(8,128)(2,1)}, u32[]{:S(2)}, u32[]{:S(2)}) %collective-permute-start.5) | collective-permute-done | bytes 655392 | tf_op jit(solution)/shard_map/ppermute | solution.py:24
  102.7 4.3 %collective-permute-done.6.refs_3_ = bf16[128,2560]{1,0:T(8,128)(2,1)} collective-permute-done((bf16[128,2560]{1,0:T(8,128)(2,1)}, bf16[128,2560]{1,0:T(8,128)(2,1)}, u32[]{:S(2)}, u32[]{:S(2)}) %collective-permute-start.6) | collective-permute-done | bytes 655392 | tf_op jit(solution)/shard_map/ppermute | solution.py:24
  107.9 1.3 add.630.refs_3_
  109.9 10.9 %collective-permute-done.18 = bf16[1024,384]{1,0:T(8,128)(2,1)} collective-permute-done((bf16[1024,384]{1,0:T(8,128)(2,1)S(1)}, bf16[1024,384]{1,0:T(8,128)(2,1)}, u32[]{:S(2)}, u32[]{:S(2)}) %collective-permute-start.18) | collective-permute-done | bytes 786464 | tf_op jit(solution)/shard_map/ppermute | solution.py:24
  120.8 1.3 collective-permute-start.24
  122.1 1.3 select_bitcast_fusion.1
  123.4 1.3 pad_maximum_fusion
  124.8 6.3 %project.1.refs_0_ = bf16[1024,384]{1,0:T(8,128)(2,1)} custom-call(bf16[128,2560]{1,0:T(8,128)(2,1)} %pad_maximum_fusion.1.refs_0_, bf16[128,2560]{1,0:T(8,128)(2,1)} %constant_dynamic-update-slice_fusion.refs_1_, bf16[128,2560]{1,0:T(8,128)(2,1)} %collective-permute-done.5.refs_2_, bf16[128,2560]{1,0:T(8,128)(2,1)} %collective-permute-done.6.refs_3_, ...), custom_call_target="tpu_custom_call" | custom-call | flops 40265318400 | bytes 5242880 | tf_op jit(solution)/shard_map/project/pallas_call | solution.py:168
  131.1 6.0 %attend.3 = (bf16[512,128]{1,0:T(8,128)(2,1)}, bf16[512,128]{1,0:T(8,128)(2,1)}) custom-call(s32[3]{0:T(128)} %pad_add_fusion.here_ref.place_ref, bf16[1024,384]{1,0:T(8,128)(2,1)} %project.1.refs_0_, bf16[2048,384]{1,0:T(8,128)(2,1)} %bitcast.59, s32[1,2048]{1,0:T(1,128)} %sub.145.refs_2_, s32[1024,1]{1,0:T(8,128)} %add.630.refs_3_), custom_call_target="tpu_custom_call" | custom-call | flops 1342177280 | bytes 1572864 | tf_op jit(solution)/shard_map/attend/pallas_call | solution.py:230
  137.8 6.1 %attend.2 = (bf16[512,128]{1,0:T(8,128)(2,1)}, bf16[512,128]{1,0:T(8,128)(2,1)}) custom-call(s32[3]{0:T(128)} %pad_add_fusion.here_ref.place_ref, bf16[1024,384]{1,0:T(8,128)(2,1)} %project.1.refs_0_, bf16[2048,384]{1,0:T(8,128)(2,1)} %bitcast.60, s32[1,2048]{1,0:T(1,128)} %sub.145.refs_2_, s32[1024,1]{1,0:T(8,128)} %add.630.refs_3_), custom_call_target="tpu_custom_call" | custom-call | flops 1342177280 | bytes 1572864 | tf_op jit(solution)/shard_map/attend/pallas_call | solution.py:230
  144.8 1.4 collective-permute-start.19
  146.3 6.3 %collective-permute-done.25 = bf16[512,128]{1,0:T(8,128)(2,1)S(1)} collective-permute-done((bf16[512,128]{1,0:T(8,128)(2,1)}, bf16[512,128]{1,0:T(8,128)(2,1)S(1)}, u32[]{:S(2)}, u32[]{:S(2)}) %collective-permute-start.25) | collective-permute-done | bytes 131104 | tf_op jit(solution)/shard_map/ppermute | solution.py:24
  152.6 11.0 %collective-permute-start.28 = (bf16[512,256]{1,0:T(8,128)(2,1)S(1)}, bf16[512,256]{1,0:T(8,128)(2,1)S(1)}, u32[]{:S(2)}, u32[]{:S(2)}) collective-permute-start(bf16[512,256]{1,0:T(8,128)(2,1)S(1)} %constant_dynamic-update-slice_fusion.5.refs_0_), channel_id=1, source_target_pairs={{0,16},{8,24},{16,0},{24,8},{1,17},{9,25},{17,1},{25,9},{2,18},{10... | collective-permute-start | bytes 786440 | tf_op jit(solution)/shard_map/ppermute | solution.py:24
  163.6 1.4 collective-permute-start.22
  165.0 1.4 collective-permute-start.26
  166.4 1.3 collective-permute-start.27
  167.7 9.3 %collective-permute-done.28.refs_4_ = bf16[512,256]{1,0:T(8,128)(2,1)S(1)} collective-permute-done((bf16[512,256]{1,0:T(8,128)(2,1)S(1)}, bf16[512,256]{1,0:T(8,128)(2,1)S(1)}, u32[]{:S(2)}, u32[]{:S(2)}) %collective-permute-start.28) | collective-permute-done | bytes 262176 | tf_op jit(solution)/shard_map/ppermute | solution.py:24
  177.0 1.3 collective-permute-start.29
  178.3 5.9 %collective-permute-start.20 = (bf16[512,256]{1,0:T(8,128)(2,1)S(1)}, bf16[512,256]{1,0:T(8,128)(2,1)}, u32[]{:S(2)}, u32[]{:S(2)}) collective-permute-start(bf16[512,256]{1,0:T(8,128)(2,1)S(1)} %constant_dynamic-update-slice_fusion.3.refs_0_), channel_id=1, source_target_pairs={{0,8},{8,16},{16,24},{1,9},{9,17},{17,25},{2,10},{10,18},{18,26},{... | collective-permute-start | bytes 786440 | tf_op jit(solution)/shard_map/ppermute | solution.py:305
  184.3 1.3 collective-permute-start.21
  185.6 1.5 collective-permute-start.23
  187.1 1.6 copy.29.refs_5_
  188.7 2.5 %copy.30.refs_6_ = bf16[2048,320]{1,0:T(8,128)(2,1)} copy(bf16[2048,320]{0,1:T(8,128)(2,1)} %collective-permute-done.24) | data formatting | bytes 2621440 | tf_op jit(solution)/shard_map/ppermute | solution.py:24
  191.7 4.8 %expel.2.refs_7_ = f32[512,640]{1,0:T(8,128)} custom-call(s32[3]{0:T(128)} %pad_add_fusion.here_ref.place_ref, bf16[512,256]{1,0:T(8,128)(2,1)} %copy-done.4, bf16[512,256]{1,0:T(8,128)(2,1)} %copy-done.8, bf16[512,256]{1,0:T(8,128)(2,1)} %collective-permute-done.27.refs_2_, bf16[512,256]{1,0:T(8,128)(2,1)} %collective-permute-done.29.refs_3_, ...), custom_call_target="tpu_custom_call" | custom-call | flops 671088640 | bytes 1310720 | tf_op jit(solution)/shard_map/expel/pallas_call | solution.py:289
  197.3 3.9 %collective-permute-done.23.refs_3_ = bf16[512,256]{1,0:T(8,128)(2,1)} collective-permute-done((bf16[512,256]{1,0:T(8,128)(2,1)S(1)}, bf16[512,256]{1,0:T(8,128)(2,1)}, u32[]{:S(2)}, u32[]{:S(2)}) %collective-permute-start.23) | collective-permute-done | bytes 262176 | tf_op jit(solution)/shard_map/ppermute | solution.py:307
  201.3 6.0 %expel.3 = (f32[4,2,32,640]{3,2,1,0:T(8,128)}, bf16[4,2,32,640]{3,2,1,0:T(8,128)(2,1)}) custom-call(s32[3]{0:T(128)} %pad_add_fusion.here_ref.place_ref, bf16[512,256]{1,0:T(8,128)(2,1)} %copy-done.3, bf16[512,256]{1,0:T(8,128)(2,1)} %collective-permute-done.20.refs_1_, bf16[512,256]{1,0:T(8,128)(2,1)} %collective-permute-done.21.refs_2_, ...), custom_call_target="tpu_custom_call" | custom-call | flops 671088640 | bytes 1310720 | tf_op jit(solution)/shard_map/expel/pallas_call | solution.py:289
  207.2 1.8 collective-permute-done.30
  210.3 1.7 collective-permute-start.31
  212.0 4.6 %collective-permute-done.31 = bf16[4,32,640]{2,1,0:T(8,128)(2,1)S(1)} collective-permute-done((bf16[4,32,640]{2,1,0:T(8,128)(2,1)S(1)}, bf16[4,32,640]{2,1,0:T(8,128)(2,1)S(1)}, u32[]{:S(2)}, u32[]{:S(2)}) %collective-permute-start.31) | collective-permute-done | bytes 163872 | tf_op jit(solution)/shard_map/ppermute | solution.py:24
  216.8 3.7 %collective-permute-start.32 = (bf16[128,640]{1,0:T(8,128)(2,1)S(1)}, bf16[128,640]{1,0:T(8,128)(2,1)S(1)}, u32[]{:S(2)}, u32[]{:S(2)}) collective-permute-start(bf16[128,640]{1,0:T(8,128)(2,1)S(1)} %pad_maximum_fusion.5), channel_id=1, source_target_pairs={{0,0},{1,8},{2,16},{3,24},{4,4},{5,12},{6,20},{7,28},{8,1},{9,9},{... | collective-permute-start | bytes 491528 | tf_op jit(solution)/shard_map/ppermute | solution.py:486
  220.5 7.8 %collective-permute-done.32 = bf16[128,640]{1,0:T(8,128)(2,1)S(1)} collective-permute-done((bf16[128,640]{1,0:T(8,128)(2,1)S(1)}, bf16[128,640]{1,0:T(8,128)(2,1)S(1)}, u32[]{:S(2)}, u32[]{:S(2)}) %collective-permute-start.32) | collective-permute-done | bytes 163872 | tf_op jit(solution)/shard_map/ppermute | solution.py:486
  (91 shorter events, 18.8 us)
Async XLA Ops:
  0.0 28.5 %copy-start = (bf16[128,2560]{1,0:T(8,128)(2,1)S(1)}, bf16[128,2560]{1,0:T(8,128)(2,1)}, u32[]{:S(2)}) copy-start(bf16[128,2560]{1,0:T(8,128)(2,1)} %param.13) | copy-start | bytes 1966084
  1.5 14.5 %collective-permute-start.11 = (bf16[16,1280]{1,0:T(8,128)(2,1)S(1)}, bf16[16,1280]{1,0:T(8,128)(2,1)S(1)}, u32[]{:S(2)}, u32[]{:S(2)}) collective-permute-start(bf16[16,1280]{1,0:T(8,128)(2,1)S(1)} %pad_maximum_fusion.6), channel_id=1, source_target_pairs={{1,0},{2,1},{3,2},{4,3},{5,4},{6,5},{7,6},{8,7},{9,8},{10,9},{11,1... | collective-permute-start | bytes 122888 | tf_op jit(solution)/shard_map/ppermute | solution.py:368
  9.1 6.0 %copy-start.5 = (bf16[768,192]{0,1:T(8,128)(2,1)S(1)}, bf16[768,192]{0,1:T(8,128)(2,1)}, u32[]{:S(2)}) copy-start(bf16[768,192]{0,1:T(8,128)(2,1)} %param.20) | copy-start | bytes 884740
  9.1 97.9 %all-to-all-start = ((bf16[8,320,384]{2,1,0:T(8,128)(2,1)}), bf16[8,320,384]{2,1,0:T(8,128)(2,1)S(1)}, u32[]{:S(2)}, u32[]{:S(2)}) async-start(bf16[8,320,384]{2,1,0:T(8,128)(2,1)} %cut.1), calls=%async_computation | async-start | bytes 3932160 | tf_op jit(solution)/shard_map/all_to_all | solution.py:361
  26.5 7.0 %collective-permute-start.14 = (bf16[64,384]{1,0:T(8,128)(2,1)S(1)}, bf16[64,384]{1,0:T(8,128)(2,1)S(1)}, u32[]{:S(2)}, u32[]{:S(2)}) collective-permute-start(bf16[64,384]{1,0:T(8,128)(2,1)S(1)} %get-tuple-element.26), channel_id=1, source_target_pairs={{0,3},{1,2},{2,1},{3,0},{4,7},{5,6},{6,5},{7,4},{8,11},{9,10},{10,... | collective-permute-start | bytes 147464 | tf_op jit(solution)/shard_map/ppermute | solution.py:24
  26.9 8.9 %collective-permute-start.13 = (bf16[64,384]{1,0:T(8,128)(2,1)S(1)}, bf16[64,384]{1,0:T(8,128)(2,1)S(1)}, u32[]{:S(2)}, u32[]{:S(2)}) collective-permute-start(bf16[64,384]{1,0:T(8,128)(2,1)S(1)} %get-tuple-element.27), channel_id=1, source_target_pairs={{0,2},{1,3},{2,0},{3,1},{4,6},{5,7},{6,4},{7,5},{8,10},{9,11},{10,... | collective-permute-start | bytes 147464 | tf_op jit(solution)/shard_map/ppermute | solution.py:24
  28.4 7.5 %collective-permute-start.12 = (bf16[64,384]{1,0:T(8,128)(2,1)S(1)}, bf16[64,384]{1,0:T(8,128)(2,1)}, u32[]{:S(2)}, u32[]{:S(2)}) collective-permute-start(bf16[64,384]{1,0:T(8,128)(2,1)S(1)} %get-tuple-element.28), channel_id=1, source_target_pairs={{0,1},{1,0},{2,3},{3,2},{4,5},{5,4},{6,7},{7,6},{8,9},{9,8},{10,11... | collective-permute-start | bytes 147464 | tf_op jit(solution)/shard_map/ppermute | solution.py:24
  29.1 47.6 %collective-permute-start = (bf16[32,2560]{1,0:T(8,128)(2,1)}, bf16[32,2560]{1,0:T(8,128)(2,1)}, u32[]{:S(2)}, u32[]{:S(2)}) collective-permute-start(bf16[32,2560]{1,0:T(8,128)(2,1)} %constant_dynamic-slice_fusion), channel_id=1, source_target_pairs={{0,16},{8,24},{16,0},{24,8},{1,17},{9,25},{17,1},{25,9},{2,18},{10... | collective-permute-start | bytes 491528 | tf_op jit(solution)/shard_map/ppermute | solution.py:24
  32.0 45.7 %collective-permute-start.2 = (bf16[32,2560]{1,0:T(8,128)(2,1)}, bf16[32,2560]{1,0:T(8,128)(2,1)}, u32[]{:S(2)}, u32[]{:S(2)}) collective-permute-start(bf16[32,2560]{1,0:T(8,128)(2,1)} %constant_dynamic-slice_fusion), channel_id=1, source_target_pairs={{0,8},{8,16},{16,24},{24,0},{1,9},{9,17},{17,25},{25,1},{2,10},{10... | collective-permute-start | bytes 491528 | tf_op jit(solution)/shard_map/ppermute | solution.py:312
  33.5 45.8 %collective-permute-start.3 = (bf16[32,2560]{1,0:T(8,128)(2,1)}, bf16[32,2560]{1,0:T(8,128)(2,1)S(1)}, u32[]{:S(2)}, u32[]{:S(2)}) collective-permute-start(bf16[32,2560]{1,0:T(8,128)(2,1)} %constant_dynamic-slice_fusion), channel_id=1, source_target_pairs={{8,0},{16,8},{24,16},{0,24},{9,1},{17,9},{25,17},{1,25},{10,2},{18... | collective-permute-start | bytes 491528 | tf_op jit(solution)/shard_map/ppermute | solution.py:313
  36.8 46.6 %collective-permute-start.15 = (bf16[256,384]{1,0:T(8,128)(2,1)S(1)}, bf16[256,384]{1,0:T(8,128)(2,1)S(1)}, u32[]{:S(2)}, u32[]{:S(2)}) collective-permute-start(bf16[256,384]{1,0:T(8,128)(2,1)S(1)} %get-tuple-element.23), channel_id=1, source_target_pairs={{0,8},{8,16},{16,24},{24,0},{1,9},{9,17},{17,25},{25,1},{2,10},{10... | collective-permute-start | bytes 589832 | tf_op jit(solution)/shard_map/ppermute | solution.py:312
  36.9 53.5 %collective-permute-start.16 = (bf16[256,384]{1,0:T(8,128)(2,1)S(1)}, bf16[256,384]{1,0:T(8,128)(2,1)S(1)}, u32[]{:S(2)}, u32[]{:S(2)}) collective-permute-start(bf16[256,384]{1,0:T(8,128)(2,1)S(1)} %get-tuple-element.23), channel_id=1, source_target_pairs={{8,0},{16,8},{24,16},{0,24},{9,1},{17,9},{25,17},{1,25},{10,2},{18... | collective-permute-start | bytes 589832 | tf_op jit(solution)/shard_map/ppermute | solution.py:313
  76.7 15.3 %collective-permute-start.17 = (bf16[256,384]{1,0:T(8,128)(2,1)S(1)}, bf16[256,384]{1,0:T(8,128)(2,1)S(1)}, u32[]{:S(2)}, u32[]{:S(2)}) collective-permute-start(bf16[256,384]{1,0:T(8,128)(2,1)S(1)} %get-tuple-element.23), channel_id=1, source_target_pairs={{0,16},{8,24},{16,0},{24,8},{1,17},{9,25},{17,1},{25,9},{2,18},{10... | collective-permute-start | bytes 589832 | tf_op jit(solution)/shard_map/ppermute | solution.py:24
  77.8 8.4 %collective-permute-start.1 = (bf16[64,2560]{1,0:T(8,128)(2,1)S(1)}, bf16[64,2560]{1,0:T(8,128)(2,1)S(1)}, u32[]{:S(2)}, u32[]{:S(2)}) collective-permute-start(bf16[64,2560]{1,0:T(8,128)(2,1)S(1)} %pad_maximum_fusion.2), channel_id=1, source_target_pairs={{0,4},{4,0},{1,5},{5,1},{2,6},{6,2},{3,7},{7,3},{8,12},{12,8},{9,1... | collective-permute-start | bytes 983048 | tf_op jit(solution)/shard_map/ppermute | solution.py:24
  80.2 8.1 %collective-permute-start.4 = (bf16[64,2560]{1,0:T(8,128)(2,1)S(1)}, bf16[64,2560]{1,0:T(8,128)(2,1)S(1)}, u32[]{:S(2)}, u32[]{:S(2)}) collective-permute-start(bf16[64,2560]{1,0:T(8,128)(2,1)S(1)} %pad_maximum_fusion.3), channel_id=1, source_target_pairs={{0,2},{1,3},{2,0},{3,1},{4,6},{5,7},{6,4},{7,5},{8,10},{9,11},{10,... | collective-permute-start | bytes 983048 | tf_op jit(solution)/shard_map/ppermute | solution.py:24
  83.4 10.3 %copy-start.11 = (s32[1,1,4,1]{2,3,1,0:T(1,128)S(1)}, s32[1,1,4,1]{2,3,1,0:T(1,128)}, u32[]{:S(2)}) copy-start(s32[1,1,4,1]{2,3,1,0:T(1,128)} %constant.475.clone) | copy-start | bytes 52
  83.4 10.3 %copy-start.10 = (s32[2,4,64]{2,1,0:T(4,128)S(1)}, s32[2,4,64]{2,1,0:T(4,128)}, u32[]{:S(2)}) copy-start(s32[2,4,64]{2,1,0:T(4,128)} %constant.478) | copy-start | bytes 6148
  88.0 14.7 %collective-permute-start.5 = (bf16[128,2560]{1,0:T(8,128)(2,1)}, bf16[128,2560]{1,0:T(8,128)(2,1)}, u32[]{:S(2)}, u32[]{:S(2)}) collective-permute-start(bf16[128,2560]{1,0:T(8,128)(2,1)} %pad_maximum_fusion.1.refs_0_), channel_id=1, source_target_pairs={{0,2},{1,3},{2,0},{3,1},{4,6},{5,7},{6,4},{7,5},{8,10},{9,11},{10,... | collective-permute-start | bytes 1966088 | tf_op jit(solution)/shard_map/ppermute | solution.py:24
  89.0 18.0 %collective-permute-start.6 = (bf16[128,2560]{1,0:T(8,128)(2,1)}, bf16[128,2560]{1,0:T(8,128)(2,1)}, u32[]{:S(2)}, u32[]{:S(2)}) collective-permute-start(bf16[128,2560]{1,0:T(8,128)(2,1)} %constant_dynamic-update-slice_fusion.refs_1_), channel_id=1, source_target_pairs={{0,4},{4,0},{1,5},{5,1},{2,6},{6,2},{3,7},{7,3},{8,12},{12,8},{9,1... | collective-permute-start | bytes 1966088 | tf_op jit(solution)/shard_map/ppermute | solution.py:24
  92.1 28.7 %collective-permute-start.18 = (bf16[1024,384]{1,0:T(8,128)(2,1)S(1)}, bf16[1024,384]{1,0:T(8,128)(2,1)}, u32[]{:S(2)}, u32[]{:S(2)}) collective-permute-start(bf16[1024,384]{1,0:T(8,128)(2,1)S(1)} %constant_dynamic-update-slice_fusion.7), channel_id=1, source_target_pairs={{0,4},{4,0},{1,5},{5,1},{2,6},{6,2},{3,7},{7,3},{8,12},{12,8},{9,1... | collective-permute-start | bytes 2359304 | tf_op jit(solution)/shard_map/ppermute | solution.py:24
  93.8 30.9 %collective-permute-start.7 = (bf16[128,2560]{1,0:T(8,128)(2,1)}, bf16[128,2560]{1,0:T(8,128)(2,1)}, u32[]{:S(2)}, u32[]{:S(2)}) collective-permute-start(bf16[128,2560]{1,0:T(8,128)(2,1)} %pad_maximum_fusion.1.refs_0_), channel_id=1, source_target_pairs={{0,1},{1,0},{2,3},{3,2},{4,5},{5,4},{6,7},{7,6},{8,9},{9,8},{10,11... | collective-permute-start | bytes 1966088 | tf_op jit(solution)/shard_map/ppermute | solution.py:24
  93.8 30.9 %collective-permute-start.8 = (bf16[128,2560]{1,0:T(8,128)(2,1)}, bf16[128,2560]{1,0:T(8,128)(2,1)}, u32[]{:S(2)}, u32[]{:S(2)}) collective-permute-start(bf16[128,2560]{1,0:T(8,128)(2,1)} %constant_dynamic-update-slice_fusion.refs_1_), channel_id=1, source_target_pairs={{0,1},{1,0},{2,3},{3,2},{4,5},{5,4},{6,7},{7,6},{8,9},{9,8},{10,11... | collective-permute-start | bytes 1966088 | tf_op jit(solution)/shard_map/ppermute | solution.py:24
  102.7 22.0 %collective-permute-start.9 = (bf16[128,2560]{1,0:T(8,128)(2,1)}, bf16[128,2560]{1,0:T(8,128)(2,1)}, u32[]{:S(2)}, u32[]{:S(2)}) collective-permute-start(bf16[128,2560]{1,0:T(8,128)(2,1)} %collective-permute-done.5.refs_2_), channel_id=1, source_target_pairs={{0,1},{1,0},{2,3},{3,2},{4,5},{5,4},{6,7},{7,6},{8,9},{9,8},{10,11... | collective-permute-start | bytes 1966088 | tf_op jit(solution)/shard_map/ppermute | solution.py:24
  107.0 16.4 %copy-start.1 = (bf16[8,320,384]{2,1,0:T(8,128)(2,1)}, bf16[8,320,384]{2,1,0:T(8,128)(2,1)S(1)}, u32[]{:S(2)}) copy-start(bf16[8,320,384]{2,1,0:T(8,128)(2,1)S(1)} %all-to-all-done) | copy-start | bytes 5898244
  107.0 17.7 %collective-permute-start.10 = (bf16[128,2560]{1,0:T(8,128)(2,1)}, bf16[128,2560]{1,0:T(8,128)(2,1)}, u32[]{:S(2)}, u32[]{:S(2)}) collective-permute-start(bf16[128,2560]{1,0:T(8,128)(2,1)} %collective-permute-done.6.refs_3_), channel_id=1, source_target_pairs={{0,1},{1,0},{2,3},{3,2},{4,5},{5,4},{6,7},{7,6},{8,9},{9,8},{10,11... | collective-permute-start | bytes 1966088 | tf_op jit(solution)/shard_map/ppermute | solution.py:24
  120.8 57.5 %collective-permute-start.24 = (bf16[2048,320]{0,1:T(8,128)(2,1)}, bf16[2048,320]{0,1:T(8,128)(2,1)}, u32[]{:S(2)}, u32[]{:S(2)}) collective-permute-start(bf16[2048,320]{0,1:T(8,128)(2,1)} %param.17), channel_id=1, source_target_pairs={{0,4},{4,0},{1,5},{5,1},{2,6},{6,2},{3,7},{7,3},{8,12},{12,8},{9,1... | collective-permute-start | bytes 3932168 | tf_op jit(solution)/shard_map/ppermute | solution.py:24
  137.1 9.1 %copy-start.9 = (bf16[512,128]{1,0:T(8,128)(2,1)S(1)}, bf16[512,128]{1,0:T(8,128)(2,1)}, u32[]{:S(2)}) copy-start(bf16[512,128]{1,0:T(8,128)(2,1)} %get-tuple-element.17) | copy-start | bytes 393220
  137.1 15.4 %collective-permute-start.25 = (bf16[512,128]{1,0:T(8,128)(2,1)}, bf16[512,128]{1,0:T(8,128)(2,1)S(1)}, u32[]{:S(2)}, u32[]{:S(2)}) collective-permute-start(bf16[512,128]{1,0:T(8,128)(2,1)} %get-tuple-element.18), channel_id=1, source_target_pairs={{0,4},{4,0},{1,5},{5,1},{2,6},{6,2},{3,7},{7,3},{8,12},{12,8},{9,1... | collective-permute-start | bytes 393224 | tf_op jit(solution)/shard_map/ppermute | solution.py:24
  137.8 49.3 %copy-start.2 = (bf16[2048,320]{0,1:T(8,128)(2,1)S(1)}, bf16[2048,320]{0,1:T(8,128)(2,1)}, u32[]{:S(2)}) copy-start(bf16[2048,320]{0,1:T(8,128)(2,1)} %param.17) | copy-start | bytes 3932164
  144.8 18.7 %collective-permute-start.19 = (bf16[512,128]{1,0:T(8,128)(2,1)}, bf16[512,128]{1,0:T(8,128)(2,1)S(1)}, u32[]{:S(2)}, u32[]{:S(2)}) collective-permute-start(bf16[512,128]{1,0:T(8,128)(2,1)} %get-tuple-element.16), channel_id=1, source_target_pairs={{0,4},{4,0},{1,5},{5,1},{2,6},{6,2},{3,7},{7,3},{8,12},{12,8},{9,1... | collective-permute-start | bytes 393224 | tf_op jit(solution)/shard_map/ppermute | solution.py:24
  152.6 36.1 %copy-start.4 = (bf16[512,256]{1,0:T(8,128)(2,1)}, bf16[512,256]{1,0:T(8,128)(2,1)S(1)}, u32[]{:S(2)}) copy-start(bf16[512,256]{1,0:T(8,128)(2,1)S(1)} %constant_dynamic-update-slice_fusion.5.refs_0_) | copy-start | bytes 786436
  152.6 24.5 %collective-permute-start.28 = (bf16[512,256]{1,0:T(8,128)(2,1)S(1)}, bf16[512,256]{1,0:T(8,128)(2,1)S(1)}, u32[]{:S(2)}, u32[]{:S(2)}) collective-permute-start(bf16[512,256]{1,0:T(8,128)(2,1)S(1)} %constant_dynamic-update-slice_fusion.5.refs_0_), channel_id=1, source_target_pairs={{0,16},{8,24},{16,0},{24,8},{1,17},{9,25},{17,1},{25,9},{2,18},{10... | collective-permute-start | bytes 786440 | tf_op jit(solution)/shard_map/ppermute | solution.py:24
  163.6 27.6 %copy-start.3 = (bf16[512,256]{1,0:T(8,128)(2,1)}, bf16[512,256]{1,0:T(8,128)(2,1)S(1)}, u32[]{:S(2)}) copy-start(bf16[512,256]{1,0:T(8,128)(2,1)S(1)} %constant_dynamic-update-slice_fusion.3.refs_0_) | copy-start | bytes 786436
  163.6 20.7 %collective-permute-start.22 = (bf16[512,256]{1,0:T(8,128)(2,1)S(1)}, bf16[512,256]{1,0:T(8,128)(2,1)S(1)}, u32[]{:S(2)}, u32[]{:S(2)}) collective-permute-start(bf16[512,256]{1,0:T(8,128)(2,1)S(1)} %constant_dynamic-update-slice_fusion.3.refs_0_), channel_id=1, source_target_pairs={{0,16},{8,24},{16,0},{24,8},{1,17},{9,25},{17,1},{25,9},{2,18},{10... | collective-permute-start | bytes 786440 | tf_op jit(solution)/shard_map/ppermute | solution.py:24
  165.0 20.6 %collective-permute-start.26 = (bf16[512,256]{1,0:T(8,128)(2,1)S(1)}, bf16[512,256]{1,0:T(8,128)(2,1)S(1)}, u32[]{:S(2)}, u32[]{:S(2)}) collective-permute-start(bf16[512,256]{1,0:T(8,128)(2,1)S(1)} %constant_dynamic-update-slice_fusion.5.refs_0_), channel_id=1, source_target_pairs={{0,8},{8,16},{16,24},{1,9},{9,17},{17,25},{2,10},{10,18},{18,26},{... | collective-permute-start | bytes 786440 | tf_op jit(solution)/shard_map/ppermute | solution.py:305
  166.4 24.8 %collective-permute-start.27 = (bf16[512,256]{1,0:T(8,128)(2,1)S(1)}, bf16[512,256]{1,0:T(8,128)(2,1)}, u32[]{:S(2)}, u32[]{:S(2)}) collective-permute-start(bf16[512,256]{1,0:T(8,128)(2,1)S(1)} %constant_dynamic-update-slice_fusion.5.refs_0_), channel_id=1, source_target_pairs={{8,0},{16,8},{24,16},{9,1},{17,9},{25,17},{10,2},{18,10},{26,18},{... | collective-permute-start | bytes 786440 | tf_op jit(solution)/shard_map/ppermute | solution.py:306
  177.0 14.2 %copy-start.7 = (bf16[512,256]{1,0:T(8,128)(2,1)}, bf16[512,256]{1,0:T(8,128)(2,1)S(1)}, u32[]{:S(2)}) copy-start(bf16[512,256]{1,0:T(8,128)(2,1)S(1)} %collective-permute-done.28.refs_4_) | copy-start | bytes 786436
  177.0 14.7 %collective-permute-start.29 = (bf16[512,256]{1,0:T(8,128)(2,1)S(1)}, bf16[512,256]{1,0:T(8,128)(2,1)}, u32[]{:S(2)}, u32[]{:S(2)}) collective-permute-start(bf16[512,256]{1,0:T(8,128)(2,1)S(1)} %collective-permute-done.28.refs_4_), channel_id=1, source_target_pairs={{8,0},{16,24},{9,1},{17,25},{10,2},{18,26},{11,3},{19,27},{12,4},{... | collective-permute-start | bytes 786440 | tf_op jit(solution)/shard_map/ppermute | solution.py:307
  178.3 18.1 %collective-permute-start.20 = (bf16[512,256]{1,0:T(8,128)(2,1)S(1)}, bf16[512,256]{1,0:T(8,128)(2,1)}, u32[]{:S(2)}, u32[]{:S(2)}) collective-permute-start(bf16[512,256]{1,0:T(8,128)(2,1)S(1)} %constant_dynamic-update-slice_fusion.3.refs_0_), channel_id=1, source_target_pairs={{0,8},{8,16},{16,24},{1,9},{9,17},{17,25},{2,10},{10,18},{18,26},{... | collective-permute-start | bytes 786440 | tf_op jit(solution)/shard_map/ppermute | solution.py:305
  184.3 6.9 %copy-start.6 = (bf16[512,256]{1,0:T(8,128)(2,1)}, bf16[512,256]{1,0:T(8,128)(2,1)S(1)}, u32[]{:S(2)}) copy-start(bf16[512,256]{1,0:T(8,128)(2,1)S(1)} %collective-permute-done.22.refs_4_) | copy-start | bytes 786436
  184.3 13.1 %collective-permute-start.21 = (bf16[512,256]{1,0:T(8,128)(2,1)S(1)}, bf16[512,256]{1,0:T(8,128)(2,1)}, u32[]{:S(2)}, u32[]{:S(2)}) collective-permute-start(bf16[512,256]{1,0:T(8,128)(2,1)S(1)} %constant_dynamic-update-slice_fusion.3.refs_0_), channel_id=1, source_target_pairs={{8,0},{16,8},{24,16},{9,1},{17,9},{25,17},{10,2},{18,10},{26,18},{... | collective-permute-start | bytes 786440 | tf_op jit(solution)/shard_map/ppermute | solution.py:306
  185.6 5.6 %copy-start.8 = (bf16[512,256]{1,0:T(8,128)(2,1)}, bf16[512,256]{1,0:T(8,128)(2,1)S(1)}, u32[]{:S(2)}) copy-start(bf16[512,256]{1,0:T(8,128)(2,1)S(1)} %collective-permute-done.26.refs_1_) | copy-start | bytes 786436
  185.6 15.7 %collective-permute-start.23 = (bf16[512,256]{1,0:T(8,128)(2,1)S(1)}, bf16[512,256]{1,0:T(8,128)(2,1)}, u32[]{:S(2)}, u32[]{:S(2)}) collective-permute-start(bf16[512,256]{1,0:T(8,128)(2,1)S(1)} %collective-permute-done.22.refs_4_), channel_id=1, source_target_pairs={{8,0},{16,24},{9,1},{17,25},{10,2},{18,26},{11,3},{19,27},{12,4},{... | collective-permute-start | bytes 786440 | tf_op jit(solution)/shard_map/ppermute | solution.py:307
  207.2 1.8 collective-permute-start.30
  210.3 6.3 %collective-permute-start.31 = (bf16[4,32,640]{2,1,0:T(8,128)(2,1)S(1)}, bf16[4,32,640]{2,1,0:T(8,128)(2,1)S(1)}, u32[]{:S(2)}, u32[]{:S(2)}) collective-permute-start(bf16[4,32,640]{2,1,0:T(8,128)(2,1)S(1)} %fusion.1), channel_id=1, source_target_pairs={{0,2},{1,3},{2,0},{3,1},{4,6},{5,7},{6,4},{7,5},{8,10},{9,11},{10,... | collective-permute-start | bytes 491528 | tf_op jit(solution)/shard_map/ppermute | solution.py:24
  216.8 11.5 %collective-permute-start.32 = (bf16[128,640]{1,0:T(8,128)(2,1)S(1)}, bf16[128,640]{1,0:T(8,128)(2,1)S(1)}, u32[]{:S(2)}, u32[]{:S(2)}) collective-permute-start(bf16[128,640]{1,0:T(8,128)(2,1)S(1)} %pad_maximum_fusion.5), channel_id=1, source_target_pairs={{0,0},{1,8},{2,16},{3,24},{4,4},{5,12},{6,20},{7,28},{8,1},{9,9},{... | collective-permute-start | bytes 491528 | tf_op jit(solution)/shard_map/ppermute | solution.py:486

commit v4 on v3

--- a/solution.py
+++ b/solution.py
@@ -12,8 +12,7 @@
 STRIDE = 16
 LANES = 128
 OUTER = 4
-VMEM_LIMIT = 56 * 1024 * 1024
-PROJECT_WEIGHT = 20
+VMEM_LIMIT = 20 * 1024 * 1024
 
 
 def round_up(value, unit):
@@ -119,45 +118,56 @@
     )(raw_keys, raw_values, edge_keys, edge_values, *weights)
 
 
-def cut(weight, shares):
+def cut(weight, shares, parts):
     rows, columns = weight.shape
-    share = columns // shares
-
-    def kernel(in_ref, out_ref):
-        out_ref[0] = in_ref[...]
+    share, part = columns // shares, rows // parts
+
+    def kernel(in_ref, *out_refs):
+        for index, out_ref in enumerate(out_refs):
+            out_ref[0] = in_ref[index * part : (index + 1) * part, :]
 
     return pl.pallas_call(
         kernel,
-        out_shape=jax.ShapeDtypeStruct((shares, rows, share), weight.dtype),
+        out_shape=(jax.ShapeDtypeStruct((shares, part, share), weight.dtype),) * parts,
         grid=(shares,),
         in_specs=[pl.BlockSpec((rows, share), lambda i: (0, i))],
-        out_specs=pl.BlockSpec((1, rows, share), lambda i: (i, 0, 0)),
+        out_specs=(pl.BlockSpec((1, part, share), lambda i: (i, 0, 0)),) * parts,
         cost_estimate=pl.CostEstimate(flops=0, bytes_accessed=0, transcendentals=0),
         name="cut",
     )(weight)
 
 
-def project(pieces, weight):
+def project(pieces, weights):
     part, depth = pieces[0].shape
     rows = part * len(pieces)
-    columns = weight.shape[1]
+    shares, share, columns = weights[0].shape
     group = len(pieces) // 2
+    count = len(pieces)
 
     def kernel(*refs):
-        piece_refs, weight_hbm = refs[: len(pieces)], refs[len(pieces)]
-        out_ref, rows_ref, weight_ref, sems = refs[len(pieces) + 1 :]
+        piece_refs, weight_refs = refs[:count], refs[count : count + len(weights)]
+        out_ref, rows_ref, weight_ref, sems = refs[count + len(weights) :]
         copies = [
             pltpu.make_async_copy(
                 piece, rows_ref.at[index * part : (index + 1) * part], sems.at[index]
             )
             for index, piece in enumerate(piece_refs)
         ]
-        bring = pltpu.make_async_copy(weight_hbm, weight_ref, sems.at[len(pieces)])
-        bring.start()
-        for copy in copies:
+        bring = []
+        for index, weight in enumerate(weight_refs):
+            for owner in range(shares):
+                start = (owner * len(weights) + index) * share
+                bring.append(
+                    pltpu.make_async_copy(
+                        weight.at[owner], weight_ref.at[start : start + share],
+                        sems.at[count + len(bring)],
+                    )
+                )
+        for copy in bring + copies:
             copy.start()
-        bring.wait()
-        for start in range(0, len(pieces), group):
+        for copy in bring:
+            copy.wait()
+        for start in range(0, count, group):
             for copy in copies[start : start + group]:
                 copy.wait()
             place = slice(start * part, (start + group) * part)
@@ -168,19 +178,18 @@
     return pl.pallas_call(
         kernel,
         out_shape=jax.ShapeDtypeStruct((rows, columns), jnp.bfloat16),
-        in_specs=[pl.BlockSpec(memory_space=pl.ANY)] * (len(pieces) + 1),
+        in_specs=[pl.BlockSpec(memory_space=pl.ANY)] * (count + len(weights)),
         scratch_shapes=[
             pltpu.VMEM((rows, depth), jnp.bfloat16),
             pltpu.VMEM((depth, columns), jnp.bfloat16),
-            pltpu.SemaphoreType.DMA((len(pieces) + 1,)),
+            pltpu.SemaphoreType.DMA((count + len(weights) * shares,)),
         ],
         compiler_params=pltpu.CompilerParams(vmem_limit_bytes=VMEM_LIMIT),
         cost_estimate=pl.CostEstimate(
-            flops=PROJECT_WEIGHT * 2 * rows * depth * columns,
-            bytes_accessed=2 * rows * depth, transcendentals=0,
+            flops=2 * rows * depth * columns, bytes_accessed=2 * rows * depth, transcendentals=0
         ),
         name="project",
-    )(*pieces, weight)
+    )(*pieces, *weights)
 
 
 def attend(here, queries, head, packed, limits, places, key_width, masked, layout):
@@ -354,14 +363,17 @@
     seq_axes = ("outer", "inner") if fast else "outer"
     shares = outer * inner if fast else outer
     share = query_weight.shape[1] // shares
-    if fast:
-        sent = cut(query_weight, shares)
+
+    def exchange(block):
+        return lax.all_to_all(block, seq_axes, split_axis=0, concat_axis=0, tiled=True)
+
+    if fast:
+        sent = cut(query_weight, shares, 2)
     else:
-        sent = jnp.stack([query_weight[:, i * share : (i + 1) * share] for i in range(shares)])
-    weight = lax.all_to_all(sent, seq_axes, split_axis=0, concat_axis=0, tiled=True)
-    if not fast:
-        weight = lax.all_gather(weight, "inner", axis=1)
-    weight = weight.reshape(model, share)
+        weight = exchange(
+            jnp.stack([query_weight[:, i * share : (i + 1) * share] for i in range(shares)])
+        )
+        weight = lax.all_gather(weight, "inner", axis=1).reshape(model, share)
     heads_here = share // key_width
 
     edge = jnp.concatenate([raw_keys[:STRIDE], raw_values[:STRIDE]], axis=1)
@@ -374,6 +386,10 @@
         quarter = row_count // heads_axis
         mine = lax.dynamic_slice_in_dim(tokens, h * quarter, quarter, 0)
         mine, before, after, far = ring_pieces(mine, "outer")
+        begin, before, after, far, raw_keys, raw_values = lax.optimization_barrier(
+            (sent[0], before, after, far, raw_keys, raw_values)
+        )
+        weight_first = exchange(begin)
         first = jnp.concatenate([mine, far], axis=0)
         second = jnp.concatenate([before, after], axis=0)
         first = jnp.concatenate([first, swap(first, "inner", 1)], axis=0)
@@ -384,9 +400,7 @@
             (0, 0, 2), (3, 0, 2), (0, 1, 2), (3, 1, 2), (1, 1, 0), (2, 1, 0), (1, 1, 2), (2, 1, 2),
         ]
         steps = steps + [(a, b, k ^ 1) for a, b, k in steps]
-        weight, late = lax.optimization_barrier((weight, pieces[3]))
-        partners = [swap(piece, "head", 1) for piece in (*pieces[:3], late)]
-        queries = [project([*pieces, *partners], weight)]
+        partners = [swap(piece, "head", 1) for piece in pieces]
 
         def of_block(block, z, h):
             line, side, turn = steps[block]
@@ -425,6 +439,9 @@
         packed = packed.reshape(heads_axis * blocks, -1)
         bound = ids
     packed = gather_line(packed, "outer", 0)
+    if fast:
+        begin, packed = lax.optimization_barrier((sent[1], packed))
+        queries = [project([*pieces, *partners], [weight_first, exchange(begin)])]
     packed = gather_pair(packed, "inner").reshape(devices * blocks, -1)
     bound = (STRIDE * bound + BLK - 1).transpose(1, 0, 2, 3).reshape(-1)
     hidden = [bool((bound[i : i + LANES] > context).any()) for i in range(0, len(bound), LANES)]

time: 230 us -> 221 us (0.961)
  Pallas kernels: 43.2 us -> 32.9 us
  local copies, waits for them, and re-layouts: 16.5 us -> 24.2 us
  starting transfers between devices: 60.2 us -> 54.9 us
  other arithmetic: 9.49 us -> 6.26 us
    ppermute x21, starting transfers between devices: 28.2 us -> 17.9 us  [swap(): lax.ppermute(block, axis, [(i, i ^ bit) for i in range(lax.axis_size(axis...]
    unnamed x31 -> x71, local copies, waits for them, and re-layouts: 6.43 us -> 16.6 us
    ppermute x2, waiting for transfers between devices: 0.01 us -> 6.35 us  [ring_pieces(): after = lax.ppermute(block, axis, [((i + 1) % 4, i) for i in range(4)])]
    ppermute x21, waiting for transfers between devices: 86.1 us -> 80.2 us  [swap(): lax.ppermute(block, axis, [(i, i ^ bit) for i in range(lax.axis_size(axis...]
    pallas_call x2, Pallas kernels: 10.7 us -> 5.87 us  [expel(): pl.pallas_call(kernel, out_shape=out_shape, in_specs=[pl.BlockSpec(memory...]
    ppermute x2, waiting for transfers between devices: 0.01 us -> 4.05 us  [ring_pieces(): before = lax.ppermute(block, axis, [(i, (i + 1) % 4) for i in range(4)])]
    pallas_call x2, Pallas kernels: 12.2 us -> 8.31 us  [attend(): pl.pallas_call(kernel, out_shape=(shape,) * outputs, in_specs=[pl.BlockSp...]
    pallas_call x1, Pallas kernels: 8.44 us -> 5.68 us  [compress(): pl.pallas_call(compress_kernel, out_shape=jax.ShapeDtypeStruct((G, blocks...]
  transfers between devices with their start and end apart: 34 -> 35, of which waited for: 15 -> 15; matrix products, arithmetic and copies ran while one was open for 10% -> 7% of each run, Pallas kernels for 16% -> 13%
where the time goes in v4:
time: 221 us; the launch traced here: 219 us
  waiting for transfers between devices  101 us (46%)
  starting transfers between devices  54.9 us (25%)
  Pallas kernels  32.9 us (15%)
  local copies, waits for them, and re-layouts  24.2 us (11%)
  other arithmetic  6.26 us (3%)
    ppermute x21, waiting for transfers between devices, swap(): lax.ppermute(block, axis, [(i, i ^ bit) for i in range(lax.axis_size(axis...  80.2 us
    ppermute x21, starting transfers between devices, swap(): lax.ppermute(block, axis, [(i, i ^ bit) for i in range(lax.axis_size(axis...  17.9 us
    unnamed x71, local copies, waits for them, and re-layouts  16.6 us
    ppermute x2, starting transfers between devices, line_pieces(): up = lax.ppermute(block, axis, [(i, i + 1) for i in range(3)])  8.55 us
    pallas_call x2, Pallas kernels, attend(): pl.pallas_call(kernel, out_shape=(shape,) * outputs, in_specs=[pl.BlockSp...  8.31 us
    pallas_call x1, Pallas kernels, project(): pl.pallas_call(kernel, out_shape=jax.ShapeDtypeStruct((rows, columns), jn...  7.46 us
    all_to_all x2, starting transfers between devices, exchange(): lax.all_to_all(block, seq_axes, split_axis=0, concat_axis=0, tiled=True)  7.3 us
    ppermute x1, waiting for transfers between devices, shards(): return lax.ppermute(result, ('outer', 'inner', 'head'), route)  7.27 us
  transfers between devices with their start and end apart: 35, of which 15 were waited for; matrix products, arithmetic and copies ran while one was open for 7% of the time, Pallas kernels for 13%

profile of v4, /device:TPU:2, one launch (start us, length us, event | category | flops | bytes accessed | tf_op | source)
XLA Modules:
  0.0 219.5 jit_solution(14470679347589624940)
XLA Ops:
  1.1 1.6 collective-permute-start
  2.7 2.2 %collective-permute-start.1 = (bf16[32,2560]{1,0:T(8,128)(2,1)S(1)}, bf16[32,2560]{1,0:T(8,128)(2,1)S(1)}, u32[]{:S(2)}, u32[]{:S(2)}) collective-permute-start(bf16[32,2560]{1,0:T(8,128)(2,1)S(1)} %constant_dynamic-slice_fusion), channel_id=1, source_target_pairs={{8,0},{16,8},{24,16},{0,24},{9,1},{17,9},{25,17},{1,25},{10,2},{18... | collective-permute-start | bytes 491528 | tf_op jit(solution)/shard_map/ppermute | solution.py:322
  7.2 1.9 collective-permute-start.11
  9.2 5.6 %cut.1 = (bf16[8,160,384]{2,1,0:T(8,128)(2,1)}, bf16[8,160,384]{2,1,0:T(8,128)(2,1)}) custom-call(bf16[320,3072]{1,0:T(8,128)(2,1)} %in_ref.1), custom_call_target="tpu_custom_call" | custom-call | tf_op jit(solution)/shard_map/cut/pallas_call | solution.py:129
  15.8 3.7 %collective-permute-done.2 = bf16[32,2560]{1,0:T(8,128)(2,1)S(1)} collective-permute-done((bf16[32,2560]{1,0:T(8,128)(2,1)S(1)}, bf16[32,2560]{1,0:T(8,128)(2,1)S(1)}, u32[]{:S(2)}, u32[]{:S(2)}) %collective-permute-start.2) | collective-permute-done | bytes 163872 | tf_op jit(solution)/shard_map/ppermute | solution.py:23
  20.3 1.5 collective-permute-start.3
  21.8 3.6 %all-to-all-start = ((bf16[8,160,384]{2,1,0:T(8,128)(2,1)}), bf16[8,160,384]{2,1,0:T(8,128)(2,1)S(1)}, u32[]{:S(2)}, u32[]{:S(2)}) async-start(bf16[8,160,384]{2,1,0:T(8,128)(2,1)} %get-tuple-element.25), calls=%async_computation | async-start | bytes 1966080 | tf_op jit(solution)/shard_map/all_to_all | solution.py:368
  31.3 5.7 %compress.1 = bf16[4,64,384]{2,1,0:T(8,128)(2,1)S(1)} custom-call(bf16[1024,768]{1,0:T(8,128)(2,1)S(1)} %copy-done.13, bf16[1024,512]{1,0:T(8,128)(2,1)S(1)} %copy-done.14, bf16[16,768]{1,0:T(8,128)(2,1)S(1)} %slice.24.edge_keys, bf16[16,512]{1,0:T(8,128)(2,1)S(1)} %slice.25.edge_values, bf16[192,768]{1,0:T(8,128)(2,1)S(1)} %copy-done.15, ...), custom_call_target="tpu_custom_call" | custom-call | flops 2013265920 | bytes 1572864 | tf_op jit(solution)/shard_map/compress/pallas_call | solution.py:105
  37.1 1.4 collective-permute-start.13
  39.7 1.4 collective-permute-done.14
  42.1 1.7 collective-permute-start.15
  43.8 2.2 collective-permute-start.16
  47.8 4.1 %collective-permute-done.15 = bf16[256,384]{1,0:T(8,128)(2,1)S(1)} collective-permute-done((bf16[256,384]{1,0:T(8,128)(2,1)S(1)}, bf16[256,384]{1,0:T(8,128)(2,1)S(1)}, u32[]{:S(2)}, u32[]{:S(2)}) %collective-permute-start.15) | collective-permute-done | bytes 196640 | tf_op jit(solution)/shard_map/ppermute | solution.py:321
  51.9 6.3 %collective-permute-done.16 = bf16[256,384]{1,0:T(8,128)(2,1)S(1)} collective-permute-done((bf16[256,384]{1,0:T(8,128)(2,1)S(1)}, bf16[256,384]{1,0:T(8,128)(2,1)S(1)}, u32[]{:S(2)}, u32[]{:S(2)}) %collective-permute-start.16) | collective-permute-done | bytes 196640 | tf_op jit(solution)/shard_map/ppermute | solution.py:322
  58.3 8.4 %collective-permute-done.17 = bf16[256,384]{1,0:T(8,128)(2,1)S(1)} collective-permute-done((bf16[256,384]{1,0:T(8,128)(2,1)S(1)}, bf16[256,384]{1,0:T(8,128)(2,1)S(1)}, u32[]{:S(2)}, u32[]{:S(2)}) %collective-permute-start.17) | collective-permute-done | bytes 196640 | tf_op jit(solution)/shard_map/ppermute | solution.py:23
  68.7 3.7 %all-to-all-start.1 = ((bf16[8,160,384]{2,1,0:T(8,128)(2,1)}), bf16[8,160,384]{2,1,0:T(8,128)(2,1)S(1)}, u32[]{:S(2)}, u32[]{:S(2)}) async-start(bf16[8,160,384]{2,1,0:T(8,128)(2,1)} %get-tuple-element.29), calls=%async_computation.1 | async-start | bytes 1966080 | tf_op jit(solution)/shard_map/all_to_all | solution.py:368
  72.5 1.7 constant_dynamic-update-slice_fusion.refs_1_
  74.2 1.9 collective-permute-start.6
  77.4 6.4 %collective-permute-done.5.refs_2_ = bf16[128,2560]{1,0:T(8,128)(2,1)} collective-permute-done((bf16[128,2560]{1,0:T(8,128)(2,1)S(1)}, bf16[128,2560]{1,0:T(8,128)(2,1)}, u32[]{:S(2)}, u32[]{:S(2)}) %collective-permute-start.5) | collective-permute-done | bytes 655392 | tf_op jit(solution)/shard_map/ppermute | solution.py:23
  83.8 16.7 %collective-permute-done.6.refs_3_ = bf16[128,2560]{1,0:T(8,128)(2,1)} collective-permute-done((bf16[128,2560]{1,0:T(8,128)(2,1)}, bf16[128,2560]{1,0:T(8,128)(2,1)}, u32[]{:S(2)}, u32[]{:S(2)}) %collective-permute-start.6) | collective-permute-done | bytes 655392 | tf_op jit(solution)/shard_map/ppermute | solution.py:23
  100.7 1.4 add.630.refs_3_
  102.2 14.2 %collective-permute-done.18 = bf16[1024,384]{1,0:T(8,128)(2,1)} collective-permute-done((bf16[1024,384]{1,0:T(8,128)(2,1)}, bf16[1024,384]{1,0:T(8,128)(2,1)}, u32[]{:S(2)}, u32[]{:S(2)}) %collective-permute-start.18) | collective-permute-done | bytes 786464 | tf_op jit(solution)/shard_map/ppermute | solution.py:23
  116.4 1.5 select_bitcast_fusion.1
  118.0 1.4 pad_maximum_fusion
  120.4 7.5 %project.1.refs_0_ = bf16[1024,384]{1,0:T(8,128)(2,1)S(1)} custom-call(bf16[128,2560]{1,0:T(8,128)(2,1)S(1)} %pad_maximum_fusion.1.refs_0_, bf16[128,2560]{1,0:T(8,128)(2,1)S(1)} %copy-done.4, bf16[128,2560]{1,0:T(8,128)(2,1)} %collective-permute-done.5.refs_2_, bf16[128,2560]{1,0:T(8,128)(2,1)} %collective-permute-done.6.refs_3_, ...), custom_call_target="tpu_custom_call" | custom-call | flops 2013265920 | bytes 5242880 | tf_op jit(solution)/shard_map/project/pallas_call | solution.py:178
  127.9 4.2 %attend.3 = (bf16[512,128]{1,0:T(8,128)(2,1)S(1)}, bf16[512,128]{1,0:T(8,128)(2,1)S(1)}) custom-call(s32[3]{0:T(128)S(1)} %pad_add_fusion.here_ref.place_ref, bf16[1024,384]{1,0:T(8,128)(2,1)S(1)} %project.1.refs_0_, bf16[2048,384]{1,0:T(8,128)(2,1)S(1)} %bitcast.57, s32[1,2048]{1,0:T(1,128)S(1)} %sub.145.refs_2_, s32[1024,1]{1,0:T(8,128)S(1)} %copy-done.5), custom_call_target="tpu_custom_call" | custom-call | flops 1342177280 | bytes 1572864 | tf_op jit(solution)/shard_map/attend/pallas_call | solution.py:239
  132.1 2.0 collective-permute-start.25
  134.1 4.2 %attend.2 = (bf16[512,128]{1,0:T(8,128)(2,1)S(1)}, bf16[512,128]{1,0:T(8,128)(2,1)S(1)}) custom-call(s32[3]{0:T(128)S(1)} %pad_add_fusion.here_ref.place_ref, bf16[1024,384]{1,0:T(8,128)(2,1)S(1)} %project.1.refs_0_, bf16[2048,384]{1,0:T(8,128)(2,1)S(1)} %bitcast.58, s32[1,2048]{1,0:T(1,128)S(1)} %sub.145.refs_2_, s32[1024,1]{1,0:T(8,128)S(1)} %copy-done.5), custom_call_target="tpu_custom_call" | custom-call | flops 1342177280 | bytes 1572864 | tf_op jit(solution)/shard_map/attend/pallas_call | solution.py:239
  138.4 12.0 %collective-permute-done.25 = bf16[512,128]{1,0:T(8,128)(2,1)S(1)} collective-permute-done((bf16[512,128]{1,0:T(8,128)(2,1)S(1)}, bf16[512,128]{1,0:T(8,128)(2,1)S(1)}, u32[]{:S(2)}, u32[]{:S(2)}) %collective-permute-start.25) | collective-permute-done | bytes 131104 | tf_op jit(solution)/shard_map/ppermute | solution.py:23
  150.5 2.8 %collective-permute-start.28 = (bf16[512,256]{1,0:T(8,128)(2,1)S(1)}, bf16[512,256]{1,0:T(8,128)(2,1)S(1)}, u32[]{:S(2)}, u32[]{:S(2)}) collective-permute-start(bf16[512,256]{1,0:T(8,128)(2,1)S(1)} %constant_dynamic-update-slice_fusion.5.refs_0_), channel_id=1, source_target_pairs={{0,16},{8,24},{16,0},{24,8},{1,17},{9,25},{17,1},{25,9},{2,18},{10... | collective-permute-start | bytes 786440 | tf_op jit(solution)/shard_map/ppermute | solution.py:23
  153.3 1.7 collective-permute-start.22
  155.0 2.6 %collective-permute-start.26 = (bf16[512,256]{1,0:T(8,128)(2,1)S(1)}, bf16[512,256]{1,0:T(8,128)(2,1)S(1)}, u32[]{:S(2)}, u32[]{:S(2)}) collective-permute-start(bf16[512,256]{1,0:T(8,128)(2,1)S(1)} %constant_dynamic-update-slice_fusion.5.refs_0_), channel_id=1, source_target_pairs={{0,8},{8,16},{16,24},{1,9},{9,17},{17,25},{2,10},{10,18},{18,26},{... | collective-permute-start | bytes 786440 | tf_op jit(solution)/shard_map/ppermute | solution.py:314
  157.7 1.3 collective-permute-start.27
  159.0 10.1 %collective-permute-done.28.refs_4_ = bf16[512,256]{1,0:T(8,128)(2,1)S(1)} collective-permute-done((bf16[512,256]{1,0:T(8,128)(2,1)S(1)}, bf16[512,256]{1,0:T(8,128)(2,1)S(1)}, u32[]{:S(2)}, u32[]{:S(2)}) %collective-permute-start.28) | collective-permute-done | bytes 262176 | tf_op jit(solution)/shard_map/ppermute | solution.py:23
  170.3 5.9 %collective-permute-start.20 = (bf16[512,256]{1,0:T(8,128)(2,1)S(1)}, bf16[512,256]{1,0:T(8,128)(2,1)}, u32[]{:S(2)}, u32[]{:S(2)}) collective-permute-start(bf16[512,256]{1,0:T(8,128)(2,1)S(1)} %constant_dynamic-update-slice_fusion.3.refs_0_), channel_id=1, source_target_pairs={{0,8},{8,16},{16,24},{1,9},{9,17},{17,25},{2,10},{10,18},{18,26},{... | collective-permute-start | bytes 786440 | tf_op jit(solution)/shard_map/ppermute | solution.py:314
  176.2 1.3 collective-permute-start.21
  177.6 1.5 collective-permute-start.23
  179.1 1.8 copy.29.refs_5_
  180.9 2.6 %copy.30.refs_6_ = bf16[2048,320]{1,0:T(8,128)(2,1)} copy(bf16[2048,320]{0,1:T(8,128)(2,1)} %collective-permute-done.24) | data formatting | bytes 2621440 | tf_op jit(solution)/shard_map/ppermute | solution.py:23
  184.2 1.4 copy-done.1
  188.5 2.3 %expel.2.refs_7_ = f32[512,640]{1,0:T(8,128)S(1)} custom-call(s32[3]{0:T(128)S(1)} %pad_add_fusion.here_ref.place_ref, bf16[512,256]{1,0:T(8,128)(2,1)S(1)} %constant_dynamic-update-slice_fusion.5.refs_0_, bf16[512,256]{1,0:T(8,128)(2,1)S(1)} %copy-done.10, bf16[512,256]{1,0:T(8,128)(2,1)S(1)} %copy-done.12, ...), custom_call_target="tpu_custom_call" | custom-call | flops 671088640 | bytes 1310720 | tf_op jit(solution)/shard_map/expel/pallas_call | solution.py:298
  190.8 2.7 %collective-permute-done.23.refs_3_ = bf16[512,256]{1,0:T(8,128)(2,1)} collective-permute-done((bf16[512,256]{1,0:T(8,128)(2,1)}, bf16[512,256]{1,0:T(8,128)(2,1)}, u32[]{:S(2)}, u32[]{:S(2)}) %collective-permute-start.23) | collective-permute-done | bytes 262176 | tf_op jit(solution)/shard_map/ppermute | solution.py:316
  193.5 3.5 %expel.3 = (f32[4,2,32,640]{3,2,1,0:T(8,128)S(1)}, bf16[4,2,32,640]{3,2,1,0:T(8,128)(2,1)S(1)}) custom-call(s32[3]{0:T(128)S(1)} %pad_add_fusion.here_ref.place_ref, bf16[512,256]{1,0:T(8,128)(2,1)S(1)} %constant_dynamic-update-slice_fusion.3.refs_0_, bf16[512,256]{1,0:T(8,128)(2,1)} %collective-permute-done.20.refs_1_, ...), custom_call_target="tpu_custom_call" | custom-call | flops 671088640 | bytes 1310720 | tf_op jit(solution)/shard_map/expel/pallas_call | solution.py:298
  197.1 1.6 collective-permute-done.30
  198.9 1.5 collective-permute-start.31
  200.4 4.8 %collective-permute-done.31 = bf16[4,32,640]{2,1,0:T(8,128)(2,1)S(1)} collective-permute-done((bf16[4,32,640]{2,1,0:T(8,128)(2,1)S(1)}, bf16[4,32,640]{2,1,0:T(8,128)(2,1)S(1)}, u32[]{:S(2)}, u32[]{:S(2)}) %collective-permute-start.31) | collective-permute-done | bytes 163872 | tf_op jit(solution)/shard_map/ppermute | solution.py:23
  205.4 6.1 %collective-permute-start.32 = (bf16[128,640]{1,0:T(8,128)(2,1)S(1)}, bf16[128,640]{1,0:T(8,128)(2,1)S(1)}, u32[]{:S(2)}, u32[]{:S(2)}) collective-permute-start(bf16[128,640]{1,0:T(8,128)(2,1)S(1)} %pad_maximum_fusion.5), channel_id=1, source_target_pairs={{0,0},{1,8},{2,16},{3,24},{4,4},{5,12},{6,20},{7,28},{8,1},{9,9},{... | collective-permute-start | bytes 491528 | tf_op jit(solution)/shard_map/ppermute | solution.py:503
  211.5 7.3 %collective-permute-done.32 = bf16[128,640]{1,0:T(8,128)(2,1)S(1)} collective-permute-done((bf16[128,640]{1,0:T(8,128)(2,1)S(1)}, bf16[128,640]{1,0:T(8,128)(2,1)S(1)}, u32[]{:S(2)}, u32[]{:S(2)}) %collective-permute-start.32) | collective-permute-done | bytes 163872 | tf_op jit(solution)/shard_map/ppermute | solution.py:503
  (133 shorter events, 26.0 us)
Async XLA Ops:
  0.0 14.8 %copy-start.29 = (bf16[768,192]{0,1:T(8,128)(2,1)S(1)}, bf16[768,192]{0,1:T(8,128)(2,1)}, u32[]{:S(2)}) copy-start(bf16[768,192]{0,1:T(8,128)(2,1)} %param.20) | copy-start | bytes 884740
  1.1 19.2 %copy-start.21 = (bf16[32,2560]{1,0:T(8,128)(2,1)}, bf16[32,2560]{1,0:T(8,128)(2,1)S(1)}, u32[]{:S(2)}) copy-start(bf16[32,2560]{1,0:T(8,128)(2,1)S(1)} %constant_dynamic-slice_fusion) | copy-start | bytes 491524
  1.1 14.7 %collective-permute-start = (bf16[32,2560]{1,0:T(8,128)(2,1)S(1)}, bf16[32,2560]{1,0:T(8,128)(2,1)S(1)}, u32[]{:S(2)}, u32[]{:S(2)}) collective-permute-start(bf16[32,2560]{1,0:T(8,128)(2,1)S(1)} %constant_dynamic-slice_fusion), channel_id=1, source_target_pairs={{0,8},{8,16},{16,24},{24,0},{1,9},{9,17},{17,25},{25,1},{2,10},{10... | collective-permute-start | bytes 491528 | tf_op jit(solution)/shard_map/ppermute | solution.py:321
  2.7 13.1 %collective-permute-start.1 = (bf16[32,2560]{1,0:T(8,128)(2,1)S(1)}, bf16[32,2560]{1,0:T(8,128)(2,1)S(1)}, u32[]{:S(2)}, u32[]{:S(2)}) collective-permute-start(bf16[32,2560]{1,0:T(8,128)(2,1)S(1)} %constant_dynamic-slice_fusion), channel_id=1, source_target_pairs={{8,0},{16,8},{24,16},{0,24},{9,1},{17,9},{25,17},{1,25},{10,2},{18... | collective-permute-start | bytes 491528 | tf_op jit(solution)/shard_map/ppermute | solution.py:322
  5.0 14.5 %collective-permute-start.2 = (bf16[32,2560]{1,0:T(8,128)(2,1)S(1)}, bf16[32,2560]{1,0:T(8,128)(2,1)S(1)}, u32[]{:S(2)}, u32[]{:S(2)}) collective-permute-start(bf16[32,2560]{1,0:T(8,128)(2,1)S(1)} %constant_dynamic-slice_fusion), channel_id=1, source_target_pairs={{0,16},{8,24},{16,0},{24,8},{1,17},{9,25},{17,1},{25,9},{2,18},{10... | collective-permute-start | bytes 491528 | tf_op jit(solution)/shard_map/ppermute | solution.py:23
  7.2 8.5 %collective-permute-start.11 = (bf16[16,1280]{1,0:T(8,128)(2,1)S(1)}, bf16[16,1280]{1,0:T(8,128)(2,1)S(1)}, u32[]{:S(2)}, u32[]{:S(2)}) collective-permute-start(bf16[16,1280]{1,0:T(8,128)(2,1)S(1)} %pad_maximum_fusion.6), channel_id=1, source_target_pairs={{1,0},{2,1},{3,2},{4,3},{5,4},{6,5},{7,6},{8,7},{9,8},{10,9},{11,1... | collective-permute-start | bytes 122888 | tf_op jit(solution)/shard_map/ppermute | solution.py:380
  14.8 10.5 %copy-start.13 = (bf16[1024,768]{1,0:T(8,128)(2,1)S(1)}, bf16[1024,768]{1,0:T(8,128)(2,1)}, u32[]{:S(2)}) copy-start(bf16[1024,768]{1,0:T(8,128)(2,1)} %raw_keys) | copy-start | bytes 4718596
  14.8 10.6 %copy-start.16 = (bf16[128,768]{1,0:T(8,128)(2,1)S(1)}, bf16[128,768]{1,0:T(8,128)(2,1)}, u32[]{:S(2)}) copy-start(bf16[128,768]{1,0:T(8,128)(2,1)} %value_expand.1) | copy-start | bytes 589828
  20.3 46.5 %collective-permute-start.3 = (bf16[64,2560]{1,0:T(8,128)(2,1)}, bf16[64,2560]{1,0:T(8,128)(2,1)}, u32[]{:S(2)}, u32[]{:S(2)}) collective-permute-start(bf16[64,2560]{1,0:T(8,128)(2,1)} %pad_maximum_fusion.2), channel_id=1, source_target_pairs={{0,4},{4,0},{1,5},{5,1},{2,6},{6,2},{3,7},{7,3},{8,12},{12,8},{9,1... | collective-permute-start | bytes 983048 | tf_op jit(solution)/shard_map/ppermute | solution.py:23
  21.8 46.9 %all-to-all-start = ((bf16[8,160,384]{2,1,0:T(8,128)(2,1)}), bf16[8,160,384]{2,1,0:T(8,128)(2,1)S(1)}, u32[]{:S(2)}, u32[]{:S(2)}) async-start(bf16[8,160,384]{2,1,0:T(8,128)(2,1)} %get-tuple-element.25), calls=%async_computation | async-start | bytes 1966080 | tf_op jit(solution)/shard_map/all_to_all | solution.py:368
  31.3 7.6 %copy-start.26 = (bf16[32,2560]{1,0:T(8,128)(2,1)S(1)}, bf16[32,2560]{1,0:T(8,128)(2,1)}, u32[]{:S(2)}) copy-start(bf16[32,2560]{1,0:T(8,128)(2,1)} %copy-done.25) | copy-start | bytes 491524
  31.3 7.6 %copy-start.28 = (bf16[32,2560]{1,0:T(8,128)(2,1)S(1)}, bf16[32,2560]{1,0:T(8,128)(2,1)}, u32[]{:S(2)}) copy-start(bf16[32,2560]{1,0:T(8,128)(2,1)} %copy-done.27) | copy-start | bytes 491524
  37.0 4.1 %collective-permute-start.14 = (bf16[64,384]{1,0:T(8,128)(2,1)S(1)}, bf16[64,384]{1,0:T(8,128)(2,1)S(1)}, u32[]{:S(2)}, u32[]{:S(2)}) collective-permute-start(bf16[64,384]{1,0:T(8,128)(2,1)S(1)} %get-tuple-element.42), channel_id=1, source_target_pairs={{0,3},{1,2},{2,1},{3,0},{4,7},{5,6},{6,5},{7,4},{8,11},{9,10},{10,... | collective-permute-start | bytes 147464 | tf_op jit(solution)/shard_map/ppermute | solution.py:23
  37.1 4.9 %collective-permute-start.13 = (bf16[64,384]{1,0:T(8,128)(2,1)S(1)}, bf16[64,384]{1,0:T(8,128)(2,1)S(1)}, u32[]{:S(2)}, u32[]{:S(2)}) collective-permute-start(bf16[64,384]{1,0:T(8,128)(2,1)S(1)} %get-tuple-element.43), channel_id=1, source_target_pairs={{0,2},{1,3},{2,0},{3,1},{4,6},{5,7},{6,4},{7,5},{8,10},{9,11},{10,... | collective-permute-start | bytes 147464 | tf_op jit(solution)/shard_map/ppermute | solution.py:23
  38.5 3.6 %collective-permute-start.12 = (bf16[64,384]{1,0:T(8,128)(2,1)S(1)}, bf16[64,384]{1,0:T(8,128)(2,1)S(1)}, u32[]{:S(2)}, u32[]{:S(2)}) collective-permute-start(bf16[64,384]{1,0:T(8,128)(2,1)S(1)} %get-tuple-element.44), channel_id=1, source_target_pairs={{0,1},{1,0},{2,3},{3,2},{4,5},{5,4},{6,7},{7,6},{8,9},{9,8},{10,11... | collective-permute-start | bytes 147464 | tf_op jit(solution)/shard_map/ppermute | solution.py:23
  39.7 27.1 %copy-start.22 = (bf16[32,2560]{1,0:T(8,128)(2,1)S(1)}, bf16[32,2560]{1,0:T(8,128)(2,1)}, u32[]{:S(2)}) copy-start(bf16[32,2560]{1,0:T(8,128)(2,1)} %copy-done.21) | copy-start | bytes 491524
  39.7 27.1 %copy-start.24 = (bf16[32,2560]{1,0:T(8,128)(2,1)S(1)}, bf16[32,2560]{1,0:T(8,128)(2,1)}, u32[]{:S(2)}) copy-start(bf16[32,2560]{1,0:T(8,128)(2,1)} %copy-done.23) | copy-start | bytes 491524
  42.1 9.7 %collective-permute-start.15 = (bf16[256,384]{1,0:T(8,128)(2,1)S(1)}, bf16[256,384]{1,0:T(8,128)(2,1)S(1)}, u32[]{:S(2)}, u32[]{:S(2)}) collective-permute-start(bf16[256,384]{1,0:T(8,128)(2,1)S(1)} %get-tuple-element.39), channel_id=1, source_target_pairs={{0,8},{8,16},{16,24},{24,0},{1,9},{9,17},{17,25},{25,1},{2,10},{10... | collective-permute-start | bytes 589832 | tf_op jit(solution)/shard_map/ppermute | solution.py:321
  43.8 14.4 %collective-permute-start.16 = (bf16[256,384]{1,0:T(8,128)(2,1)S(1)}, bf16[256,384]{1,0:T(8,128)(2,1)S(1)}, u32[]{:S(2)}, u32[]{:S(2)}) collective-permute-start(bf16[256,384]{1,0:T(8,128)(2,1)S(1)} %get-tuple-element.39), channel_id=1, source_target_pairs={{8,0},{16,8},{24,16},{0,24},{9,1},{17,9},{25,17},{1,25},{10,2},{18... | collective-permute-start | bytes 589832 | tf_op jit(solution)/shard_map/ppermute | solution.py:322
  46.0 20.8 %copy-start.3 = (bf16[128,2560]{1,0:T(8,128)(2,1)}, bf16[128,2560]{1,0:T(8,128)(2,1)S(1)}, u32[]{:S(2)}) copy-start(bf16[128,2560]{1,0:T(8,128)(2,1)S(1)} %constant_dynamic-update-slice_fusion.1) | copy-start | bytes 1966084
  46.0 26.4 %collective-permute-start.4 = (bf16[64,2560]{1,0:T(8,128)(2,1)}, bf16[64,2560]{1,0:T(8,128)(2,1)}, u32[]{:S(2)}, u32[]{:S(2)}) collective-permute-start(bf16[64,2560]{1,0:T(8,128)(2,1)} %pad_maximum_fusion.3), channel_id=1, source_target_pairs={{0,2},{1,3},{2,0},{3,1},{4,6},{5,7},{6,4},{7,5},{8,10},{9,11},{10,... | collective-permute-start | bytes 983048 | tf_op jit(solution)/shard_map/ppermute | solution.py:23
  47.0 19.8 %collective-permute-start.17 = (bf16[256,384]{1,0:T(8,128)(2,1)S(1)}, bf16[256,384]{1,0:T(8,128)(2,1)S(1)}, u32[]{:S(2)}, u32[]{:S(2)}) collective-permute-start(bf16[256,384]{1,0:T(8,128)(2,1)S(1)} %get-tuple-element.39), channel_id=1, source_target_pairs={{0,16},{8,24},{16,0},{24,8},{1,17},{9,25},{17,1},{25,9},{2,18},{10... | collective-permute-start | bytes 589832 | tf_op jit(solution)/shard_map/ppermute | solution.py:23
  68.1 8.7 %copy-start.31 = (s32[1,1,4,1]{2,3,1,0:T(1,128)S(1)}, s32[1,1,4,1]{2,3,1,0:T(1,128)}, u32[]{:S(2)}) copy-start(s32[1,1,4,1]{2,3,1,0:T(1,128)} %constant.475.clone) | copy-start | bytes 52
  68.1 8.7 %copy-start.30 = (s32[2,4,64]{2,1,0:T(4,128)S(1)}, s32[2,4,64]{2,1,0:T(4,128)}, u32[]{:S(2)}) copy-start(s32[2,4,64]{2,1,0:T(4,128)} %constant.478) | copy-start | bytes 6148
  68.1 15.7 %collective-permute-start.5 = (bf16[128,2560]{1,0:T(8,128)(2,1)S(1)}, bf16[128,2560]{1,0:T(8,128)(2,1)}, u32[]{:S(2)}, u32[]{:S(2)}) collective-permute-start(bf16[128,2560]{1,0:T(8,128)(2,1)S(1)} %pad_maximum_fusion.1.refs_0_), channel_id=1, source_target_pairs={{0,2},{1,3},{2,0},{3,1},{4,6},{5,7},{6,4},{7,5},{8,10},{9,11},{10,... | collective-permute-start | bytes 1966088 | tf_op jit(solution)/shard_map/ppermute | solution.py:23
  68.7 50.6 %all-to-all-start.1 = ((bf16[8,160,384]{2,1,0:T(8,128)(2,1)}), bf16[8,160,384]{2,1,0:T(8,128)(2,1)S(1)}, u32[]{:S(2)}, u32[]{:S(2)}) async-start(bf16[8,160,384]{2,1,0:T(8,128)(2,1)} %get-tuple-element.29), calls=%async_computation.1 | async-start | bytes 1966080 | tf_op jit(solution)/shard_map/all_to_all | solution.py:368
  74.2 26.4 %collective-permute-start.6 = (bf16[128,2560]{1,0:T(8,128)(2,1)}, bf16[128,2560]{1,0:T(8,128)(2,1)}, u32[]{:S(2)}, u32[]{:S(2)}) collective-permute-start(bf16[128,2560]{1,0:T(8,128)(2,1)} %constant_dynamic-update-slice_fusion.refs_1_), channel_id=1, source_target_pairs={{0,4},{4,0},{1,5},{5,1},{2,6},{6,2},{3,7},{7,3},{8,12},{12,8},{9,1... | collective-permute-start | bytes 1966088 | tf_op jit(solution)/shard_map/ppermute | solution.py:23
  76.1 40.2 %collective-permute-start.18 = (bf16[1024,384]{1,0:T(8,128)(2,1)}, bf16[1024,384]{1,0:T(8,128)(2,1)}, u32[]{:S(2)}, u32[]{:S(2)}) collective-permute-start(bf16[1024,384]{1,0:T(8,128)(2,1)} %copy-done.20), channel_id=1, source_target_pairs={{0,4},{4,0},{1,5},{5,1},{2,6},{6,2},{3,7},{7,3},{8,12},{12,8},{9,1... | collective-permute-start | bytes 2359304 | tf_op jit(solution)/shard_map/ppermute | solution.py:23
  76.9 42.4 %collective-permute-start.7 = (bf16[128,2560]{1,0:T(8,128)(2,1)S(1)}, bf16[128,2560]{1,0:T(8,128)(2,1)}, u32[]{:S(2)}, u32[]{:S(2)}) collective-permute-start(bf16[128,2560]{1,0:T(8,128)(2,1)S(1)} %pad_maximum_fusion.1.refs_0_), channel_id=1, source_target_pairs={{0,1},{1,0},{2,3},{3,2},{4,5},{5,4},{6,7},{7,6},{8,9},{9,8},{10,11... | collective-permute-start | bytes 1966088 | tf_op jit(solution)/shard_map/ppermute | solution.py:23
  76.9 42.4 %collective-permute-start.8 = (bf16[128,2560]{1,0:T(8,128)(2,1)}, bf16[128,2560]{1,0:T(8,128)(2,1)}, u32[]{:S(2)}, u32[]{:S(2)}) collective-permute-start(bf16[128,2560]{1,0:T(8,128)(2,1)} %constant_dynamic-update-slice_fusion.refs_1_), channel_id=1, source_target_pairs={{0,1},{1,0},{2,3},{3,2},{4,5},{5,4},{6,7},{7,6},{8,9},{9,8},{10,11... | collective-permute-start | bytes 1966088 | tf_op jit(solution)/shard_map/ppermute | solution.py:23
  83.8 35.5 %collective-permute-start.9 = (bf16[128,2560]{1,0:T(8,128)(2,1)}, bf16[128,2560]{1,0:T(8,128)(2,1)}, u32[]{:S(2)}, u32[]{:S(2)}) collective-permute-start(bf16[128,2560]{1,0:T(8,128)(2,1)} %collective-permute-done.5.refs_2_), channel_id=1, source_target_pairs={{0,1},{1,0},{2,3},{3,2},{4,5},{5,4},{6,7},{7,6},{8,9},{9,8},{10,11... | collective-permute-start | bytes 1966088 | tf_op jit(solution)/shard_map/ppermute | solution.py:23
  100.6 18.7 %collective-permute-start.10 = (bf16[128,2560]{1,0:T(8,128)(2,1)}, bf16[128,2560]{1,0:T(8,128)(2,1)}, u32[]{:S(2)}, u32[]{:S(2)}) collective-permute-start(bf16[128,2560]{1,0:T(8,128)(2,1)} %collective-permute-done.6.refs_3_), channel_id=1, source_target_pairs={{0,1},{1,0},{2,3},{3,2},{4,5},{5,4},{6,7},{7,6},{8,9},{9,8},{10,11... | collective-permute-start | bytes 1966088 | tf_op jit(solution)/shard_map/ppermute | solution.py:23
  116.3 54.0 %collective-permute-start.24 = (bf16[2048,320]{0,1:T(8,128)(2,1)}, bf16[2048,320]{0,1:T(8,128)(2,1)}, u32[]{:S(2)}, u32[]{:S(2)}) collective-permute-start(bf16[2048,320]{0,1:T(8,128)(2,1)} %param.17), channel_id=1, source_target_pairs={{0,4},{4,0},{1,5},{5,1},{2,6},{6,2},{3,7},{7,3},{8,12},{12,8},{9,1... | collective-permute-start | bytes 3932168 | tf_op jit(solution)/shard_map/ppermute | solution.py:23
  120.4 7.5 %copy-start.5 = (s32[1024,1]{1,0:T(8,128)S(1)}, s32[1024,1]{1,0:T(8,128)}, u32[]{:S(2)}) copy-start(s32[1024,1]{1,0:T(8,128)} %add.630.refs_3_) | copy-start | bytes 12292
  132.1 18.4 %collective-permute-start.25 = (bf16[512,128]{1,0:T(8,128)(2,1)S(1)}, bf16[512,128]{1,0:T(8,128)(2,1)S(1)}, u32[]{:S(2)}, u32[]{:S(2)}) collective-permute-start(bf16[512,128]{1,0:T(8,128)(2,1)S(1)} %get-tuple-element.34), channel_id=1, source_target_pairs={{0,4},{4,0},{1,5},{5,1},{2,6},{6,2},{3,7},{7,3},{8,12},{12,8},{9,1... | collective-permute-start | bytes 393224 | tf_op jit(solution)/shard_map/ppermute | solution.py:23
  138.3 15.0 %collective-permute-start.19 = (bf16[512,128]{1,0:T(8,128)(2,1)S(1)}, bf16[512,128]{1,0:T(8,128)(2,1)S(1)}, u32[]{:S(2)}, u32[]{:S(2)}) collective-permute-start(bf16[512,128]{1,0:T(8,128)(2,1)S(1)} %get-tuple-element.32), channel_id=1, source_target_pairs={{0,4},{4,0},{1,5},{5,1},{2,6},{6,2},{3,7},{7,3},{8,12},{12,8},{9,1... | collective-permute-start | bytes 393224 | tf_op jit(solution)/shard_map/ppermute | solution.py:23
  150.5 18.5 %collective-permute-start.28 = (bf16[512,256]{1,0:T(8,128)(2,1)S(1)}, bf16[512,256]{1,0:T(8,128)(2,1)S(1)}, u32[]{:S(2)}, u32[]{:S(2)}) collective-permute-start(bf16[512,256]{1,0:T(8,128)(2,1)S(1)} %constant_dynamic-update-slice_fusion.5.refs_0_), channel_id=1, source_target_pairs={{0,16},{8,24},{16,0},{24,8},{1,17},{9,25},{17,1},{25,9},{2,18},{10... | collective-permute-start | bytes 786440 | tf_op jit(solution)/shard_map/ppermute | solution.py:23
  153.3 22.9 %collective-permute-start.22 = (bf16[512,256]{1,0:T(8,128)(2,1)S(1)}, bf16[512,256]{1,0:T(8,128)(2,1)}, u32[]{:S(2)}, u32[]{:S(2)}) collective-permute-start(bf16[512,256]{1,0:T(8,128)(2,1)S(1)} %constant_dynamic-update-slice_fusion.3.refs_0_), channel_id=1, source_target_pairs={{0,16},{8,24},{16,0},{24,8},{1,17},{9,25},{17,1},{25,9},{2,18},{10... | collective-permute-start | bytes 786440 | tf_op jit(solution)/shard_map/ppermute | solution.py:23
  155.0 22.5 %collective-permute-start.26 = (bf16[512,256]{1,0:T(8,128)(2,1)S(1)}, bf16[512,256]{1,0:T(8,128)(2,1)S(1)}, u32[]{:S(2)}, u32[]{:S(2)}) collective-permute-start(bf16[512,256]{1,0:T(8,128)(2,1)S(1)} %constant_dynamic-update-slice_fusion.5.refs_0_), channel_id=1, source_target_pairs={{0,8},{8,16},{16,24},{1,9},{9,17},{17,25},{2,10},{10,18},{18,26},{... | collective-permute-start | bytes 786440 | tf_op jit(solution)/shard_map/ppermute | solution.py:314
  157.7 25.8 %collective-permute-start.27 = (bf16[512,256]{1,0:T(8,128)(2,1)S(1)}, bf16[512,256]{1,0:T(8,128)(2,1)S(1)}, u32[]{:S(2)}, u32[]{:S(2)}) collective-permute-start(bf16[512,256]{1,0:T(8,128)(2,1)S(1)} %constant_dynamic-update-slice_fusion.5.refs_0_), channel_id=1, source_target_pairs={{8,0},{16,8},{24,16},{9,1},{17,9},{25,17},{10,2},{18,10},{26,18},{... | collective-permute-start | bytes 786440 | tf_op jit(solution)/shard_map/ppermute | solution.py:315
  169.0 14.5 %copy-start.7 = (bf16[512,256]{1,0:T(8,128)(2,1)}, bf16[512,256]{1,0:T(8,128)(2,1)S(1)}, u32[]{:S(2)}) copy-start(bf16[512,256]{1,0:T(8,128)(2,1)S(1)} %collective-permute-done.28.refs_4_) | copy-start | bytes 786436
  169.0 15.2 %collective-permute-start.29 = (bf16[512,256]{1,0:T(8,128)(2,1)S(1)}, bf16[512,256]{1,0:T(8,128)(2,1)}, u32[]{:S(2)}, u32[]{:S(2)}) collective-permute-start(bf16[512,256]{1,0:T(8,128)(2,1)S(1)} %collective-permute-done.28.refs_4_), channel_id=1, source_target_pairs={{8,0},{16,24},{9,1},{17,25},{10,2},{18,26},{11,3},{19,27},{12,4},{... | collective-permute-start | bytes 786440 | tf_op jit(solution)/shard_map/ppermute | solution.py:316
  170.3 20.5 %collective-permute-start.20 = (bf16[512,256]{1,0:T(8,128)(2,1)S(1)}, bf16[512,256]{1,0:T(8,128)(2,1)}, u32[]{:S(2)}, u32[]{:S(2)}) collective-permute-start(bf16[512,256]{1,0:T(8,128)(2,1)S(1)} %constant_dynamic-update-slice_fusion.3.refs_0_), channel_id=1, source_target_pairs={{0,8},{8,16},{16,24},{1,9},{9,17},{17,25},{2,10},{10,18},{18,26},{... | collective-permute-start | bytes 786440 | tf_op jit(solution)/shard_map/ppermute | solution.py:314
  176.2 14.6 %collective-permute-start.21 = (bf16[512,256]{1,0:T(8,128)(2,1)S(1)}, bf16[512,256]{1,0:T(8,128)(2,1)}, u32[]{:S(2)}, u32[]{:S(2)}) collective-permute-start(bf16[512,256]{1,0:T(8,128)(2,1)S(1)} %constant_dynamic-update-slice_fusion.3.refs_0_), channel_id=1, source_target_pairs={{8,0},{16,8},{24,16},{9,1},{17,9},{25,17},{10,2},{18,10},{26,18},{... | collective-permute-start | bytes 786440 | tf_op jit(solution)/shard_map/ppermute | solution.py:315
  177.6 16.0 %collective-permute-start.23 = (bf16[512,256]{1,0:T(8,128)(2,1)}, bf16[512,256]{1,0:T(8,128)(2,1)}, u32[]{:S(2)}, u32[]{:S(2)}) collective-permute-start(bf16[512,256]{1,0:T(8,128)(2,1)} %collective-permute-done.22.refs_4_), channel_id=1, source_target_pairs={{8,0},{16,24},{9,1},{17,25},{10,2},{18,26},{11,3},{19,27},{12,4},{... | collective-permute-start | bytes 786440 | tf_op jit(solution)/shard_map/ppermute | solution.py:316
  197.1 1.7 collective-permute-start.30
  198.9 6.3 %collective-permute-start.31 = (bf16[4,32,640]{2,1,0:T(8,128)(2,1)S(1)}, bf16[4,32,640]{2,1,0:T(8,128)(2,1)S(1)}, u32[]{:S(2)}, u32[]{:S(2)}) collective-permute-start(bf16[4,32,640]{2,1,0:T(8,128)(2,1)S(1)} %fusion.1), channel_id=1, source_target_pairs={{0,2},{1,3},{2,0},{3,1},{4,6},{5,7},{6,4},{7,5},{8,10},{9,11},{10,... | collective-permute-start | bytes 491528 | tf_op jit(solution)/shard_map/ppermute | solution.py:23
  205.4 13.4 %collective-permute-start.32 = (bf16[128,640]{1,0:T(8,128)(2,1)S(1)}, bf16[128,640]{1,0:T(8,128)(2,1)S(1)}, u32[]{:S(2)}, u32[]{:S(2)}) collective-permute-start(bf16[128,640]{1,0:T(8,128)(2,1)S(1)} %pad_maximum_fusion.5), channel_id=1, source_target_pairs={{0,0},{1,8},{2,16},{3,24},{4,4},{5,12},{6,20},{7,28},{8,1},{9,9},{... | collective-permute-start | bytes 491528 | tf_op jit(solution)/shard_map/ppermute | solution.py:503
  (19 other events, 42.7 us)

commit v5 on v4

--- a/solution.py
+++ b/solution.py
@@ -253,7 +253,7 @@
 
 def expel(place, pieces, weights, before, chunk, chunks, shape):
     rows, width = pieces[0].shape
-    depth, step, single = 4 * width, weights[0].shape[1], width // 2
+    depth, step, single = 4 * width, weights[0].shape[0], width // 2
     last = shape is not None
 
     def kernel(place_ref, *refs):
@@ -271,9 +271,10 @@
                 (own[...], z), (lower, (z + 3) & 3), (upper, (z + 1) & 3), (far[...], z ^ 2)
             ):
                 starts = [((at * 2 + inner) * chunks + chunk) * single for inner in (y, 1 - y)]
-                both = [weight[pl.ds(pl.multiple_of(start, single), single), :] for start in starts]
-                product = jnp.dot(
-                    block, jnp.concatenate(both, axis=0), preferred_element_type=jnp.float32
+                both = [weight[:, pl.ds(pl.multiple_of(start, single), single)] for start in starts]
+                product = lax.dot_general(
+                    block, jnp.concatenate(both, axis=1), (((1,), (1,)), ((), ())),
+                    preferred_element_type=jnp.float32,
                 )
                 total = product if total is None else total + product
             if not last:
@@ -360,6 +361,12 @@
     part = query_weight.shape[0]
     fast = inner == 2 and outer == 4 and heads_axis == 4
 
+    if fast:
+        turned = output_weight.T
+        out_weights = [turned, swap(turned, "inner", 1)]
+    else:
+        out_weights = lax.all_gather(output_weight, "inner", axis=1, tiled=True)
+
     seq_axes = ("outer", "inner") if fast else "outer"
     shares = outer * inner if fast else outer
     share = query_weight.shape[1] // shares
@@ -390,18 +397,11 @@
             (sent[0], before, after, far, raw_keys, raw_values)
         )
         weight_first = exchange(begin)
-        first = jnp.concatenate([mine, far], axis=0)
-        second = jnp.concatenate([before, after], axis=0)
-        first = jnp.concatenate([first, swap(first, "inner", 1)], axis=0)
-        second = jnp.concatenate([second, swap(second, "head", 2)], axis=0)
-        pieces = [first, second, swap(first, "head", 2), swap(second, "inner", 1)]
-        steps = [
-            (0, 0, 0), (3, 0, 0), (0, 1, 0), (3, 1, 0), (1, 0, 0), (2, 0, 0), (1, 0, 2), (2, 0, 2),
-            (0, 0, 2), (3, 0, 2), (0, 1, 2), (3, 1, 2), (1, 1, 0), (2, 1, 0), (1, 1, 2), (2, 1, 2),
-        ]
+        near = jnp.concatenate([mine, before, after, far], axis=0)
+        beside = swap(near, "inner", 1)
+        pieces = [near, beside, swap(near, "head", 2)]
+        steps = [(line, side, turn) for turn in (0, 2) for side in (0, 1) for line in range(4)]
         steps = steps + [(a, b, k ^ 1) for a, b, k in steps]
-        partners = [swap(piece, "head", 1) for piece in pieces]
-
         def of_block(block, z, h):
             line, side, turn = steps[block]
             there = (z, (z + 3) & 3, (z + 1) & 3, z ^ 2)[line]
@@ -438,6 +438,10 @@
         packed = lax.all_to_all(packed, "head", split_axis=0, concat_axis=0, tiled=True)
         packed = packed.reshape(heads_axis * blocks, -1)
         bound = ids
+    if fast:
+        packed, out_weights[1], pieces = lax.optimization_barrier((packed, out_weights[1], pieces))
+        pieces.append(swap(pieces[1], "head", 2))
+        partners = [swap(piece, "head", 1) for piece in pieces]
     packed = gather_line(packed, "outer", 0)
     if fast:
         begin, packed = lax.optimization_barrier((sent[1], packed))
@@ -457,11 +461,6 @@
     else:
         limits = (STRIDE * ids + BLK - 1).transpose(1, 0, 2, 3).reshape(1, -1)
         limits = jnp.asarray(limits, jnp.int32)
-
-    if fast:
-        out_weights = [output_weight, swap(output_weight, "inner", 1)]
-    else:
-        out_weights = lax.all_gather(output_weight, "inner", axis=1, tiled=True)
 
     total = None
     for head in range(heads_here):

time: 221 us -> 211 us (0.955)
  local copies, waits for them, and re-layouts: 24.2 us -> 11.9 us
  waiting for transfers between devices: 101 us -> 106 us
    ppermute x21 -> x20, waiting for transfers between devices: 80.2 us -> 63.8 us  [swap(): lax.ppermute(block, axis, [(i, i ^ bit) for i in range(lax.axis_size(axis...]
    ppermute x1, waiting for transfers between devices: 0.01 us -> 10.8 us  [shards(): lax.ppermute(edge, ('outer', 'inner', 'head'), [(i + 1, i) for i in range...]
    ppermute x2, waiting for transfers between devices: 2.69 us -> 9.43 us  [line_pieces(): passed = lax.ppermute(far, axis, [(1, 0), (2, 3)])]
    unnamed x71 -> x34, local copies, waits for them, and re-layouts: 16.6 us -> 10.8 us
    ppermute x2, waiting for transfers between devices: 0.01 us -> 4.82 us  [line_pieces(): down = lax.ppermute(block, axis, [(i + 1, i) for i in range(3)])]
    ppermute x1, starting transfers between devices: 6.11 us -> 1.92 us  [shards(): return lax.ppermute(result, ('outer', 'inner', 'head'), route)]
    ppermute x2, waiting for transfers between devices: 6.35 us -> 3.37 us  [ring_pieces(): after = lax.ppermute(block, axis, [((i + 1) % 4, i) for i in range(4)])]
    all_to_all x2, starting transfers between devices: 7.3 us -> 9.96 us  [exchange(): lax.all_to_all(block, seq_axes, split_axis=0, concat_axis=0, tiled=True)]
  transfers between devices with their start and end apart: 35 -> 34, of which waited for: 15 -> 19; matrix products, arithmetic and copies ran while one was open for 7% -> 3% of each run, Pallas kernels for 13% -> 6%
where the time goes in v5:
time: 211 us; the launch traced here: 210 us
  waiting for transfers between devices  106 us (50%)
  starting transfers between devices  53.6 us (25%)
  Pallas kernels  31.4 us (15%)
  local copies, waits for them, and re-layouts  11.9 us (6%)
  other arithmetic  5.31 us (3%)
    ppermute x20, waiting for transfers between devices, swap(): lax.ppermute(block, axis, [(i, i ^ bit) for i in range(lax.axis_size(axis...  63.8 us
    ppermute x20, starting transfers between devices, swap(): lax.ppermute(block, axis, [(i, i ^ bit) for i in range(lax.axis_size(axis...  20 us
    unnamed x34, local copies, waits for them, and re-layouts  10.8 us
    ppermute x1, waiting for transfers between devices, shards(): lax.ppermute(edge, ('outer', 'inner', 'head'), [(i + 1, i) for i in range...  10.8 us
    all_to_all x2, starting transfers between devices, exchange(): lax.all_to_all(block, seq_axes, split_axis=0, concat_axis=0, tiled=True)  9.96 us
    ppermute x1, waiting for transfers between devices, shards(): return lax.ppermute(result, ('outer', 'inner', 'head'), route)  9.67 us
    ppermute x2, waiting for transfers between devices, line_pieces(): passed = lax.ppermute(far, axis, [(1, 0), (2, 3)])  9.43 us
    pallas_call x2, Pallas kernels, attend(): pl.pallas_call(kernel, out_shape=(shape,) * outputs, in_specs=[pl.BlockSp...  8.34 us
  transfers between devices with their start and end apart: 34, of which 19 were waited for; matrix products, arithmetic and copies ran while one was open for 3% of the time, Pallas kernels for 6%

profile of v5, /device:TPU:2, one launch (start us, length us, event | category | flops | bytes accessed | tf_op | source)
XLA Modules:
  0.0 210.1 jit_solution(18167793210118118969)
XLA Ops:
  1.1 1.6 collective-permute-start
  2.7 2.2 %collective-permute-start.1 = (bf16[32,2560]{1,0:T(8,128)(2,1)S(1)}, bf16[32,2560]{1,0:T(8,128)(2,1)S(1)}, u32[]{:S(2)}, u32[]{:S(2)}) collective-permute-start(bf16[32,2560]{1,0:T(8,128)(2,1)S(1)} %constant_dynamic-slice_fusion), channel_id=1, source_target_pairs={{8,0},{16,8},{24,16},{0,24},{9,1},{17,9},{25,17},{1,25},{10,2},{18... | collective-permute-start | bytes 491528 | tf_op jit(solution)/shard_map/ppermute | solution.py:323
  5.8 1.5 collective-permute-start.7
  7.3 5.7 %cut.1 = (bf16[8,160,384]{2,1,0:T(8,128)(2,1)}, bf16[8,160,384]{2,1,0:T(8,128)(2,1)}) custom-call(bf16[320,3072]{1,0:T(8,128)(2,1)} %in_ref.1), custom_call_target="tpu_custom_call" | custom-call | tf_op jit(solution)/shard_map/cut/pallas_call | solution.py:129
  13.0 6.5 %collective-permute-done.2 = bf16[32,2560]{1,0:T(8,128)(2,1)S(1)} collective-permute-done((bf16[32,2560]{1,0:T(8,128)(2,1)S(1)}, bf16[32,2560]{1,0:T(8,128)(2,1)S(1)}, u32[]{:S(2)}, u32[]{:S(2)}) %collective-permute-start.2) | collective-permute-done | bytes 163872 | tf_op jit(solution)/shard_map/ppermute | solution.py:23
  20.2 3.9 %all-to-all-start = ((bf16[8,160,384]{2,1,0:T(8,128)(2,1)}), bf16[8,160,384]{2,1,0:T(8,128)(2,1)S(1)}, u32[]{:S(2)}, u32[]{:S(2)}) async-start(bf16[8,160,384]{2,1,0:T(8,128)(2,1)} %get-tuple-element.35), calls=%async_computation | async-start | bytes 1966080 | tf_op jit(solution)/shard_map/all_to_all | solution.py:375
  24.0 1.9 pad_maximum_fusion.1.refs_0_
  25.9 2.0 collective-permute-start.8
  28.5 1.9 collective-permute-start.3
  31.6 10.8 %collective-permute-done.3 = bf16[16,1280]{1,0:T(8,128)(2,1)S(1)} collective-permute-done((bf16[16,1280]{1,0:T(8,128)(2,1)S(1)}, bf16[16,1280]{1,0:T(8,128)(2,1)S(1)}, u32[]{:S(2)}, u32[]{:S(2)}) %collective-permute-start.3) | collective-permute-done | bytes 40992 | tf_op jit(solution)/shard_map/ppermute | solution.py:387
  42.4 1.4 copy-done.3
  43.8 1.2 copy-done.4
  48.7 6.0 %compress.1 = bf16[4,64,384]{2,1,0:T(8,128)(2,1)S(1)} custom-call(bf16[1024,768]{1,0:T(8,128)(2,1)S(1)} %copy-done.3, bf16[1024,512]{1,0:T(8,128)(2,1)S(1)} %copy-done.4, bf16[16,768]{1,0:T(8,128)(2,1)S(1)} %slice.24.edge_keys, bf16[16,512]{1,0:T(8,128)(2,1)S(1)} %slice.25.edge_values, bf16[192,768]{1,0:T(8,128)(2,1)S(1)} %copy-done.5, ...), custom_call_target="tpu_custom_call" | custom-call | flops 2013265920 | bytes 1572864 | tf_op jit(solution)/shard_map/compress/pallas_call | solution.py:105
  54.7 2.3 %collective-permute-start.6 = (bf16[64,384]{1,0:T(8,128)(2,1)S(1)}, bf16[64,384]{1,0:T(8,128)(2,1)S(1)}, u32[]{:S(2)}, u32[]{:S(2)}) collective-permute-start(bf16[64,384]{1,0:T(8,128)(2,1)S(1)} %get-tuple-element.50), channel_id=1, source_target_pairs={{0,3},{1,2},{2,1},{3,0},{4,7},{5,6},{6,5},{7,4},{8,11},{9,10},{10,... | collective-permute-start | bytes 147464 | tf_op jit(solution)/shard_map/ppermute | solution.py:23
  58.7 1.6 collective-permute-start.4
  61.3 1.9 collective-permute-start.15
  63.2 1.9 collective-permute-start.16
  66.4 4.5 %collective-permute-done.15 = bf16[256,384]{1,0:T(8,128)(2,1)S(1)} collective-permute-done((bf16[256,384]{1,0:T(8,128)(2,1)S(1)}, bf16[256,384]{1,0:T(8,128)(2,1)S(1)}, u32[]{:S(2)}, u32[]{:S(2)}) %collective-permute-start.15) | collective-permute-done | bytes 196640 | tf_op jit(solution)/shard_map/ppermute | solution.py:322
  70.9 3.4 %collective-permute-done.16 = bf16[256,384]{1,0:T(8,128)(2,1)S(1)} collective-permute-done((bf16[256,384]{1,0:T(8,128)(2,1)S(1)}, bf16[256,384]{1,0:T(8,128)(2,1)S(1)}, u32[]{:S(2)}, u32[]{:S(2)}) %collective-permute-start.16) | collective-permute-done | bytes 196640 | tf_op jit(solution)/shard_map/ppermute | solution.py:323
  74.4 8.6 %collective-permute-done.17 = bf16[256,384]{1,0:T(8,128)(2,1)S(1)} collective-permute-done((bf16[256,384]{1,0:T(8,128)(2,1)S(1)}, bf16[256,384]{1,0:T(8,128)(2,1)S(1)}, u32[]{:S(2)}, u32[]{:S(2)}) %collective-permute-start.17) | collective-permute-done | bytes 196640 | tf_op jit(solution)/shard_map/ppermute | solution.py:23
  83.9 6.1 %all-to-all-start.1 = ((bf16[8,160,384]{2,1,0:T(8,128)(2,1)}), bf16[8,160,384]{2,1,0:T(8,128)(2,1)}, u32[]{:S(2)}, u32[]{:S(2)}) async-start(bf16[8,160,384]{2,1,0:T(8,128)(2,1)} %get-tuple-element.38), calls=%async_computation.1 | async-start | bytes 1966080 | tf_op jit(solution)/shard_map/all_to_all | solution.py:375
  92.8 13.6 %collective-permute-done.10.refs_3_ = bf16[128,2560]{1,0:T(8,128)(2,1)} collective-permute-done((bf16[128,2560]{1,0:T(8,128)(2,1)}, bf16[128,2560]{1,0:T(8,128)(2,1)}, u32[]{:S(2)}, u32[]{:S(2)}) %collective-permute-start.10) | collective-permute-done | bytes 655392 | tf_op jit(solution)/shard_map/ppermute | solution.py:23
  107.2 12.6 %collective-permute-done.18 = bf16[1024,384]{1,0:T(8,128)(2,1)} collective-permute-done((bf16[1024,384]{1,0:T(8,128)(2,1)}, bf16[1024,384]{1,0:T(8,128)(2,1)}, u32[]{:S(2)}, u32[]{:S(2)}) %collective-permute-start.18) | collective-permute-done | bytes 786464 | tf_op jit(solution)/shard_map/ppermute | solution.py:23
  119.8 1.5 select_bitcast_fusion.1
  121.3 1.3 pad_maximum_fusion
  122.7 6.6 %project.1.refs_0_ = bf16[1024,384]{1,0:T(8,128)(2,1)S(1)} custom-call(bf16[128,2560]{1,0:T(8,128)(2,1)} %pad_maximum_fusion.1.refs_0_, bf16[128,2560]{1,0:T(8,128)(2,1)} %collective-permute-done.8.refs_1_, bf16[128,2560]{1,0:T(8,128)(2,1)} %collective-permute-done.9.refs_2_, bf16[128,2560]{1,0:T(8,128)(2,1)} %collective-permute-done.10.refs_3_, ...), custom_call_target="tpu_custom_call" | custom-call | flops 2013265920 | bytes 5242880 | tf_op jit(solution)/shard_map/project/pallas_call | solution.py:178
  129.3 4.2 %attend.2 = (bf16[512,128]{1,0:T(8,128)(2,1)S(1)}, bf16[512,128]{1,0:T(8,128)(2,1)S(1)}) custom-call(s32[3]{0:T(128)S(1)} %pad_add_fusion.here_ref.place_ref, bf16[1024,384]{1,0:T(8,128)(2,1)S(1)} %project.1.refs_0_, bf16[2048,384]{1,0:T(8,128)(2,1)S(1)} %bitcast.61, s32[1,2048]{1,0:T(1,128)S(1)} %sub.145.refs_2_, s32[1024,1]{1,0:T(8,128)S(1)} %add.630.refs_3_), custom_call_target="tpu_custom_call" | custom-call | flops 1342177280 | bytes 1572864 | tf_op jit(solution)/shard_map/attend/pallas_call | solution.py:239
  133.5 4.2 %attend.3 = (bf16[512,128]{1,0:T(8,128)(2,1)S(1)}, bf16[512,128]{1,0:T(8,128)(2,1)S(1)}) custom-call(s32[3]{0:T(128)S(1)} %pad_add_fusion.here_ref.place_ref, bf16[1024,384]{1,0:T(8,128)(2,1)S(1)} %project.1.refs_0_, bf16[2048,384]{1,0:T(8,128)(2,1)S(1)} %bitcast.62, s32[1,2048]{1,0:T(1,128)S(1)} %sub.145.refs_2_, s32[1024,1]{1,0:T(8,128)S(1)} %add.630.refs_3_), custom_call_target="tpu_custom_call" | custom-call | flops 1342177280 | bytes 1572864 | tf_op jit(solution)/shard_map/attend/pallas_call | solution.py:239
  138.0 1.8 collective-permute-start.19
  139.9 3.2 %collective-permute-done.24 = bf16[512,128]{1,0:T(8,128)(2,1)S(1)} collective-permute-done((bf16[512,128]{1,0:T(8,128)(2,1)S(1)}, bf16[512,128]{1,0:T(8,128)(2,1)S(1)}, u32[]{:S(2)}, u32[]{:S(2)}) %collective-permute-start.24) | collective-permute-done | bytes 131104 | tf_op jit(solution)/shard_map/ppermute | solution.py:23
  143.1 3.4 %collective-permute-start.27 = (bf16[512,256]{1,0:T(8,128)(2,1)S(1)}, bf16[512,256]{1,0:T(8,128)(2,1)S(1)}, u32[]{:S(2)}, u32[]{:S(2)}) collective-permute-start(bf16[512,256]{1,0:T(8,128)(2,1)S(1)} %constant_dynamic-update-slice_fusion.2.refs_0_), channel_id=1, source_target_pairs={{0,16},{8,24},{16,0},{24,8},{1,17},{9,25},{17,1},{25,9},{2,18},{10... | collective-permute-start | bytes 786440 | tf_op jit(solution)/shard_map/ppermute | solution.py:23
  146.6 1.8 collective-permute-start.22
  148.4 2.1 %collective-permute-start.25 = (bf16[512,256]{1,0:T(8,128)(2,1)S(1)}, bf16[512,256]{1,0:T(8,128)(2,1)S(1)}, u32[]{:S(2)}, u32[]{:S(2)}) collective-permute-start(bf16[512,256]{1,0:T(8,128)(2,1)S(1)} %constant_dynamic-update-slice_fusion.2.refs_0_), channel_id=1, source_target_pairs={{0,8},{8,16},{16,24},{1,9},{9,17},{17,25},{2,10},{10,18},{18,26},{... | collective-permute-start | bytes 786440 | tf_op jit(solution)/shard_map/ppermute | solution.py:315
  150.5 1.3 collective-permute-start.26
  151.8 9.9 %collective-permute-done.27.refs_4_ = bf16[512,256]{1,0:T(8,128)(2,1)S(1)} collective-permute-done((bf16[512,256]{1,0:T(8,128)(2,1)S(1)}, bf16[512,256]{1,0:T(8,128)(2,1)S(1)}, u32[]{:S(2)}, u32[]{:S(2)}) %collective-permute-start.27) | collective-permute-done | bytes 262176 | tf_op jit(solution)/shard_map/ppermute | solution.py:23
  161.7 1.3 collective-permute-start.28
  163.0 4.6 %collective-permute-start.20 = (bf16[512,256]{1,0:T(8,128)(2,1)S(1)}, bf16[512,256]{1,0:T(8,128)(2,1)S(1)}, u32[]{:S(2)}, u32[]{:S(2)}) collective-permute-start(bf16[512,256]{1,0:T(8,128)(2,1)S(1)} %constant_dynamic-update-slice_fusion.refs_0_), channel_id=1, source_target_pairs={{0,8},{8,16},{16,24},{1,9},{9,17},{17,25},{2,10},{10,18},{18,26},{... | collective-permute-start | bytes 786440 | tf_op jit(solution)/shard_map/ppermute | solution.py:315
  167.5 1.3 collective-permute-start.21
  168.9 1.5 collective-permute-start.23
  171.6 5.6 %collective-permute-done.28.refs_3_ = bf16[512,256]{1,0:T(8,128)(2,1)S(1)} collective-permute-done((bf16[512,256]{1,0:T(8,128)(2,1)S(1)}, bf16[512,256]{1,0:T(8,128)(2,1)S(1)}, u32[]{:S(2)}, u32[]{:S(2)}) %collective-permute-start.28) | collective-permute-done | bytes 262176 | tf_op jit(solution)/shard_map/ppermute | solution.py:317
  177.2 1.9 expel.2.refs_7_
  179.1 3.6 %collective-permute-done.21.refs_2_ = bf16[512,256]{1,0:T(8,128)(2,1)S(1)} collective-permute-done((bf16[512,256]{1,0:T(8,128)(2,1)S(1)}, bf16[512,256]{1,0:T(8,128)(2,1)S(1)}, u32[]{:S(2)}, u32[]{:S(2)}) %collective-permute-start.21) | collective-permute-done | bytes 262176 | tf_op jit(solution)/shard_map/ppermute | solution.py:316
  182.8 3.8 %collective-permute-done.23.refs_3_ = bf16[512,256]{1,0:T(8,128)(2,1)S(1)} collective-permute-done((bf16[512,256]{1,0:T(8,128)(2,1)S(1)}, bf16[512,256]{1,0:T(8,128)(2,1)S(1)}, u32[]{:S(2)}, u32[]{:S(2)}) %collective-permute-start.23) | collective-permute-done | bytes 262176 | tf_op jit(solution)/shard_map/ppermute | solution.py:317
  186.6 2.8 %expel.3 = (f32[4,2,32,640]{3,2,1,0:T(8,128)S(1)}, bf16[4,2,32,640]{3,2,1,0:T(8,128)(2,1)S(1)}) custom-call(s32[3]{0:T(128)S(1)} %pad_add_fusion.here_ref.place_ref, bf16[512,256]{1,0:T(8,128)(2,1)S(1)} %constant_dynamic-update-slice_fusion.refs_0_, bf16[512,256]{1,0:T(8,128)(2,1)S(1)} %collective-permute-done.20.refs_1_, ...), custom_call_target="tpu_custom_call" | custom-call | flops 671088640 | bytes 1310720 | tf_op jit(solution)/shard_map/expel/pallas_call | solution.py:299
  189.6 1.6 collective-permute-done.29
  191.3 6.2 %collective-permute-done.30 = bf16[4,32,640]{2,1,0:T(8,128)(2,1)S(1)} collective-permute-done((bf16[4,32,640]{2,1,0:T(8,128)(2,1)S(1)}, bf16[4,32,640]{2,1,0:T(8,128)(2,1)S(1)}, u32[]{:S(2)}, u32[]{:S(2)}) %collective-permute-start.30) | collective-permute-done | bytes 163872 | tf_op jit(solution)/shard_map/ppermute | solution.py:23
  197.8 1.9 collective-permute-start.31
  199.7 9.7 %collective-permute-done.31 = bf16[128,640]{1,0:T(8,128)(2,1)S(1)} collective-permute-done((bf16[128,640]{1,0:T(8,128)(2,1)S(1)}, bf16[128,640]{1,0:T(8,128)(2,1)S(1)}, u32[]{:S(2)}, u32[]{:S(2)}) %collective-permute-start.31) | collective-permute-done | bytes 163872 | tf_op jit(solution)/shard_map/ppermute | solution.py:502
  (93 shorter events, 18.2 us)
Async XLA Ops:
  0.0 1.1 copy-start
  1.1 11.8 %collective-permute-start = (bf16[32,2560]{1,0:T(8,128)(2,1)S(1)}, bf16[32,2560]{1,0:T(8,128)(2,1)S(1)}, u32[]{:S(2)}, u32[]{:S(2)}) collective-permute-start(bf16[32,2560]{1,0:T(8,128)(2,1)S(1)} %constant_dynamic-slice_fusion), channel_id=1, source_target_pairs={{0,8},{8,16},{16,24},{24,0},{1,9},{9,17},{17,25},{25,1},{2,10},{10... | collective-permute-start | bytes 491528 | tf_op jit(solution)/shard_map/ppermute | solution.py:322
  2.7 10.2 %collective-permute-start.1 = (bf16[32,2560]{1,0:T(8,128)(2,1)S(1)}, bf16[32,2560]{1,0:T(8,128)(2,1)S(1)}, u32[]{:S(2)}, u32[]{:S(2)}) collective-permute-start(bf16[32,2560]{1,0:T(8,128)(2,1)S(1)} %constant_dynamic-slice_fusion), channel_id=1, source_target_pairs={{8,0},{16,8},{24,16},{0,24},{9,1},{17,9},{25,17},{1,25},{10,2},{18... | collective-permute-start | bytes 491528 | tf_op jit(solution)/shard_map/ppermute | solution.py:323
  5.0 14.5 %collective-permute-start.2 = (bf16[32,2560]{1,0:T(8,128)(2,1)S(1)}, bf16[32,2560]{1,0:T(8,128)(2,1)S(1)}, u32[]{:S(2)}, u32[]{:S(2)}) collective-permute-start(bf16[32,2560]{1,0:T(8,128)(2,1)S(1)} %constant_dynamic-slice_fusion), channel_id=1, source_target_pairs={{0,16},{8,24},{16,0},{24,8},{1,17},{9,25},{17,1},{25,9},{2,18},{10... | collective-permute-start | bytes 491528 | tf_op jit(solution)/shard_map/ppermute | solution.py:23
  5.8 55.5 %collective-permute-start.7 = (bf16[320,2048]{1,0:T(8,128)(2,1)}, bf16[320,2048]{1,0:T(8,128)(2,1)S(1)}, u32[]{:S(2)}, u32[]{:S(2)}) collective-permute-start(bf16[320,2048]{1,0:T(8,128)(2,1)} %bitcast.58), channel_id=1, source_target_pairs={{0,4},{4,0},{1,5},{5,1},{2,6},{6,2},{3,7},{7,3},{8,12},{12,8},{9,1... | collective-permute-start | bytes 3932168 | tf_op jit(solution)/shard_map/ppermute | solution.py:23
  13.0 6.5 %copy-start.11 = (bf16[32,2560]{1,0:T(8,128)(2,1)}, bf16[32,2560]{1,0:T(8,128)(2,1)S(1)}, u32[]{:S(2)}) copy-start(bf16[32,2560]{1,0:T(8,128)(2,1)S(1)} %collective-permute-done.1) | copy-start | bytes 491524
  19.5 9.0 %slice-start = ((bf16[1024,768]{1,0:T(8,128)(2,1)}), bf16[16,768]{1,0:T(8,128)(2,1)S(1)}, s32[]{:S(2)}) async-start(bf16[1024,768]{1,0:T(8,128)(2,1)} %raw_keys), calls=%async_computation.2 | async-start | bytes 49152 | tf_op jit(solution)/shard_map/slice | solution.py:386
  19.5 9.0 %slice-start.1 = ((bf16[1024,512]{1,0:T(8,128)(2,1)}), bf16[16,512]{1,0:T(8,128)(2,1)S(1)}, s32[]{:S(2)}) async-start(bf16[1024,512]{1,0:T(8,128)(2,1)} %raw_values), calls=%async_computation.3 | async-start | bytes 32768 | tf_op jit(solution)/shard_map/slice | solution.py:386
  20.2 63.7 %all-to-all-start = ((bf16[8,160,384]{2,1,0:T(8,128)(2,1)}), bf16[8,160,384]{2,1,0:T(8,128)(2,1)S(1)}, u32[]{:S(2)}, u32[]{:S(2)}) async-start(bf16[8,160,384]{2,1,0:T(8,128)(2,1)} %get-tuple-element.35), calls=%async_computation | async-start | bytes 1966080 | tf_op jit(solution)/shard_map/all_to_all | solution.py:375
  24.0 18.3 %copy-start.8 = (f32[32,768]{1,0:T(8,128)S(1)}, f32[32,768]{1,0:T(8,128)}, u32[]{:S(2)}) copy-start(f32[32,768]{1,0:T(8,128)} %key_mix.1) | copy-start | bytes 294916
  25.9 35.3 %collective-permute-start.8 = (bf16[128,2560]{1,0:T(8,128)(2,1)}, bf16[128,2560]{1,0:T(8,128)(2,1)}, u32[]{:S(2)}, u32[]{:S(2)}) collective-permute-start(bf16[128,2560]{1,0:T(8,128)(2,1)} %pad_maximum_fusion.1.refs_0_), channel_id=1, source_target_pairs={{0,4},{4,0},{1,5},{5,1},{2,6},{6,2},{3,7},{7,3},{8,12},{12,8},{9,1... | collective-permute-start | bytes 1966088 | tf_op jit(solution)/shard_map/ppermute | solution.py:23
  27.9 33.3 %collective-permute-start.9 = (bf16[128,2560]{1,0:T(8,128)(2,1)}, bf16[128,2560]{1,0:T(8,128)(2,1)}, u32[]{:S(2)}, u32[]{:S(2)}) collective-permute-start(bf16[128,2560]{1,0:T(8,128)(2,1)} %pad_maximum_fusion.1.refs_0_), channel_id=1, source_target_pairs={{0,2},{1,3},{2,0},{3,1},{4,6},{5,7},{6,4},{7,5},{8,10},{9,11},{10,... | collective-permute-start | bytes 1966088 | tf_op jit(solution)/shard_map/ppermute | solution.py:23
  28.5 13.9 %collective-permute-start.3 = (bf16[16,1280]{1,0:T(8,128)(2,1)S(1)}, bf16[16,1280]{1,0:T(8,128)(2,1)S(1)}, u32[]{:S(2)}, u32[]{:S(2)}) collective-permute-start(bf16[16,1280]{1,0:T(8,128)(2,1)S(1)} %pad_maximum_fusion.4), channel_id=1, source_target_pairs={{1,0},{2,1},{3,2},{4,3},{5,4},{6,5},{7,6},{8,7},{9,8},{10,9},{11,1... | collective-permute-start | bytes 122888 | tf_op jit(solution)/shard_map/ppermute | solution.py:387
  42.4 1.4 copy-start.3
  43.8 1.2 copy-start.4
  45.0 1.0 copy-start.5
  45.9 0.9 copy-start.6
  46.9 0.9 copy-start.7
  54.7 4.0 %collective-permute-start.6 = (bf16[64,384]{1,0:T(8,128)(2,1)S(1)}, bf16[64,384]{1,0:T(8,128)(2,1)S(1)}, u32[]{:S(2)}, u32[]{:S(2)}) collective-permute-start(bf16[64,384]{1,0:T(8,128)(2,1)S(1)} %get-tuple-element.50), channel_id=1, source_target_pairs={{0,3},{1,2},{2,1},{3,0},{4,7},{5,6},{6,5},{7,4},{8,11},{9,10},{10,... | collective-permute-start | bytes 147464 | tf_op jit(solution)/shard_map/ppermute | solution.py:23
  57.0 4.1 %collective-permute-start.5 = (bf16[64,384]{1,0:T(8,128)(2,1)S(1)}, bf16[64,384]{1,0:T(8,128)(2,1)S(1)}, u32[]{:S(2)}, u32[]{:S(2)}) collective-permute-start(bf16[64,384]{1,0:T(8,128)(2,1)S(1)} %get-tuple-element.51), channel_id=1, source_target_pairs={{0,2},{1,3},{2,0},{3,1},{4,6},{5,7},{6,4},{7,5},{8,10},{9,11},{10,... | collective-permute-start | bytes 147464 | tf_op jit(solution)/shard_map/ppermute | solution.py:23
  58.7 2.5 %collective-permute-start.4 = (bf16[64,384]{1,0:T(8,128)(2,1)S(1)}, bf16[64,384]{1,0:T(8,128)(2,1)S(1)}, u32[]{:S(2)}, u32[]{:S(2)}) collective-permute-start(bf16[64,384]{1,0:T(8,128)(2,1)S(1)} %get-tuple-element.52), channel_id=1, source_target_pairs={{0,1},{1,0},{2,3},{3,2},{4,5},{5,4},{6,7},{7,6},{8,9},{9,8},{10,11... | collective-permute-start | bytes 147464 | tf_op jit(solution)/shard_map/ppermute | solution.py:23
  61.3 9.6 %collective-permute-start.15 = (bf16[256,384]{1,0:T(8,128)(2,1)S(1)}, bf16[256,384]{1,0:T(8,128)(2,1)S(1)}, u32[]{:S(2)}, u32[]{:S(2)}) collective-permute-start(bf16[256,384]{1,0:T(8,128)(2,1)S(1)} %pad_maximum_fusion.2), channel_id=1, source_target_pairs={{0,8},{8,16},{16,24},{24,0},{1,9},{9,17},{17,25},{25,1},{2,10},{10... | collective-permute-start | bytes 589832 | tf_op jit(solution)/shard_map/ppermute | solution.py:322
  63.2 11.1 %collective-permute-start.16 = (bf16[256,384]{1,0:T(8,128)(2,1)S(1)}, bf16[256,384]{1,0:T(8,128)(2,1)S(1)}, u32[]{:S(2)}, u32[]{:S(2)}) collective-permute-start(bf16[256,384]{1,0:T(8,128)(2,1)S(1)} %pad_maximum_fusion.2), channel_id=1, source_target_pairs={{8,0},{16,8},{24,16},{0,24},{9,1},{17,9},{25,17},{1,25},{10,2},{18... | collective-permute-start | bytes 589832 | tf_op jit(solution)/shard_map/ppermute | solution.py:323
  65.2 17.8 %collective-permute-start.17 = (bf16[256,384]{1,0:T(8,128)(2,1)S(1)}, bf16[256,384]{1,0:T(8,128)(2,1)S(1)}, u32[]{:S(2)}, u32[]{:S(2)}) collective-permute-start(bf16[256,384]{1,0:T(8,128)(2,1)S(1)} %pad_maximum_fusion.2), channel_id=1, source_target_pairs={{0,16},{8,24},{16,0},{24,8},{1,17},{9,25},{17,1},{25,9},{2,18},{10... | collective-permute-start | bytes 589832 | tf_op jit(solution)/shard_map/ppermute | solution.py:23
  83.9 8.3 %copy-start.14 = (s32[1,1,4,1]{2,3,1,0:T(1,128)S(1)}, s32[1,1,4,1]{2,3,1,0:T(1,128)}, u32[]{:S(2)}) copy-start(s32[1,1,4,1]{2,3,1,0:T(1,128)} %constant.475.clone) | copy-start | bytes 52
  83.9 8.3 %copy-start.13 = (s32[2,4,64]{2,1,0:T(4,128)S(1)}, s32[2,4,64]{2,1,0:T(4,128)}, u32[]{:S(2)}) copy-start(s32[2,4,64]{2,1,0:T(4,128)} %constant.478) | copy-start | bytes 6148
  83.9 38.8 %all-to-all-start.1 = ((bf16[8,160,384]{2,1,0:T(8,128)(2,1)}), bf16[8,160,384]{2,1,0:T(8,128)(2,1)}, u32[]{:S(2)}, u32[]{:S(2)}) async-start(bf16[8,160,384]{2,1,0:T(8,128)(2,1)} %get-tuple-element.38), calls=%async_computation.1 | async-start | bytes 1966080 | tf_op jit(solution)/shard_map/all_to_all | solution.py:375
  90.0 16.4 %collective-permute-start.10 = (bf16[128,2560]{1,0:T(8,128)(2,1)}, bf16[128,2560]{1,0:T(8,128)(2,1)}, u32[]{:S(2)}, u32[]{:S(2)}) collective-permute-start(bf16[128,2560]{1,0:T(8,128)(2,1)} %collective-permute-done.8.refs_1_), channel_id=1, source_target_pairs={{0,2},{1,3},{2,0},{3,1},{4,6},{5,7},{6,4},{7,5},{8,10},{9,11},{10,... | collective-permute-start | bytes 1966088 | tf_op jit(solution)/shard_map/ppermute | solution.py:23
  91.1 28.6 %collective-permute-start.18 = (bf16[1024,384]{1,0:T(8,128)(2,1)}, bf16[1024,384]{1,0:T(8,128)(2,1)}, u32[]{:S(2)}, u32[]{:S(2)}) collective-permute-start(bf16[1024,384]{1,0:T(8,128)(2,1)} %copy-done.10), channel_id=1, source_target_pairs={{0,4},{4,0},{1,5},{5,1},{2,6},{6,2},{3,7},{7,3},{8,12},{12,8},{9,1... | collective-permute-start | bytes 2359304 | tf_op jit(solution)/shard_map/ppermute | solution.py:23
  92.2 30.4 %collective-permute-start.12 = (bf16[128,2560]{1,0:T(8,128)(2,1)}, bf16[128,2560]{1,0:T(8,128)(2,1)}, u32[]{:S(2)}, u32[]{:S(2)}) collective-permute-start(bf16[128,2560]{1,0:T(8,128)(2,1)} %collective-permute-done.8.refs_1_), channel_id=1, source_target_pairs={{0,1},{1,0},{2,3},{3,2},{4,5},{5,4},{6,7},{7,6},{8,9},{9,8},{10,11... | collective-permute-start | bytes 1966088 | tf_op jit(solution)/shard_map/ppermute | solution.py:23
  92.3 30.4 %collective-permute-start.11 = (bf16[128,2560]{1,0:T(8,128)(2,1)}, bf16[128,2560]{1,0:T(8,128)(2,1)}, u32[]{:S(2)}, u32[]{:S(2)}) collective-permute-start(bf16[128,2560]{1,0:T(8,128)(2,1)} %pad_maximum_fusion.1.refs_0_), channel_id=1, source_target_pairs={{0,1},{1,0},{2,3},{3,2},{4,5},{5,4},{6,7},{7,6},{8,9},{9,8},{10,11... | collective-permute-start | bytes 1966088 | tf_op jit(solution)/shard_map/ppermute | solution.py:23
  92.8 29.9 %collective-permute-start.13 = (bf16[128,2560]{1,0:T(8,128)(2,1)}, bf16[128,2560]{1,0:T(8,128)(2,1)}, u32[]{:S(2)}, u32[]{:S(2)}) collective-permute-start(bf16[128,2560]{1,0:T(8,128)(2,1)} %collective-permute-done.9.refs_2_), channel_id=1, source_target_pairs={{0,1},{1,0},{2,3},{3,2},{4,5},{5,4},{6,7},{7,6},{8,9},{9,8},{10,11... | collective-permute-start | bytes 1966088 | tf_op jit(solution)/shard_map/ppermute | solution.py:23
  106.4 16.2 %collective-permute-start.14 = (bf16[128,2560]{1,0:T(8,128)(2,1)}, bf16[128,2560]{1,0:T(8,128)(2,1)}, u32[]{:S(2)}, u32[]{:S(2)}) collective-permute-start(bf16[128,2560]{1,0:T(8,128)(2,1)} %collective-permute-done.10.refs_3_), channel_id=1, source_target_pairs={{0,1},{1,0},{2,3},{3,2},{4,5},{5,4},{6,7},{7,6},{8,9},{9,8},{10,11... | collective-permute-start | bytes 1966088 | tf_op jit(solution)/shard_map/ppermute | solution.py:23
  122.7 6.6 %copy-start.2 = (bf16[2,1024,384]{2,1,0:T(8,128)(2,1)S(1)}, bf16[2,1024,384]{2,1,0:T(8,128)(2,1)}, u32[]{:S(2)}) copy-start(bf16[2,1024,384]{2,1,0:T(8,128)(2,1)} %pad_maximum_fusion) | copy-start | bytes 4718596
  133.5 43.7 %copy-start.1 = (bf16[2048,320]{0,1:T(8,128)(2,1)S(1)}, bf16[2048,320]{0,1:T(8,128)(2,1)}, u32[]{:S(2)}) copy-start(bf16[2048,320]{0,1:T(8,128)(2,1)} %param.17) | copy-start | bytes 3932164
  137.7 5.4 %collective-permute-start.24 = (bf16[512,128]{1,0:T(8,128)(2,1)S(1)}, bf16[512,128]{1,0:T(8,128)(2,1)S(1)}, u32[]{:S(2)}, u32[]{:S(2)}) collective-permute-start(bf16[512,128]{1,0:T(8,128)(2,1)S(1)} %get-tuple-element.44), channel_id=1, source_target_pairs={{0,4},{4,0},{1,5},{5,1},{2,6},{6,2},{3,7},{7,3},{8,12},{12,8},{9,1... | collective-permute-start | bytes 393224 | tf_op jit(solution)/shard_map/ppermute | solution.py:23
  138.0 8.5 %collective-permute-start.19 = (bf16[512,128]{1,0:T(8,128)(2,1)S(1)}, bf16[512,128]{1,0:T(8,128)(2,1)S(1)}, u32[]{:S(2)}, u32[]{:S(2)}) collective-permute-start(bf16[512,128]{1,0:T(8,128)(2,1)S(1)} %get-tuple-element.41), channel_id=1, source_target_pairs={{0,4},{4,0},{1,5},{5,1},{2,6},{6,2},{3,7},{7,3},{8,12},{12,8},{9,1... | collective-permute-start | bytes 393224 | tf_op jit(solution)/shard_map/ppermute | solution.py:23
  143.1 18.5 %collective-permute-start.27 = (bf16[512,256]{1,0:T(8,128)(2,1)S(1)}, bf16[512,256]{1,0:T(8,128)(2,1)S(1)}, u32[]{:S(2)}, u32[]{:S(2)}) collective-permute-start(bf16[512,256]{1,0:T(8,128)(2,1)S(1)} %constant_dynamic-update-slice_fusion.2.refs_0_), channel_id=1, source_target_pairs={{0,16},{8,24},{16,0},{24,8},{1,17},{9,25},{17,1},{25,9},{2,18},{10... | collective-permute-start | bytes 786440 | tf_op jit(solution)/shard_map/ppermute | solution.py:23
  146.6 20.9 %collective-permute-start.22 = (bf16[512,256]{1,0:T(8,128)(2,1)S(1)}, bf16[512,256]{1,0:T(8,128)(2,1)S(1)}, u32[]{:S(2)}, u32[]{:S(2)}) collective-permute-start(bf16[512,256]{1,0:T(8,128)(2,1)S(1)} %constant_dynamic-update-slice_fusion.refs_0_), channel_id=1, source_target_pairs={{0,16},{8,24},{16,0},{24,8},{1,17},{9,25},{17,1},{25,9},{2,18},{10... | collective-permute-start | bytes 786440 | tf_op jit(solution)/shard_map/ppermute | solution.py:23
  148.4 20.5 %collective-permute-start.25 = (bf16[512,256]{1,0:T(8,128)(2,1)S(1)}, bf16[512,256]{1,0:T(8,128)(2,1)S(1)}, u32[]{:S(2)}, u32[]{:S(2)}) collective-permute-start(bf16[512,256]{1,0:T(8,128)(2,1)S(1)} %constant_dynamic-update-slice_fusion.2.refs_0_), channel_id=1, source_target_pairs={{0,8},{8,16},{16,24},{1,9},{9,17},{17,25},{2,10},{10,18},{18,26},{... | collective-permute-start | bytes 786440 | tf_op jit(solution)/shard_map/ppermute | solution.py:315
  150.5 21.1 %collective-permute-start.26 = (bf16[512,256]{1,0:T(8,128)(2,1)S(1)}, bf16[512,256]{1,0:T(8,128)(2,1)S(1)}, u32[]{:S(2)}, u32[]{:S(2)}) collective-permute-start(bf16[512,256]{1,0:T(8,128)(2,1)S(1)} %constant_dynamic-update-slice_fusion.2.refs_0_), channel_id=1, source_target_pairs={{8,0},{16,8},{24,16},{9,1},{17,9},{25,17},{10,2},{18,10},{26,18},{... | collective-permute-start | bytes 786440 | tf_op jit(solution)/shard_map/ppermute | solution.py:316
  161.7 15.5 %collective-permute-start.28 = (bf16[512,256]{1,0:T(8,128)(2,1)S(1)}, bf16[512,256]{1,0:T(8,128)(2,1)S(1)}, u32[]{:S(2)}, u32[]{:S(2)}) collective-permute-start(bf16[512,256]{1,0:T(8,128)(2,1)S(1)} %collective-permute-done.27.refs_4_), channel_id=1, source_target_pairs={{8,0},{16,24},{9,1},{17,25},{10,2},{18,26},{11,3},{19,27},{12,4},{... | collective-permute-start | bytes 786440 | tf_op jit(solution)/shard_map/ppermute | solution.py:317
  163.0 16.2 %collective-permute-start.20 = (bf16[512,256]{1,0:T(8,128)(2,1)S(1)}, bf16[512,256]{1,0:T(8,128)(2,1)S(1)}, u32[]{:S(2)}, u32[]{:S(2)}) collective-permute-start(bf16[512,256]{1,0:T(8,128)(2,1)S(1)} %constant_dynamic-update-slice_fusion.refs_0_), channel_id=1, source_target_pairs={{0,8},{8,16},{16,24},{1,9},{9,17},{17,25},{2,10},{10,18},{18,26},{... | collective-permute-start | bytes 786440 | tf_op jit(solution)/shard_map/ppermute | solution.py:315
  167.5 15.2 %collective-permute-start.21 = (bf16[512,256]{1,0:T(8,128)(2,1)S(1)}, bf16[512,256]{1,0:T(8,128)(2,1)S(1)}, u32[]{:S(2)}, u32[]{:S(2)}) collective-permute-start(bf16[512,256]{1,0:T(8,128)(2,1)S(1)} %constant_dynamic-update-slice_fusion.refs_0_), channel_id=1, source_target_pairs={{8,0},{16,8},{24,16},{9,1},{17,9},{25,17},{10,2},{18,10},{26,18},{... | collective-permute-start | bytes 786440 | tf_op jit(solution)/shard_map/ppermute | solution.py:316
  168.9 17.7 %collective-permute-start.23 = (bf16[512,256]{1,0:T(8,128)(2,1)S(1)}, bf16[512,256]{1,0:T(8,128)(2,1)S(1)}, u32[]{:S(2)}, u32[]{:S(2)}) collective-permute-start(bf16[512,256]{1,0:T(8,128)(2,1)S(1)} %collective-permute-done.22.refs_4_), channel_id=1, source_target_pairs={{8,0},{16,24},{9,1},{17,25},{10,2},{18,26},{11,3},{19,27},{12,4},{... | collective-permute-start | bytes 786440 | tf_op jit(solution)/shard_map/ppermute | solution.py:317
  189.5 1.7 collective-permute-start.29
  191.3 6.3 %collective-permute-start.30 = (bf16[4,32,640]{2,1,0:T(8,128)(2,1)S(1)}, bf16[4,32,640]{2,1,0:T(8,128)(2,1)S(1)}, u32[]{:S(2)}, u32[]{:S(2)}) collective-permute-start(bf16[4,32,640]{2,1,0:T(8,128)(2,1)S(1)} %fusion.1), channel_id=1, source_target_pairs={{0,2},{1,3},{2,0},{3,1},{4,6},{5,7},{6,4},{7,5},{8,10},{9,11},{10,... | collective-permute-start | bytes 491528 | tf_op jit(solution)/shard_map/ppermute | solution.py:23
  197.8 11.6 %collective-permute-start.31 = (bf16[128,640]{1,0:T(8,128)(2,1)S(1)}, bf16[128,640]{1,0:T(8,128)(2,1)S(1)}, u32[]{:S(2)}, u32[]{:S(2)}) collective-permute-start(bf16[128,640]{1,0:T(8,128)(2,1)S(1)} %pad_maximum_fusion.3), channel_id=1, source_target_pairs={{0,0},{1,8},{2,16},{3,24},{4,4},{5,12},{6,20},{7,28},{8,1},{9,9},{... | collective-permute-start | bytes 491528 | tf_op jit(solution)/shard_map/ppermute | solution.py:502
  (3 other events, 2.4 us)

commit v6 on v5

--- a/solution.py
+++ b/solution.py
@@ -122,16 +122,28 @@
     rows, columns = weight.shape
     share, part = columns // shares, rows // parts
 
-    def kernel(in_ref, *out_refs):
-        for index, out_ref in enumerate(out_refs):
-            out_ref[0] = in_ref[index * part : (index + 1) * part, :]
+    def kernel(in_ref, *refs):
+        out_refs, sems = refs[:-1], refs[-1]
+        copies = [
+            pltpu.make_async_copy(
+                in_ref.at[index * part : (index + 1) * part, owner * share : (owner + 1) * share],
+                out_ref.at[owner],
+                sems.at[index * shares + owner],
+            )
+            for index, out_ref in enumerate(out_refs)
+            for owner in range(shares)
+        ]
+        for copy in copies:
+            copy.start()
+        for copy in copies:
+            copy.wait()
 
     return pl.pallas_call(
         kernel,
         out_shape=(jax.ShapeDtypeStruct((shares, part, share), weight.dtype),) * parts,
-        grid=(shares,),
-        in_specs=[pl.BlockSpec((rows, share), lambda i: (0, i))],
-        out_specs=(pl.BlockSpec((1, part, share), lambda i: (i, 0, 0)),) * parts,
+        in_specs=[pl.BlockSpec(memory_space=pl.ANY)],
+        out_specs=(pl.BlockSpec(memory_space=pl.ANY),) * parts,
+        scratch_shapes=[pltpu.SemaphoreType.DMA((parts * shares,))],
         cost_estimate=pl.CostEstimate(flops=0, bytes_accessed=0, transcendentals=0),
         name="cut",
     )(weight)
@@ -361,8 +373,13 @@
     part = query_weight.shape[0]
     fast = inner == 2 and outer == 4 and heads_axis == 4
 
-    if fast:
-        turned = output_weight.T
+    edge = jnp.concatenate([raw_keys[:STRIDE], raw_values[:STRIDE]], axis=1)
+    edge = lax.ppermute(
+        edge, ("outer", "inner", "head"), [(i + 1, i) for i in range(devices - 1)]
+    )
+
+    if fast:
+        turned, edge = lax.optimization_barrier((output_weight.T, edge))
         out_weights = [turned, swap(turned, "inner", 1)]
     else:
         out_weights = lax.all_gather(output_weight, "inner", axis=1, tiled=True)
@@ -383,18 +400,18 @@
         weight = lax.all_gather(weight, "inner", axis=1).reshape(model, share)
     heads_here = share // key_width
 
-    edge = jnp.concatenate([raw_keys[:STRIDE], raw_values[:STRIDE]], axis=1)
-    edge = lax.ppermute(
-        edge, ("outer", "inner", "head"), [(i + 1, i) for i in range(devices - 1)]
-    )
     edge_keys, edge_values = edge[:, : raw_keys.shape[1]], edge[:, raw_keys.shape[1] :]
+    packed = compress(
+        raw_keys, raw_values, edge_keys, edge_values,
+        key_expand, key_mix, key_reduce, value_expand, value_mix, value_reduce,
+    )
 
     if fast:
         quarter = row_count // heads_axis
         mine = lax.dynamic_slice_in_dim(tokens, h * quarter, quarter, 0)
         mine, before, after, far = ring_pieces(mine, "outer")
-        begin, before, after, far, raw_keys, raw_values = lax.optimization_barrier(
-            (sent[0], before, after, far, raw_keys, raw_values)
+        begin, before, after, far, packed = lax.optimization_barrier(
+            (sent[0], before, after, far, packed)
         )
         weight_first = exchange(begin)
         near = jnp.concatenate([mine, before, after, far], axis=0)
@@ -421,10 +438,6 @@
     places = (context + bases).astype(jnp.int32).reshape(-1, 1)
     here = jnp.stack([z, h, y]).astype(jnp.int32)
 
-    packed = compress(
-        raw_keys, raw_values, edge_keys, edge_values,
-        key_expand, key_mix, key_reduce, value_expand, value_mix, value_reduce,
-    )
     ids = np.arange(devices * blocks).reshape(outer, inner, heads_axis, blocks)
     if fast:
         stay = lax.dynamic_index_in_dim(packed, h, 0, False)

time: 211 us -> 274 us (1.30)
  Pallas kernels: 31.4 us -> 86.4 us
  local copies, waits for them, and re-layouts: 11.9 us -> 19.4 us
  starting transfers between devices: 53.6 us -> 50.8 us
    pallas_call x1, Pallas kernels: 5.65 us -> 60.8 us  [cut(): pl.pallas_call(kernel, out_shape=(jax.ShapeDtypeStruct((shares, part, sha...]
    ppermute x20, waiting for transfers between devices: 63.8 us -> 80.8 us  [swap(): lax.ppermute(block, axis, [(i, i ^ bit) for i in range(lax.axis_size(axis...]
    ppermute x1, waiting for transfers between devices: 10.8 us -> 0.01 us  [shards(): lax.ppermute(edge, ('outer', 'inner', 'head'), [(i + 1, i) for i in range...]
    dynamic_update_slice x4, local copies, waits for them, and re-layouts: 0.13 us -> 3.76 us  [gather_line(): out = lax.dynamic_update_slice_in_dim(out, piece, place * size, dim)]
    ppermute x2, waiting for transfers between devices: 3.37 us -> 0.01 us  [ring_pieces(): after = lax.ppermute(block, axis, [((i + 1) % 4, i) for i in range(4)])]
    unnamed x34 -> x36, local copies, waits for them, and re-layouts: 10.8 us -> 10.7 us
  transfers between devices with their start and end apart: 34 -> 34, of which waited for: 19 -> 17; matrix products, arithmetic and copies ran while one was open for 3% -> 5% of each run, Pallas kernels for 6% -> 25%
where the time goes in v6:
time: 274 us; the launch traced here: 273 us
  waiting for transfers between devices  108 us (39%)
  Pallas kernels  86.4 us (32%)
  starting transfers between devices  50.8 us (19%)
  local copies, waits for them, and re-layouts  19.4 us (7%)
  other arithmetic  6.56 us (2%)
    ppermute x20, waiting for transfers between devices, swap(): lax.ppermute(block, axis, [(i, i ^ bit) for i in range(lax.axis_size(axis...  80.8 us
    pallas_call x1, Pallas kernels, cut(): pl.pallas_call(kernel, out_shape=(jax.ShapeDtypeStruct((shares, part, sha...  60.8 us
    ppermute x20, starting transfers between devices, swap(): lax.ppermute(block, axis, [(i, i ^ bit) for i in range(lax.axis_size(axis...  18.2 us
    unnamed x36, local copies, waits for them, and re-layouts  10.7 us
    ppermute x1, waiting for transfers between devices, shards(): return lax.ppermute(result, ('outer', 'inner', 'head'), route)  9.68 us
    ppermute x2, waiting for transfers between devices, line_pieces(): passed = lax.ppermute(far, axis, [(1, 0), (2, 3)])  9.3 us
    all_to_all x2, starting transfers between devices, exchange(): lax.all_to_all(block, seq_axes, split_axis=0, concat_axis=0, tiled=True)  8.8 us
    pallas_call x2, Pallas kernels, attend(): pl.pallas_call(kernel, out_shape=(shape,) * outputs, in_specs=[pl.BlockSp...  8.35 us
  transfers between devices with their start and end apart: 34, of which 17 were waited for; matrix products, arithmetic and copies ran while one was open for 5% of the time, Pallas kernels for 25%

profile of v6, /device:TPU:2, one launch (start us, length us, event | category | flops | bytes accessed | tf_op | source)
XLA Modules:
  0.0 273.1 jit_solution(10350903389241253313)
XLA Ops:
  1.6 1.9 collective-permute-start.3
  4.2 1.6 collective-permute-start
  5.7 2.2 collective-permute-start.1
  8.8 60.8 %cut.1 = (bf16[8,160,384]{2,1,0:T(8,128)(2,1)}, bf16[8,160,384]{2,1,0:T(8,128)(2,1)}) custom-call(bf16[320,3072]{1,0:T(8,128)(2,1)} %in_ref.1), custom_call_target="tpu_custom_call" | custom-call | tf_op jit(solution)/shard_map/cut/pallas_call | solution.py:141
  70.6 1.6 collective-permute-start.7
  73.1 1.4 copy-done.6
  80.4 6.0 %compress.1 = bf16[4,64,384]{2,1,0:T(8,128)(2,1)S(1)} custom-call(bf16[1024,768]{1,0:T(8,128)(2,1)S(1)} %copy-done.6, bf16[1024,512]{1,0:T(8,128)(2,1)S(1)} %copy-done.7, bf16[16,768]{1,0:T(8,128)(2,1)S(1)} %slice.20.edge_keys, bf16[16,512]{1,0:T(8,128)(2,1)S(1)} %slice.21.edge_values, bf16[192,768]{1,0:T(8,128)(2,1)S(1)} %copy-done.8, ...), custom_call_target="tpu_custom_call" | custom-call | flops 2013265920 | bytes 1572864 | tf_op jit(solution)/shard_map/compress/pallas_call | solution.py:105
  86.4 4.2 %all-to-all-start = ((bf16[8,160,384]{2,1,0:T(8,128)(2,1)}), bf16[8,160,384]{2,1,0:T(8,128)(2,1)}, u32[]{:S(2)}, u32[]{:S(2)}) async-start(bf16[8,160,384]{2,1,0:T(8,128)(2,1)} %get-tuple-element.37), calls=%async_computation | async-start | bytes 1966080 | tf_op jit(solution)/shard_map/all_to_all | solution.py:392
  90.6 2.1 pad_maximum_fusion.1.refs_0_
  92.7 1.9 collective-permute-start.8
  94.6 1.4 collective-permute-start.9
  96.8 13.1 %collective-permute-done.6 = bf16[64,384]{1,0:T(8,128)(2,1)S(1)} collective-permute-done((bf16[64,384]{1,0:T(8,128)(2,1)S(1)}, bf16[64,384]{1,0:T(8,128)(2,1)S(1)}, u32[]{:S(2)}, u32[]{:S(2)}) %collective-permute-start.6) | collective-permute-done | bytes 49184 | tf_op jit(solution)/shard_map/ppermute | solution.py:23
  109.9 2.2 collective-permute-start.4
  113.0 12.7 %collective-permute-done.8.refs_1_ = bf16[128,2560]{1,0:T(8,128)(2,1)} collective-permute-done((bf16[128,2560]{1,0:T(8,128)(2,1)}, bf16[128,2560]{1,0:T(8,128)(2,1)}, u32[]{:S(2)}, u32[]{:S(2)}) %collective-permute-start.8) | collective-permute-done | bytes 655392 | tf_op jit(solution)/shard_map/ppermute | solution.py:23
  125.7 1.6 collective-permute-start.15
  127.2 2.2 collective-permute-start.16
  131.6 3.8 %collective-permute-done.15 = bf16[256,384]{1,0:T(8,128)(2,1)} collective-permute-done((bf16[256,384]{1,0:T(8,128)(2,1)S(1)}, bf16[256,384]{1,0:T(8,128)(2,1)}, u32[]{:S(2)}, u32[]{:S(2)}) %collective-permute-start.15) | collective-permute-done | bytes 196640 | tf_op jit(solution)/shard_map/ppermute | solution.py:334
  135.4 1.6 constant_dynamic-update-slice_fusion.6
  137.8 7.9 %collective-permute-done.17 = bf16[256,384]{1,0:T(8,128)(2,1)S(1)} collective-permute-done((bf16[256,384]{1,0:T(8,128)(2,1)S(1)}, bf16[256,384]{1,0:T(8,128)(2,1)S(1)}, u32[]{:S(2)}, u32[]{:S(2)}) %collective-permute-start.17) | collective-permute-done | bytes 196640 | tf_op jit(solution)/shard_map/ppermute | solution.py:23
  146.4 4.6 %all-to-all-start.1 = ((bf16[8,160,384]{2,1,0:T(8,128)(2,1)}), bf16[8,160,384]{2,1,0:T(8,128)(2,1)}, u32[]{:S(2)}, u32[]{:S(2)}) async-start(bf16[8,160,384]{2,1,0:T(8,128)(2,1)} %get-tuple-element.40), calls=%async_computation.1 | async-start | bytes 1966080 | tf_op jit(solution)/shard_map/all_to_all | solution.py:392
  152.2 1.5 collective-permute-start.18
  154.5 13.2 %collective-permute-done.10.refs_3_ = bf16[128,2560]{1,0:T(8,128)(2,1)} collective-permute-done((bf16[128,2560]{1,0:T(8,128)(2,1)}, bf16[128,2560]{1,0:T(8,128)(2,1)}, u32[]{:S(2)}, u32[]{:S(2)}) %collective-permute-start.10) | collective-permute-done | bytes 655392 | tf_op jit(solution)/shard_map/ppermute | solution.py:23
  167.9 1.3 add.630.refs_3_
  169.3 11.4 %collective-permute-done.18 = bf16[1024,384]{1,0:T(8,128)(2,1)} collective-permute-done((bf16[1024,384]{1,0:T(8,128)(2,1)}, bf16[1024,384]{1,0:T(8,128)(2,1)}, u32[]{:S(2)}, u32[]{:S(2)}) %collective-permute-start.18) | collective-permute-done | bytes 786464 | tf_op jit(solution)/shard_map/ppermute | solution.py:23
  180.7 1.5 select_bitcast_fusion.1
  182.2 1.4 pad_maximum_fusion
  183.6 5.8 %project.1.refs_0_ = bf16[1024,384]{1,0:T(8,128)(2,1)S(1)} custom-call(bf16[128,2560]{1,0:T(8,128)(2,1)} %pad_maximum_fusion.1.refs_0_, bf16[128,2560]{1,0:T(8,128)(2,1)} %collective-permute-done.8.refs_1_, bf16[128,2560]{1,0:T(8,128)(2,1)} %collective-permute-done.9.refs_2_, bf16[128,2560]{1,0:T(8,128)(2,1)} %collective-permute-done.10.refs_3_, ...), custom_call_target="tpu_custom_call" | custom-call | flops 2013265920 | bytes 5242880 | tf_op jit(solution)/shard_map/project/pallas_call | solution.py:190
  189.4 4.2 %attend.2 = (bf16[512,128]{1,0:T(8,128)(2,1)S(1)}, bf16[512,128]{1,0:T(8,128)(2,1)S(1)}) custom-call(s32[3]{0:T(128)S(1)} %pad_add_fusion.here_ref.place_ref, bf16[1024,384]{1,0:T(8,128)(2,1)S(1)} %project.1.refs_0_, bf16[2048,384]{1,0:T(8,128)(2,1)S(1)} %bitcast.61, s32[1,2048]{1,0:T(1,128)S(1)} %sub.145.refs_2_, s32[1024,1]{1,0:T(8,128)S(1)} %copy-done.4), custom_call_target="tpu_custom_call" | custom-call | flops 1342177280 | bytes 1572864 | tf_op jit(solution)/shard_map/attend/pallas_call | solution.py:251
  193.6 4.2 %attend.3 = (bf16[512,128]{1,0:T(8,128)(2,1)S(1)}, bf16[512,128]{1,0:T(8,128)(2,1)S(1)}) custom-call(s32[3]{0:T(128)S(1)} %pad_add_fusion.here_ref.place_ref, bf16[1024,384]{1,0:T(8,128)(2,1)S(1)} %project.1.refs_0_, bf16[2048,384]{1,0:T(8,128)(2,1)S(1)} %bitcast.62, s32[1,2048]{1,0:T(1,128)S(1)} %sub.145.refs_2_, s32[1024,1]{1,0:T(8,128)S(1)} %copy-done.4), custom_call_target="tpu_custom_call" | custom-call | flops 1342177280 | bytes 1572864 | tf_op jit(solution)/shard_map/attend/pallas_call | solution.py:251
  198.5 1.5 collective-permute-start.19
  200.0 3.7 %collective-permute-done.24 = bf16[512,128]{1,0:T(8,128)(2,1)S(1)} collective-permute-done((bf16[512,128]{1,0:T(8,128)(2,1)S(1)}, bf16[512,128]{1,0:T(8,128)(2,1)S(1)}, u32[]{:S(2)}, u32[]{:S(2)}) %collective-permute-start.24) | collective-permute-done | bytes 131104 | tf_op jit(solution)/shard_map/ppermute | solution.py:23
  203.8 2.9 %collective-permute-start.27 = (bf16[512,256]{1,0:T(8,128)(2,1)S(1)}, bf16[512,256]{1,0:T(8,128)(2,1)S(1)}, u32[]{:S(2)}, u32[]{:S(2)}) collective-permute-start(bf16[512,256]{1,0:T(8,128)(2,1)S(1)} %constant_dynamic-update-slice_fusion.2.refs_0_), channel_id=1, source_target_pairs={{0,16},{8,24},{16,0},{24,8},{1,17},{9,25},{17,1},{25,9},{2,18},{10... | collective-permute-start | bytes 786440 | tf_op jit(solution)/shard_map/ppermute | solution.py:23
  206.7 1.8 collective-permute-start.22
  208.5 2.4 collective-permute-start.25
  210.9 1.3 collective-permute-start.26
  212.2 9.9 %collective-permute-done.27.refs_4_ = bf16[512,256]{1,0:T(8,128)(2,1)S(1)} collective-permute-done((bf16[512,256]{1,0:T(8,128)(2,1)S(1)}, bf16[512,256]{1,0:T(8,128)(2,1)S(1)}, u32[]{:S(2)}, u32[]{:S(2)}) %collective-permute-start.27) | collective-permute-done | bytes 262176 | tf_op jit(solution)/shard_map/ppermute | solution.py:23
  223.4 4.6 %collective-permute-start.20 = (bf16[512,256]{1,0:T(8,128)(2,1)S(1)}, bf16[512,256]{1,0:T(8,128)(2,1)S(1)}, u32[]{:S(2)}, u32[]{:S(2)}) collective-permute-start(bf16[512,256]{1,0:T(8,128)(2,1)S(1)} %constant_dynamic-update-slice_fusion.refs_0_), channel_id=1, source_target_pairs={{0,8},{8,16},{16,24},{1,9},{9,17},{17,25},{2,10},{10,18},{18,26},{... | collective-permute-start | bytes 786440 | tf_op jit(solution)/shard_map/ppermute | solution.py:327
  228.0 1.3 collective-permute-start.21
  229.3 1.5 collective-permute-start.23
  231.9 5.6 %collective-permute-done.28.refs_3_ = bf16[512,256]{1,0:T(8,128)(2,1)S(1)} collective-permute-done((bf16[512,256]{1,0:T(8,128)(2,1)S(1)}, bf16[512,256]{1,0:T(8,128)(2,1)S(1)}, u32[]{:S(2)}, u32[]{:S(2)}) %collective-permute-start.28) | collective-permute-done | bytes 262176 | tf_op jit(solution)/shard_map/ppermute | solution.py:329
  237.5 2.0 expel.2.refs_7_
  239.5 3.6 %collective-permute-done.21.refs_2_ = bf16[512,256]{1,0:T(8,128)(2,1)S(1)} collective-permute-done((bf16[512,256]{1,0:T(8,128)(2,1)S(1)}, bf16[512,256]{1,0:T(8,128)(2,1)S(1)}, u32[]{:S(2)}, u32[]{:S(2)}) %collective-permute-start.21) | collective-permute-done | bytes 262176 | tf_op jit(solution)/shard_map/ppermute | solution.py:328
  243.1 3.7 %collective-permute-done.23.refs_3_ = bf16[512,256]{1,0:T(8,128)(2,1)S(1)} collective-permute-done((bf16[512,256]{1,0:T(8,128)(2,1)S(1)}, bf16[512,256]{1,0:T(8,128)(2,1)S(1)}, u32[]{:S(2)}, u32[]{:S(2)}) %collective-permute-start.23) | collective-permute-done | bytes 262176 | tf_op jit(solution)/shard_map/ppermute | solution.py:329
  246.8 3.5 %expel.3 = (f32[4,2,32,640]{3,2,1,0:T(8,128)S(1)}, bf16[4,2,32,640]{3,2,1,0:T(8,128)(2,1)}) custom-call(s32[3]{0:T(128)S(1)} %pad_add_fusion.here_ref.place_ref, bf16[512,256]{1,0:T(8,128)(2,1)S(1)} %constant_dynamic-update-slice_fusion.refs_0_, bf16[512,256]{1,0:T(8,128)(2,1)S(1)} %collective-permute-done.20.refs_1_, ...), custom_call_target="tpu_custom_call" | custom-call | flops 671088640 | bytes 1310720 | tf_op jit(solution)/shard_map/expel/pallas_call | solution.py:311
  251.2 1.8 collective-permute-done.29
  254.3 6.2 %collective-permute-done.30 = bf16[4,32,640]{2,1,0:T(8,128)(2,1)S(1)} collective-permute-done((bf16[4,32,640]{2,1,0:T(8,128)(2,1)S(1)}, bf16[4,32,640]{2,1,0:T(8,128)(2,1)S(1)}, u32[]{:S(2)}, u32[]{:S(2)}) %collective-permute-start.30) | collective-permute-done | bytes 163872 | tf_op jit(solution)/shard_map/ppermute | solution.py:23
  260.8 1.9 collective-permute-start.31
  262.7 9.7 %collective-permute-done.31 = bf16[128,640]{1,0:T(8,128)(2,1)S(1)} collective-permute-done((bf16[128,640]{1,0:T(8,128)(2,1)S(1)}, bf16[128,640]{1,0:T(8,128)(2,1)S(1)}, u32[]{:S(2)}, u32[]{:S(2)}) %collective-permute-start.31) | collective-permute-done | bytes 163872 | tf_op jit(solution)/shard_map/ppermute | solution.py:515
  (93 shorter events, 23.2 us)
Async XLA Ops:
  0.0 3.5 %copy-start = (bf16[128,2560]{1,0:T(8,128)(2,1)S(1)}, bf16[128,2560]{1,0:T(8,128)(2,1)}, u32[]{:S(2)}) copy-start(bf16[128,2560]{1,0:T(8,128)(2,1)} %param.13) | copy-start | bytes 1966084
  0.0 69.6 %copy-start.13 = (bf16[768,192]{0,1:T(8,128)(2,1)S(1)}, bf16[768,192]{0,1:T(8,128)(2,1)}, u32[]{:S(2)}) copy-start(bf16[768,192]{0,1:T(8,128)(2,1)} %param.20) | copy-start | bytes 884740
  1.6 69.0 %collective-permute-start.3 = (bf16[16,1280]{1,0:T(8,128)(2,1)S(1)}, bf16[16,1280]{1,0:T(8,128)(2,1)S(1)}, u32[]{:S(2)}, u32[]{:S(2)}) collective-permute-start(bf16[16,1280]{1,0:T(8,128)(2,1)S(1)} %pad_maximum_fusion.4), channel_id=1, source_target_pairs={{1,0},{2,1},{3,2},{4,3},{5,4},{6,5},{7,6},{8,7},{9,8},{10,9},{11,1... | collective-permute-start | bytes 122888 | tf_op jit(solution)/shard_map/ppermute | solution.py:377
  4.2 66.4 %copy-start.1 = (bf16[2048,320]{0,1:T(8,128)(2,1)S(1)}, bf16[2048,320]{0,1:T(8,128)(2,1)}, u32[]{:S(2)}) copy-start(bf16[2048,320]{0,1:T(8,128)(2,1)} %param.17) | copy-start | bytes 3932164
  4.2 82.2 %collective-permute-start = (bf16[32,2560]{1,0:T(8,128)(2,1)}, bf16[32,2560]{1,0:T(8,128)(2,1)}, u32[]{:S(2)}, u32[]{:S(2)}) collective-permute-start(bf16[32,2560]{1,0:T(8,128)(2,1)} %constant_dynamic-slice_fusion), channel_id=1, source_target_pairs={{0,8},{8,16},{16,24},{24,0},{1,9},{9,17},{17,25},{25,1},{2,10},{10... | collective-permute-start | bytes 491528 | tf_op jit(solution)/shard_map/ppermute | solution.py:334
  5.7 80.6 %collective-permute-start.1 = (bf16[32,2560]{1,0:T(8,128)(2,1)}, bf16[32,2560]{1,0:T(8,128)(2,1)}, u32[]{:S(2)}, u32[]{:S(2)}) collective-permute-start(bf16[32,2560]{1,0:T(8,128)(2,1)} %constant_dynamic-slice_fusion), channel_id=1, source_target_pairs={{8,0},{16,8},{24,16},{0,24},{9,1},{17,9},{25,17},{1,25},{10,2},{18... | collective-permute-start | bytes 491528 | tf_op jit(solution)/shard_map/ppermute | solution.py:335
  8.0 78.4 %collective-permute-start.2 = (bf16[32,2560]{1,0:T(8,128)(2,1)}, bf16[32,2560]{1,0:T(8,128)(2,1)}, u32[]{:S(2)}, u32[]{:S(2)}) collective-permute-start(bf16[32,2560]{1,0:T(8,128)(2,1)} %constant_dynamic-slice_fusion), channel_id=1, source_target_pairs={{0,16},{8,24},{16,0},{24,8},{1,17},{9,25},{17,1},{25,9},{2,18},{10... | collective-permute-start | bytes 491528 | tf_op jit(solution)/shard_map/ppermute | solution.py:23
  70.6 55.1 %collective-permute-start.7 = (bf16[320,2048]{1,0:T(8,128)(2,1)S(1)}, bf16[320,2048]{1,0:T(8,128)(2,1)S(1)}, u32[]{:S(2)}, u32[]{:S(2)}) collective-permute-start(bf16[320,2048]{1,0:T(8,128)(2,1)S(1)} %bitcast.58), channel_id=1, source_target_pairs={{0,4},{4,0},{1,5},{5,1},{2,6},{6,2},{3,7},{7,3},{8,12},{12,8},{9,1... | collective-permute-start | bytes 3932168 | tf_op jit(solution)/shard_map/ppermute | solution.py:23
  72.1 1.0 copy-start.5
  73.1 1.4 copy-start.6
  74.6 1.2 copy-start.7
  75.8 1.0 copy-start.8
  76.7 0.9 copy-start.9
  77.7 0.9 copy-start.10
  78.6 0.9 copy-start.11
  86.4 60.0 %all-to-all-start = ((bf16[8,160,384]{2,1,0:T(8,128)(2,1)}), bf16[8,160,384]{2,1,0:T(8,128)(2,1)}, u32[]{:S(2)}, u32[]{:S(2)}) async-start(bf16[8,160,384]{2,1,0:T(8,128)(2,1)} %get-tuple-element.37), calls=%async_computation | async-start | bytes 1966080 | tf_op jit(solution)/shard_map/all_to_all | solution.py:392
  92.7 33.0 %collective-permute-start.8 = (bf16[128,2560]{1,0:T(8,128)(2,1)}, bf16[128,2560]{1,0:T(8,128)(2,1)}, u32[]{:S(2)}, u32[]{:S(2)}) collective-permute-start(bf16[128,2560]{1,0:T(8,128)(2,1)} %pad_maximum_fusion.1.refs_0_), channel_id=1, source_target_pairs={{0,4},{4,0},{1,5},{5,1},{2,6},{6,2},{3,7},{7,3},{8,12},{12,8},{9,1... | collective-permute-start | bytes 1966088 | tf_op jit(solution)/shard_map/ppermute | solution.py:23
  94.6 31.1 %collective-permute-start.9 = (bf16[128,2560]{1,0:T(8,128)(2,1)}, bf16[128,2560]{1,0:T(8,128)(2,1)}, u32[]{:S(2)}, u32[]{:S(2)}) collective-permute-start(bf16[128,2560]{1,0:T(8,128)(2,1)} %pad_maximum_fusion.1.refs_0_), channel_id=1, source_target_pairs={{0,2},{1,3},{2,0},{3,1},{4,6},{5,7},{6,4},{7,5},{8,10},{9,11},{10,... | collective-permute-start | bytes 1966088 | tf_op jit(solution)/shard_map/ppermute | solution.py:23
  96.0 13.9 %collective-permute-start.6 = (bf16[64,384]{1,0:T(8,128)(2,1)S(1)}, bf16[64,384]{1,0:T(8,128)(2,1)S(1)}, u32[]{:S(2)}, u32[]{:S(2)}) collective-permute-start(bf16[64,384]{1,0:T(8,128)(2,1)S(1)} %get-tuple-element.52), channel_id=1, source_target_pairs={{0,3},{1,2},{2,1},{3,0},{4,7},{5,6},{6,5},{7,4},{8,11},{9,10},{10,... | collective-permute-start | bytes 147464 | tf_op jit(solution)/shard_map/ppermute | solution.py:23
  96.1 16.3 %collective-permute-start.5 = (bf16[64,384]{1,0:T(8,128)(2,1)S(1)}, bf16[64,384]{1,0:T(8,128)(2,1)S(1)}, u32[]{:S(2)}, u32[]{:S(2)}) collective-permute-start(bf16[64,384]{1,0:T(8,128)(2,1)S(1)} %get-tuple-element.53), channel_id=1, source_target_pairs={{0,2},{1,3},{2,0},{3,1},{4,6},{5,7},{6,4},{7,5},{8,10},{9,11},{10,... | collective-permute-start | bytes 147464 | tf_op jit(solution)/shard_map/ppermute | solution.py:23
  109.9 3.1 %collective-permute-start.4 = (bf16[64,384]{1,0:T(8,128)(2,1)S(1)}, bf16[64,384]{1,0:T(8,128)(2,1)S(1)}, u32[]{:S(2)}, u32[]{:S(2)}) collective-permute-start(bf16[64,384]{1,0:T(8,128)(2,1)S(1)} %get-tuple-element.54), channel_id=1, source_target_pairs={{0,1},{1,0},{2,3},{3,2},{4,5},{5,4},{6,7},{7,6},{8,9},{9,8},{10,11... | collective-permute-start | bytes 147464 | tf_op jit(solution)/shard_map/ppermute | solution.py:23
  125.7 9.8 %collective-permute-start.15 = (bf16[256,384]{1,0:T(8,128)(2,1)S(1)}, bf16[256,384]{1,0:T(8,128)(2,1)}, u32[]{:S(2)}, u32[]{:S(2)}) collective-permute-start(bf16[256,384]{1,0:T(8,128)(2,1)S(1)} %pad_maximum_fusion.2), channel_id=1, source_target_pairs={{0,8},{8,16},{16,24},{24,0},{1,9},{9,17},{17,25},{25,1},{2,10},{10... | collective-permute-start | bytes 589832 | tf_op jit(solution)/shard_map/ppermute | solution.py:334
  127.2 9.8 %collective-permute-start.16 = (bf16[256,384]{1,0:T(8,128)(2,1)S(1)}, bf16[256,384]{1,0:T(8,128)(2,1)S(1)}, u32[]{:S(2)}, u32[]{:S(2)}) collective-permute-start(bf16[256,384]{1,0:T(8,128)(2,1)S(1)} %pad_maximum_fusion.2), channel_id=1, source_target_pairs={{8,0},{16,8},{24,16},{0,24},{9,1},{17,9},{25,17},{1,25},{10,2},{18... | collective-permute-start | bytes 589832 | tf_op jit(solution)/shard_map/ppermute | solution.py:335
  129.5 16.2 %collective-permute-start.17 = (bf16[256,384]{1,0:T(8,128)(2,1)S(1)}, bf16[256,384]{1,0:T(8,128)(2,1)S(1)}, u32[]{:S(2)}, u32[]{:S(2)}) collective-permute-start(bf16[256,384]{1,0:T(8,128)(2,1)S(1)} %pad_maximum_fusion.2), channel_id=1, source_target_pairs={{0,16},{8,24},{16,0},{24,8},{1,17},{9,25},{17,1},{25,9},{2,18},{10... | collective-permute-start | bytes 589832 | tf_op jit(solution)/shard_map/ppermute | solution.py:23
  146.4 7.5 %copy-start.15 = (s32[1,1,4,1]{2,3,1,0:T(1,128)S(1)}, s32[1,1,4,1]{2,3,1,0:T(1,128)}, u32[]{:S(2)}) copy-start(s32[1,1,4,1]{2,3,1,0:T(1,128)} %constant.475.clone) | copy-start | bytes 52
  146.4 7.5 %copy-start.14 = (s32[2,4,64]{2,1,0:T(4,128)S(1)}, s32[2,4,64]{2,1,0:T(4,128)}, u32[]{:S(2)}) copy-start(s32[2,4,64]{2,1,0:T(4,128)} %constant.478) | copy-start | bytes 6148
  146.4 37.2 %all-to-all-start.1 = ((bf16[8,160,384]{2,1,0:T(8,128)(2,1)}), bf16[8,160,384]{2,1,0:T(8,128)(2,1)}, u32[]{:S(2)}, u32[]{:S(2)}) async-start(bf16[8,160,384]{2,1,0:T(8,128)(2,1)} %get-tuple-element.40), calls=%async_computation.1 | async-start | bytes 1966080 | tf_op jit(solution)/shard_map/all_to_all | solution.py:392
  150.9 16.8 %collective-permute-start.10 = (bf16[128,2560]{1,0:T(8,128)(2,1)}, bf16[128,2560]{1,0:T(8,128)(2,1)}, u32[]{:S(2)}, u32[]{:S(2)}) collective-permute-start(bf16[128,2560]{1,0:T(8,128)(2,1)} %collective-permute-done.8.refs_1_), channel_id=1, source_target_pairs={{0,2},{1,3},{2,0},{3,1},{4,6},{5,7},{6,4},{7,5},{8,10},{9,11},{10,... | collective-permute-start | bytes 1966088 | tf_op jit(solution)/shard_map/ppermute | solution.py:23
  152.2 28.5 %collective-permute-start.18 = (bf16[1024,384]{1,0:T(8,128)(2,1)}, bf16[1024,384]{1,0:T(8,128)(2,1)}, u32[]{:S(2)}, u32[]{:S(2)}) collective-permute-start(bf16[1024,384]{1,0:T(8,128)(2,1)} %constant_dynamic-update-slice_fusion.4), channel_id=1, source_target_pairs={{0,4},{4,0},{1,5},{5,1},{2,6},{6,2},{3,7},{7,3},{8,12},{12,8},{9,1... | collective-permute-start | bytes 2359304 | tf_op jit(solution)/shard_map/ppermute | solution.py:23
  153.9 29.6 %collective-permute-start.12 = (bf16[128,2560]{1,0:T(8,128)(2,1)}, bf16[128,2560]{1,0:T(8,128)(2,1)}, u32[]{:S(2)}, u32[]{:S(2)}) collective-permute-start(bf16[128,2560]{1,0:T(8,128)(2,1)} %collective-permute-done.8.refs_1_), channel_id=1, source_target_pairs={{0,1},{1,0},{2,3},{3,2},{4,5},{5,4},{6,7},{7,6},{8,9},{9,8},{10,11... | collective-permute-start | bytes 1966088 | tf_op jit(solution)/shard_map/ppermute | solution.py:23
  154.0 29.6 %collective-permute-start.11 = (bf16[128,2560]{1,0:T(8,128)(2,1)}, bf16[128,2560]{1,0:T(8,128)(2,1)}, u32[]{:S(2)}, u32[]{:S(2)}) collective-permute-start(bf16[128,2560]{1,0:T(8,128)(2,1)} %pad_maximum_fusion.1.refs_0_), channel_id=1, source_target_pairs={{0,1},{1,0},{2,3},{3,2},{4,5},{5,4},{6,7},{7,6},{8,9},{9,8},{10,11... | collective-permute-start | bytes 1966088 | tf_op jit(solution)/shard_map/ppermute | solution.py:23
  154.4 29.1 %collective-permute-start.13 = (bf16[128,2560]{1,0:T(8,128)(2,1)}, bf16[128,2560]{1,0:T(8,128)(2,1)}, u32[]{:S(2)}, u32[]{:S(2)}) collective-permute-start(bf16[128,2560]{1,0:T(8,128)(2,1)} %collective-permute-done.9.refs_2_), channel_id=1, source_target_pairs={{0,1},{1,0},{2,3},{3,2},{4,5},{5,4},{6,7},{7,6},{8,9},{9,8},{10,11... | collective-permute-start | bytes 1966088 | tf_op jit(solution)/shard_map/ppermute | solution.py:23
  167.7 15.9 %collective-permute-start.14 = (bf16[128,2560]{1,0:T(8,128)(2,1)}, bf16[128,2560]{1,0:T(8,128)(2,1)}, u32[]{:S(2)}, u32[]{:S(2)}) collective-permute-start(bf16[128,2560]{1,0:T(8,128)(2,1)} %collective-permute-done.10.refs_3_), channel_id=1, source_target_pairs={{0,1},{1,0},{2,3},{3,2},{4,5},{5,4},{6,7},{7,6},{8,9},{9,8},{10,11... | collective-permute-start | bytes 1966088 | tf_op jit(solution)/shard_map/ppermute | solution.py:23
  183.6 5.8 %copy-start.2 = (bf16[2,1024,384]{2,1,0:T(8,128)(2,1)S(1)}, bf16[2,1024,384]{2,1,0:T(8,128)(2,1)}, u32[]{:S(2)}) copy-start(bf16[2,1024,384]{2,1,0:T(8,128)(2,1)} %pad_maximum_fusion) | copy-start | bytes 4718596
  183.6 5.8 %copy-start.4 = (s32[1024,1]{1,0:T(8,128)S(1)}, s32[1024,1]{1,0:T(8,128)}, u32[]{:S(2)}) copy-start(s32[1024,1]{1,0:T(8,128)} %add.630.refs_3_) | copy-start | bytes 12292
  197.8 5.9 %collective-permute-start.24 = (bf16[512,128]{1,0:T(8,128)(2,1)S(1)}, bf16[512,128]{1,0:T(8,128)(2,1)S(1)}, u32[]{:S(2)}, u32[]{:S(2)}) collective-permute-start(bf16[512,128]{1,0:T(8,128)(2,1)S(1)} %get-tuple-element.46), channel_id=1, source_target_pairs={{0,4},{4,0},{1,5},{5,1},{2,6},{6,2},{3,7},{7,3},{8,12},{12,8},{9,1... | collective-permute-start | bytes 393224 | tf_op jit(solution)/shard_map/ppermute | solution.py:23
  198.5 8.2 %collective-permute-start.19 = (bf16[512,128]{1,0:T(8,128)(2,1)S(1)}, bf16[512,128]{1,0:T(8,128)(2,1)S(1)}, u32[]{:S(2)}, u32[]{:S(2)}) collective-permute-start(bf16[512,128]{1,0:T(8,128)(2,1)S(1)} %get-tuple-element.43), channel_id=1, source_target_pairs={{0,4},{4,0},{1,5},{5,1},{2,6},{6,2},{3,7},{7,3},{8,12},{12,8},{9,1... | collective-permute-start | bytes 393224 | tf_op jit(solution)/shard_map/ppermute | solution.py:23
  203.8 18.4 %collective-permute-start.27 = (bf16[512,256]{1,0:T(8,128)(2,1)S(1)}, bf16[512,256]{1,0:T(8,128)(2,1)S(1)}, u32[]{:S(2)}, u32[]{:S(2)}) collective-permute-start(bf16[512,256]{1,0:T(8,128)(2,1)S(1)} %constant_dynamic-update-slice_fusion.2.refs_0_), channel_id=1, source_target_pairs={{0,16},{8,24},{16,0},{24,8},{1,17},{9,25},{17,1},{25,9},{2,18},{10... | collective-permute-start | bytes 786440 | tf_op jit(solution)/shard_map/ppermute | solution.py:23
  206.7 21.3 %collective-permute-start.22 = (bf16[512,256]{1,0:T(8,128)(2,1)S(1)}, bf16[512,256]{1,0:T(8,128)(2,1)S(1)}, u32[]{:S(2)}, u32[]{:S(2)}) collective-permute-start(bf16[512,256]{1,0:T(8,128)(2,1)S(1)} %constant_dynamic-update-slice_fusion.refs_0_), channel_id=1, source_target_pairs={{0,16},{8,24},{16,0},{24,8},{1,17},{9,25},{17,1},{25,9},{2,18},{10... | collective-permute-start | bytes 786440 | tf_op jit(solution)/shard_map/ppermute | solution.py:23
  208.5 20.8 %collective-permute-start.25 = (bf16[512,256]{1,0:T(8,128)(2,1)S(1)}, bf16[512,256]{1,0:T(8,128)(2,1)S(1)}, u32[]{:S(2)}, u32[]{:S(2)}) collective-permute-start(bf16[512,256]{1,0:T(8,128)(2,1)S(1)} %constant_dynamic-update-slice_fusion.2.refs_0_), channel_id=1, source_target_pairs={{0,8},{8,16},{16,24},{1,9},{9,17},{17,25},{2,10},{10,18},{18,26},{... | collective-permute-start | bytes 786440 | tf_op jit(solution)/shard_map/ppermute | solution.py:327
  210.9 20.9 %collective-permute-start.26 = (bf16[512,256]{1,0:T(8,128)(2,1)S(1)}, bf16[512,256]{1,0:T(8,128)(2,1)S(1)}, u32[]{:S(2)}, u32[]{:S(2)}) collective-permute-start(bf16[512,256]{1,0:T(8,128)(2,1)S(1)} %constant_dynamic-update-slice_fusion.2.refs_0_), channel_id=1, source_target_pairs={{8,0},{16,8},{24,16},{9,1},{17,9},{25,17},{10,2},{18,10},{26,18},{... | collective-permute-start | bytes 786440 | tf_op jit(solution)/shard_map/ppermute | solution.py:328
  222.1 15.4 %collective-permute-start.28 = (bf16[512,256]{1,0:T(8,128)(2,1)S(1)}, bf16[512,256]{1,0:T(8,128)(2,1)S(1)}, u32[]{:S(2)}, u32[]{:S(2)}) collective-permute-start(bf16[512,256]{1,0:T(8,128)(2,1)S(1)} %collective-permute-done.27.refs_4_), channel_id=1, source_target_pairs={{8,0},{16,24},{9,1},{17,25},{10,2},{18,26},{11,3},{19,27},{12,4},{... | collective-permute-start | bytes 786440 | tf_op jit(solution)/shard_map/ppermute | solution.py:329
  223.4 16.1 %collective-permute-start.20 = (bf16[512,256]{1,0:T(8,128)(2,1)S(1)}, bf16[512,256]{1,0:T(8,128)(2,1)S(1)}, u32[]{:S(2)}, u32[]{:S(2)}) collective-permute-start(bf16[512,256]{1,0:T(8,128)(2,1)S(1)} %constant_dynamic-update-slice_fusion.refs_0_), channel_id=1, source_target_pairs={{0,8},{8,16},{16,24},{1,9},{9,17},{17,25},{2,10},{10,18},{18,26},{... | collective-permute-start | bytes 786440 | tf_op jit(solution)/shard_map/ppermute | solution.py:327
  228.0 15.1 %collective-permute-start.21 = (bf16[512,256]{1,0:T(8,128)(2,1)S(1)}, bf16[512,256]{1,0:T(8,128)(2,1)S(1)}, u32[]{:S(2)}, u32[]{:S(2)}) collective-permute-start(bf16[512,256]{1,0:T(8,128)(2,1)S(1)} %constant_dynamic-update-slice_fusion.refs_0_), channel_id=1, source_target_pairs={{8,0},{16,8},{24,16},{9,1},{17,9},{25,17},{10,2},{18,10},{26,18},{... | collective-permute-start | bytes 786440 | tf_op jit(solution)/shard_map/ppermute | solution.py:328
  229.3 17.5 %collective-permute-start.23 = (bf16[512,256]{1,0:T(8,128)(2,1)S(1)}, bf16[512,256]{1,0:T(8,128)(2,1)S(1)}, u32[]{:S(2)}, u32[]{:S(2)}) collective-permute-start(bf16[512,256]{1,0:T(8,128)(2,1)S(1)} %collective-permute-done.22.refs_4_), channel_id=1, source_target_pairs={{8,0},{16,24},{9,1},{17,25},{10,2},{18,26},{11,3},{19,27},{12,4},{... | collective-permute-start | bytes 786440 | tf_op jit(solution)/shard_map/ppermute | solution.py:329
  251.2 1.8 collective-permute-start.29
  254.2 6.3 %collective-permute-start.30 = (bf16[4,32,640]{2,1,0:T(8,128)(2,1)S(1)}, bf16[4,32,640]{2,1,0:T(8,128)(2,1)S(1)}, u32[]{:S(2)}, u32[]{:S(2)}) collective-permute-start(bf16[4,32,640]{2,1,0:T(8,128)(2,1)S(1)} %fusion.1), channel_id=1, source_target_pairs={{0,2},{1,3},{2,0},{3,1},{4,6},{5,7},{6,4},{7,5},{8,10},{9,11},{10,... | collective-permute-start | bytes 491528 | tf_op jit(solution)/shard_map/ppermute | solution.py:23
  260.8 11.6 %collective-permute-start.31 = (bf16[128,640]{1,0:T(8,128)(2,1)S(1)}, bf16[128,640]{1,0:T(8,128)(2,1)S(1)}, u32[]{:S(2)}, u32[]{:S(2)}) collective-permute-start(bf16[128,640]{1,0:T(8,128)(2,1)S(1)} %pad_maximum_fusion.3), channel_id=1, source_target_pairs={{0,0},{1,8},{2,16},{3,24},{4,4},{5,12},{6,20},{7,28},{8,1},{9,9},{... | collective-permute-start | bytes 491528 | tf_op jit(solution)/shard_map/ppermute | solution.py:515
  (2 other events, 1.7 us)

commit v7 on v5

--- a/solution.py
+++ b/solution.py
@@ -110,7 +110,7 @@
             pltpu.VMEM(raw_values.shape, jnp.bfloat16),
             pltpu.VMEM((G * blocks, units), jnp.bfloat16),
         ],
-        compiler_params=pltpu.CompilerParams(vmem_limit_bytes=VMEM_LIMIT),
+        compiler_params=pltpu.CompilerParams(vmem_limit_bytes=56 * 1024 * 1024),
         cost_estimate=pl.CostEstimate(
             flops=flops, bytes_accessed=2 * raw_keys.size, transcendentals=0
         ),
@@ -361,9 +361,13 @@
     part = query_weight.shape[0]
     fast = inner == 2 and outer == 4 and heads_axis == 4
 
-    if fast:
-        turned = output_weight.T
-        out_weights = [turned, swap(turned, "inner", 1)]
+    edge = jnp.concatenate([raw_keys[:STRIDE], raw_values[:STRIDE]], axis=1)
+    edge = lax.ppermute(
+        edge, ("outer", "inner", "head"), [(i + 1, i) for i in range(devices - 1)]
+    )
+
+    if fast:
+        out_weights = [output_weight.T]
     else:
         out_weights = lax.all_gather(output_weight, "inner", axis=1, tiled=True)
 
@@ -383,22 +387,18 @@
         weight = lax.all_gather(weight, "inner", axis=1).reshape(model, share)
     heads_here = share // key_width
 
-    edge = jnp.concatenate([raw_keys[:STRIDE], raw_values[:STRIDE]], axis=1)
-    edge = lax.ppermute(
-        edge, ("outer", "inner", "head"), [(i + 1, i) for i in range(devices - 1)]
-    )
-    edge_keys, edge_values = edge[:, : raw_keys.shape[1]], edge[:, raw_keys.shape[1] :]
-
     if fast:
         quarter = row_count // heads_axis
         mine = lax.dynamic_slice_in_dim(tokens, h * quarter, quarter, 0)
         mine, before, after, far = ring_pieces(mine, "outer")
-        begin, before, after, far, raw_keys, raw_values = lax.optimization_barrier(
-            (sent[0], before, after, far, raw_keys, raw_values)
+        begin, before, after, far, edge = lax.optimization_barrier(
+            (sent[0], before, after, far, edge)
         )
         weight_first = exchange(begin)
         near = jnp.concatenate([mine, before, after, far], axis=0)
         beside = swap(near, "inner", 1)
+        beside, turned = lax.optimization_barrier((beside, out_weights[0]))
+        out_weights.append(swap(turned, "inner", 1))
         pieces = [near, beside, swap(near, "head", 2)]
         steps = [(line, side, turn) for turn in (0, 2) for side in (0, 1) for line in range(4)]
         steps = steps + [(a, b, k ^ 1) for a, b, k in steps]
@@ -421,6 +421,7 @@
     places = (context + bases).astype(jnp.int32).reshape(-1, 1)
     here = jnp.stack([z, h, y]).astype(jnp.int32)
 
+    edge_keys, edge_values = edge[:, : raw_keys.shape[1]], edge[:, raw_keys.shape[1] :]
     packed = compress(
         raw_keys, raw_values, edge_keys, edge_values,
         key_expand, key_mix, key_reduce, value_expand, value_mix, value_reduce,
@@ -439,8 +440,9 @@
         packed = packed.reshape(heads_axis * blocks, -1)
         bound = ids
     if fast:
-        packed, out_weights[1], pieces = lax.optimization_barrier((packed, out_weights[1], pieces))
+        packed, pieces = lax.optimization_barrier((packed, pieces))
         pieces.append(swap(pieces[1], "head", 2))
+        pieces, out_weights[1] = lax.optimization_barrier((pieces, out_weights[1]))
         partners = [swap(piece, "head", 1) for piece in pieces]
     packed = gather_line(packed, "outer", 0)
     if fast:

time: 211 us -> 204 us (0.967)
  starting transfers between devices: 53.6 us -> 47.8 us
  waiting for transfers between devices: 106 us -> 101 us
  local copies, waits for them, and re-layouts: 11.9 us -> 15.7 us
    ppermute x20, waiting for transfers between devices: 63.8 us -> 75.2 us  [swap(): lax.ppermute(block, axis, [(i, i ^ bit) for i in range(lax.axis_size(axis...]
    ppermute x1, waiting for transfers between devices: 10.8 us -> 0.01 us  [shards(): lax.ppermute(edge, ('outer', 'inner', 'head'), [(i + 1, i) for i in range...]
    ppermute x20, starting transfers between devices: 20 us -> 14.8 us  [swap(): lax.ppermute(block, axis, [(i, i ^ bit) for i in range(lax.axis_size(axis...]
    unnamed x34 -> x28, local copies, waits for them, and re-layouts: 10.8 us -> 5.78 us
    dynamic_update_slice x4, local copies, waits for them, and re-layouts: 0.13 us -> 3.77 us  [gather_line(): out = lax.dynamic_update_slice_in_dim(out, piece, place * size, dim)]
    ppermute x2, waiting for transfers between devices: 3.37 us -> 0.54 us  [ring_pieces(): after = lax.ppermute(block, axis, [((i + 1) % 4, i) for i in range(4)])]
    pallas_call x1, Pallas kernels: 5.96 us -> 8.52 us  [compress(): pl.pallas_call(compress_kernel, out_shape=jax.ShapeDtypeStruct((G, blocks...]
  transfers between devices with their start and end apart: 34 -> 34, of which waited for: 19 -> 17; matrix products, arithmetic and copies ran while one was open for 3% -> 7% of each run, Pallas kernels for 6% -> 8%
where the time goes in v7:
time: 204 us; the launch traced here: 203 us
  waiting for transfers between devices  101 us (50%)
  starting transfers between devices  47.8 us (23%)
  Pallas kernels  33.5 us (16%)
  local copies, waits for them, and re-layouts  15.7 us (8%)
  other arithmetic  4.54 us (2%)
    ppermute x20, waiting for transfers between devices, swap(): lax.ppermute(block, axis, [(i, i ^ bit) for i in range(lax.axis_size(axis...  75.2 us
    ppermute x20, starting transfers between devices, swap(): lax.ppermute(block, axis, [(i, i ^ bit) for i in range(lax.axis_size(axis...  14.8 us
    ppermute x1, waiting for transfers between devices, shards(): return lax.ppermute(result, ('outer', 'inner', 'head'), route)  9.68 us
    all_to_all x2, starting transfers between devices, exchange(): lax.all_to_all(block, seq_axes, split_axis=0, concat_axis=0, tiled=True)  8.93 us
    ppermute x2, waiting for transfers between devices, line_pieces(): passed = lax.ppermute(far, axis, [(1, 0), (2, 3)])  8.64 us
    pallas_call x1, Pallas kernels, compress(): pl.pallas_call(compress_kernel, out_shape=jax.ShapeDtypeStruct((G, blocks...  8.52 us
    pallas_call x2, Pallas kernels, attend(): pl.pallas_call(kernel, out_shape=(shape,) * outputs, in_specs=[pl.BlockSp...  8.35 us
    ppermute x2, starting transfers between devices, line_pieces(): up = lax.ppermute(block, axis, [(i, i + 1) for i in range(3)])  7.13 us
  transfers between devices with their start and end apart: 34, of which 17 were waited for; matrix products, arithmetic and copies ran while one was open for 7% of the time, Pallas kernels for 8%

profile of v7, /device:TPU:2, one launch (start us, length us, event | category | flops | bytes accessed | tf_op | source)
XLA Modules:
  0.0 203.3 jit_solution(13611234826487029871)
XLA Ops:
  0.0 1.1 copy-done
  1.1 1.6 collective-permute-start
  2.7 2.2 %collective-permute-start.1 = (bf16[32,2560]{1,0:T(8,128)(2,1)S(1)}, bf16[32,2560]{1,0:T(8,128)(2,1)S(1)}, u32[]{:S(2)}, u32[]{:S(2)}) collective-permute-start(bf16[32,2560]{1,0:T(8,128)(2,1)S(1)} %constant_dynamic-slice_fusion), channel_id=1, source_target_pairs={{8,0},{16,8},{24,16},{0,24},{9,1},{17,9},{25,17},{1,25},{10,2},{18... | collective-permute-start | bytes 491528 | tf_op jit(solution)/shard_map/ppermute | solution.py:323
  7.2 1.9 collective-permute-start.3
  9.2 5.6 %cut.1 = (bf16[8,160,384]{2,1,0:T(8,128)(2,1)}, bf16[8,160,384]{2,1,0:T(8,128)(2,1)}) custom-call(bf16[320,3072]{1,0:T(8,128)(2,1)} %in_ref.1), custom_call_target="tpu_custom_call" | custom-call | tf_op jit(solution)/shard_map/cut/pallas_call | solution.py:129
  14.8 4.7 %collective-permute-done.2 = bf16[32,2560]{1,0:T(8,128)(2,1)S(1)} collective-permute-done((bf16[32,2560]{1,0:T(8,128)(2,1)S(1)}, bf16[32,2560]{1,0:T(8,128)(2,1)S(1)}, u32[]{:S(2)}, u32[]{:S(2)}) %collective-permute-start.2) | collective-permute-done | bytes 163872 | tf_op jit(solution)/shard_map/ppermute | solution.py:23
  19.5 4.4 %all-to-all-start = ((bf16[8,160,384]{2,1,0:T(8,128)(2,1)}), bf16[8,160,384]{2,1,0:T(8,128)(2,1)}, u32[]{:S(2)}, u32[]{:S(2)}) async-start(bf16[8,160,384]{2,1,0:T(8,128)(2,1)} %get-tuple-element.45), calls=%async_computation | async-start | bytes 1966080 | tf_op jit(solution)/shard_map/all_to_all | solution.py:379
  23.9 2.0 collective-permute-start.7
  28.6 8.5 %compress.1 = bf16[4,64,384]{2,1,0:T(8,128)(2,1)} custom-call(bf16[1024,768]{1,0:T(8,128)(2,1)} %raw_keys.1, bf16[1024,512]{1,0:T(8,128)(2,1)} %raw_values.1, bf16[16,768]{1,0:T(8,128)(2,1)} %slice.20.edge_keys, bf16[16,512]{1,0:T(8,128)(2,1)} %slice.21.edge_values, bf16[192,768]{1,0:T(8,128)(2,1)} %key_expand.1, f32[32,768]{1,0:T(8,128)} %key_mix.1, ...), custom_call_target="tpu_custom_call" | custom-call | flops 2013265920 | bytes 1572864 | tf_op jit(solution)/shard_map/compress/pallas_call | solution.py:105
  38.3 1.3 collective-permute-start.5
  39.9 2.2 %collective-permute-done.6 = bf16[64,384]{1,0:T(8,128)(2,1)S(1)} collective-permute-done((bf16[64,384]{1,0:T(8,128)(2,1)S(1)}, bf16[64,384]{1,0:T(8,128)(2,1)S(1)}, u32[]{:S(2)}, u32[]{:S(2)}) %collective-permute-start.6) | collective-permute-done | bytes 49184 | tf_op jit(solution)/shard_map/ppermute | solution.py:23
  42.2 1.9 collective-permute-done.5
  44.1 7.0 %collective-permute-done.7.refs_1_ = bf16[128,2560]{1,0:T(8,128)(2,1)S(1)} collective-permute-done((bf16[128,2560]{1,0:T(8,128)(2,1)S(1)}, bf16[128,2560]{1,0:T(8,128)(2,1)S(1)}, u32[]{:S(2)}, u32[]{:S(2)}) %collective-permute-start.7) | collective-permute-done | bytes 655392 | tf_op jit(solution)/shard_map/ppermute | solution.py:23
  51.1 1.5 collective-permute-start.15
  52.6 2.3 %collective-permute-start.16 = (bf16[256,384]{1,0:T(8,128)(2,1)S(1)}, bf16[256,384]{1,0:T(8,128)(2,1)S(1)}, u32[]{:S(2)}, u32[]{:S(2)}) collective-permute-start(bf16[256,384]{1,0:T(8,128)(2,1)S(1)} %pad_maximum_fusion.2), channel_id=1, source_target_pairs={{8,0},{16,8},{24,16},{0,24},{9,1},{17,9},{25,17},{1,25},{10,2},{18... | collective-permute-start | bytes 589832 | tf_op jit(solution)/shard_map/ppermute | solution.py:323
  57.8 3.1 %collective-permute-done.15 = bf16[256,384]{1,0:T(8,128)(2,1)} collective-permute-done((bf16[256,384]{1,0:T(8,128)(2,1)S(1)}, bf16[256,384]{1,0:T(8,128)(2,1)}, u32[]{:S(2)}, u32[]{:S(2)}) %collective-permute-start.15) | collective-permute-done | bytes 196640 | tf_op jit(solution)/shard_map/ppermute | solution.py:322
  60.9 1.6 constant_dynamic-update-slice_fusion.6
  63.8 7.8 %collective-permute-done.17 = bf16[256,384]{1,0:T(8,128)(2,1)S(1)} collective-permute-done((bf16[256,384]{1,0:T(8,128)(2,1)S(1)}, bf16[256,384]{1,0:T(8,128)(2,1)S(1)}, u32[]{:S(2)}, u32[]{:S(2)}) %collective-permute-start.17) | collective-permute-done | bytes 196640 | tf_op jit(solution)/shard_map/ppermute | solution.py:23
  72.3 4.6 %all-to-all-start.1 = ((bf16[8,160,384]{2,1,0:T(8,128)(2,1)}), bf16[8,160,384]{2,1,0:T(8,128)(2,1)}, u32[]{:S(2)}, u32[]{:S(2)}) async-start(bf16[8,160,384]{2,1,0:T(8,128)(2,1)} %get-tuple-element.48), calls=%async_computation.1 | async-start | bytes 1966080 | tf_op jit(solution)/shard_map/all_to_all | solution.py:379
  79.4 14.6 %collective-permute-done.9.refs_3_ = bf16[128,2560]{1,0:T(8,128)(2,1)} collective-permute-done((bf16[128,2560]{1,0:T(8,128)(2,1)}, bf16[128,2560]{1,0:T(8,128)(2,1)}, u32[]{:S(2)}, u32[]{:S(2)}) %collective-permute-start.9) | collective-permute-done | bytes 655392 | tf_op jit(solution)/shard_map/ppermute | solution.py:23
  95.1 1.3 add.630.refs_3_
  96.5 16.4 %collective-permute-done.18 = bf16[1024,384]{1,0:T(8,128)(2,1)} collective-permute-done((bf16[1024,384]{1,0:T(8,128)(2,1)}, bf16[1024,384]{1,0:T(8,128)(2,1)}, u32[]{:S(2)}, u32[]{:S(2)}) %collective-permute-start.18) | collective-permute-done | bytes 786464 | tf_op jit(solution)/shard_map/ppermute | solution.py:23
  112.9 1.5 select_bitcast_fusion.1
  114.4 1.3 pad_maximum_fusion
  118.0 5.5 %project.1.refs_0_ = bf16[1024,384]{1,0:T(8,128)(2,1)S(1)} custom-call(bf16[128,2560]{1,0:T(8,128)(2,1)S(1)} %copy-done.3, bf16[128,2560]{1,0:T(8,128)(2,1)S(1)} %copy-done.7, bf16[128,2560]{1,0:T(8,128)(2,1)} %collective-permute-done.8.refs_2_, bf16[128,2560]{1,0:T(8,128)(2,1)} %collective-permute-done.9.refs_3_, ...), custom_call_target="tpu_custom_call" | custom-call | flops 2013265920 | bytes 5242880 | tf_op jit(solution)/shard_map/project/pallas_call | solution.py:178
  123.5 4.2 %attend.2 = (bf16[512,128]{1,0:T(8,128)(2,1)S(1)}, bf16[512,128]{1,0:T(8,128)(2,1)S(1)}) custom-call(s32[3]{0:T(128)S(1)} %pad_add_fusion.here_ref.place_ref, bf16[1024,384]{1,0:T(8,128)(2,1)S(1)} %project.1.refs_0_, bf16[2048,384]{1,0:T(8,128)(2,1)S(1)} %bitcast.61, s32[1,2048]{1,0:T(1,128)S(1)} %sub.145.refs_2_, s32[1024,1]{1,0:T(8,128)S(1)} %copy-done.8), custom_call_target="tpu_custom_call" | custom-call | flops 1342177280 | bytes 1572864 | tf_op jit(solution)/shard_map/attend/pallas_call | solution.py:239
  127.6 4.2 %attend.3 = (bf16[512,128]{1,0:T(8,128)(2,1)S(1)}, bf16[512,128]{1,0:T(8,128)(2,1)S(1)}) custom-call(s32[3]{0:T(128)S(1)} %pad_add_fusion.here_ref.place_ref, bf16[1024,384]{1,0:T(8,128)(2,1)S(1)} %project.1.refs_0_, bf16[2048,384]{1,0:T(8,128)(2,1)S(1)} %bitcast.62, s32[1,2048]{1,0:T(1,128)S(1)} %sub.145.refs_2_, s32[1024,1]{1,0:T(8,128)S(1)} %copy-done.8), custom_call_target="tpu_custom_call" | custom-call | flops 1342177280 | bytes 1572864 | tf_op jit(solution)/shard_map/attend/pallas_call | solution.py:239
  132.2 1.8 collective-permute-start.19
  134.0 2.9 %collective-permute-done.24 = bf16[512,128]{1,0:T(8,128)(2,1)S(1)} collective-permute-done((bf16[512,128]{1,0:T(8,128)(2,1)S(1)}, bf16[512,128]{1,0:T(8,128)(2,1)S(1)}, u32[]{:S(2)}, u32[]{:S(2)}) %collective-permute-start.24) | collective-permute-done | bytes 131104 | tf_op jit(solution)/shard_map/ppermute | solution.py:23
  137.0 1.5 collective-permute-start.27
  138.5 1.6 collective-permute-start.22
  140.1 2.6 %collective-permute-start.25 = (bf16[512,256]{1,0:T(8,128)(2,1)S(1)}, bf16[512,256]{1,0:T(8,128)(2,1)S(1)}, u32[]{:S(2)}, u32[]{:S(2)}) collective-permute-start(bf16[512,256]{1,0:T(8,128)(2,1)S(1)} %constant_dynamic-update-slice_fusion.2.refs_0_), channel_id=1, source_target_pairs={{0,8},{8,16},{16,24},{1,9},{9,17},{17,25},{2,10},{10,18},{18,26},{... | collective-permute-start | bytes 786440 | tf_op jit(solution)/shard_map/ppermute | solution.py:315
  142.6 1.3 collective-permute-start.26
  143.9 10.1 %collective-permute-done.27.refs_4_ = bf16[512,256]{1,0:T(8,128)(2,1)S(1)} collective-permute-done((bf16[512,256]{1,0:T(8,128)(2,1)S(1)}, bf16[512,256]{1,0:T(8,128)(2,1)S(1)}, u32[]{:S(2)}, u32[]{:S(2)}) %collective-permute-start.27) | collective-permute-done | bytes 262176 | tf_op jit(solution)/shard_map/ppermute | solution.py:23
  154.1 1.3 collective-permute-start.28
  155.4 4.6 %collective-permute-start.20 = (bf16[512,256]{1,0:T(8,128)(2,1)S(1)}, bf16[512,256]{1,0:T(8,128)(2,1)S(1)}, u32[]{:S(2)}, u32[]{:S(2)}) collective-permute-start(bf16[512,256]{1,0:T(8,128)(2,1)S(1)} %constant_dynamic-update-slice_fusion.refs_0_), channel_id=1, source_target_pairs={{0,8},{8,16},{16,24},{1,9},{9,17},{17,25},{2,10},{10,18},{18,26},{... | collective-permute-start | bytes 786440 | tf_op jit(solution)/shard_map/ppermute | solution.py:315
  160.0 1.3 collective-permute-start.21
  161.3 1.5 collective-permute-start.23
  162.8 3.6 %collective-permute-done.28.refs_3_ = bf16[512,256]{1,0:T(8,128)(2,1)S(1)} collective-permute-done((bf16[512,256]{1,0:T(8,128)(2,1)S(1)}, bf16[512,256]{1,0:T(8,128)(2,1)S(1)}, u32[]{:S(2)}, u32[]{:S(2)}) %collective-permute-start.28) | collective-permute-done | bytes 262176 | tf_op jit(solution)/shard_map/ppermute | solution.py:317
  166.4 2.0 expel.2.refs_7_
  168.3 3.6 %collective-permute-done.21.refs_2_ = bf16[512,256]{1,0:T(8,128)(2,1)S(1)} collective-permute-done((bf16[512,256]{1,0:T(8,128)(2,1)S(1)}, bf16[512,256]{1,0:T(8,128)(2,1)S(1)}, u32[]{:S(2)}, u32[]{:S(2)}) %collective-permute-start.21) | collective-permute-done | bytes 262176 | tf_op jit(solution)/shard_map/ppermute | solution.py:316
  172.0 5.1 %collective-permute-done.23.refs_3_ = bf16[512,256]{1,0:T(8,128)(2,1)S(1)} collective-permute-done((bf16[512,256]{1,0:T(8,128)(2,1)S(1)}, bf16[512,256]{1,0:T(8,128)(2,1)S(1)}, u32[]{:S(2)}, u32[]{:S(2)}) %collective-permute-start.23) | collective-permute-done | bytes 262176 | tf_op jit(solution)/shard_map/ppermute | solution.py:317
  177.1 3.5 %expel.3 = (f32[4,2,32,640]{3,2,1,0:T(8,128)S(1)}, bf16[4,2,32,640]{3,2,1,0:T(8,128)(2,1)}) custom-call(s32[3]{0:T(128)S(1)} %pad_add_fusion.here_ref.place_ref, bf16[512,256]{1,0:T(8,128)(2,1)S(1)} %constant_dynamic-update-slice_fusion.refs_0_, bf16[512,256]{1,0:T(8,128)(2,1)S(1)} %collective-permute-done.20.refs_1_, ...), custom_call_target="tpu_custom_call" | custom-call | flops 671088640 | bytes 1310720 | tf_op jit(solution)/shard_map/expel/pallas_call | solution.py:299
  181.5 1.8 collective-permute-done.29
  183.3 1.1 convert_add_fusion
  185.1 5.7 %collective-permute-done.30 = bf16[4,32,640]{2,1,0:T(8,128)(2,1)S(1)} collective-permute-done((bf16[4,32,640]{2,1,0:T(8,128)(2,1)S(1)}, bf16[4,32,640]{2,1,0:T(8,128)(2,1)S(1)}, u32[]{:S(2)}, u32[]{:S(2)}) %collective-permute-start.30) | collective-permute-done | bytes 163872 | tf_op jit(solution)/shard_map/ppermute | solution.py:23
  191.1 1.9 collective-permute-start.31
  193.0 9.7 %collective-permute-done.31 = bf16[128,640]{1,0:T(8,128)(2,1)S(1)} collective-permute-done((bf16[128,640]{1,0:T(8,128)(2,1)S(1)}, bf16[128,640]{1,0:T(8,128)(2,1)S(1)}, u32[]{:S(2)}, u32[]{:S(2)}) %collective-permute-start.31) | collective-permute-done | bytes 163872 | tf_op jit(solution)/shard_map/ppermute | solution.py:504
  (85 shorter events, 19.5 us)
Async XLA Ops:
  0.0 1.1 copy-start
  1.1 13.7 %collective-permute-start = (bf16[32,2560]{1,0:T(8,128)(2,1)S(1)}, bf16[32,2560]{1,0:T(8,128)(2,1)S(1)}, u32[]{:S(2)}, u32[]{:S(2)}) collective-permute-start(bf16[32,2560]{1,0:T(8,128)(2,1)S(1)} %constant_dynamic-slice_fusion), channel_id=1, source_target_pairs={{0,8},{8,16},{16,24},{24,0},{1,9},{9,17},{17,25},{25,1},{2,10},{10... | collective-permute-start | bytes 491528 | tf_op jit(solution)/shard_map/ppermute | solution.py:322
  2.7 12.1 %collective-permute-start.1 = (bf16[32,2560]{1,0:T(8,128)(2,1)S(1)}, bf16[32,2560]{1,0:T(8,128)(2,1)S(1)}, u32[]{:S(2)}, u32[]{:S(2)}) collective-permute-start(bf16[32,2560]{1,0:T(8,128)(2,1)S(1)} %constant_dynamic-slice_fusion), channel_id=1, source_target_pairs={{8,0},{16,8},{24,16},{0,24},{9,1},{17,9},{25,17},{1,25},{10,2},{18... | collective-permute-start | bytes 491528 | tf_op jit(solution)/shard_map/ppermute | solution.py:323
  5.0 14.5 %collective-permute-start.2 = (bf16[32,2560]{1,0:T(8,128)(2,1)S(1)}, bf16[32,2560]{1,0:T(8,128)(2,1)S(1)}, u32[]{:S(2)}, u32[]{:S(2)}) collective-permute-start(bf16[32,2560]{1,0:T(8,128)(2,1)S(1)} %constant_dynamic-slice_fusion), channel_id=1, source_target_pairs={{0,16},{8,24},{16,0},{24,8},{1,17},{9,25},{17,1},{25,9},{2,18},{10... | collective-permute-start | bytes 491528 | tf_op jit(solution)/shard_map/ppermute | solution.py:23
  7.2 7.6 %collective-permute-start.3 = (bf16[16,1280]{1,0:T(8,128)(2,1)S(1)}, bf16[16,1280]{1,0:T(8,128)(2,1)S(1)}, u32[]{:S(2)}, u32[]{:S(2)}) collective-permute-start(bf16[16,1280]{1,0:T(8,128)(2,1)S(1)} %pad_maximum_fusion.4), channel_id=1, source_target_pairs={{1,0},{2,1},{3,2},{4,3},{5,4},{6,5},{7,6},{8,7},{9,8},{10,9},{11,1... | collective-permute-start | bytes 122888 | tf_op jit(solution)/shard_map/ppermute | solution.py:365
  19.5 6.9 %copy-start.9 = (bf16[768,192]{0,1:T(8,128)(2,1)S(1)}, bf16[768,192]{0,1:T(8,128)(2,1)}, u32[]{:S(2)}) copy-start(bf16[768,192]{0,1:T(8,128)(2,1)} %param.20) | copy-start | bytes 884740
  19.5 52.8 %all-to-all-start = ((bf16[8,160,384]{2,1,0:T(8,128)(2,1)}), bf16[8,160,384]{2,1,0:T(8,128)(2,1)}, u32[]{:S(2)}, u32[]{:S(2)}) async-start(bf16[8,160,384]{2,1,0:T(8,128)(2,1)} %get-tuple-element.45), calls=%async_computation | async-start | bytes 1966080 | tf_op jit(solution)/shard_map/all_to_all | solution.py:379
  23.9 13.2 %copy-start.2 = (bf16[128,2560]{1,0:T(8,128)(2,1)}, bf16[128,2560]{1,0:T(8,128)(2,1)S(1)}, u32[]{:S(2)}) copy-start(bf16[128,2560]{1,0:T(8,128)(2,1)S(1)} %pad_maximum_fusion.1.refs_0_) | copy-start | bytes 1966084
  23.9 27.2 %collective-permute-start.7 = (bf16[128,2560]{1,0:T(8,128)(2,1)S(1)}, bf16[128,2560]{1,0:T(8,128)(2,1)S(1)}, u32[]{:S(2)}, u32[]{:S(2)}) collective-permute-start(bf16[128,2560]{1,0:T(8,128)(2,1)S(1)} %pad_maximum_fusion.1.refs_0_), channel_id=1, source_target_pairs={{0,4},{4,0},{1,5},{5,1},{2,6},{6,2},{3,7},{7,3},{8,12},{12,8},{9,1... | collective-permute-start | bytes 1966088 | tf_op jit(solution)/shard_map/ppermute | solution.py:23
  25.9 25.3 %collective-permute-start.8 = (bf16[128,2560]{1,0:T(8,128)(2,1)S(1)}, bf16[128,2560]{1,0:T(8,128)(2,1)}, u32[]{:S(2)}, u32[]{:S(2)}) collective-permute-start(bf16[128,2560]{1,0:T(8,128)(2,1)S(1)} %pad_maximum_fusion.1.refs_0_), channel_id=1, source_target_pairs={{0,2},{1,3},{2,0},{3,1},{4,6},{5,7},{6,4},{7,5},{8,10},{9,11},{10,... | collective-permute-start | bytes 1966088 | tf_op jit(solution)/shard_map/ppermute | solution.py:23
  28.6 27.0 %copy-start.1 = (bf16[2048,320]{0,1:T(8,128)(2,1)S(1)}, bf16[2048,320]{0,1:T(8,128)(2,1)}, u32[]{:S(2)}) copy-start(bf16[2048,320]{0,1:T(8,128)(2,1)} %param.17) | copy-start | bytes 3932164
  38.0 4.2 %collective-permute-start.6 = (bf16[64,384]{1,0:T(8,128)(2,1)S(1)}, bf16[64,384]{1,0:T(8,128)(2,1)S(1)}, u32[]{:S(2)}, u32[]{:S(2)}) collective-permute-start(bf16[64,384]{1,0:T(8,128)(2,1)S(1)} %get-tuple-element.60), channel_id=1, source_target_pairs={{0,3},{1,2},{2,1},{3,0},{4,7},{5,6},{6,5},{7,4},{8,11},{9,10},{10,... | collective-permute-start | bytes 147464 | tf_op jit(solution)/shard_map/ppermute | solution.py:23
  38.3 5.8 %collective-permute-start.5 = (bf16[64,384]{1,0:T(8,128)(2,1)S(1)}, bf16[64,384]{1,0:T(8,128)(2,1)S(1)}, u32[]{:S(2)}, u32[]{:S(2)}) collective-permute-start(bf16[64,384]{1,0:T(8,128)(2,1)S(1)} %get-tuple-element.61), channel_id=1, source_target_pairs={{0,2},{1,3},{2,0},{3,1},{4,6},{5,7},{6,4},{7,5},{8,10},{9,11},{10,... | collective-permute-start | bytes 147464 | tf_op jit(solution)/shard_map/ppermute | solution.py:23
  39.6 4.5 %collective-permute-start.4 = (bf16[64,384]{1,0:T(8,128)(2,1)S(1)}, bf16[64,384]{1,0:T(8,128)(2,1)S(1)}, u32[]{:S(2)}, u32[]{:S(2)}) collective-permute-start(bf16[64,384]{1,0:T(8,128)(2,1)S(1)} %get-tuple-element.62), channel_id=1, source_target_pairs={{0,1},{1,0},{2,3},{3,2},{4,5},{5,4},{6,7},{7,6},{8,9},{9,8},{10,11... | collective-permute-start | bytes 147464 | tf_op jit(solution)/shard_map/ppermute | solution.py:23
  51.1 3.8 %copy-start.6 = (bf16[128,2560]{1,0:T(8,128)(2,1)}, bf16[128,2560]{1,0:T(8,128)(2,1)S(1)}, u32[]{:S(2)}) copy-start(bf16[128,2560]{1,0:T(8,128)(2,1)S(1)} %collective-permute-done.7.refs_1_) | copy-start | bytes 1966084
  51.1 9.8 %collective-permute-start.15 = (bf16[256,384]{1,0:T(8,128)(2,1)S(1)}, bf16[256,384]{1,0:T(8,128)(2,1)}, u32[]{:S(2)}, u32[]{:S(2)}) collective-permute-start(bf16[256,384]{1,0:T(8,128)(2,1)S(1)} %pad_maximum_fusion.2), channel_id=1, source_target_pairs={{0,8},{8,16},{16,24},{24,0},{1,9},{9,17},{17,25},{25,1},{2,10},{10... | collective-permute-start | bytes 589832 | tf_op jit(solution)/shard_map/ppermute | solution.py:322
  52.6 10.5 %collective-permute-start.16 = (bf16[256,384]{1,0:T(8,128)(2,1)S(1)}, bf16[256,384]{1,0:T(8,128)(2,1)S(1)}, u32[]{:S(2)}, u32[]{:S(2)}) collective-permute-start(bf16[256,384]{1,0:T(8,128)(2,1)S(1)} %pad_maximum_fusion.2), channel_id=1, source_target_pairs={{8,0},{16,8},{24,16},{0,24},{9,1},{17,9},{25,17},{1,25},{10,2},{18... | collective-permute-start | bytes 589832 | tf_op jit(solution)/shard_map/ppermute | solution.py:323
  55.0 16.6 %collective-permute-start.17 = (bf16[256,384]{1,0:T(8,128)(2,1)S(1)}, bf16[256,384]{1,0:T(8,128)(2,1)S(1)}, u32[]{:S(2)}, u32[]{:S(2)}) collective-permute-start(bf16[256,384]{1,0:T(8,128)(2,1)S(1)} %pad_maximum_fusion.2), channel_id=1, source_target_pairs={{0,16},{8,24},{16,0},{24,8},{1,17},{9,25},{17,1},{25,9},{2,18},{10... | collective-permute-start | bytes 589832 | tf_op jit(solution)/shard_map/ppermute | solution.py:23
  55.5 38.4 %collective-permute-start.10 = (bf16[320,2048]{1,0:T(8,128)(2,1)S(1)}, bf16[320,2048]{1,0:T(8,128)(2,1)S(1)}, u32[]{:S(2)}, u32[]{:S(2)}) collective-permute-start(bf16[320,2048]{1,0:T(8,128)(2,1)S(1)} %bitcast.58), channel_id=1, source_target_pairs={{0,4},{4,0},{1,5},{5,1},{2,6},{6,2},{3,7},{7,3},{8,12},{12,8},{9,1... | collective-permute-start | bytes 3932168 | tf_op jit(solution)/shard_map/ppermute | solution.py:23
  72.3 6.9 %copy-start.11 = (s32[1,1,4,1]{2,3,1,0:T(1,128)S(1)}, s32[1,1,4,1]{2,3,1,0:T(1,128)}, u32[]{:S(2)}) copy-start(s32[1,1,4,1]{2,3,1,0:T(1,128)} %constant.475.clone) | copy-start | bytes 52
  72.3 7.0 %copy-start.10 = (s32[2,4,64]{2,1,0:T(4,128)S(1)}, s32[2,4,64]{2,1,0:T(4,128)}, u32[]{:S(2)}) copy-start(s32[2,4,64]{2,1,0:T(4,128)} %constant.478) | copy-start | bytes 6148
  72.3 43.4 %all-to-all-start.1 = ((bf16[8,160,384]{2,1,0:T(8,128)(2,1)}), bf16[8,160,384]{2,1,0:T(8,128)(2,1)}, u32[]{:S(2)}, u32[]{:S(2)}) async-start(bf16[8,160,384]{2,1,0:T(8,128)(2,1)} %get-tuple-element.48), calls=%async_computation.1 | async-start | bytes 1966080 | tf_op jit(solution)/shard_map/all_to_all | solution.py:379
  76.9 17.0 %collective-permute-start.9 = (bf16[128,2560]{1,0:T(8,128)(2,1)}, bf16[128,2560]{1,0:T(8,128)(2,1)}, u32[]{:S(2)}, u32[]{:S(2)}) collective-permute-start(bf16[128,2560]{1,0:T(8,128)(2,1)} %copy-done.6), channel_id=1, source_target_pairs={{0,2},{1,3},{2,0},{3,1},{4,6},{5,7},{6,4},{7,5},{8,10},{9,11},{10,... | collective-permute-start | bytes 1966088 | tf_op jit(solution)/shard_map/ppermute | solution.py:23
  78.1 34.8 %collective-permute-start.18 = (bf16[1024,384]{1,0:T(8,128)(2,1)}, bf16[1024,384]{1,0:T(8,128)(2,1)}, u32[]{:S(2)}, u32[]{:S(2)}) collective-permute-start(bf16[1024,384]{1,0:T(8,128)(2,1)} %constant_dynamic-update-slice_fusion.4), channel_id=1, source_target_pairs={{0,4},{4,0},{1,5},{5,1},{2,6},{6,2},{3,7},{7,3},{8,12},{12,8},{9,1... | collective-permute-start | bytes 2359304 | tf_op jit(solution)/shard_map/ppermute | solution.py:23
  93.9 21.8 %collective-permute-start.11 = (bf16[128,2560]{1,0:T(8,128)(2,1)}, bf16[128,2560]{1,0:T(8,128)(2,1)}, u32[]{:S(2)}, u32[]{:S(2)}) collective-permute-start(bf16[128,2560]{1,0:T(8,128)(2,1)} %copy-done.2), channel_id=1, source_target_pairs={{0,1},{1,0},{2,3},{3,2},{4,5},{5,4},{6,7},{7,6},{8,9},{9,8},{10,11... | collective-permute-start | bytes 1966088 | tf_op jit(solution)/shard_map/ppermute | solution.py:23
  93.9 21.8 %collective-permute-start.12 = (bf16[128,2560]{1,0:T(8,128)(2,1)}, bf16[128,2560]{1,0:T(8,128)(2,1)}, u32[]{:S(2)}, u32[]{:S(2)}) collective-permute-start(bf16[128,2560]{1,0:T(8,128)(2,1)} %copy-done.6), channel_id=1, source_target_pairs={{0,1},{1,0},{2,3},{3,2},{4,5},{5,4},{6,7},{7,6},{8,9},{9,8},{10,11... | collective-permute-start | bytes 1966088 | tf_op jit(solution)/shard_map/ppermute | solution.py:23
  94.4 21.3 %collective-permute-start.13 = (bf16[128,2560]{1,0:T(8,128)(2,1)}, bf16[128,2560]{1,0:T(8,128)(2,1)}, u32[]{:S(2)}, u32[]{:S(2)}) collective-permute-start(bf16[128,2560]{1,0:T(8,128)(2,1)} %collective-permute-done.8.refs_2_), channel_id=1, source_target_pairs={{0,1},{1,0},{2,3},{3,2},{4,5},{5,4},{6,7},{7,6},{8,9},{9,8},{10,11... | collective-permute-start | bytes 1966088 | tf_op jit(solution)/shard_map/ppermute | solution.py:23
  94.5 21.3 %collective-permute-start.14 = (bf16[128,2560]{1,0:T(8,128)(2,1)}, bf16[128,2560]{1,0:T(8,128)(2,1)}, u32[]{:S(2)}, u32[]{:S(2)}) collective-permute-start(bf16[128,2560]{1,0:T(8,128)(2,1)} %collective-permute-done.9.refs_3_), channel_id=1, source_target_pairs={{0,1},{1,0},{2,3},{3,2},{4,5},{5,4},{6,7},{7,6},{8,9},{9,8},{10,11... | collective-permute-start | bytes 1966088 | tf_op jit(solution)/shard_map/ppermute | solution.py:23
  115.8 1.1 copy-start.3
  116.9 1.1 copy-start.7
  118.0 5.5 %copy-start.4 = (bf16[2,1024,384]{2,1,0:T(8,128)(2,1)S(1)}, bf16[2,1024,384]{2,1,0:T(8,128)(2,1)}, u32[]{:S(2)}) copy-start(bf16[2,1024,384]{2,1,0:T(8,128)(2,1)} %pad_maximum_fusion) | copy-start | bytes 4718596
  118.0 5.5 %copy-start.8 = (s32[1024,1]{1,0:T(8,128)S(1)}, s32[1024,1]{1,0:T(8,128)}, u32[]{:S(2)}) copy-start(s32[1024,1]{1,0:T(8,128)} %add.630.refs_3_) | copy-start | bytes 12292
  131.8 5.1 %collective-permute-start.24 = (bf16[512,128]{1,0:T(8,128)(2,1)S(1)}, bf16[512,128]{1,0:T(8,128)(2,1)S(1)}, u32[]{:S(2)}, u32[]{:S(2)}) collective-permute-start(bf16[512,128]{1,0:T(8,128)(2,1)S(1)} %get-tuple-element.54), channel_id=1, source_target_pairs={{0,4},{4,0},{1,5},{5,1},{2,6},{6,2},{3,7},{7,3},{8,12},{12,8},{9,1... | collective-permute-start | bytes 393224 | tf_op jit(solution)/shard_map/ppermute | solution.py:23
  132.2 6.3 %collective-permute-start.19 = (bf16[512,128]{1,0:T(8,128)(2,1)S(1)}, bf16[512,128]{1,0:T(8,128)(2,1)S(1)}, u32[]{:S(2)}, u32[]{:S(2)}) collective-permute-start(bf16[512,128]{1,0:T(8,128)(2,1)S(1)} %get-tuple-element.51), channel_id=1, source_target_pairs={{0,4},{4,0},{1,5},{5,1},{2,6},{6,2},{3,7},{7,3},{8,12},{12,8},{9,1... | collective-permute-start | bytes 393224 | tf_op jit(solution)/shard_map/ppermute | solution.py:23
  137.0 17.1 %collective-permute-start.27 = (bf16[512,256]{1,0:T(8,128)(2,1)S(1)}, bf16[512,256]{1,0:T(8,128)(2,1)S(1)}, u32[]{:S(2)}, u32[]{:S(2)}) collective-permute-start(bf16[512,256]{1,0:T(8,128)(2,1)S(1)} %constant_dynamic-update-slice_fusion.2.refs_0_), channel_id=1, source_target_pairs={{0,16},{8,24},{16,0},{24,8},{1,17},{9,25},{17,1},{25,9},{2,18},{10... | collective-permute-start | bytes 786440 | tf_op jit(solution)/shard_map/ppermute | solution.py:23
  138.5 21.5 %collective-permute-start.22 = (bf16[512,256]{1,0:T(8,128)(2,1)S(1)}, bf16[512,256]{1,0:T(8,128)(2,1)S(1)}, u32[]{:S(2)}, u32[]{:S(2)}) collective-permute-start(bf16[512,256]{1,0:T(8,128)(2,1)S(1)} %constant_dynamic-update-slice_fusion.refs_0_), channel_id=1, source_target_pairs={{0,16},{8,24},{16,0},{24,8},{1,17},{9,25},{17,1},{25,9},{2,18},{10... | collective-permute-start | bytes 786440 | tf_op jit(solution)/shard_map/ppermute | solution.py:23
  140.1 21.2 %collective-permute-start.25 = (bf16[512,256]{1,0:T(8,128)(2,1)S(1)}, bf16[512,256]{1,0:T(8,128)(2,1)S(1)}, u32[]{:S(2)}, u32[]{:S(2)}) collective-permute-start(bf16[512,256]{1,0:T(8,128)(2,1)S(1)} %constant_dynamic-update-slice_fusion.2.refs_0_), channel_id=1, source_target_pairs={{0,8},{8,16},{16,24},{1,9},{9,17},{17,25},{2,10},{10,18},{18,26},{... | collective-permute-start | bytes 786440 | tf_op jit(solution)/shard_map/ppermute | solution.py:315
  142.6 20.2 %collective-permute-start.26 = (bf16[512,256]{1,0:T(8,128)(2,1)S(1)}, bf16[512,256]{1,0:T(8,128)(2,1)S(1)}, u32[]{:S(2)}, u32[]{:S(2)}) collective-permute-start(bf16[512,256]{1,0:T(8,128)(2,1)S(1)} %constant_dynamic-update-slice_fusion.2.refs_0_), channel_id=1, source_target_pairs={{8,0},{16,8},{24,16},{9,1},{17,9},{25,17},{10,2},{18,10},{26,18},{... | collective-permute-start | bytes 786440 | tf_op jit(solution)/shard_map/ppermute | solution.py:316
  154.1 12.3 %collective-permute-start.28 = (bf16[512,256]{1,0:T(8,128)(2,1)S(1)}, bf16[512,256]{1,0:T(8,128)(2,1)S(1)}, u32[]{:S(2)}, u32[]{:S(2)}) collective-permute-start(bf16[512,256]{1,0:T(8,128)(2,1)S(1)} %collective-permute-done.27.refs_4_), channel_id=1, source_target_pairs={{8,0},{16,24},{9,1},{17,25},{10,2},{18,26},{11,3},{19,27},{12,4},{... | collective-permute-start | bytes 786440 | tf_op jit(solution)/shard_map/ppermute | solution.py:317
  155.4 13.0 %collective-permute-start.20 = (bf16[512,256]{1,0:T(8,128)(2,1)S(1)}, bf16[512,256]{1,0:T(8,128)(2,1)S(1)}, u32[]{:S(2)}, u32[]{:S(2)}) collective-permute-start(bf16[512,256]{1,0:T(8,128)(2,1)S(1)} %constant_dynamic-update-slice_fusion.refs_0_), channel_id=1, source_target_pairs={{0,8},{8,16},{16,24},{1,9},{9,17},{17,25},{2,10},{10,18},{18,26},{... | collective-permute-start | bytes 786440 | tf_op jit(solution)/shard_map/ppermute | solution.py:315
  160.0 12.0 %collective-permute-start.21 = (bf16[512,256]{1,0:T(8,128)(2,1)S(1)}, bf16[512,256]{1,0:T(8,128)(2,1)S(1)}, u32[]{:S(2)}, u32[]{:S(2)}) collective-permute-start(bf16[512,256]{1,0:T(8,128)(2,1)S(1)} %constant_dynamic-update-slice_fusion.refs_0_), channel_id=1, source_target_pairs={{8,0},{16,8},{24,16},{9,1},{17,9},{25,17},{10,2},{18,10},{26,18},{... | collective-permute-start | bytes 786440 | tf_op jit(solution)/shard_map/ppermute | solution.py:316
  161.3 15.8 %collective-permute-start.23 = (bf16[512,256]{1,0:T(8,128)(2,1)S(1)}, bf16[512,256]{1,0:T(8,128)(2,1)S(1)}, u32[]{:S(2)}, u32[]{:S(2)}) collective-permute-start(bf16[512,256]{1,0:T(8,128)(2,1)S(1)} %collective-permute-done.22.refs_4_), channel_id=1, source_target_pairs={{8,0},{16,24},{9,1},{17,25},{10,2},{18,26},{11,3},{19,27},{12,4},{... | collective-permute-start | bytes 786440 | tf_op jit(solution)/shard_map/ppermute | solution.py:317
  180.6 0.9 copy-start.5
  181.5 1.8 collective-permute-start.29
  184.5 6.3 %collective-permute-start.30 = (bf16[4,32,640]{2,1,0:T(8,128)(2,1)S(1)}, bf16[4,32,640]{2,1,0:T(8,128)(2,1)S(1)}, u32[]{:S(2)}, u32[]{:S(2)}) collective-permute-start(bf16[4,32,640]{2,1,0:T(8,128)(2,1)S(1)} %fusion.1), channel_id=1, source_target_pairs={{0,2},{1,3},{2,0},{3,1},{4,6},{5,7},{6,4},{7,5},{8,10},{9,11},{10,... | collective-permute-start | bytes 491528 | tf_op jit(solution)/shard_map/ppermute | solution.py:23
  191.1 11.6 %collective-permute-start.31 = (bf16[128,640]{1,0:T(8,128)(2,1)S(1)}, bf16[128,640]{1,0:T(8,128)(2,1)S(1)}, u32[]{:S(2)}, u32[]{:S(2)}) collective-permute-start(bf16[128,640]{1,0:T(8,128)(2,1)S(1)} %pad_maximum_fusion.3), channel_id=1, source_target_pairs={{0,0},{1,8},{2,16},{3,24},{4,4},{5,12},{6,20},{7,28},{8,1},{9,9},{... | collective-permute-start | bytes 491528 | tf_op jit(solution)/shard_map/ppermute | solution.py:504

commit v8 on v7

--- a/solution.py
+++ b/solution.py
@@ -367,7 +367,8 @@
     )
 
     if fast:
-        out_weights = [output_weight.T]
+        turned, edge = lax.optimization_barrier((output_weight.T, edge))
+        out_weights = [turned, swap(turned, "inner", 1)]
     else:
         out_weights = lax.all_gather(output_weight, "inner", axis=1, tiled=True)
 
@@ -397,8 +398,6 @@
         weight_first = exchange(begin)
         near = jnp.concatenate([mine, before, after, far], axis=0)
         beside = swap(near, "inner", 1)
-        beside, turned = lax.optimization_barrier((beside, out_weights[0]))
-        out_weights.append(swap(turned, "inner", 1))
         pieces = [near, beside, swap(near, "head", 2)]
         steps = [(line, side, turn) for turn in (0, 2) for side in (0, 1) for line in range(4)]
         steps = steps + [(a, b, k ^ 1) for a, b, k in steps]
@@ -440,13 +439,12 @@
         packed = packed.reshape(heads_axis * blocks, -1)
         bound = ids
     if fast:
-        packed, pieces = lax.optimization_barrier((packed, pieces))
+        packed, out_weights[1] = lax.optimization_barrier((packed, out_weights[1]))
+    packed = gather_line(packed, "outer", 0)
+    if fast:
+        begin, packed, pieces = lax.optimization_barrier((sent[1], packed, pieces))
         pieces.append(swap(pieces[1], "head", 2))
-        pieces, out_weights[1] = lax.optimization_barrier((pieces, out_weights[1]))
         partners = [swap(piece, "head", 1) for piece in pieces]
-    packed = gather_line(packed, "outer", 0)
-    if fast:
-        begin, packed = lax.optimization_barrier((sent[1], packed))
         queries = [project([*pieces, *partners], [weight_first, exchange(begin)])]
     packed = gather_pair(packed, "inner").reshape(devices * blocks, -1)
     bound = (STRIDE * bound + BLK - 1).transpose(1, 0, 2, 3).reshape(-1)

time: 204 us -> 195 us (0.956)
  local copies, waits for them, and re-layouts: 15.7 us -> 7.91 us
  waiting for transfers between devices: 101 us -> 97.4 us
    ppermute x20, waiting for transfers between devices: 75.2 us -> 64.8 us  [swap(): lax.ppermute(block, axis, [(i, i ^ bit) for i in range(lax.axis_size(axis...]
    ppermute x2, waiting for transfers between devices: 0.54 us -> 6.24 us  [ring_pieces(): after = lax.ppermute(block, axis, [((i + 1) % 4, i) for i in range(4)])]
    dynamic_update_slice x4, local copies, waits for them, and re-layouts: 3.77 us -> 0.13 us  [gather_line(): out = lax.dynamic_update_slice_in_dim(out, piece, place * size, dim)]
    unnamed x28 -> x30, local copies, waits for them, and re-layouts: 5.78 us -> 3.26 us
    ppermute x20, starting transfers between devices: 14.8 us -> 17.3 us  [swap(): lax.ppermute(block, axis, [(i, i ^ bit) for i in range(lax.axis_size(axis...]
  transfers between devices with their start and end apart: 34 -> 34, of which waited for: 17 -> 16; matrix products, arithmetic and copies ran while one was open for 7% -> 4% of each run, Pallas kernels for 8% -> 8%
where the time goes in v8:
time: 195 us
  waiting for transfers between devices  97.4 us (50%)
  starting transfers between devices  49.8 us (26%)
  Pallas kernels  33.9 us (17%)
  local copies, waits for them, and re-layouts  7.91 us (4%)
  other arithmetic  4.29 us (2%)
    ppermute x20, waiting for transfers between devices, swap(): lax.ppermute(block, axis, [(i, i ^ bit) for i in range(lax.axis_size(axis...  64.8 us
    ppermute x20, starting transfers between devices, swap(): lax.ppermute(block, axis, [(i, i ^ bit) for i in range(lax.axis_size(axis...  17.3 us
    ppermute x1, waiting for transfers between devices, shards(): return lax.ppermute(result, ('outer', 'inner', 'head'), route)  9.66 us
    ppermute x2, waiting for transfers between devices, line_pieces(): passed = lax.ppermute(far, axis, [(1, 0), (2, 3)])  9.37 us
    all_to_all x2, starting transfers between devices, exchange(): lax.all_to_all(block, seq_axes, split_axis=0, concat_axis=0, tiled=True)  8.71 us
    pallas_call x1, Pallas kernels, compress(): pl.pallas_call(compress_kernel, out_shape=jax.ShapeDtypeStruct((G, blocks...  8.46 us
    pallas_call x2, Pallas kernels, attend(): pl.pallas_call(kernel, out_shape=(shape,) * outputs, in_specs=[pl.BlockSp...  8.37 us
    ppermute x2, starting transfers between devices, line_pieces(): up = lax.ppermute(block, axis, [(i, i + 1) for i in range(3)])  6.84 us
  transfers between devices with their start and end apart: 34, of which 16 were waited for; matrix products, arithmetic and copies ran while one was open for 4% of the time, Pallas kernels for 8%

profile of v8, /device:TPU:2, one launch (start us, length us, event | category | flops | bytes accessed | tf_op | source)
XLA Modules:
  0.0 194.6 jit_solution(8577551217219132393)
XLA Ops:
  1.5 1.9 collective-permute-start.3
  3.5 1.6 collective-permute-start
  5.1 2.2 %collective-permute-start.1 = (bf16[32,2560]{1,0:T(8,128)(2,1)S(1)}, bf16[32,2560]{1,0:T(8,128)(2,1)S(1)}, u32[]{:S(2)}, u32[]{:S(2)}) collective-permute-start(bf16[32,2560]{1,0:T(8,128)(2,1)S(1)} %constant_dynamic-slice_fusion), channel_id=1, source_target_pairs={{8,0},{16,8},{24,16},{0,24},{9,1},{17,9},{25,17},{1,25},{10,2},{18... | collective-permute-start | bytes 491528 | tf_op jit(solution)/shard_map/ppermute | solution.py:323
  8.2 1.5 collective-permute-start.7
  9.7 5.7 %cut.1 = (bf16[8,160,384]{2,1,0:T(8,128)(2,1)}, bf16[8,160,384]{2,1,0:T(8,128)(2,1)}) custom-call(bf16[320,3072]{1,0:T(8,128)(2,1)} %in_ref.1), custom_call_target="tpu_custom_call" | custom-call | tf_op jit(solution)/shard_map/cut/pallas_call | solution.py:129
  15.4 7.2 %collective-permute-done.2 = bf16[32,2560]{1,0:T(8,128)(2,1)S(1)} collective-permute-done((bf16[32,2560]{1,0:T(8,128)(2,1)S(1)}, bf16[32,2560]{1,0:T(8,128)(2,1)S(1)}, u32[]{:S(2)}, u32[]{:S(2)}) %collective-permute-start.2) | collective-permute-done | bytes 163872 | tf_op jit(solution)/shard_map/ppermute | solution.py:23
  23.2 3.9 %all-to-all-start = ((bf16[8,160,384]{2,1,0:T(8,128)(2,1)}), bf16[8,160,384]{2,1,0:T(8,128)(2,1)S(1)}, u32[]{:S(2)}, u32[]{:S(2)}) async-start(bf16[8,160,384]{2,1,0:T(8,128)(2,1)} %get-tuple-element.39), calls=%async_computation | async-start | bytes 1966080 | tf_op jit(solution)/shard_map/all_to_all | solution.py:380
  27.1 0.9 copy.15.key_reduce
  29.2 8.5 %compress.1 = bf16[4,64,384]{2,1,0:T(8,128)(2,1)} custom-call(bf16[1024,768]{1,0:T(8,128)(2,1)} %raw_keys.1, bf16[1024,512]{1,0:T(8,128)(2,1)} %raw_values.1, bf16[16,768]{1,0:T(8,128)(2,1)} %slice.20.edge_keys, bf16[16,512]{1,0:T(8,128)(2,1)} %slice.21.edge_values, bf16[192,768]{1,0:T(8,128)(2,1)} %key_expand.1, f32[32,768]{1,0:T(8,128)} %key_mix.1, ...), custom_call_target="tpu_custom_call" | custom-call | flops 2013265920 | bytes 1572864 | tf_op jit(solution)/shard_map/compress/pallas_call | solution.py:105
  38.6 1.4 collective-permute-start.5
  41.4 2.0 %collective-permute-start.11 = (bf16[128,2560]{1,0:T(8,128)(2,1)}, bf16[128,2560]{1,0:T(8,128)(2,1)}, u32[]{:S(2)}, u32[]{:S(2)}) collective-permute-start(bf16[128,2560]{1,0:T(8,128)(2,1)} %pad_maximum_fusion.1.refs_0_), channel_id=1, source_target_pairs={{0,4},{4,0},{1,5},{5,1},{2,6},{6,2},{3,7},{7,3},{8,12},{12,8},{9,1... | collective-permute-start | bytes 1966088 | tf_op jit(solution)/shard_map/ppermute | solution.py:23
  44.0 2.0 %collective-permute-done.7.refs_6_ = bf16[320,2048]{1,0:T(8,128)(2,1)S(1)} collective-permute-done((bf16[320,2048]{1,0:T(8,128)(2,1)}, bf16[320,2048]{1,0:T(8,128)(2,1)S(1)}, u32[]{:S(2)}, u32[]{:S(2)}) %collective-permute-start.7) | collective-permute-done | bytes 1310752 | tf_op jit(solution)/shard_map/ppermute | solution.py:23
  46.0 2.0 %collective-permute-start.8 = (bf16[256,384]{1,0:T(8,128)(2,1)S(1)}, bf16[256,384]{1,0:T(8,128)(2,1)S(1)}, u32[]{:S(2)}, u32[]{:S(2)}) collective-permute-start(bf16[256,384]{1,0:T(8,128)(2,1)S(1)} %pad_maximum_fusion.2), channel_id=1, source_target_pairs={{0,8},{8,16},{16,24},{24,0},{1,9},{9,17},{17,25},{25,1},{2,10},{10... | collective-permute-start | bytes 589832 | tf_op jit(solution)/shard_map/ppermute | solution.py:322
  47.9 1.8 collective-permute-start.9
  49.8 1.2 collective-permute-start.10
  51.1 2.6 %collective-permute-done.8 = bf16[256,384]{1,0:T(8,128)(2,1)S(1)} collective-permute-done((bf16[256,384]{1,0:T(8,128)(2,1)S(1)}, bf16[256,384]{1,0:T(8,128)(2,1)S(1)}, u32[]{:S(2)}, u32[]{:S(2)}) %collective-permute-start.8) | collective-permute-done | bytes 196640 | tf_op jit(solution)/shard_map/ppermute | solution.py:322
  53.7 6.2 %collective-permute-done.9 = bf16[256,384]{1,0:T(8,128)(2,1)S(1)} collective-permute-done((bf16[256,384]{1,0:T(8,128)(2,1)S(1)}, bf16[256,384]{1,0:T(8,128)(2,1)S(1)}, u32[]{:S(2)}, u32[]{:S(2)}) %collective-permute-start.9) | collective-permute-done | bytes 196640 | tf_op jit(solution)/shard_map/ppermute | solution.py:323
  59.9 8.5 %collective-permute-done.10 = bf16[256,384]{1,0:T(8,128)(2,1)S(1)} collective-permute-done((bf16[256,384]{1,0:T(8,128)(2,1)S(1)}, bf16[256,384]{1,0:T(8,128)(2,1)S(1)}, u32[]{:S(2)}, u32[]{:S(2)}) %collective-permute-start.10) | collective-permute-done | bytes 196640 | tf_op jit(solution)/shard_map/ppermute | solution.py:23
  69.4 4.9 %all-to-all-start.1 = ((bf16[8,160,384]{2,1,0:T(8,128)(2,1)}), bf16[8,160,384]{2,1,0:T(8,128)(2,1)}, u32[]{:S(2)}, u32[]{:S(2)}) async-start(bf16[8,160,384]{2,1,0:T(8,128)(2,1)} %get-tuple-element.40), calls=%async_computation.1 | async-start | bytes 1966080 | tf_op jit(solution)/shard_map/all_to_all | solution.py:380
  75.4 1.3 collective-permute-start.18
  77.5 13.5 %collective-permute-done.13.refs_3_ = bf16[128,2560]{1,0:T(8,128)(2,1)} collective-permute-done((bf16[128,2560]{1,0:T(8,128)(2,1)}, bf16[128,2560]{1,0:T(8,128)(2,1)}, u32[]{:S(2)}, u32[]{:S(2)}) %collective-permute-start.13) | collective-permute-done | bytes 655392 | tf_op jit(solution)/shard_map/ppermute | solution.py:23
  91.8 12.4 %collective-permute-done.18 = bf16[1024,384]{1,0:T(8,128)(2,1)} collective-permute-done((bf16[1024,384]{1,0:T(8,128)(2,1)}, bf16[1024,384]{1,0:T(8,128)(2,1)}, u32[]{:S(2)}, u32[]{:S(2)}) %collective-permute-start.18) | collective-permute-done | bytes 786464 | tf_op jit(solution)/shard_map/ppermute | solution.py:23
  104.2 1.5 select_bitcast_fusion.1
  105.8 1.4 pad_maximum_fusion
  107.2 6.6 %project.1.refs_0_ = bf16[1024,384]{1,0:T(8,128)(2,1)S(1)} custom-call(bf16[128,2560]{1,0:T(8,128)(2,1)} %pad_maximum_fusion.1.refs_0_, bf16[128,2560]{1,0:T(8,128)(2,1)} %collective-permute-done.11.refs_1_, bf16[128,2560]{1,0:T(8,128)(2,1)} %collective-permute-done.12.refs_2_, bf16[128,2560]{1,0:T(8,128)(2,1)} %collective-permute-done.13.refs_3_, ...), custom_call_target="tpu_custom_call" | custom-call | flops 2013265920 | bytes 5242880 | tf_op jit(solution)/shard_map/project/pallas_call | solution.py:178
  113.8 4.2 %attend.2 = (bf16[512,128]{1,0:T(8,128)(2,1)S(1)}, bf16[512,128]{1,0:T(8,128)(2,1)S(1)}) custom-call(s32[3]{0:T(128)S(1)} %pad_add_fusion.here_ref.place_ref, bf16[1024,384]{1,0:T(8,128)(2,1)S(1)} %project.1.refs_0_, bf16[2048,384]{1,0:T(8,128)(2,1)S(1)} %bitcast.61, s32[1,2048]{1,0:T(1,128)S(1)} %sub.145.refs_2_, s32[1024,1]{1,0:T(8,128)S(1)} %add.630.refs_3_), custom_call_target="tpu_custom_call" | custom-call | flops 1342177280 | bytes 1572864 | tf_op jit(solution)/shard_map/attend/pallas_call | solution.py:239
  118.0 4.2 %attend.3 = (bf16[512,128]{1,0:T(8,128)(2,1)S(1)}, bf16[512,128]{1,0:T(8,128)(2,1)S(1)}) custom-call(s32[3]{0:T(128)S(1)} %pad_add_fusion.here_ref.place_ref, bf16[1024,384]{1,0:T(8,128)(2,1)S(1)} %project.1.refs_0_, bf16[2048,384]{1,0:T(8,128)(2,1)S(1)} %bitcast.62, s32[1,2048]{1,0:T(1,128)S(1)} %sub.145.refs_2_, s32[1024,1]{1,0:T(8,128)S(1)} %add.630.refs_3_), custom_call_target="tpu_custom_call" | custom-call | flops 1342177280 | bytes 1572864 | tf_op jit(solution)/shard_map/attend/pallas_call | solution.py:239
  122.6 1.8 collective-permute-start.19
  124.4 3.5 %collective-permute-done.24 = bf16[512,128]{1,0:T(8,128)(2,1)S(1)} collective-permute-done((bf16[512,128]{1,0:T(8,128)(2,1)S(1)}, bf16[512,128]{1,0:T(8,128)(2,1)S(1)}, u32[]{:S(2)}, u32[]{:S(2)}) %collective-permute-start.24) | collective-permute-done | bytes 131104 | tf_op jit(solution)/shard_map/ppermute | solution.py:23
  127.9 3.1 %collective-permute-start.27 = (bf16[512,256]{1,0:T(8,128)(2,1)S(1)}, bf16[512,256]{1,0:T(8,128)(2,1)S(1)}, u32[]{:S(2)}, u32[]{:S(2)}) collective-permute-start(bf16[512,256]{1,0:T(8,128)(2,1)S(1)} %constant_dynamic-update-slice_fusion.2.refs_0_), channel_id=1, source_target_pairs={{0,16},{8,24},{16,0},{24,8},{1,17},{9,25},{17,1},{25,9},{2,18},{10... | collective-permute-start | bytes 786440 | tf_op jit(solution)/shard_map/ppermute | solution.py:23
  131.1 1.8 collective-permute-start.22
  132.9 2.3 %collective-permute-start.25 = (bf16[512,256]{1,0:T(8,128)(2,1)S(1)}, bf16[512,256]{1,0:T(8,128)(2,1)S(1)}, u32[]{:S(2)}, u32[]{:S(2)}) collective-permute-start(bf16[512,256]{1,0:T(8,128)(2,1)S(1)} %constant_dynamic-update-slice_fusion.2.refs_0_), channel_id=1, source_target_pairs={{0,8},{8,16},{16,24},{1,9},{9,17},{17,25},{2,10},{10,18},{18,26},{... | collective-permute-start | bytes 786440 | tf_op jit(solution)/shard_map/ppermute | solution.py:315
  135.2 1.3 collective-permute-start.26
  136.5 9.9 %collective-permute-done.27.refs_4_ = bf16[512,256]{1,0:T(8,128)(2,1)S(1)} collective-permute-done((bf16[512,256]{1,0:T(8,128)(2,1)S(1)}, bf16[512,256]{1,0:T(8,128)(2,1)S(1)}, u32[]{:S(2)}, u32[]{:S(2)}) %collective-permute-start.27) | collective-permute-done | bytes 262176 | tf_op jit(solution)/shard_map/ppermute | solution.py:23
  146.4 1.3 collective-permute-start.28
  147.7 4.6 %collective-permute-start.20 = (bf16[512,256]{1,0:T(8,128)(2,1)S(1)}, bf16[512,256]{1,0:T(8,128)(2,1)S(1)}, u32[]{:S(2)}, u32[]{:S(2)}) collective-permute-start(bf16[512,256]{1,0:T(8,128)(2,1)S(1)} %constant_dynamic-update-slice_fusion.refs_0_), channel_id=1, source_target_pairs={{0,8},{8,16},{16,24},{1,9},{9,17},{17,25},{2,10},{10,18},{18,26},{... | collective-permute-start | bytes 786440 | tf_op jit(solution)/shard_map/ppermute | solution.py:315
  152.3 1.3 collective-permute-start.21
  153.6 1.5 collective-permute-start.23
  155.1 1.1 collective-permute-done.26.refs_2_
  156.2 5.6 %collective-permute-done.28.refs_3_ = bf16[512,256]{1,0:T(8,128)(2,1)S(1)} collective-permute-done((bf16[512,256]{1,0:T(8,128)(2,1)S(1)}, bf16[512,256]{1,0:T(8,128)(2,1)S(1)}, u32[]{:S(2)}, u32[]{:S(2)}) %collective-permute-start.28) | collective-permute-done | bytes 262176 | tf_op jit(solution)/shard_map/ppermute | solution.py:317
  161.8 2.0 %expel.2.refs_7_ = f32[512,640]{1,0:T(8,128)S(1)} custom-call(s32[3]{0:T(128)S(1)} %pad_add_fusion.here_ref.place_ref, bf16[512,256]{1,0:T(8,128)(2,1)S(1)} %constant_dynamic-update-slice_fusion.2.refs_0_, bf16[512,256]{1,0:T(8,128)(2,1)S(1)} %collective-permute-done.25.refs_1_, bf16[512,256]{1,0:T(8,128)(2,1)S(1)} %collective-permute-done.26.refs_2_, ...), custom_call_target="tpu_custom_call" | custom-call | flops 671088640 | bytes 1310720 | tf_op jit(solution)/shard_map/expel/pallas_call | solution.py:299
  163.8 3.6 %collective-permute-done.21.refs_2_ = bf16[512,256]{1,0:T(8,128)(2,1)S(1)} collective-permute-done((bf16[512,256]{1,0:T(8,128)(2,1)S(1)}, bf16[512,256]{1,0:T(8,128)(2,1)S(1)}, u32[]{:S(2)}, u32[]{:S(2)}) %collective-permute-start.21) | collective-permute-done | bytes 262176 | tf_op jit(solution)/shard_map/ppermute | solution.py:316
  167.4 3.8 %collective-permute-done.23.refs_3_ = bf16[512,256]{1,0:T(8,128)(2,1)S(1)} collective-permute-done((bf16[512,256]{1,0:T(8,128)(2,1)S(1)}, bf16[512,256]{1,0:T(8,128)(2,1)S(1)}, u32[]{:S(2)}, u32[]{:S(2)}) %collective-permute-start.23) | collective-permute-done | bytes 262176 | tf_op jit(solution)/shard_map/ppermute | solution.py:317
  171.2 2.8 %expel.3 = (f32[4,2,32,640]{3,2,1,0:T(8,128)S(1)}, bf16[4,2,32,640]{3,2,1,0:T(8,128)(2,1)S(1)}) custom-call(s32[3]{0:T(128)S(1)} %pad_add_fusion.here_ref.place_ref, bf16[512,256]{1,0:T(8,128)(2,1)S(1)} %constant_dynamic-update-slice_fusion.refs_0_, bf16[512,256]{1,0:T(8,128)(2,1)S(1)} %collective-permute-done.20.refs_1_, ...), custom_call_target="tpu_custom_call" | custom-call | flops 671088640 | bytes 1310720 | tf_op jit(solution)/shard_map/expel/pallas_call | solution.py:299
  174.1 1.6 collective-permute-done.29
  175.9 6.2 %collective-permute-done.30 = bf16[4,32,640]{2,1,0:T(8,128)(2,1)S(1)} collective-permute-done((bf16[4,32,640]{2,1,0:T(8,128)(2,1)S(1)}, bf16[4,32,640]{2,1,0:T(8,128)(2,1)S(1)}, u32[]{:S(2)}, u32[]{:S(2)}) %collective-permute-start.30) | collective-permute-done | bytes 163872 | tf_op jit(solution)/shard_map/ppermute | solution.py:23
  182.4 1.9 collective-permute-start.31
  184.3 9.7 %collective-permute-done.31 = bf16[128,640]{1,0:T(8,128)(2,1)S(1)} collective-permute-done((bf16[128,640]{1,0:T(8,128)(2,1)S(1)}, bf16[128,640]{1,0:T(8,128)(2,1)S(1)}, u32[]{:S(2)}, u32[]{:S(2)}) %collective-permute-start.31) | collective-permute-done | bytes 163872 | tf_op jit(solution)/shard_map/ppermute | solution.py:502
  (87 shorter events, 11.7 us)
Async XLA Ops:
  0.0 3.5 %copy-start = (bf16[128,2560]{1,0:T(8,128)(2,1)S(1)}, bf16[128,2560]{1,0:T(8,128)(2,1)}, u32[]{:S(2)}) copy-start(bf16[128,2560]{1,0:T(8,128)(2,1)} %param.13) | copy-start | bytes 1966084
  1.5 6.6 %collective-permute-start.3 = (bf16[16,1280]{1,0:T(8,128)(2,1)S(1)}, bf16[16,1280]{1,0:T(8,128)(2,1)S(1)}, u32[]{:S(2)}, u32[]{:S(2)}) collective-permute-start(bf16[16,1280]{1,0:T(8,128)(2,1)S(1)} %pad_maximum_fusion.4), channel_id=1, source_target_pairs={{1,0},{2,1},{3,2},{4,3},{5,4},{6,5},{7,6},{8,7},{9,8},{10,9},{11,1... | collective-permute-start | bytes 122888 | tf_op jit(solution)/shard_map/ppermute | solution.py:365
  3.5 11.9 %collective-permute-start = (bf16[32,2560]{1,0:T(8,128)(2,1)S(1)}, bf16[32,2560]{1,0:T(8,128)(2,1)S(1)}, u32[]{:S(2)}, u32[]{:S(2)}) collective-permute-start(bf16[32,2560]{1,0:T(8,128)(2,1)S(1)} %constant_dynamic-slice_fusion), channel_id=1, source_target_pairs={{0,8},{8,16},{16,24},{24,0},{1,9},{9,17},{17,25},{25,1},{2,10},{10... | collective-permute-start | bytes 491528 | tf_op jit(solution)/shard_map/ppermute | solution.py:322
  5.1 10.2 %collective-permute-start.1 = (bf16[32,2560]{1,0:T(8,128)(2,1)S(1)}, bf16[32,2560]{1,0:T(8,128)(2,1)S(1)}, u32[]{:S(2)}, u32[]{:S(2)}) collective-permute-start(bf16[32,2560]{1,0:T(8,128)(2,1)S(1)} %constant_dynamic-slice_fusion), channel_id=1, source_target_pairs={{8,0},{16,8},{24,16},{0,24},{9,1},{17,9},{25,17},{1,25},{10,2},{18... | collective-permute-start | bytes 491528 | tf_op jit(solution)/shard_map/ppermute | solution.py:323
  7.4 15.2 %collective-permute-start.2 = (bf16[32,2560]{1,0:T(8,128)(2,1)S(1)}, bf16[32,2560]{1,0:T(8,128)(2,1)S(1)}, u32[]{:S(2)}, u32[]{:S(2)}) collective-permute-start(bf16[32,2560]{1,0:T(8,128)(2,1)S(1)} %constant_dynamic-slice_fusion), channel_id=1, source_target_pairs={{0,16},{8,24},{16,0},{24,8},{1,17},{9,25},{17,1},{25,9},{2,18},{10... | collective-permute-start | bytes 491528 | tf_op jit(solution)/shard_map/ppermute | solution.py:23
  8.2 37.8 %collective-permute-start.7 = (bf16[320,2048]{1,0:T(8,128)(2,1)}, bf16[320,2048]{1,0:T(8,128)(2,1)S(1)}, u32[]{:S(2)}, u32[]{:S(2)}) collective-permute-start(bf16[320,2048]{1,0:T(8,128)(2,1)} %bitcast.58), channel_id=1, source_target_pairs={{0,4},{4,0},{1,5},{5,1},{2,6},{6,2},{3,7},{7,3},{8,12},{12,8},{9,1... | collective-permute-start | bytes 3932168 | tf_op jit(solution)/shard_map/ppermute | solution.py:23
  15.3 11.7 %copy-start.4 = (bf16[768,192]{0,1:T(8,128)(2,1)S(1)}, bf16[768,192]{0,1:T(8,128)(2,1)}, u32[]{:S(2)}) copy-start(bf16[768,192]{0,1:T(8,128)(2,1)} %param.20) | copy-start | bytes 884740
  15.3 7.2 %copy-start.5 = (bf16[32,2560]{1,0:T(8,128)(2,1)}, bf16[32,2560]{1,0:T(8,128)(2,1)S(1)}, u32[]{:S(2)}) copy-start(bf16[32,2560]{1,0:T(8,128)(2,1)S(1)} %collective-permute-done) | copy-start | bytes 491524
  15.4 7.2 %copy-start.7 = (bf16[32,2560]{1,0:T(8,128)(2,1)}, bf16[32,2560]{1,0:T(8,128)(2,1)S(1)}, u32[]{:S(2)}) copy-start(bf16[32,2560]{1,0:T(8,128)(2,1)S(1)} %collective-permute-done.1) | copy-start | bytes 491524
  22.5 0.7 copy-start.9
  23.2 46.2 %all-to-all-start = ((bf16[8,160,384]{2,1,0:T(8,128)(2,1)}), bf16[8,160,384]{2,1,0:T(8,128)(2,1)S(1)}, u32[]{:S(2)}, u32[]{:S(2)}) async-start(bf16[8,160,384]{2,1,0:T(8,128)(2,1)} %get-tuple-element.39), calls=%async_computation | async-start | bytes 1966080 | tf_op jit(solution)/shard_map/all_to_all | solution.py:380
  29.2 11.3 %copy-start.6 = (bf16[32,2560]{1,0:T(8,128)(2,1)S(1)}, bf16[32,2560]{1,0:T(8,128)(2,1)}, u32[]{:S(2)}) copy-start(bf16[32,2560]{1,0:T(8,128)(2,1)} %copy-done.5) | copy-start | bytes 491524
  29.2 11.3 %copy-start.8 = (bf16[32,2560]{1,0:T(8,128)(2,1)S(1)}, bf16[32,2560]{1,0:T(8,128)(2,1)}, u32[]{:S(2)}) copy-start(bf16[32,2560]{1,0:T(8,128)(2,1)} %copy-done.7) | copy-start | bytes 491524
  29.2 11.3 %copy-start.10 = (bf16[32,2560]{1,0:T(8,128)(2,1)S(1)}, bf16[32,2560]{1,0:T(8,128)(2,1)}, u32[]{:S(2)}) copy-start(bf16[32,2560]{1,0:T(8,128)(2,1)} %copy-done.9) | copy-start | bytes 491524
  38.6 4.8 %collective-permute-start.6 = (bf16[64,384]{1,0:T(8,128)(2,1)S(1)}, bf16[64,384]{1,0:T(8,128)(2,1)S(1)}, u32[]{:S(2)}, u32[]{:S(2)}) collective-permute-start(bf16[64,384]{1,0:T(8,128)(2,1)S(1)} %get-tuple-element.52), channel_id=1, source_target_pairs={{0,3},{1,2},{2,1},{3,0},{4,7},{5,6},{6,5},{7,4},{8,11},{9,10},{10,... | collective-permute-start | bytes 147464 | tf_op jit(solution)/shard_map/ppermute | solution.py:23
  38.6 5.3 %collective-permute-start.5 = (bf16[64,384]{1,0:T(8,128)(2,1)S(1)}, bf16[64,384]{1,0:T(8,128)(2,1)S(1)}, u32[]{:S(2)}, u32[]{:S(2)}) collective-permute-start(bf16[64,384]{1,0:T(8,128)(2,1)S(1)} %get-tuple-element.53), channel_id=1, source_target_pairs={{0,2},{1,3},{2,0},{3,1},{4,6},{5,7},{6,4},{7,5},{8,10},{9,11},{10,... | collective-permute-start | bytes 147464 | tf_op jit(solution)/shard_map/ppermute | solution.py:23
  40.1 3.9 %collective-permute-start.4 = (bf16[64,384]{1,0:T(8,128)(2,1)S(1)}, bf16[64,384]{1,0:T(8,128)(2,1)S(1)}, u32[]{:S(2)}, u32[]{:S(2)}) collective-permute-start(bf16[64,384]{1,0:T(8,128)(2,1)S(1)} %get-tuple-element.54), channel_id=1, source_target_pairs={{0,1},{1,0},{2,3},{3,2},{4,5},{5,4},{6,7},{7,6},{8,9},{9,8},{10,11... | collective-permute-start | bytes 147464 | tf_op jit(solution)/shard_map/ppermute | solution.py:23
  41.4 27.1 %collective-permute-start.11 = (bf16[128,2560]{1,0:T(8,128)(2,1)}, bf16[128,2560]{1,0:T(8,128)(2,1)}, u32[]{:S(2)}, u32[]{:S(2)}) collective-permute-start(bf16[128,2560]{1,0:T(8,128)(2,1)} %pad_maximum_fusion.1.refs_0_), channel_id=1, source_target_pairs={{0,4},{4,0},{1,5},{5,1},{2,6},{6,2},{3,7},{7,3},{8,12},{12,8},{9,1... | collective-permute-start | bytes 1966088 | tf_op jit(solution)/shard_map/ppermute | solution.py:23
  43.4 25.1 %collective-permute-start.12 = (bf16[128,2560]{1,0:T(8,128)(2,1)}, bf16[128,2560]{1,0:T(8,128)(2,1)}, u32[]{:S(2)}, u32[]{:S(2)}) collective-permute-start(bf16[128,2560]{1,0:T(8,128)(2,1)} %pad_maximum_fusion.1.refs_0_), channel_id=1, source_target_pairs={{0,2},{1,3},{2,0},{3,1},{4,6},{5,7},{6,4},{7,5},{8,10},{9,11},{10,... | collective-permute-start | bytes 1966088 | tf_op jit(solution)/shard_map/ppermute | solution.py:23
  46.0 7.7 %collective-permute-start.8 = (bf16[256,384]{1,0:T(8,128)(2,1)S(1)}, bf16[256,384]{1,0:T(8,128)(2,1)S(1)}, u32[]{:S(2)}, u32[]{:S(2)}) collective-permute-start(bf16[256,384]{1,0:T(8,128)(2,1)S(1)} %pad_maximum_fusion.2), channel_id=1, source_target_pairs={{0,8},{8,16},{16,24},{24,0},{1,9},{9,17},{17,25},{25,1},{2,10},{10... | collective-permute-start | bytes 589832 | tf_op jit(solution)/shard_map/ppermute | solution.py:322
  47.9 12.0 %collective-permute-start.9 = (bf16[256,384]{1,0:T(8,128)(2,1)S(1)}, bf16[256,384]{1,0:T(8,128)(2,1)S(1)}, u32[]{:S(2)}, u32[]{:S(2)}) collective-permute-start(bf16[256,384]{1,0:T(8,128)(2,1)S(1)} %pad_maximum_fusion.2), channel_id=1, source_target_pairs={{8,0},{16,8},{24,16},{0,24},{9,1},{17,9},{25,17},{1,25},{10,2},{18... | collective-permute-start | bytes 589832 | tf_op jit(solution)/shard_map/ppermute | solution.py:323
  49.8 18.7 %collective-permute-start.10 = (bf16[256,384]{1,0:T(8,128)(2,1)S(1)}, bf16[256,384]{1,0:T(8,128)(2,1)S(1)}, u32[]{:S(2)}, u32[]{:S(2)}) collective-permute-start(bf16[256,384]{1,0:T(8,128)(2,1)S(1)} %pad_maximum_fusion.2), channel_id=1, source_target_pairs={{0,16},{8,24},{16,0},{24,8},{1,17},{9,25},{17,1},{25,9},{2,18},{10... | collective-permute-start | bytes 589832 | tf_op jit(solution)/shard_map/ppermute | solution.py:23
  68.5 0.9 copy-start.3
  69.4 7.4 %copy-start.12 = (s32[1,1,4,1]{2,3,1,0:T(1,128)S(1)}, s32[1,1,4,1]{2,3,1,0:T(1,128)}, u32[]{:S(2)}) copy-start(s32[1,1,4,1]{2,3,1,0:T(1,128)} %constant.475.clone) | copy-start | bytes 52
  69.4 7.4 %copy-start.11 = (s32[2,4,64]{2,1,0:T(4,128)S(1)}, s32[2,4,64]{2,1,0:T(4,128)}, u32[]{:S(2)}) copy-start(s32[2,4,64]{2,1,0:T(4,128)} %constant.478) | copy-start | bytes 6148
  69.4 37.7 %all-to-all-start.1 = ((bf16[8,160,384]{2,1,0:T(8,128)(2,1)}), bf16[8,160,384]{2,1,0:T(8,128)(2,1)}, u32[]{:S(2)}, u32[]{:S(2)}) async-start(bf16[8,160,384]{2,1,0:T(8,128)(2,1)} %get-tuple-element.40), calls=%async_computation.1 | async-start | bytes 1966080 | tf_op jit(solution)/shard_map/all_to_all | solution.py:380
  74.3 16.8 %collective-permute-start.13 = (bf16[128,2560]{1,0:T(8,128)(2,1)}, bf16[128,2560]{1,0:T(8,128)(2,1)}, u32[]{:S(2)}, u32[]{:S(2)}) collective-permute-start(bf16[128,2560]{1,0:T(8,128)(2,1)} %collective-permute-done.11.refs_1_), channel_id=1, source_target_pairs={{0,2},{1,3},{2,0},{3,1},{4,6},{5,7},{6,4},{7,5},{8,10},{9,11},{10,... | collective-permute-start | bytes 1966088 | tf_op jit(solution)/shard_map/ppermute | solution.py:23
  75.4 28.8 %collective-permute-start.18 = (bf16[1024,384]{1,0:T(8,128)(2,1)}, bf16[1024,384]{1,0:T(8,128)(2,1)}, u32[]{:S(2)}, u32[]{:S(2)}) collective-permute-start(bf16[1024,384]{1,0:T(8,128)(2,1)} %copy-done.3), channel_id=1, source_target_pairs={{0,4},{4,0},{1,5},{5,1},{2,6},{6,2},{3,7},{7,3},{8,12},{12,8},{9,1... | collective-permute-start | bytes 2359304 | tf_op jit(solution)/shard_map/ppermute | solution.py:23
  76.9 30.2 %collective-permute-start.15 = (bf16[128,2560]{1,0:T(8,128)(2,1)}, bf16[128,2560]{1,0:T(8,128)(2,1)}, u32[]{:S(2)}, u32[]{:S(2)}) collective-permute-start(bf16[128,2560]{1,0:T(8,128)(2,1)} %collective-permute-done.11.refs_1_), channel_id=1, source_target_pairs={{0,1},{1,0},{2,3},{3,2},{4,5},{5,4},{6,7},{7,6},{8,9},{9,8},{10,11... | collective-permute-start | bytes 1966088 | tf_op jit(solution)/shard_map/ppermute | solution.py:23
  76.9 30.2 %collective-permute-start.14 = (bf16[128,2560]{1,0:T(8,128)(2,1)}, bf16[128,2560]{1,0:T(8,128)(2,1)}, u32[]{:S(2)}, u32[]{:S(2)}) collective-permute-start(bf16[128,2560]{1,0:T(8,128)(2,1)} %pad_maximum_fusion.1.refs_0_), channel_id=1, source_target_pairs={{0,1},{1,0},{2,3},{3,2},{4,5},{5,4},{6,7},{7,6},{8,9},{9,8},{10,11... | collective-permute-start | bytes 1966088 | tf_op jit(solution)/shard_map/ppermute | solution.py:23
  77.4 29.7 %collective-permute-start.16 = (bf16[128,2560]{1,0:T(8,128)(2,1)}, bf16[128,2560]{1,0:T(8,128)(2,1)}, u32[]{:S(2)}, u32[]{:S(2)}) collective-permute-start(bf16[128,2560]{1,0:T(8,128)(2,1)} %collective-permute-done.12.refs_2_), channel_id=1, source_target_pairs={{0,1},{1,0},{2,3},{3,2},{4,5},{5,4},{6,7},{7,6},{8,9},{9,8},{10,11... | collective-permute-start | bytes 1966088 | tf_op jit(solution)/shard_map/ppermute | solution.py:23
  91.0 16.1 %collective-permute-start.17 = (bf16[128,2560]{1,0:T(8,128)(2,1)}, bf16[128,2560]{1,0:T(8,128)(2,1)}, u32[]{:S(2)}, u32[]{:S(2)}) collective-permute-start(bf16[128,2560]{1,0:T(8,128)(2,1)} %collective-permute-done.13.refs_3_), channel_id=1, source_target_pairs={{0,1},{1,0},{2,3},{3,2},{4,5},{5,4},{6,7},{7,6},{8,9},{9,8},{10,11... | collective-permute-start | bytes 1966088 | tf_op jit(solution)/shard_map/ppermute | solution.py:23
  107.1 6.6 %copy-start.2 = (bf16[2,1024,384]{2,1,0:T(8,128)(2,1)S(1)}, bf16[2,1024,384]{2,1,0:T(8,128)(2,1)}, u32[]{:S(2)}) copy-start(bf16[2,1024,384]{2,1,0:T(8,128)(2,1)} %pad_maximum_fusion) | copy-start | bytes 4718596
  118.0 43.8 %copy-start.1 = (bf16[2048,320]{0,1:T(8,128)(2,1)S(1)}, bf16[2048,320]{0,1:T(8,128)(2,1)}, u32[]{:S(2)}) copy-start(bf16[2048,320]{0,1:T(8,128)(2,1)} %param.17) | copy-start | bytes 3932164
  122.2 5.7 %collective-permute-start.24 = (bf16[512,128]{1,0:T(8,128)(2,1)S(1)}, bf16[512,128]{1,0:T(8,128)(2,1)S(1)}, u32[]{:S(2)}, u32[]{:S(2)}) collective-permute-start(bf16[512,128]{1,0:T(8,128)(2,1)S(1)} %get-tuple-element.46), channel_id=1, source_target_pairs={{0,4},{4,0},{1,5},{5,1},{2,6},{6,2},{3,7},{7,3},{8,12},{12,8},{9,1... | collective-permute-start | bytes 393224 | tf_op jit(solution)/shard_map/ppermute | solution.py:23
  122.6 8.5 %collective-permute-start.19 = (bf16[512,128]{1,0:T(8,128)(2,1)S(1)}, bf16[512,128]{1,0:T(8,128)(2,1)S(1)}, u32[]{:S(2)}, u32[]{:S(2)}) collective-permute-start(bf16[512,128]{1,0:T(8,128)(2,1)S(1)} %get-tuple-element.43), channel_id=1, source_target_pairs={{0,4},{4,0},{1,5},{5,1},{2,6},{6,2},{3,7},{7,3},{8,12},{12,8},{9,1... | collective-permute-start | bytes 393224 | tf_op jit(solution)/shard_map/ppermute | solution.py:23
  127.9 18.5 %collective-permute-start.27 = (bf16[512,256]{1,0:T(8,128)(2,1)S(1)}, bf16[512,256]{1,0:T(8,128)(2,1)S(1)}, u32[]{:S(2)}, u32[]{:S(2)}) collective-permute-start(bf16[512,256]{1,0:T(8,128)(2,1)S(1)} %constant_dynamic-update-slice_fusion.2.refs_0_), channel_id=1, source_target_pairs={{0,16},{8,24},{16,0},{24,8},{1,17},{9,25},{17,1},{25,9},{2,18},{10... | collective-permute-start | bytes 786440 | tf_op jit(solution)/shard_map/ppermute | solution.py:23
  131.1 21.2 %collective-permute-start.22 = (bf16[512,256]{1,0:T(8,128)(2,1)S(1)}, bf16[512,256]{1,0:T(8,128)(2,1)S(1)}, u32[]{:S(2)}, u32[]{:S(2)}) collective-permute-start(bf16[512,256]{1,0:T(8,128)(2,1)S(1)} %constant_dynamic-update-slice_fusion.refs_0_), channel_id=1, source_target_pairs={{0,16},{8,24},{16,0},{24,8},{1,17},{9,25},{17,1},{25,9},{2,18},{10... | collective-permute-start | bytes 786440 | tf_op jit(solution)/shard_map/ppermute | solution.py:23
  132.9 20.7 %collective-permute-start.25 = (bf16[512,256]{1,0:T(8,128)(2,1)S(1)}, bf16[512,256]{1,0:T(8,128)(2,1)S(1)}, u32[]{:S(2)}, u32[]{:S(2)}) collective-permute-start(bf16[512,256]{1,0:T(8,128)(2,1)S(1)} %constant_dynamic-update-slice_fusion.2.refs_0_), channel_id=1, source_target_pairs={{0,8},{8,16},{16,24},{1,9},{9,17},{17,25},{2,10},{10,18},{18,26},{... | collective-permute-start | bytes 786440 | tf_op jit(solution)/shard_map/ppermute | solution.py:315
  135.2 21.0 %collective-permute-start.26 = (bf16[512,256]{1,0:T(8,128)(2,1)S(1)}, bf16[512,256]{1,0:T(8,128)(2,1)S(1)}, u32[]{:S(2)}, u32[]{:S(2)}) collective-permute-start(bf16[512,256]{1,0:T(8,128)(2,1)S(1)} %constant_dynamic-update-slice_fusion.2.refs_0_), channel_id=1, source_target_pairs={{8,0},{16,8},{24,16},{9,1},{17,9},{25,17},{10,2},{18,10},{26,18},{... | collective-permute-start | bytes 786440 | tf_op jit(solution)/shard_map/ppermute | solution.py:316
  146.4 15.4 %collective-permute-start.28 = (bf16[512,256]{1,0:T(8,128)(2,1)S(1)}, bf16[512,256]{1,0:T(8,128)(2,1)S(1)}, u32[]{:S(2)}, u32[]{:S(2)}) collective-permute-start(bf16[512,256]{1,0:T(8,128)(2,1)S(1)} %collective-permute-done.27.refs_4_), channel_id=1, source_target_pairs={{8,0},{16,24},{9,1},{17,25},{10,2},{18,26},{11,3},{19,27},{12,4},{... | collective-permute-start | bytes 786440 | tf_op jit(solution)/shard_map/ppermute | solution.py:317
  147.7 16.1 %collective-permute-start.20 = (bf16[512,256]{1,0:T(8,128)(2,1)S(1)}, bf16[512,256]{1,0:T(8,128)(2,1)S(1)}, u32[]{:S(2)}, u32[]{:S(2)}) collective-permute-start(bf16[512,256]{1,0:T(8,128)(2,1)S(1)} %constant_dynamic-update-slice_fusion.refs_0_), channel_id=1, source_target_pairs={{0,8},{8,16},{16,24},{1,9},{9,17},{17,25},{2,10},{10,18},{18,26},{... | collective-permute-start | bytes 786440 | tf_op jit(solution)/shard_map/ppermute | solution.py:315
  152.3 15.2 %collective-permute-start.21 = (bf16[512,256]{1,0:T(8,128)(2,1)S(1)}, bf16[512,256]{1,0:T(8,128)(2,1)S(1)}, u32[]{:S(2)}, u32[]{:S(2)}) collective-permute-start(bf16[512,256]{1,0:T(8,128)(2,1)S(1)} %constant_dynamic-update-slice_fusion.refs_0_), channel_id=1, source_target_pairs={{8,0},{16,8},{24,16},{9,1},{17,9},{25,17},{10,2},{18,10},{26,18},{... | collective-permute-start | bytes 786440 | tf_op jit(solution)/shard_map/ppermute | solution.py:316
  153.6 17.6 %collective-permute-start.23 = (bf16[512,256]{1,0:T(8,128)(2,1)S(1)}, bf16[512,256]{1,0:T(8,128)(2,1)S(1)}, u32[]{:S(2)}, u32[]{:S(2)}) collective-permute-start(bf16[512,256]{1,0:T(8,128)(2,1)S(1)} %collective-permute-done.22.refs_4_), channel_id=1, source_target_pairs={{8,0},{16,24},{9,1},{17,25},{10,2},{18,26},{11,3},{19,27},{12,4},{... | collective-permute-start | bytes 786440 | tf_op jit(solution)/shard_map/ppermute | solution.py:317
  174.0 1.7 collective-permute-start.29
  175.8 6.3 %collective-permute-start.30 = (bf16[4,32,640]{2,1,0:T(8,128)(2,1)S(1)}, bf16[4,32,640]{2,1,0:T(8,128)(2,1)S(1)}, u32[]{:S(2)}, u32[]{:S(2)}) collective-permute-start(bf16[4,32,640]{2,1,0:T(8,128)(2,1)S(1)} %fusion.1), channel_id=1, source_target_pairs={{0,2},{1,3},{2,0},{3,1},{4,6},{5,7},{6,4},{7,5},{8,10},{9,11},{10,... | collective-permute-start | bytes 491528 | tf_op jit(solution)/shard_map/ppermute | solution.py:23
  182.4 11.6 %collective-permute-start.31 = (bf16[128,640]{1,0:T(8,128)(2,1)S(1)}, bf16[128,640]{1,0:T(8,128)(2,1)S(1)}, u32[]{:S(2)}, u32[]{:S(2)}) collective-permute-start(bf16[128,640]{1,0:T(8,128)(2,1)S(1)} %pad_maximum_fusion.3), channel_id=1, source_target_pairs={{0,0},{1,8},{2,16},{3,24},{4,4},{5,12},{6,20},{7,28},{8,1},{9,9},{... | collective-permute-start | bytes 491528 | tf_op jit(solution)/shard_map/ppermute | solution.py:502

commit v9 on v8

--- a/solution.py
+++ b/solution.py
@@ -192,20 +192,34 @@
     )(*pieces, *weights)
 
 
-def attend(here, queries, head, packed, limits, places, key_width, masked, layout):
+def attend(here, queries, head, packed, starts, limits, places, key_width, masked, layout):
     rows_each = queries[0].shape[0]
     rows = rows_each * len(queries)
     value_start = round_up(key_width, LANES)
-    value_width = packed.shape[1] - value_start
-    columns = packed.shape[0]
+    value_width = packed[0].shape[1] - value_start
+    size = packed[0].shape[0]
+    columns = size * len(packed)
+    count = len(packed)
     factor = np.float32(key_width**-0.5 * np.log2(np.e))
     tile = min(256, rows_each)
     unit, outputs, sends = layout
 
     def kernel(here_ref, *refs):
-        query_refs = refs[: len(queries)]
-        kv_ref, limit_ref, place_ref = refs[len(queries) : len(queries) + 3]
-        out_refs = refs[len(queries) + 3 :]
+        piece_refs, query_refs = refs[:count], refs[count : count + len(queries)]
+        limit_ref, place_ref = refs[count + len(queries) : count + len(queries) + 2]
+        out_refs, kv_ref, sems = refs[count + len(queries) + 2 : -2], refs[-2], refs[-1]
+        copies = []
+        for index, piece in enumerate(piece_refs):
+            start = starts(index, here_ref[0], here_ref[2])
+            if not isinstance(start, int):
+                start = pl.multiple_of(start * size, size)
+            copies.append(
+                pltpu.make_async_copy(piece, kv_ref.at[pl.ds(start, size)], sems.at[index])
+            )
+        for copy in copies:
+            copy.start()
+        for copy in copies:
+            copy.wait()
         keys = kv_ref[:, :key_width]
         values = kv_ref[:, value_start:]
         for start in range(0, rows, tile):
@@ -240,15 +254,20 @@
         kernel,
         out_shape=(shape,) * outputs,
         in_specs=[pl.BlockSpec(memory_space=pltpu.SMEM)]
-        + [pl.BlockSpec(memory_space=pltpu.VMEM)] * (len(queries) + 3),
+        + [pl.BlockSpec(memory_space=pl.ANY)] * count
+        + [pl.BlockSpec(memory_space=pltpu.VMEM)] * (len(queries) + 2),
+        scratch_shapes=[
+            pltpu.VMEM((columns, packed[0].shape[1]), jnp.bfloat16),
+            pltpu.SemaphoreType.DMA((count,)),
+        ],
         compiler_params=pltpu.CompilerParams(vmem_limit_bytes=VMEM_LIMIT),
         cost_estimate=pl.CostEstimate(
             flops=2 * rows * columns * (key_width + value_width),
-            bytes_accessed=2 * packed.size,
+            bytes_accessed=2 * columns * packed[0].shape[1],
             transcendentals=0,
         ),
         name="attend",
-    )(here, *queries, packed, limits, places)
+    )(here, *packed, *queries, limits, places)
 
 
 def expel(place, pieces, weights, before, chunk, chunks, shape):
@@ -397,7 +416,8 @@
         )
         weight_first = exchange(begin)
         near = jnp.concatenate([mine, before, after, far], axis=0)
-        beside = swap(near, "inner", 1)
+        follow, out_weights[1] = lax.optimization_barrier((near, out_weights[1]))
+        beside = swap(follow, "inner", 1)
         pieces = [near, beside, swap(near, "head", 2)]
         steps = [(line, side, turn) for turn in (0, 2) for side in (0, 1) for line in range(4)]
         steps = steps + [(a, b, k ^ 1) for a, b, k in steps]
@@ -439,14 +459,26 @@
         packed = packed.reshape(heads_axis * blocks, -1)
         bound = ids
     if fast:
-        packed, out_weights[1] = lax.optimization_barrier((packed, out_weights[1]))
-    packed = gather_line(packed, "outer", 0)
-    if fast:
-        begin, packed, pieces = lax.optimization_barrier((sent[1], packed, pieces))
+        packed = list(ring_pieces(packed, "outer"))
+        first = swap(packed[0], "inner", 1)
+        begin, rest, pieces, first = lax.optimization_barrier((sent[1], packed[1:], pieces, first))
+        packed = [packed[0], *rest]
+        packed += [first, *(swap(piece, "inner", 1) for piece in rest)]
         pieces.append(swap(pieces[1], "head", 2))
-        partners = [swap(piece, "head", 1) for piece in pieces]
+        packed, late = lax.optimization_barrier((packed, pieces[3]))
+        partners = [swap(piece, "head", 1) for piece in (*pieces[:3], late)]
         queries = [project([*pieces, *partners], [weight_first, exchange(begin)])]
-    packed = gather_pair(packed, "inner").reshape(devices * blocks, -1)
+
+        def starts(index, z, y):
+            return (y ^ (index // 4)) * 4 + (z, (z + 3) & 3, (z + 1) & 3, z ^ 2)[index % 4]
+
+    else:
+        packed = gather_line(packed, "outer", 0)
+        packed = [gather_pair(packed, "inner").reshape(devices * blocks, -1)]
+
+        def starts(index, z, y):
+            return 0
+
     bound = (STRIDE * bound + BLK - 1).transpose(1, 0, 2, 3).reshape(-1)
     hidden = [bool((bound[i : i + LANES] > context).any()) for i in range(0, len(bound), LANES)]
     masked, start = [], 0
@@ -465,7 +497,7 @@
     total = None
     for head in range(heads_here):
         attended = attend(
-            here, queries, head, packed, limits, places, key_width, masked, layout
+            here, queries, head, packed, starts, limits, places, key_width, masked, layout
         )
         if fast:
             last = head == heads_here - 1

time: 195 us -> 206 us (1.056)
  local copies, waits for them, and re-layouts: 7.91 us -> 17.3 us
  starting transfers between devices: 49.8 us -> 58 us
  waiting for transfers between devices: 97.4 us -> 89.2 us
  Pallas kernels: 33.9 us -> 37.7 us
  other arithmetic: 4.29 us -> 1.67 us
    unnamed x30 -> x64, local copies, waits for them, and re-layouts: 3.26 us -> 12.8 us
    ppermute x20 -> x23, starting transfers between devices: 17.3 us -> 24.1 us  [swap(): lax.ppermute(block, axis, [(i, i ^ bit) for i in range(lax.axis_size(axis...]
    ppermute x20 -> x23, waiting for transfers between devices: 64.8 us -> 58.3 us  [swap(): lax.ppermute(block, axis, [(i, i ^ bit) for i in range(lax.axis_size(axis...]
    ppermute x2, waiting for transfers between devices: 6.24 us -> 1.78 us  [ring_pieces(): after = lax.ppermute(block, axis, [((i + 1) % 4, i) for i in range(4)])]
    pallas_call x2, Pallas kernels: 8.37 us -> 12.6 us  [attend(): pl.pallas_call(kernel, out_shape=(shape,) * outputs, in_specs=[pl.BlockSp...]
    another operation x2 -> x0, other arithmetic: 2.87 us -> none  [gather_pair(): jnp.stack([jnp.where(first, block, other), jnp.where(first, other, block)])]
  transfers between devices with their start and end apart: 34 -> 37, of which waited for: 16 -> 20; matrix products, arithmetic and copies ran while one was open for 4% -> 3% of each run, Pallas kernels for 8% -> 8%
where the time goes in v9:
time: 206 us; the launch traced here: 205 us
  waiting for transfers between devices  89.2 us (43%)
  starting transfers between devices  58 us (28%)
  Pallas kernels  37.7 us (18%)
  local copies, waits for them, and re-layouts  17.3 us (8%)
    ppermute x23, waiting for transfers between devices, swap(): lax.ppermute(block, axis, [(i, i ^ bit) for i in range(lax.axis_size(axis...  58.3 us
    ppermute x23, starting transfers between devices, swap(): lax.ppermute(block, axis, [(i, i ^ bit) for i in range(lax.axis_size(axis...  24.1 us
    unnamed x64, local copies, waits for them, and re-layouts  12.8 us
    pallas_call x2, Pallas kernels, attend(): pl.pallas_call(kernel, out_shape=(shape,) * outputs, in_specs=[pl.BlockSp...  12.6 us
    ppermute x1, waiting for transfers between devices, shards(): return lax.ppermute(result, ('outer', 'inner', 'head'), route)  9.66 us
    ppermute x2, waiting for transfers between devices, line_pieces(): passed = lax.ppermute(far, axis, [(1, 0), (2, 3)])  9.63 us
    all_to_all x2, starting transfers between devices, exchange(): lax.all_to_all(block, seq_axes, split_axis=0, concat_axis=0, tiled=True)  8.96 us
    pallas_call x1, Pallas kernels, compress(): pl.pallas_call(compress_kernel, out_shape=jax.ShapeDtypeStruct((G, blocks...  8.4 us
  transfers between devices with their start and end apart: 37, of which 20 were waited for; matrix products, arithmetic and copies ran while one was open for 3% of the time, Pallas kernels for 8%

profile of v9, /device:TPU:2, one launch (start us, length us, event | category | flops | bytes accessed | tf_op | source)
XLA Modules:
  0.0 205.5 jit_solution(10520186895608173587)
XLA Ops:
  1.5 1.9 collective-permute-start.3
  3.5 1.6 collective-permute-done.3
  5.1 1.5 collective-permute-start.10
  6.6 1.6 collective-permute-start
  8.3 2.2 %collective-permute-start.1 = (bf16[32,2560]{1,0:T(8,128)(2,1)S(1)}, bf16[32,2560]{1,0:T(8,128)(2,1)S(1)}, u32[]{:S(2)}, u32[]{:S(2)}) collective-permute-start(bf16[32,2560]{1,0:T(8,128)(2,1)S(1)} %constant_dynamic-slice_fusion), channel_id=1, source_target_pairs={{8,0},{16,8},{24,16},{0,24},{9,1},{17,9},{25,17},{1,25},{10,2},{18... | collective-permute-start | bytes 491528 | tf_op jit(solution)/shard_map/ppermute | solution.py:342
  11.3 5.6 %cut.1 = (bf16[8,160,384]{2,1,0:T(8,128)(2,1)}, bf16[8,160,384]{2,1,0:T(8,128)(2,1)}) custom-call(bf16[320,3072]{1,0:T(8,128)(2,1)} %in_ref.1), custom_call_target="tpu_custom_call" | custom-call | tf_op jit(solution)/shard_map/cut/pallas_call | solution.py:129
  17.0 1.5 collective-permute-done.1
  18.4 7.0 %collective-permute-done.2 = bf16[32,2560]{1,0:T(8,128)(2,1)S(1)} collective-permute-done((bf16[32,2560]{1,0:T(8,128)(2,1)S(1)}, bf16[32,2560]{1,0:T(8,128)(2,1)S(1)}, u32[]{:S(2)}, u32[]{:S(2)}) %collective-permute-start.2) | collective-permute-done | bytes 163872 | tf_op jit(solution)/shard_map/ppermute | solution.py:23
  26.1 3.6 %all-to-all-start = ((bf16[8,160,384]{2,1,0:T(8,128)(2,1)}), bf16[8,160,384]{2,1,0:T(8,128)(2,1)S(1)}, u32[]{:S(2)}, u32[]{:S(2)}) async-start(bf16[8,160,384]{2,1,0:T(8,128)(2,1)} %get-tuple-element.64), calls=%async_computation | async-start | bytes 1966080 | tf_op jit(solution)/shard_map/all_to_all | solution.py:399
  32.9 1.7 collective-permute-start.12
  34.6 8.4 %compress.1 = bf16[4,64,384]{2,1,0:T(8,128)(2,1)} custom-call(bf16[1024,768]{1,0:T(8,128)(2,1)} %raw_keys.1, bf16[1024,512]{1,0:T(8,128)(2,1)} %raw_values.1, bf16[16,768]{1,0:T(8,128)(2,1)} %slice.20.edge_keys, bf16[16,512]{1,0:T(8,128)(2,1)} %slice.21.edge_values, bf16[192,768]{1,0:T(8,128)(2,1)} %key_expand.1, f32[32,768]{1,0:T(8,128)} %key_mix.1, ...), custom_call_target="tpu_custom_call" | custom-call | flops 2013265920 | bytes 1572864 | tf_op jit(solution)/shard_map/compress/pallas_call | solution.py:105
  43.1 2.0 collective-permute-start.11
  46.0 2.6 %collective-permute-start.5 = (bf16[64,384]{1,0:T(8,128)(2,1)S(1)}, bf16[64,384]{1,0:T(8,128)(2,1)S(1)}, u32[]{:S(2)}, u32[]{:S(2)}) collective-permute-start(bf16[64,384]{1,0:T(8,128)(2,1)S(1)} %get-tuple-element.75), channel_id=1, source_target_pairs={{0,2},{1,3},{2,0},{3,1},{4,6},{5,7},{6,4},{7,5},{8,10},{9,11},{10,... | collective-permute-start | bytes 147464 | tf_op jit(solution)/shard_map/ppermute | solution.py:23
  48.6 2.2 %collective-permute-done.6 = bf16[64,384]{1,0:T(8,128)(2,1)S(1)} collective-permute-done((bf16[64,384]{1,0:T(8,128)(2,1)S(1)}, bf16[64,384]{1,0:T(8,128)(2,1)S(1)}, u32[]{:S(2)}, u32[]{:S(2)}) %collective-permute-start.6) | collective-permute-done | bytes 49184 | tf_op jit(solution)/shard_map/ppermute | solution.py:23
  50.8 1.4 collective-permute-done.5
  52.3 1.7 collective-permute-start.7
  53.9 2.2 %collective-permute-start.8 = (bf16[256,384]{1,0:T(8,128)(2,1)S(1)}, bf16[256,384]{1,0:T(8,128)(2,1)S(1)}, u32[]{:S(2)}, u32[]{:S(2)}) collective-permute-start(bf16[256,384]{1,0:T(8,128)(2,1)S(1)} %pad_maximum_fusion.1.refs_0_), channel_id=1, source_target_pairs={{8,0},{16,8},{24,16},{0,24},{9,1},{17,9},{25,17},{1,25},{10,2},{18... | collective-permute-start | bytes 589832 | tf_op jit(solution)/shard_map/ppermute | solution.py:342
  56.1 1.3 collective-permute-start.9
  57.5 4.5 %collective-permute-done.7.refs_1_ = bf16[256,384]{1,0:T(8,128)(2,1)S(1)} collective-permute-done((bf16[256,384]{1,0:T(8,128)(2,1)S(1)}, bf16[256,384]{1,0:T(8,128)(2,1)S(1)}, u32[]{:S(2)}, u32[]{:S(2)}) %collective-permute-start.7) | collective-permute-done | bytes 196640 | tf_op jit(solution)/shard_map/ppermute | solution.py:341
  61.9 1.6 collective-permute-start.13
  64.6 8.9 %collective-permute-done.9.refs_3_ = bf16[256,384]{1,0:T(8,128)(2,1)S(1)} collective-permute-done((bf16[256,384]{1,0:T(8,128)(2,1)S(1)}, bf16[256,384]{1,0:T(8,128)(2,1)S(1)}, u32[]{:S(2)}, u32[]{:S(2)}) %collective-permute-start.9) | collective-permute-done | bytes 196640 | tf_op jit(solution)/shard_map/ppermute | solution.py:23
  75.8 5.4 %all-to-all-start.1 = ((bf16[8,160,384]{2,1,0:T(8,128)(2,1)}), bf16[8,160,384]{2,1,0:T(8,128)(2,1)}, u32[]{:S(2)}, u32[]{:S(2)}) async-start(bf16[8,160,384]{2,1,0:T(8,128)(2,1)} %get-tuple-element.65), calls=%async_computation.1 | async-start | bytes 1966080 | tf_op jit(solution)/shard_map/all_to_all | solution.py:399
  81.2 1.4 collective-permute-start.17
  82.6 2.0 collective-permute-start.14
  86.1 2.0 collective-permute-start.16
  88.8 9.5 %collective-permute-done.14.refs_5_ = bf16[256,384]{1,0:T(8,128)(2,1)S(1)} collective-permute-done((bf16[256,384]{1,0:T(8,128)(2,1)S(1)}, bf16[256,384]{1,0:T(8,128)(2,1)S(1)}, u32[]{:S(2)}, u32[]{:S(2)}) %collective-permute-start.14) | collective-permute-done | bytes 196640 | tf_op jit(solution)/shard_map/ppermute | solution.py:23
  99.0 4.8 %collective-permute-done.15.refs_6_ = bf16[256,384]{1,0:T(8,128)(2,1)S(1)} collective-permute-done((bf16[256,384]{1,0:T(8,128)(2,1)S(1)}, bf16[256,384]{1,0:T(8,128)(2,1)S(1)}, u32[]{:S(2)}, u32[]{:S(2)}) %collective-permute-start.15) | collective-permute-done | bytes 196640 | tf_op jit(solution)/shard_map/ppermute | solution.py:23
  104.5 1.8 collective-permute-done.16.refs_7_
  112.8 6.3 %project.1.refs_8_ = bf16[1024,384]{1,0:T(8,128)(2,1)S(1)} custom-call(bf16[128,2560]{1,0:T(8,128)(2,1)S(1)} %copy-done.3, bf16[128,2560]{1,0:T(8,128)(2,1)S(1)} %copy-done.7, bf16[128,2560]{1,0:T(8,128)(2,1)S(1)} %copy-done.5, bf16[128,2560]{1,0:T(8,128)(2,1)} %collective-permute-done.17.refs_3_, bf16[128,2560]{1,0:T(8,128)(2,1)} %collective-permute-done.18.refs_4_, ...), custom_call_target="tpu_custom_call" | custom-call | flops 2013265920 | bytes 5242880 | tf_op jit(solution)/shard_map/project/pallas_call | solution.py:178
  119.2 6.3 %attend.2 = (bf16[512,128]{1,0:T(8,128)(2,1)S(1)}, bf16[512,128]{1,0:T(8,128)(2,1)S(1)}) custom-call(s32[3]{0:T(128)S(1)} %pad_add_fusion.here_ref.place_ref, bf16[256,384]{1,0:T(8,128)(2,1)S(1)} %copy-done.9, bf16[256,384]{1,0:T(8,128)(2,1)S(1)} %copy-done.11, bf16[256,384]{1,0:T(8,128)(2,1)S(1)} %copy-done.13, bf16[256,384]{1,0:T(8,128)(2,1)S(1)} %copy-done.15, ...), custom_call_target="tpu_custom_call" | custom-call | flops 1342177280 | bytes 1572864 | tf_op jit(solution)/shard_map/attend/pallas_call | solution.py:253
  125.5 6.3 %attend.3 = (bf16[512,128]{1,0:T(8,128)(2,1)S(1)}, bf16[512,128]{1,0:T(8,128)(2,1)S(1)}) custom-call(s32[3]{0:T(128)S(1)} %pad_add_fusion.here_ref.place_ref, bf16[256,384]{1,0:T(8,128)(2,1)S(1)} %copy-done.9, bf16[256,384]{1,0:T(8,128)(2,1)S(1)} %copy-done.11, bf16[256,384]{1,0:T(8,128)(2,1)S(1)} %copy-done.13, bf16[256,384]{1,0:T(8,128)(2,1)S(1)} %copy-done.15, ...), custom_call_target="tpu_custom_call" | custom-call | flops 1342177280 | bytes 1572864 | tf_op jit(solution)/shard_map/attend/pallas_call | solution.py:253
  132.2 1.8 collective-permute-start.22
  134.0 4.2 %collective-permute-done.27 = bf16[512,128]{1,0:T(8,128)(2,1)S(1)} collective-permute-done((bf16[512,128]{1,0:T(8,128)(2,1)S(1)}, bf16[512,128]{1,0:T(8,128)(2,1)S(1)}, u32[]{:S(2)}, u32[]{:S(2)}) %collective-permute-start.27) | collective-permute-done | bytes 131104 | tf_op jit(solution)/shard_map/ppermute | solution.py:23
  138.2 2.2 %collective-permute-start.30 = (bf16[512,256]{1,0:T(8,128)(2,1)S(1)}, bf16[512,256]{1,0:T(8,128)(2,1)S(1)}, u32[]{:S(2)}, u32[]{:S(2)}) collective-permute-start(bf16[512,256]{1,0:T(8,128)(2,1)S(1)} %constant_dynamic-update-slice_fusion.2.refs_0_), channel_id=1, source_target_pairs={{0,16},{8,24},{16,0},{24,8},{1,17},{9,25},{17,1},{25,9},{2,18},{10... | collective-permute-start | bytes 786440 | tf_op jit(solution)/shard_map/ppermute | solution.py:23
  140.5 2.0 collective-permute-start.25
  142.4 3.4 %collective-permute-start.28 = (bf16[512,256]{1,0:T(8,128)(2,1)S(1)}, bf16[512,256]{1,0:T(8,128)(2,1)S(1)}, u32[]{:S(2)}, u32[]{:S(2)}) collective-permute-start(bf16[512,256]{1,0:T(8,128)(2,1)S(1)} %constant_dynamic-update-slice_fusion.2.refs_0_), channel_id=1, source_target_pairs={{0,8},{8,16},{16,24},{1,9},{9,17},{17,25},{2,10},{10,18},{18,26},{... | collective-permute-start | bytes 786440 | tf_op jit(solution)/shard_map/ppermute | solution.py:334
  147.1 11.0 %collective-permute-done.30.refs_4_ = bf16[512,256]{1,0:T(8,128)(2,1)S(1)} collective-permute-done((bf16[512,256]{1,0:T(8,128)(2,1)S(1)}, bf16[512,256]{1,0:T(8,128)(2,1)S(1)}, u32[]{:S(2)}, u32[]{:S(2)}) %collective-permute-start.30) | collective-permute-done | bytes 262176 | tf_op jit(solution)/shard_map/ppermute | solution.py:23
  159.4 4.6 %collective-permute-start.23 = (bf16[512,256]{1,0:T(8,128)(2,1)S(1)}, bf16[512,256]{1,0:T(8,128)(2,1)S(1)}, u32[]{:S(2)}, u32[]{:S(2)}) collective-permute-start(bf16[512,256]{1,0:T(8,128)(2,1)S(1)} %constant_dynamic-update-slice_fusion.refs_0_), channel_id=1, source_target_pairs={{0,8},{8,16},{16,24},{1,9},{9,17},{17,25},{2,10},{10,18},{18,26},{... | collective-permute-start | bytes 786440 | tf_op jit(solution)/shard_map/ppermute | solution.py:334
  165.3 1.5 collective-permute-start.26
  166.8 5.6 %collective-permute-done.31.refs_3_ = bf16[512,256]{1,0:T(8,128)(2,1)S(1)} collective-permute-done((bf16[512,256]{1,0:T(8,128)(2,1)S(1)}, bf16[512,256]{1,0:T(8,128)(2,1)S(1)}, u32[]{:S(2)}, u32[]{:S(2)}) %collective-permute-start.31) | collective-permute-done | bytes 262176 | tf_op jit(solution)/shard_map/ppermute | solution.py:336
  172.4 2.0 expel.2.refs_7_
  174.4 3.6 %collective-permute-done.24.refs_2_ = bf16[512,256]{1,0:T(8,128)(2,1)S(1)} collective-permute-done((bf16[512,256]{1,0:T(8,128)(2,1)S(1)}, bf16[512,256]{1,0:T(8,128)(2,1)S(1)}, u32[]{:S(2)}, u32[]{:S(2)}) %collective-permute-start.24) | collective-permute-done | bytes 262176 | tf_op jit(solution)/shard_map/ppermute | solution.py:335
  178.0 4.0 %collective-permute-done.26.refs_3_ = bf16[512,256]{1,0:T(8,128)(2,1)S(1)} collective-permute-done((bf16[512,256]{1,0:T(8,128)(2,1)S(1)}, bf16[512,256]{1,0:T(8,128)(2,1)S(1)}, u32[]{:S(2)}, u32[]{:S(2)}) %collective-permute-start.26) | collective-permute-done | bytes 262176 | tf_op jit(solution)/shard_map/ppermute | solution.py:336
  182.0 2.8 %expel.3 = (f32[4,2,32,640]{3,2,1,0:T(8,128)S(1)}, bf16[4,2,32,640]{3,2,1,0:T(8,128)(2,1)S(1)}) custom-call(s32[3]{0:T(128)S(1)} %pad_add_fusion.here_ref.place_ref, bf16[512,256]{1,0:T(8,128)(2,1)S(1)} %constant_dynamic-update-slice_fusion.refs_0_, bf16[512,256]{1,0:T(8,128)(2,1)S(1)} %collective-permute-done.23.refs_1_, ...), custom_call_target="tpu_custom_call" | custom-call | flops 671088640 | bytes 1310720 | tf_op jit(solution)/shard_map/expel/pallas_call | solution.py:318
  185.0 1.6 collective-permute-done.32
  187.4 5.6 %collective-permute-done.33 = bf16[4,32,640]{2,1,0:T(8,128)(2,1)S(1)} collective-permute-done((bf16[4,32,640]{2,1,0:T(8,128)(2,1)S(1)}, bf16[4,32,640]{2,1,0:T(8,128)(2,1)S(1)}, u32[]{:S(2)}, u32[]{:S(2)}) %collective-permute-start.33) | collective-permute-done | bytes 163872 | tf_op jit(solution)/shard_map/ppermute | solution.py:23
  193.2 1.9 collective-permute-start.34
  195.2 9.7 %collective-permute-done.34 = bf16[128,640]{1,0:T(8,128)(2,1)S(1)} collective-permute-done((bf16[128,640]{1,0:T(8,128)(2,1)S(1)}, bf16[128,640]{1,0:T(8,128)(2,1)S(1)}, u32[]{:S(2)}, u32[]{:S(2)}) %collective-permute-start.34) | collective-permute-done | bytes 163872 | tf_op jit(solution)/shard_map/ppermute | solution.py:534
  (120 shorter events, 25.5 us)
Async XLA Ops:
  0.0 6.6 %copy-start = (bf16[128,2560]{1,0:T(8,128)(2,1)S(1)}, bf16[128,2560]{1,0:T(8,128)(2,1)}, u32[]{:S(2)}) copy-start(bf16[128,2560]{1,0:T(8,128)(2,1)} %param.13) | copy-start | bytes 1966084
  1.5 3.6 %collective-permute-start.3 = (bf16[16,1280]{1,0:T(8,128)(2,1)S(1)}, bf16[16,1280]{1,0:T(8,128)(2,1)S(1)}, u32[]{:S(2)}, u32[]{:S(2)}) collective-permute-start(bf16[16,1280]{1,0:T(8,128)(2,1)S(1)} %pad_maximum_fusion.3), channel_id=1, source_target_pairs={{1,0},{2,1},{3,2},{4,3},{5,4},{6,5},{7,6},{8,7},{9,8},{10,9},{11,1... | collective-permute-start | bytes 122888 | tf_op jit(solution)/shard_map/ppermute | solution.py:384
  5.1 37.9 %collective-permute-start.10 = (bf16[320,2048]{1,0:T(8,128)(2,1)}, bf16[320,2048]{1,0:T(8,128)(2,1)S(1)}, u32[]{:S(2)}, u32[]{:S(2)}) collective-permute-start(bf16[320,2048]{1,0:T(8,128)(2,1)} %bitcast.53), channel_id=1, source_target_pairs={{0,4},{4,0},{1,5},{5,1},{2,6},{6,2},{3,7},{7,3},{8,12},{12,8},{9,1... | collective-permute-start | bytes 3932168 | tf_op jit(solution)/shard_map/ppermute | solution.py:23
  6.6 10.3 %collective-permute-start = (bf16[32,2560]{1,0:T(8,128)(2,1)S(1)}, bf16[32,2560]{1,0:T(8,128)(2,1)S(1)}, u32[]{:S(2)}, u32[]{:S(2)}) collective-permute-start(bf16[32,2560]{1,0:T(8,128)(2,1)S(1)} %constant_dynamic-slice_fusion), channel_id=1, source_target_pairs={{0,8},{8,16},{16,24},{24,0},{1,9},{9,17},{17,25},{25,1},{2,10},{10... | collective-permute-start | bytes 491528 | tf_op jit(solution)/shard_map/ppermute | solution.py:341
  8.3 10.1 %collective-permute-start.1 = (bf16[32,2560]{1,0:T(8,128)(2,1)S(1)}, bf16[32,2560]{1,0:T(8,128)(2,1)S(1)}, u32[]{:S(2)}, u32[]{:S(2)}) collective-permute-start(bf16[32,2560]{1,0:T(8,128)(2,1)S(1)} %constant_dynamic-slice_fusion), channel_id=1, source_target_pairs={{8,0},{16,8},{24,16},{0,24},{9,1},{17,9},{25,17},{1,25},{10,2},{18... | collective-permute-start | bytes 491528 | tf_op jit(solution)/shard_map/ppermute | solution.py:342
  10.5 14.9 %collective-permute-start.2 = (bf16[32,2560]{1,0:T(8,128)(2,1)S(1)}, bf16[32,2560]{1,0:T(8,128)(2,1)S(1)}, u32[]{:S(2)}, u32[]{:S(2)}) collective-permute-start(bf16[32,2560]{1,0:T(8,128)(2,1)S(1)} %constant_dynamic-slice_fusion), channel_id=1, source_target_pairs={{0,16},{8,24},{16,0},{24,8},{1,17},{9,25},{17,1},{25,9},{2,18},{10... | collective-permute-start | bytes 491528 | tf_op jit(solution)/shard_map/ppermute | solution.py:23
  17.0 12.7 %copy-start.24 = (bf16[768,192]{0,1:T(8,128)(2,1)S(1)}, bf16[768,192]{0,1:T(8,128)(2,1)}, u32[]{:S(2)}) copy-start(bf16[768,192]{0,1:T(8,128)(2,1)} %param.20) | copy-start | bytes 884740
  17.0 8.5 %copy-start.25 = (bf16[32,2560]{1,0:T(8,128)(2,1)}, bf16[32,2560]{1,0:T(8,128)(2,1)S(1)}, u32[]{:S(2)}) copy-start(bf16[32,2560]{1,0:T(8,128)(2,1)S(1)} %collective-permute-done) | copy-start | bytes 491524
  18.4 7.0 %copy-start.26 = (bf16[32,2560]{1,0:T(8,128)(2,1)}, bf16[32,2560]{1,0:T(8,128)(2,1)S(1)}, u32[]{:S(2)}) copy-start(bf16[32,2560]{1,0:T(8,128)(2,1)S(1)} %collective-permute-done.1) | copy-start | bytes 491524
  26.1 49.8 %all-to-all-start = ((bf16[8,160,384]{2,1,0:T(8,128)(2,1)}), bf16[8,160,384]{2,1,0:T(8,128)(2,1)S(1)}, u32[]{:S(2)}, u32[]{:S(2)}) async-start(bf16[8,160,384]{2,1,0:T(8,128)(2,1)} %get-tuple-element.64), calls=%async_computation | async-start | bytes 1966080 | tf_op jit(solution)/shard_map/all_to_all | solution.py:399
  32.9 10.1 %copy-start.2 = (bf16[128,2560]{1,0:T(8,128)(2,1)}, bf16[128,2560]{1,0:T(8,128)(2,1)S(1)}, u32[]{:S(2)}) copy-start(bf16[128,2560]{1,0:T(8,128)(2,1)S(1)} %pad_maximum_fusion.refs_0_) | copy-start | bytes 1966084
  32.9 41.2 %collective-permute-start.12 = (bf16[128,2560]{1,0:T(8,128)(2,1)S(1)}, bf16[128,2560]{1,0:T(8,128)(2,1)S(1)}, u32[]{:S(2)}, u32[]{:S(2)}) collective-permute-start(bf16[128,2560]{1,0:T(8,128)(2,1)S(1)} %pad_maximum_fusion.refs_0_), channel_id=1, source_target_pairs={{0,2},{1,3},{2,0},{3,1},{4,6},{5,7},{6,4},{7,5},{8,10},{9,11},{10,... | collective-permute-start | bytes 1966088 | tf_op jit(solution)/shard_map/ppermute | solution.py:23
  43.0 64.0 %copy-start.29 = (s32[1,1,4,1]{2,3,1,0:T(1,128)S(1)}, s32[1,1,4,1]{2,3,1,0:T(1,128)}, u32[]{:S(2)}) copy-start(s32[1,1,4,1]{2,3,1,0:T(1,128)} %constant.461.clone) | copy-start | bytes 52
  43.1 31.1 %collective-permute-start.11 = (bf16[128,2560]{1,0:T(8,128)(2,1)S(1)}, bf16[128,2560]{1,0:T(8,128)(2,1)S(1)}, u32[]{:S(2)}, u32[]{:S(2)}) collective-permute-start(bf16[128,2560]{1,0:T(8,128)(2,1)S(1)} %pad_maximum_fusion.refs_0_), channel_id=1, source_target_pairs={{0,4},{4,0},{1,5},{5,1},{2,6},{6,2},{3,7},{7,3},{8,12},{12,8},{9,1... | collective-permute-start | bytes 1966088 | tf_op jit(solution)/shard_map/ppermute | solution.py:23
  45.9 4.9 %collective-permute-start.6 = (bf16[64,384]{1,0:T(8,128)(2,1)S(1)}, bf16[64,384]{1,0:T(8,128)(2,1)S(1)}, u32[]{:S(2)}, u32[]{:S(2)}) collective-permute-start(bf16[64,384]{1,0:T(8,128)(2,1)S(1)} %get-tuple-element.74), channel_id=1, source_target_pairs={{0,3},{1,2},{2,1},{3,0},{4,7},{5,6},{6,5},{7,4},{8,11},{9,10},{10,... | collective-permute-start | bytes 147464 | tf_op jit(solution)/shard_map/ppermute | solution.py:23
  46.0 6.2 %collective-permute-start.5 = (bf16[64,384]{1,0:T(8,128)(2,1)S(1)}, bf16[64,384]{1,0:T(8,128)(2,1)S(1)}, u32[]{:S(2)}, u32[]{:S(2)}) collective-permute-start(bf16[64,384]{1,0:T(8,128)(2,1)S(1)} %get-tuple-element.75), channel_id=1, source_target_pairs={{0,2},{1,3},{2,0},{3,1},{4,6},{5,7},{6,4},{7,5},{8,10},{9,11},{10,... | collective-permute-start | bytes 147464 | tf_op jit(solution)/shard_map/ppermute | solution.py:23
  48.6 3.7 %collective-permute-start.4 = (bf16[64,384]{1,0:T(8,128)(2,1)S(1)}, bf16[64,384]{1,0:T(8,128)(2,1)S(1)}, u32[]{:S(2)}, u32[]{:S(2)}) collective-permute-start(bf16[64,384]{1,0:T(8,128)(2,1)S(1)} %get-tuple-element.76), channel_id=1, source_target_pairs={{0,1},{1,0},{2,3},{3,2},{4,5},{5,4},{6,7},{7,6},{8,9},{9,8},{10,11... | collective-permute-start | bytes 147464 | tf_op jit(solution)/shard_map/ppermute | solution.py:23
  52.3 9.7 %collective-permute-start.7 = (bf16[256,384]{1,0:T(8,128)(2,1)S(1)}, bf16[256,384]{1,0:T(8,128)(2,1)S(1)}, u32[]{:S(2)}, u32[]{:S(2)}) collective-permute-start(bf16[256,384]{1,0:T(8,128)(2,1)S(1)} %pad_maximum_fusion.1.refs_0_), channel_id=1, source_target_pairs={{0,8},{8,16},{16,24},{24,0},{1,9},{9,17},{17,25},{25,1},{2,10},{10... | collective-permute-start | bytes 589832 | tf_op jit(solution)/shard_map/ppermute | solution.py:341
  53.9 10.6 %collective-permute-start.8 = (bf16[256,384]{1,0:T(8,128)(2,1)S(1)}, bf16[256,384]{1,0:T(8,128)(2,1)S(1)}, u32[]{:S(2)}, u32[]{:S(2)}) collective-permute-start(bf16[256,384]{1,0:T(8,128)(2,1)S(1)} %pad_maximum_fusion.1.refs_0_), channel_id=1, source_target_pairs={{8,0},{16,8},{24,16},{0,24},{9,1},{17,9},{25,17},{1,25},{10,2},{18... | collective-permute-start | bytes 589832 | tf_op jit(solution)/shard_map/ppermute | solution.py:342
  56.1 17.3 %collective-permute-start.9 = (bf16[256,384]{1,0:T(8,128)(2,1)S(1)}, bf16[256,384]{1,0:T(8,128)(2,1)S(1)}, u32[]{:S(2)}, u32[]{:S(2)}) collective-permute-start(bf16[256,384]{1,0:T(8,128)(2,1)S(1)} %pad_maximum_fusion.1.refs_0_), channel_id=1, source_target_pairs={{0,16},{8,24},{16,0},{24,8},{1,17},{9,25},{17,1},{25,9},{2,18},{10... | collective-permute-start | bytes 589832 | tf_op jit(solution)/shard_map/ppermute | solution.py:23
  61.9 11.5 %collective-permute-start.13 = (bf16[256,384]{1,0:T(8,128)(2,1)S(1)}, bf16[256,384]{1,0:T(8,128)(2,1)S(1)}, u32[]{:S(2)}, u32[]{:S(2)}) collective-permute-start(bf16[256,384]{1,0:T(8,128)(2,1)S(1)} %pad_maximum_fusion.1.refs_0_), channel_id=1, source_target_pairs={{0,4},{4,0},{1,5},{5,1},{2,6},{6,2},{3,7},{7,3},{8,12},{12,8},{9,1... | collective-permute-start | bytes 589832 | tf_op jit(solution)/shard_map/ppermute | solution.py:23
  75.8 32.0 %copy-start.28 = (s32[2,4,64]{2,1,0:T(4,128)S(1)}, s32[2,4,64]{2,1,0:T(4,128)}, u32[]{:S(2)}) copy-start(s32[2,4,64]{2,1,0:T(4,128)} %constant.464) | copy-start | bytes 6148
  75.8 33.6 %all-to-all-start.1 = ((bf16[8,160,384]{2,1,0:T(8,128)(2,1)}), bf16[8,160,384]{2,1,0:T(8,128)(2,1)}, u32[]{:S(2)}, u32[]{:S(2)}) async-start(bf16[8,160,384]{2,1,0:T(8,128)(2,1)} %get-tuple-element.65), calls=%async_computation.1 | async-start | bytes 1966080 | tf_op jit(solution)/shard_map/all_to_all | solution.py:399
  81.2 25.7 %collective-permute-start.17 = (bf16[128,2560]{1,0:T(8,128)(2,1)}, bf16[128,2560]{1,0:T(8,128)(2,1)}, u32[]{:S(2)}, u32[]{:S(2)}) collective-permute-start(bf16[128,2560]{1,0:T(8,128)(2,1)} %copy-done.6), channel_id=1, source_target_pairs={{0,2},{1,3},{2,0},{3,1},{4,6},{5,7},{6,4},{7,5},{8,10},{9,11},{10,... | collective-permute-start | bytes 1966088 | tf_op jit(solution)/shard_map/ppermute | solution.py:23
  82.6 15.7 %collective-permute-start.14 = (bf16[256,384]{1,0:T(8,128)(2,1)S(1)}, bf16[256,384]{1,0:T(8,128)(2,1)S(1)}, u32[]{:S(2)}, u32[]{:S(2)}) collective-permute-start(bf16[256,384]{1,0:T(8,128)(2,1)S(1)} %collective-permute-done.7.refs_1_), channel_id=1, source_target_pairs={{0,4},{4,0},{1,5},{5,1},{2,6},{6,2},{3,7},{7,3},{8,12},{12,8},{9,1... | collective-permute-start | bytes 589832 | tf_op jit(solution)/shard_map/ppermute | solution.py:23
  85.4 18.5 %collective-permute-start.15 = (bf16[256,384]{1,0:T(8,128)(2,1)S(1)}, bf16[256,384]{1,0:T(8,128)(2,1)S(1)}, u32[]{:S(2)}, u32[]{:S(2)}) collective-permute-start(bf16[256,384]{1,0:T(8,128)(2,1)S(1)} %collective-permute-done.8.refs_2_), channel_id=1, source_target_pairs={{0,4},{4,0},{1,5},{5,1},{2,6},{6,2},{3,7},{7,3},{8,12},{12,8},{9,1... | collective-permute-start | bytes 589832 | tf_op jit(solution)/shard_map/ppermute | solution.py:23
  86.1 20.2 %collective-permute-start.16 = (bf16[256,384]{1,0:T(8,128)(2,1)S(1)}, bf16[256,384]{1,0:T(8,128)(2,1)S(1)}, u32[]{:S(2)}, u32[]{:S(2)}) collective-permute-start(bf16[256,384]{1,0:T(8,128)(2,1)S(1)} %collective-permute-done.9.refs_3_), channel_id=1, source_target_pairs={{0,4},{4,0},{1,5},{5,1},{2,6},{6,2},{3,7},{7,3},{8,12},{12,8},{9,1... | collective-permute-start | bytes 589832 | tf_op jit(solution)/shard_map/ppermute | solution.py:23
  88.8 20.4 %collective-permute-start.19 = (bf16[128,2560]{1,0:T(8,128)(2,1)}, bf16[128,2560]{1,0:T(8,128)(2,1)}, u32[]{:S(2)}, u32[]{:S(2)}) collective-permute-start(bf16[128,2560]{1,0:T(8,128)(2,1)} %copy-done.6), channel_id=1, source_target_pairs={{0,1},{1,0},{2,3},{3,2},{4,5},{5,4},{6,7},{7,6},{8,9},{9,8},{10,11... | collective-permute-start | bytes 1966088 | tf_op jit(solution)/shard_map/ppermute | solution.py:23
  99.0 10.2 %collective-permute-start.18 = (bf16[128,2560]{1,0:T(8,128)(2,1)}, bf16[128,2560]{1,0:T(8,128)(2,1)}, u32[]{:S(2)}, u32[]{:S(2)}) collective-permute-start(bf16[128,2560]{1,0:T(8,128)(2,1)} %copy-done.2), channel_id=1, source_target_pairs={{0,1},{1,0},{2,3},{3,2},{4,5},{5,4},{6,7},{7,6},{8,9},{9,8},{10,11... | collective-permute-start | bytes 1966088 | tf_op jit(solution)/shard_map/ppermute | solution.py:23
  104.5 4.7 %collective-permute-start.20 = (bf16[128,2560]{1,0:T(8,128)(2,1)}, bf16[128,2560]{1,0:T(8,128)(2,1)}, u32[]{:S(2)}, u32[]{:S(2)}) collective-permute-start(bf16[128,2560]{1,0:T(8,128)(2,1)} %copy-done.4), channel_id=1, source_target_pairs={{0,1},{1,0},{2,3},{3,2},{4,5},{5,4},{6,7},{7,6},{8,9},{9,8},{10,11... | collective-permute-start | bytes 1966088 | tf_op jit(solution)/shard_map/ppermute | solution.py:23
  107.0 2.4 %collective-permute-start.21 = (bf16[128,2560]{1,0:T(8,128)(2,1)}, bf16[128,2560]{1,0:T(8,128)(2,1)}, u32[]{:S(2)}, u32[]{:S(2)}) collective-permute-start(bf16[128,2560]{1,0:T(8,128)(2,1)} %collective-permute-done.17.refs_3_), channel_id=1, source_target_pairs={{0,1},{1,0},{2,3},{3,2},{4,5},{5,4},{6,7},{7,6},{8,9},{9,8},{10,11... | collective-permute-start | bytes 1966088 | tf_op jit(solution)/shard_map/ppermute | solution.py:23
  112.7 6.4 %copy-start.17 = (bf16[256,384]{1,0:T(8,128)(2,1)S(1)}, bf16[256,384]{1,0:T(8,128)(2,1)}, u32[]{:S(2)}) copy-start(bf16[256,384]{1,0:T(8,128)(2,1)} %copy-done.16) | copy-start | bytes 589828
  112.7 6.4 %copy-start.19 = (bf16[256,384]{1,0:T(8,128)(2,1)S(1)}, bf16[256,384]{1,0:T(8,128)(2,1)}, u32[]{:S(2)}) copy-start(bf16[256,384]{1,0:T(8,128)(2,1)} %copy-done.18) | copy-start | bytes 589828
  112.7 6.4 %copy-start.21 = (bf16[256,384]{1,0:T(8,128)(2,1)S(1)}, bf16[256,384]{1,0:T(8,128)(2,1)}, u32[]{:S(2)}) copy-start(bf16[256,384]{1,0:T(8,128)(2,1)} %copy-done.20) | copy-start | bytes 589828
  125.5 46.9 %copy-start.1 = (bf16[2048,320]{0,1:T(8,128)(2,1)S(1)}, bf16[2048,320]{0,1:T(8,128)(2,1)}, u32[]{:S(2)}) copy-start(bf16[2048,320]{0,1:T(8,128)(2,1)} %param.17) | copy-start | bytes 3932164
  131.8 6.4 %collective-permute-start.27 = (bf16[512,128]{1,0:T(8,128)(2,1)S(1)}, bf16[512,128]{1,0:T(8,128)(2,1)S(1)}, u32[]{:S(2)}, u32[]{:S(2)}) collective-permute-start(bf16[512,128]{1,0:T(8,128)(2,1)S(1)} %get-tuple-element.70), channel_id=1, source_target_pairs={{0,4},{4,0},{1,5},{5,1},{2,6},{6,2},{3,7},{7,3},{8,12},{12,8},{9,1... | collective-permute-start | bytes 393224 | tf_op jit(solution)/shard_map/ppermute | solution.py:23
  132.2 8.2 %collective-permute-start.22 = (bf16[512,128]{1,0:T(8,128)(2,1)S(1)}, bf16[512,128]{1,0:T(8,128)(2,1)S(1)}, u32[]{:S(2)}, u32[]{:S(2)}) collective-permute-start(bf16[512,128]{1,0:T(8,128)(2,1)S(1)} %get-tuple-element.67), channel_id=1, source_target_pairs={{0,4},{4,0},{1,5},{5,1},{2,6},{6,2},{3,7},{7,3},{8,12},{12,8},{9,1... | collective-permute-start | bytes 393224 | tf_op jit(solution)/shard_map/ppermute | solution.py:23
  138.2 19.9 %collective-permute-start.30 = (bf16[512,256]{1,0:T(8,128)(2,1)S(1)}, bf16[512,256]{1,0:T(8,128)(2,1)S(1)}, u32[]{:S(2)}, u32[]{:S(2)}) collective-permute-start(bf16[512,256]{1,0:T(8,128)(2,1)S(1)} %constant_dynamic-update-slice_fusion.2.refs_0_), channel_id=1, source_target_pairs={{0,16},{8,24},{16,0},{24,8},{1,17},{9,25},{17,1},{25,9},{2,18},{10... | collective-permute-start | bytes 786440 | tf_op jit(solution)/shard_map/ppermute | solution.py:23
  140.5 23.5 %collective-permute-start.25 = (bf16[512,256]{1,0:T(8,128)(2,1)S(1)}, bf16[512,256]{1,0:T(8,128)(2,1)S(1)}, u32[]{:S(2)}, u32[]{:S(2)}) collective-permute-start(bf16[512,256]{1,0:T(8,128)(2,1)S(1)} %constant_dynamic-update-slice_fusion.refs_0_), channel_id=1, source_target_pairs={{0,16},{8,24},{16,0},{24,8},{1,17},{9,25},{17,1},{25,9},{2,18},{10... | collective-permute-start | bytes 786440 | tf_op jit(solution)/shard_map/ppermute | solution.py:23
  142.4 22.8 %collective-permute-start.28 = (bf16[512,256]{1,0:T(8,128)(2,1)S(1)}, bf16[512,256]{1,0:T(8,128)(2,1)S(1)}, u32[]{:S(2)}, u32[]{:S(2)}) collective-permute-start(bf16[512,256]{1,0:T(8,128)(2,1)S(1)} %constant_dynamic-update-slice_fusion.2.refs_0_), channel_id=1, source_target_pairs={{0,8},{8,16},{16,24},{1,9},{9,17},{17,25},{2,10},{10,18},{18,26},{... | collective-permute-start | bytes 786440 | tf_op jit(solution)/shard_map/ppermute | solution.py:334
  145.8 21.0 %collective-permute-start.29 = (bf16[512,256]{1,0:T(8,128)(2,1)S(1)}, bf16[512,256]{1,0:T(8,128)(2,1)S(1)}, u32[]{:S(2)}, u32[]{:S(2)}) collective-permute-start(bf16[512,256]{1,0:T(8,128)(2,1)S(1)} %constant_dynamic-update-slice_fusion.2.refs_0_), channel_id=1, source_target_pairs={{8,0},{16,8},{24,16},{9,1},{17,9},{25,17},{10,2},{18,10},{26,18},{... | collective-permute-start | bytes 786440 | tf_op jit(solution)/shard_map/ppermute | solution.py:335
  158.1 14.3 %collective-permute-start.31 = (bf16[512,256]{1,0:T(8,128)(2,1)S(1)}, bf16[512,256]{1,0:T(8,128)(2,1)S(1)}, u32[]{:S(2)}, u32[]{:S(2)}) collective-permute-start(bf16[512,256]{1,0:T(8,128)(2,1)S(1)} %collective-permute-done.30.refs_4_), channel_id=1, source_target_pairs={{8,0},{16,24},{9,1},{17,25},{10,2},{18,26},{11,3},{19,27},{12,4},{... | collective-permute-start | bytes 786440 | tf_op jit(solution)/shard_map/ppermute | solution.py:336
  159.4 15.0 %collective-permute-start.23 = (bf16[512,256]{1,0:T(8,128)(2,1)S(1)}, bf16[512,256]{1,0:T(8,128)(2,1)S(1)}, u32[]{:S(2)}, u32[]{:S(2)}) collective-permute-start(bf16[512,256]{1,0:T(8,128)(2,1)S(1)} %constant_dynamic-update-slice_fusion.refs_0_), channel_id=1, source_target_pairs={{0,8},{8,16},{16,24},{1,9},{9,17},{17,25},{2,10},{10,18},{18,26},{... | collective-permute-start | bytes 786440 | tf_op jit(solution)/shard_map/ppermute | solution.py:334
  164.0 14.1 %collective-permute-start.24 = (bf16[512,256]{1,0:T(8,128)(2,1)S(1)}, bf16[512,256]{1,0:T(8,128)(2,1)S(1)}, u32[]{:S(2)}, u32[]{:S(2)}) collective-permute-start(bf16[512,256]{1,0:T(8,128)(2,1)S(1)} %constant_dynamic-update-slice_fusion.refs_0_), channel_id=1, source_target_pairs={{8,0},{16,8},{24,16},{9,1},{17,9},{25,17},{10,2},{18,10},{26,18},{... | collective-permute-start | bytes 786440 | tf_op jit(solution)/shard_map/ppermute | solution.py:335
  165.3 16.8 %collective-permute-start.26 = (bf16[512,256]{1,0:T(8,128)(2,1)S(1)}, bf16[512,256]{1,0:T(8,128)(2,1)S(1)}, u32[]{:S(2)}, u32[]{:S(2)}) collective-permute-start(bf16[512,256]{1,0:T(8,128)(2,1)S(1)} %collective-permute-done.25.refs_4_), channel_id=1, source_target_pairs={{8,0},{16,24},{9,1},{17,25},{10,2},{18,26},{11,3},{19,27},{12,4},{... | collective-permute-start | bytes 786440 | tf_op jit(solution)/shard_map/ppermute | solution.py:336
  184.9 1.7 collective-permute-start.32
  186.7 6.3 %collective-permute-start.33 = (bf16[4,32,640]{2,1,0:T(8,128)(2,1)S(1)}, bf16[4,32,640]{2,1,0:T(8,128)(2,1)S(1)}, u32[]{:S(2)}, u32[]{:S(2)}) collective-permute-start(bf16[4,32,640]{2,1,0:T(8,128)(2,1)S(1)} %fusion.1), channel_id=1, source_target_pairs={{0,2},{1,3},{2,0},{3,1},{4,6},{5,7},{6,4},{7,5},{8,10},{9,11},{10,... | collective-permute-start | bytes 491528 | tf_op jit(solution)/shard_map/ppermute | solution.py:23
  193.2 11.6 %collective-permute-start.34 = (bf16[128,640]{1,0:T(8,128)(2,1)S(1)}, bf16[128,640]{1,0:T(8,128)(2,1)S(1)}, u32[]{:S(2)}, u32[]{:S(2)}) collective-permute-start(bf16[128,640]{1,0:T(8,128)(2,1)S(1)} %pad_maximum_fusion.2), channel_id=1, source_target_pairs={{0,0},{1,8},{2,16},{3,24},{4,4},{5,12},{6,20},{7,28},{8,1},{9,9},{... | collective-permute-start | bytes 491528 | tf_op jit(solution)/shard_map/ppermute | solution.py:534
  (19 other events, 43.2 us)

commit v10 on v8

--- a/solution.py
+++ b/solution.py
@@ -392,9 +392,7 @@
         quarter = row_count // heads_axis
         mine = lax.dynamic_slice_in_dim(tokens, h * quarter, quarter, 0)
         mine, before, after, far = ring_pieces(mine, "outer")
-        begin, before, after, far, edge = lax.optimization_barrier(
-            (sent[0], before, after, far, edge)
-        )
+        begin, before, edge = lax.optimization_barrier((sent[0], before, edge))
         weight_first = exchange(begin)
         near = jnp.concatenate([mine, before, after, far], axis=0)
         beside = swap(near, "inner", 1)

time: 195 us -> 204 us (1.046)
  starting transfers between devices: 49.8 us -> 59.6 us
    ppermute x20, starting transfers between devices: 17.3 us -> 26.6 us  [swap(): lax.ppermute(block, axis, [(i, i ^ bit) for i in range(lax.axis_size(axis...]
    ppermute x2, waiting for transfers between devices: 6.24 us -> 2.92 us  [ring_pieces(): after = lax.ppermute(block, axis, [((i + 1) % 4, i) for i in range(4)])]
    ppermute x2, waiting for transfers between devices: 2.57 us -> 5.04 us  [ring_pieces(): before = lax.ppermute(block, axis, [(i, (i + 1) % 4) for i in range(4)])]
  transfers between devices with their start and end apart: 34 -> 34, of which waited for: 16 -> 15; matrix products, arithmetic and copies ran while one was open for 4% -> 4% of each run, Pallas kernels for 8% -> 8%
where the time goes in v10:
time: 204 us
  waiting for transfers between devices  96.5 us (47%)
  starting transfers between devices  59.6 us (29%)
  Pallas kernels  33.9 us (17%)
  local copies, waits for them, and re-layouts  7.9 us (4%)
  other arithmetic  5.33 us (3%)
    ppermute x20, waiting for transfers between devices, swap(): lax.ppermute(block, axis, [(i, i ^ bit) for i in range(lax.axis_size(axis...  64.9 us
    ppermute x20, starting transfers between devices, swap(): lax.ppermute(block, axis, [(i, i ^ bit) for i in range(lax.axis_size(axis...  26.6 us
    ppermute x1, waiting for transfers between devices, shards(): return lax.ppermute(result, ('outer', 'inner', 'head'), route)  9.67 us
    ppermute x2, waiting for transfers between devices, line_pieces(): passed = lax.ppermute(far, axis, [(1, 0), (2, 3)])  9.42 us
    all_to_all x2, starting transfers between devices, exchange(): lax.all_to_all(block, seq_axes, split_axis=0, concat_axis=0, tiled=True)  9.39 us
    pallas_call x1, Pallas kernels, compress(): pl.pallas_call(compress_kernel, out_shape=jax.ShapeDtypeStruct((G, blocks...  8.45 us
    pallas_call x2, Pallas kernels, attend(): pl.pallas_call(kernel, out_shape=(shape,) * outputs, in_specs=[pl.BlockSp...  8.36 us
    ppermute x2, starting transfers between devices, line_pieces(): up = lax.ppermute(block, axis, [(i, i + 1) for i in range(3)])  7.23 us
  transfers between devices with their start and end apart: 34, of which 15 were waited for; matrix products, arithmetic and copies ran while one was open for 4% of the time, Pallas kernels for 8%

profile of v10, /device:TPU:2, one launch (start us, length us, event | category | flops | bytes accessed | tf_op | source)
XLA Modules:
  0.0 203.7 jit_solution(15602439936871534595)
XLA Ops:
  1.5 1.9 collective-permute-start.1
  3.5 1.6 collective-permute-start
  5.1 1.5 collective-permute-start.5
  6.6 5.7 %cut.1 = (bf16[8,160,384]{2,1,0:T(8,128)(2,1)}, bf16[8,160,384]{2,1,0:T(8,128)(2,1)}) custom-call(bf16[320,3072]{1,0:T(8,128)(2,1)} %in_ref.1), custom_call_target="tpu_custom_call" | custom-call | tf_op jit(solution)/shard_map/cut/pallas_call | solution.py:129
  13.0 4.9 %all-to-all-start = ((bf16[8,160,384]{2,1,0:T(8,128)(2,1)}), bf16[8,160,384]{2,1,0:T(8,128)(2,1)S(1)}, u32[]{:S(2)}, u32[]{:S(2)}) async-start(bf16[8,160,384]{2,1,0:T(8,128)(2,1)} %get-tuple-element.35), calls=%async_computation | async-start | bytes 1966080 | tf_op jit(solution)/shard_map/all_to_all | solution.py:380
  17.8 2.9 %collective-permute-start.10 = (bf16[32,2560]{1,0:T(8,128)(2,1)S(1)}, bf16[32,2560]{1,0:T(8,128)(2,1)}, u32[]{:S(2)}, u32[]{:S(2)}) collective-permute-start(bf16[32,2560]{1,0:T(8,128)(2,1)S(1)} %constant_dynamic-slice_fusion), channel_id=1, source_target_pairs={{0,16},{8,24},{16,0},{24,8},{1,17},{9,25},{17,1},{25,9},{2,18},{10... | collective-permute-start | bytes 491528 | tf_op jit(solution)/shard_map/ppermute | solution.py:23
  20.8 1.5 collective-permute-start.9
  24.4 8.5 %compress.1 = bf16[4,64,384]{2,1,0:T(8,128)(2,1)} custom-call(bf16[1024,768]{1,0:T(8,128)(2,1)} %raw_keys.1, bf16[1024,512]{1,0:T(8,128)(2,1)} %raw_values.1, bf16[16,768]{1,0:T(8,128)(2,1)} %slice.20.edge_keys, bf16[16,512]{1,0:T(8,128)(2,1)} %slice.21.edge_values, bf16[192,768]{1,0:T(8,128)(2,1)} %key_expand.1, f32[32,768]{1,0:T(8,128)} %key_mix.1, ...), custom_call_target="tpu_custom_call" | custom-call | flops 2013265920 | bytes 1572864 | tf_op jit(solution)/shard_map/compress/pallas_call | solution.py:105
  34.1 4.2 %collective-permute-start.3 = (bf16[64,384]{1,0:T(8,128)(2,1)S(1)}, bf16[64,384]{1,0:T(8,128)(2,1)S(1)}, u32[]{:S(2)}, u32[]{:S(2)}) collective-permute-start(bf16[64,384]{1,0:T(8,128)(2,1)S(1)} %get-tuple-element.49), channel_id=1, source_target_pairs={{0,2},{1,3},{2,0},{3,1},{4,6},{5,7},{6,4},{7,5},{8,10},{9,11},{10,... | collective-permute-start | bytes 147464 | tf_op jit(solution)/shard_map/ppermute | solution.py:23
  38.3 10.4 %collective-permute-done.10 = bf16[32,2560]{1,0:T(8,128)(2,1)} collective-permute-done((bf16[32,2560]{1,0:T(8,128)(2,1)S(1)}, bf16[32,2560]{1,0:T(8,128)(2,1)}, u32[]{:S(2)}, u32[]{:S(2)}) %collective-permute-start.10) | collective-permute-done | bytes 163872 | tf_op jit(solution)/shard_map/ppermute | solution.py:23
  48.7 4.0 %collective-permute-start.2 = (bf16[64,384]{1,0:T(8,128)(2,1)S(1)}, bf16[64,384]{1,0:T(8,128)(2,1)S(1)}, u32[]{:S(2)}, u32[]{:S(2)}) collective-permute-start(bf16[64,384]{1,0:T(8,128)(2,1)S(1)} %get-tuple-element.50), channel_id=1, source_target_pairs={{0,1},{1,0},{2,3},{3,2},{4,5},{5,4},{6,7},{7,6},{8,9},{9,8},{10,11... | collective-permute-start | bytes 147464 | tf_op jit(solution)/shard_map/ppermute | solution.py:23
  52.7 1.9 pad_maximum_fusion.1.refs_0_
  55.8 3.1 %collective-permute-start.6 = (bf16[256,384]{1,0:T(8,128)(2,1)S(1)}, bf16[256,384]{1,0:T(8,128)(2,1)S(1)}, u32[]{:S(2)}, u32[]{:S(2)}) collective-permute-start(bf16[256,384]{1,0:T(8,128)(2,1)S(1)} %pad_maximum_fusion.2), channel_id=1, source_target_pairs={{0,8},{8,16},{16,24},{24,0},{1,9},{9,17},{17,25},{25,1},{2,10},{10... | collective-permute-start | bytes 589832 | tf_op jit(solution)/shard_map/ppermute | solution.py:322
  58.8 1.1 collective-permute-start.7
  60.5 5.0 %collective-permute-done.6 = bf16[256,384]{1,0:T(8,128)(2,1)S(1)} collective-permute-done((bf16[256,384]{1,0:T(8,128)(2,1)S(1)}, bf16[256,384]{1,0:T(8,128)(2,1)S(1)}, u32[]{:S(2)}, u32[]{:S(2)}) %collective-permute-start.6) | collective-permute-done | bytes 196640 | tf_op jit(solution)/shard_map/ppermute | solution.py:322
  65.6 2.9 %collective-permute-done.7 = bf16[256,384]{1,0:T(8,128)(2,1)S(1)} collective-permute-done((bf16[256,384]{1,0:T(8,128)(2,1)S(1)}, bf16[256,384]{1,0:T(8,128)(2,1)S(1)}, u32[]{:S(2)}, u32[]{:S(2)}) %collective-permute-start.7) | collective-permute-done | bytes 196640 | tf_op jit(solution)/shard_map/ppermute | solution.py:323
  68.5 8.9 %collective-permute-done.8 = bf16[256,384]{1,0:T(8,128)(2,1)S(1)} collective-permute-done((bf16[256,384]{1,0:T(8,128)(2,1)S(1)}, bf16[256,384]{1,0:T(8,128)(2,1)S(1)}, u32[]{:S(2)}, u32[]{:S(2)}) %collective-permute-start.8) | collective-permute-done | bytes 196640 | tf_op jit(solution)/shard_map/ppermute | solution.py:23
  78.4 4.5 %all-to-all-start.1 = ((bf16[8,160,384]{2,1,0:T(8,128)(2,1)}), bf16[8,160,384]{2,1,0:T(8,128)(2,1)}, u32[]{:S(2)}, u32[]{:S(2)}) async-start(bf16[8,160,384]{2,1,0:T(8,128)(2,1)} %get-tuple-element.36), calls=%async_computation.1 | async-start | bytes 1966080 | tf_op jit(solution)/shard_map/all_to_all | solution.py:380
  83.0 1.4 collective-permute-start.13
  84.4 1.6 collective-permute-start.18
  86.9 13.1 %collective-permute-done.13.refs_3_ = bf16[128,2560]{1,0:T(8,128)(2,1)} collective-permute-done((bf16[128,2560]{1,0:T(8,128)(2,1)}, bf16[128,2560]{1,0:T(8,128)(2,1)}, u32[]{:S(2)}, u32[]{:S(2)}) %collective-permute-start.13) | collective-permute-done | bytes 655392 | tf_op jit(solution)/shard_map/ppermute | solution.py:23
  100.8 12.2 %collective-permute-done.18 = bf16[1024,384]{1,0:T(8,128)(2,1)} collective-permute-done((bf16[1024,384]{1,0:T(8,128)(2,1)}, bf16[1024,384]{1,0:T(8,128)(2,1)}, u32[]{:S(2)}, u32[]{:S(2)}) %collective-permute-start.18) | collective-permute-done | bytes 786464 | tf_op jit(solution)/shard_map/ppermute | solution.py:23
  113.0 1.5 select_bitcast_fusion.1
  114.5 1.4 pad_maximum_fusion
  115.9 6.6 %project.1.refs_0_ = bf16[1024,384]{1,0:T(8,128)(2,1)S(1)} custom-call(bf16[128,2560]{1,0:T(8,128)(2,1)} %pad_maximum_fusion.1.refs_0_, bf16[128,2560]{1,0:T(8,128)(2,1)} %collective-permute-done.11.refs_1_, bf16[128,2560]{1,0:T(8,128)(2,1)} %collective-permute-done.12.refs_2_, bf16[128,2560]{1,0:T(8,128)(2,1)} %collective-permute-done.13.refs_3_, ...), custom_call_target="tpu_custom_call" | custom-call | flops 2013265920 | bytes 5242880 | tf_op jit(solution)/shard_map/project/pallas_call | solution.py:178
  122.5 4.2 %attend.2 = (bf16[512,128]{1,0:T(8,128)(2,1)S(1)}, bf16[512,128]{1,0:T(8,128)(2,1)S(1)}) custom-call(s32[3]{0:T(128)S(1)} %pad_add_fusion.here_ref.place_ref, bf16[1024,384]{1,0:T(8,128)(2,1)S(1)} %project.1.refs_0_, bf16[2048,384]{1,0:T(8,128)(2,1)S(1)} %bitcast.61, s32[1,2048]{1,0:T(1,128)S(1)} %sub.145.refs_2_, s32[1024,1]{1,0:T(8,128)S(1)} %add.630.refs_3_), custom_call_target="tpu_custom_call" | custom-call | flops 1342177280 | bytes 1572864 | tf_op jit(solution)/shard_map/attend/pallas_call | solution.py:239
  126.8 4.2 %attend.3 = (bf16[512,128]{1,0:T(8,128)(2,1)S(1)}, bf16[512,128]{1,0:T(8,128)(2,1)S(1)}) custom-call(s32[3]{0:T(128)S(1)} %pad_add_fusion.here_ref.place_ref, bf16[1024,384]{1,0:T(8,128)(2,1)S(1)} %project.1.refs_0_, bf16[2048,384]{1,0:T(8,128)(2,1)S(1)} %bitcast.62, s32[1,2048]{1,0:T(1,128)S(1)} %sub.145.refs_2_, s32[1024,1]{1,0:T(8,128)S(1)} %add.630.refs_3_), custom_call_target="tpu_custom_call" | custom-call | flops 1342177280 | bytes 1572864 | tf_op jit(solution)/shard_map/attend/pallas_call | solution.py:239
  131.6 1.5 collective-permute-start.19
  133.1 3.8 %collective-permute-done.24 = bf16[512,128]{1,0:T(8,128)(2,1)S(1)} collective-permute-done((bf16[512,128]{1,0:T(8,128)(2,1)S(1)}, bf16[512,128]{1,0:T(8,128)(2,1)S(1)}, u32[]{:S(2)}, u32[]{:S(2)}) %collective-permute-start.24) | collective-permute-done | bytes 131104 | tf_op jit(solution)/shard_map/ppermute | solution.py:23
  137.0 2.8 %collective-permute-start.27 = (bf16[512,256]{1,0:T(8,128)(2,1)S(1)}, bf16[512,256]{1,0:T(8,128)(2,1)S(1)}, u32[]{:S(2)}, u32[]{:S(2)}) collective-permute-start(bf16[512,256]{1,0:T(8,128)(2,1)S(1)} %constant_dynamic-update-slice_fusion.2.refs_0_), channel_id=1, source_target_pairs={{0,16},{8,24},{16,0},{24,8},{1,17},{9,25},{17,1},{25,9},{2,18},{10... | collective-permute-start | bytes 786440 | tf_op jit(solution)/shard_map/ppermute | solution.py:23
  139.8 1.8 collective-permute-start.22
  141.7 2.7 %collective-permute-start.25 = (bf16[512,256]{1,0:T(8,128)(2,1)S(1)}, bf16[512,256]{1,0:T(8,128)(2,1)S(1)}, u32[]{:S(2)}, u32[]{:S(2)}) collective-permute-start(bf16[512,256]{1,0:T(8,128)(2,1)S(1)} %constant_dynamic-update-slice_fusion.2.refs_0_), channel_id=1, source_target_pairs={{0,8},{8,16},{16,24},{1,9},{9,17},{17,25},{2,10},{10,18},{18,26},{... | collective-permute-start | bytes 786440 | tf_op jit(solution)/shard_map/ppermute | solution.py:315
  144.3 1.3 collective-permute-start.26
  145.6 9.9 %collective-permute-done.27.refs_4_ = bf16[512,256]{1,0:T(8,128)(2,1)S(1)} collective-permute-done((bf16[512,256]{1,0:T(8,128)(2,1)S(1)}, bf16[512,256]{1,0:T(8,128)(2,1)S(1)}, u32[]{:S(2)}, u32[]{:S(2)}) %collective-permute-start.27) | collective-permute-done | bytes 262176 | tf_op jit(solution)/shard_map/ppermute | solution.py:23
  155.5 1.3 collective-permute-start.28
  156.8 4.6 %collective-permute-start.20 = (bf16[512,256]{1,0:T(8,128)(2,1)S(1)}, bf16[512,256]{1,0:T(8,128)(2,1)S(1)}, u32[]{:S(2)}, u32[]{:S(2)}) collective-permute-start(bf16[512,256]{1,0:T(8,128)(2,1)S(1)} %constant_dynamic-update-slice_fusion.refs_0_), channel_id=1, source_target_pairs={{0,8},{8,16},{16,24},{1,9},{9,17},{17,25},{2,10},{10,18},{18,26},{... | collective-permute-start | bytes 786440 | tf_op jit(solution)/shard_map/ppermute | solution.py:315
  161.4 1.3 collective-permute-start.21
  162.7 1.5 collective-permute-start.23
  165.2 5.6 %collective-permute-done.28.refs_3_ = bf16[512,256]{1,0:T(8,128)(2,1)S(1)} collective-permute-done((bf16[512,256]{1,0:T(8,128)(2,1)S(1)}, bf16[512,256]{1,0:T(8,128)(2,1)S(1)}, u32[]{:S(2)}, u32[]{:S(2)}) %collective-permute-start.28) | collective-permute-done | bytes 262176 | tf_op jit(solution)/shard_map/ppermute | solution.py:317
  170.8 2.0 expel.2.refs_7_
  172.8 3.6 %collective-permute-done.21.refs_2_ = bf16[512,256]{1,0:T(8,128)(2,1)S(1)} collective-permute-done((bf16[512,256]{1,0:T(8,128)(2,1)S(1)}, bf16[512,256]{1,0:T(8,128)(2,1)S(1)}, u32[]{:S(2)}, u32[]{:S(2)}) %collective-permute-start.21) | collective-permute-done | bytes 262176 | tf_op jit(solution)/shard_map/ppermute | solution.py:316
  176.4 3.8 %collective-permute-done.23.refs_3_ = bf16[512,256]{1,0:T(8,128)(2,1)S(1)} collective-permute-done((bf16[512,256]{1,0:T(8,128)(2,1)S(1)}, bf16[512,256]{1,0:T(8,128)(2,1)S(1)}, u32[]{:S(2)}, u32[]{:S(2)}) %collective-permute-start.23) | collective-permute-done | bytes 262176 | tf_op jit(solution)/shard_map/ppermute | solution.py:317
  180.2 2.8 %expel.3 = (f32[4,2,32,640]{3,2,1,0:T(8,128)S(1)}, bf16[4,2,32,640]{3,2,1,0:T(8,128)(2,1)S(1)}) custom-call(s32[3]{0:T(128)S(1)} %pad_add_fusion.here_ref.place_ref, bf16[512,256]{1,0:T(8,128)(2,1)S(1)} %constant_dynamic-update-slice_fusion.refs_0_, bf16[512,256]{1,0:T(8,128)(2,1)S(1)} %collective-permute-done.20.refs_1_, ...), custom_call_target="tpu_custom_call" | custom-call | flops 671088640 | bytes 1310720 | tf_op jit(solution)/shard_map/expel/pallas_call | solution.py:299
  183.1 1.6 collective-permute-done.29
  184.8 1.4 collective-permute-start.30
  186.3 4.9 %collective-permute-done.30 = bf16[4,32,640]{2,1,0:T(8,128)(2,1)S(1)} collective-permute-done((bf16[4,32,640]{2,1,0:T(8,128)(2,1)S(1)}, bf16[4,32,640]{2,1,0:T(8,128)(2,1)S(1)}, u32[]{:S(2)}, u32[]{:S(2)}) %collective-permute-start.30) | collective-permute-done | bytes 163872 | tf_op jit(solution)/shard_map/ppermute | solution.py:23
  191.4 1.9 collective-permute-start.31
  193.3 9.7 %collective-permute-done.31 = bf16[128,640]{1,0:T(8,128)(2,1)S(1)} collective-permute-done((bf16[128,640]{1,0:T(8,128)(2,1)S(1)}, bf16[128,640]{1,0:T(8,128)(2,1)S(1)}, u32[]{:S(2)}, u32[]{:S(2)}) %collective-permute-start.31) | collective-permute-done | bytes 163872 | tf_op jit(solution)/shard_map/ppermute | solution.py:500
  (79 shorter events, 12.8 us)
Async XLA Ops:
  0.0 3.5 %copy-start = (bf16[128,2560]{1,0:T(8,128)(2,1)S(1)}, bf16[128,2560]{1,0:T(8,128)(2,1)}, u32[]{:S(2)}) copy-start(bf16[128,2560]{1,0:T(8,128)(2,1)} %param.13) | copy-start | bytes 1966084
  1.5 3.6 %collective-permute-start.1 = (bf16[16,1280]{1,0:T(8,128)(2,1)S(1)}, bf16[16,1280]{1,0:T(8,128)(2,1)S(1)}, u32[]{:S(2)}, u32[]{:S(2)}) collective-permute-start(bf16[16,1280]{1,0:T(8,128)(2,1)S(1)} %pad_maximum_fusion.4), channel_id=1, source_target_pairs={{1,0},{2,1},{3,2},{4,3},{5,4},{6,5},{7,6},{8,7},{9,8},{10,9},{11,1... | collective-permute-start | bytes 122888 | tf_op jit(solution)/shard_map/ppermute | solution.py:365
  3.5 8.8 %collective-permute-start = (bf16[32,2560]{1,0:T(8,128)(2,1)S(1)}, bf16[32,2560]{1,0:T(8,128)(2,1)S(1)}, u32[]{:S(2)}, u32[]{:S(2)}) collective-permute-start(bf16[32,2560]{1,0:T(8,128)(2,1)S(1)} %constant_dynamic-slice_fusion), channel_id=1, source_target_pairs={{0,8},{8,16},{16,24},{24,0},{1,9},{9,17},{17,25},{25,1},{2,10},{10... | collective-permute-start | bytes 491528 | tf_op jit(solution)/shard_map/ppermute | solution.py:322
  5.1 50.6 %collective-permute-start.5 = (bf16[320,2048]{1,0:T(8,128)(2,1)}, bf16[320,2048]{1,0:T(8,128)(2,1)S(1)}, u32[]{:S(2)}, u32[]{:S(2)}) collective-permute-start(bf16[320,2048]{1,0:T(8,128)(2,1)} %bitcast.58), channel_id=1, source_target_pairs={{0,4},{4,0},{1,5},{5,1},{2,6},{6,2},{3,7},{7,3},{8,12},{12,8},{9,1... | collective-permute-start | bytes 3932168 | tf_op jit(solution)/shard_map/ppermute | solution.py:23
  12.3 9.9 %copy-start.4 = (bf16[768,192]{0,1:T(8,128)(2,1)S(1)}, bf16[768,192]{0,1:T(8,128)(2,1)}, u32[]{:S(2)}) copy-start(bf16[768,192]{0,1:T(8,128)(2,1)} %param.20) | copy-start | bytes 884740
  12.3 0.7 copy-start.5
  13.0 65.4 %all-to-all-start = ((bf16[8,160,384]{2,1,0:T(8,128)(2,1)}), bf16[8,160,384]{2,1,0:T(8,128)(2,1)S(1)}, u32[]{:S(2)}, u32[]{:S(2)}) async-start(bf16[8,160,384]{2,1,0:T(8,128)(2,1)} %get-tuple-element.35), calls=%async_computation | async-start | bytes 1966080 | tf_op jit(solution)/shard_map/all_to_all | solution.py:380
  17.8 30.9 %collective-permute-start.10 = (bf16[32,2560]{1,0:T(8,128)(2,1)S(1)}, bf16[32,2560]{1,0:T(8,128)(2,1)}, u32[]{:S(2)}, u32[]{:S(2)}) collective-permute-start(bf16[32,2560]{1,0:T(8,128)(2,1)S(1)} %constant_dynamic-slice_fusion), channel_id=1, source_target_pairs={{0,16},{8,24},{16,0},{24,8},{1,17},{9,25},{17,1},{25,9},{2,18},{10... | collective-permute-start | bytes 491528 | tf_op jit(solution)/shard_map/ppermute | solution.py:23
  20.8 31.9 %collective-permute-start.9 = (bf16[32,2560]{1,0:T(8,128)(2,1)S(1)}, bf16[32,2560]{1,0:T(8,128)(2,1)}, u32[]{:S(2)}, u32[]{:S(2)}) collective-permute-start(bf16[32,2560]{1,0:T(8,128)(2,1)S(1)} %constant_dynamic-slice_fusion), channel_id=1, source_target_pairs={{8,0},{16,8},{24,16},{0,24},{9,1},{17,9},{25,17},{1,25},{10,2},{18... | collective-permute-start | bytes 491528 | tf_op jit(solution)/shard_map/ppermute | solution.py:323
  24.4 28.3 %copy-start.6 = (bf16[32,2560]{1,0:T(8,128)(2,1)S(1)}, bf16[32,2560]{1,0:T(8,128)(2,1)}, u32[]{:S(2)}) copy-start(bf16[32,2560]{1,0:T(8,128)(2,1)} %copy-done.5) | copy-start | bytes 491524
  33.7 21.7 %collective-permute-start.4 = (bf16[64,384]{1,0:T(8,128)(2,1)S(1)}, bf16[64,384]{1,0:T(8,128)(2,1)S(1)}, u32[]{:S(2)}, u32[]{:S(2)}) collective-permute-start(bf16[64,384]{1,0:T(8,128)(2,1)S(1)} %get-tuple-element.48), channel_id=1, source_target_pairs={{0,3},{1,2},{2,1},{3,0},{4,7},{5,6},{6,5},{7,4},{8,11},{9,10},{10,... | collective-permute-start | bytes 147464 | tf_op jit(solution)/shard_map/ppermute | solution.py:23
  34.1 21.6 %collective-permute-start.3 = (bf16[64,384]{1,0:T(8,128)(2,1)S(1)}, bf16[64,384]{1,0:T(8,128)(2,1)S(1)}, u32[]{:S(2)}, u32[]{:S(2)}) collective-permute-start(bf16[64,384]{1,0:T(8,128)(2,1)S(1)} %get-tuple-element.49), channel_id=1, source_target_pairs={{0,2},{1,3},{2,0},{3,1},{4,6},{5,7},{6,4},{7,5},{8,10},{9,11},{10,... | collective-permute-start | bytes 147464 | tf_op jit(solution)/shard_map/ppermute | solution.py:23
  48.7 7.0 %collective-permute-start.2 = (bf16[64,384]{1,0:T(8,128)(2,1)S(1)}, bf16[64,384]{1,0:T(8,128)(2,1)S(1)}, u32[]{:S(2)}, u32[]{:S(2)}) collective-permute-start(bf16[64,384]{1,0:T(8,128)(2,1)S(1)} %get-tuple-element.50), channel_id=1, source_target_pairs={{0,1},{1,0},{2,3},{3,2},{4,5},{5,4},{6,7},{7,6},{8,9},{9,8},{10,11... | collective-permute-start | bytes 147464 | tf_op jit(solution)/shard_map/ppermute | solution.py:23
  54.6 22.9 %collective-permute-start.11 = (bf16[128,2560]{1,0:T(8,128)(2,1)}, bf16[128,2560]{1,0:T(8,128)(2,1)}, u32[]{:S(2)}, u32[]{:S(2)}) collective-permute-start(bf16[128,2560]{1,0:T(8,128)(2,1)} %pad_maximum_fusion.1.refs_0_), channel_id=1, source_target_pairs={{0,4},{4,0},{1,5},{5,1},{2,6},{6,2},{3,7},{7,3},{8,12},{12,8},{9,1... | collective-permute-start | bytes 1966088 | tf_op jit(solution)/shard_map/ppermute | solution.py:23
  55.4 22.1 %collective-permute-start.12 = (bf16[128,2560]{1,0:T(8,128)(2,1)}, bf16[128,2560]{1,0:T(8,128)(2,1)}, u32[]{:S(2)}, u32[]{:S(2)}) collective-permute-start(bf16[128,2560]{1,0:T(8,128)(2,1)} %pad_maximum_fusion.1.refs_0_), channel_id=1, source_target_pairs={{0,2},{1,3},{2,0},{3,1},{4,6},{5,7},{6,4},{7,5},{8,10},{9,11},{10,... | collective-permute-start | bytes 1966088 | tf_op jit(solution)/shard_map/ppermute | solution.py:23
  55.8 9.8 %collective-permute-start.6 = (bf16[256,384]{1,0:T(8,128)(2,1)S(1)}, bf16[256,384]{1,0:T(8,128)(2,1)S(1)}, u32[]{:S(2)}, u32[]{:S(2)}) collective-permute-start(bf16[256,384]{1,0:T(8,128)(2,1)S(1)} %pad_maximum_fusion.2), channel_id=1, source_target_pairs={{0,8},{8,16},{16,24},{24,0},{1,9},{9,17},{17,25},{25,1},{2,10},{10... | collective-permute-start | bytes 589832 | tf_op jit(solution)/shard_map/ppermute | solution.py:322
  58.8 9.7 %collective-permute-start.7 = (bf16[256,384]{1,0:T(8,128)(2,1)S(1)}, bf16[256,384]{1,0:T(8,128)(2,1)S(1)}, u32[]{:S(2)}, u32[]{:S(2)}) collective-permute-start(bf16[256,384]{1,0:T(8,128)(2,1)S(1)} %pad_maximum_fusion.2), channel_id=1, source_target_pairs={{8,0},{16,8},{24,16},{0,24},{9,1},{17,9},{25,17},{1,25},{10,2},{18... | collective-permute-start | bytes 589832 | tf_op jit(solution)/shard_map/ppermute | solution.py:323
  59.9 17.5 %collective-permute-start.8 = (bf16[256,384]{1,0:T(8,128)(2,1)S(1)}, bf16[256,384]{1,0:T(8,128)(2,1)S(1)}, u32[]{:S(2)}, u32[]{:S(2)}) collective-permute-start(bf16[256,384]{1,0:T(8,128)(2,1)S(1)} %pad_maximum_fusion.2), channel_id=1, source_target_pairs={{0,16},{8,24},{16,0},{24,8},{1,17},{9,25},{17,1},{25,9},{2,18},{10... | collective-permute-start | bytes 589832 | tf_op jit(solution)/shard_map/ppermute | solution.py:23
  77.5 0.9 copy-start.3
  78.4 7.7 %copy-start.8 = (s32[1,1,4,1]{2,3,1,0:T(1,128)S(1)}, s32[1,1,4,1]{2,3,1,0:T(1,128)}, u32[]{:S(2)}) copy-start(s32[1,1,4,1]{2,3,1,0:T(1,128)} %constant.475.clone) | copy-start | bytes 52
  78.4 7.8 %copy-start.7 = (s32[2,4,64]{2,1,0:T(4,128)S(1)}, s32[2,4,64]{2,1,0:T(4,128)}, u32[]{:S(2)}) copy-start(s32[2,4,64]{2,1,0:T(4,128)} %constant.478) | copy-start | bytes 6148
  78.4 37.5 %all-to-all-start.1 = ((bf16[8,160,384]{2,1,0:T(8,128)(2,1)}), bf16[8,160,384]{2,1,0:T(8,128)(2,1)}, u32[]{:S(2)}, u32[]{:S(2)}) async-start(bf16[8,160,384]{2,1,0:T(8,128)(2,1)} %get-tuple-element.36), calls=%async_computation.1 | async-start | bytes 1966080 | tf_op jit(solution)/shard_map/all_to_all | solution.py:380
  83.0 17.0 %collective-permute-start.13 = (bf16[128,2560]{1,0:T(8,128)(2,1)}, bf16[128,2560]{1,0:T(8,128)(2,1)}, u32[]{:S(2)}, u32[]{:S(2)}) collective-permute-start(bf16[128,2560]{1,0:T(8,128)(2,1)} %collective-permute-done.11.refs_1_), channel_id=1, source_target_pairs={{0,2},{1,3},{2,0},{3,1},{4,6},{5,7},{6,4},{7,5},{8,10},{9,11},{10,... | collective-permute-start | bytes 1966088 | tf_op jit(solution)/shard_map/ppermute | solution.py:23
  84.4 28.6 %collective-permute-start.18 = (bf16[1024,384]{1,0:T(8,128)(2,1)}, bf16[1024,384]{1,0:T(8,128)(2,1)}, u32[]{:S(2)}, u32[]{:S(2)}) collective-permute-start(bf16[1024,384]{1,0:T(8,128)(2,1)} %copy-done.3), channel_id=1, source_target_pairs={{0,4},{4,0},{1,5},{5,1},{2,6},{6,2},{3,7},{7,3},{8,12},{12,8},{9,1... | collective-permute-start | bytes 2359304 | tf_op jit(solution)/shard_map/ppermute | solution.py:23
  86.3 29.6 %collective-permute-start.15 = (bf16[128,2560]{1,0:T(8,128)(2,1)}, bf16[128,2560]{1,0:T(8,128)(2,1)}, u32[]{:S(2)}, u32[]{:S(2)}) collective-permute-start(bf16[128,2560]{1,0:T(8,128)(2,1)} %collective-permute-done.11.refs_1_), channel_id=1, source_target_pairs={{0,1},{1,0},{2,3},{3,2},{4,5},{5,4},{6,7},{7,6},{8,9},{9,8},{10,11... | collective-permute-start | bytes 1966088 | tf_op jit(solution)/shard_map/ppermute | solution.py:23
  86.3 29.6 %collective-permute-start.14 = (bf16[128,2560]{1,0:T(8,128)(2,1)}, bf16[128,2560]{1,0:T(8,128)(2,1)}, u32[]{:S(2)}, u32[]{:S(2)}) collective-permute-start(bf16[128,2560]{1,0:T(8,128)(2,1)} %pad_maximum_fusion.1.refs_0_), channel_id=1, source_target_pairs={{0,1},{1,0},{2,3},{3,2},{4,5},{5,4},{6,7},{7,6},{8,9},{9,8},{10,11... | collective-permute-start | bytes 1966088 | tf_op jit(solution)/shard_map/ppermute | solution.py:23
  86.8 29.1 %collective-permute-start.16 = (bf16[128,2560]{1,0:T(8,128)(2,1)}, bf16[128,2560]{1,0:T(8,128)(2,1)}, u32[]{:S(2)}, u32[]{:S(2)}) collective-permute-start(bf16[128,2560]{1,0:T(8,128)(2,1)} %collective-permute-done.12.refs_2_), channel_id=1, source_target_pairs={{0,1},{1,0},{2,3},{3,2},{4,5},{5,4},{6,7},{7,6},{8,9},{9,8},{10,11... | collective-permute-start | bytes 1966088 | tf_op jit(solution)/shard_map/ppermute | solution.py:23
  100.0 15.9 %collective-permute-start.17 = (bf16[128,2560]{1,0:T(8,128)(2,1)}, bf16[128,2560]{1,0:T(8,128)(2,1)}, u32[]{:S(2)}, u32[]{:S(2)}) collective-permute-start(bf16[128,2560]{1,0:T(8,128)(2,1)} %collective-permute-done.13.refs_3_), channel_id=1, source_target_pairs={{0,1},{1,0},{2,3},{3,2},{4,5},{5,4},{6,7},{7,6},{8,9},{9,8},{10,11... | collective-permute-start | bytes 1966088 | tf_op jit(solution)/shard_map/ppermute | solution.py:23
  115.9 6.6 %copy-start.2 = (bf16[2,1024,384]{2,1,0:T(8,128)(2,1)S(1)}, bf16[2,1024,384]{2,1,0:T(8,128)(2,1)}, u32[]{:S(2)}) copy-start(bf16[2,1024,384]{2,1,0:T(8,128)(2,1)} %pad_maximum_fusion) | copy-start | bytes 4718596
  126.7 44.0 %copy-start.1 = (bf16[2048,320]{0,1:T(8,128)(2,1)S(1)}, bf16[2048,320]{0,1:T(8,128)(2,1)}, u32[]{:S(2)}) copy-start(bf16[2048,320]{0,1:T(8,128)(2,1)} %param.17) | copy-start | bytes 3932164
  130.9 6.0 %collective-permute-start.24 = (bf16[512,128]{1,0:T(8,128)(2,1)S(1)}, bf16[512,128]{1,0:T(8,128)(2,1)S(1)}, u32[]{:S(2)}, u32[]{:S(2)}) collective-permute-start(bf16[512,128]{1,0:T(8,128)(2,1)S(1)} %get-tuple-element.42), channel_id=1, source_target_pairs={{0,4},{4,0},{1,5},{5,1},{2,6},{6,2},{3,7},{7,3},{8,12},{12,8},{9,1... | collective-permute-start | bytes 393224 | tf_op jit(solution)/shard_map/ppermute | solution.py:23
  131.6 8.2 %collective-permute-start.19 = (bf16[512,128]{1,0:T(8,128)(2,1)S(1)}, bf16[512,128]{1,0:T(8,128)(2,1)S(1)}, u32[]{:S(2)}, u32[]{:S(2)}) collective-permute-start(bf16[512,128]{1,0:T(8,128)(2,1)S(1)} %get-tuple-element.39), channel_id=1, source_target_pairs={{0,4},{4,0},{1,5},{5,1},{2,6},{6,2},{3,7},{7,3},{8,12},{12,8},{9,1... | collective-permute-start | bytes 393224 | tf_op jit(solution)/shard_map/ppermute | solution.py:23
  137.0 18.5 %collective-permute-start.27 = (bf16[512,256]{1,0:T(8,128)(2,1)S(1)}, bf16[512,256]{1,0:T(8,128)(2,1)S(1)}, u32[]{:S(2)}, u32[]{:S(2)}) collective-permute-start(bf16[512,256]{1,0:T(8,128)(2,1)S(1)} %constant_dynamic-update-slice_fusion.2.refs_0_), channel_id=1, source_target_pairs={{0,16},{8,24},{16,0},{24,8},{1,17},{9,25},{17,1},{25,9},{2,18},{10... | collective-permute-start | bytes 786440 | tf_op jit(solution)/shard_map/ppermute | solution.py:23
  139.8 21.6 %collective-permute-start.22 = (bf16[512,256]{1,0:T(8,128)(2,1)S(1)}, bf16[512,256]{1,0:T(8,128)(2,1)S(1)}, u32[]{:S(2)}, u32[]{:S(2)}) collective-permute-start(bf16[512,256]{1,0:T(8,128)(2,1)S(1)} %constant_dynamic-update-slice_fusion.refs_0_), channel_id=1, source_target_pairs={{0,16},{8,24},{16,0},{24,8},{1,17},{9,25},{17,1},{25,9},{2,18},{10... | collective-permute-start | bytes 786440 | tf_op jit(solution)/shard_map/ppermute | solution.py:23
  141.7 21.0 %collective-permute-start.25 = (bf16[512,256]{1,0:T(8,128)(2,1)S(1)}, bf16[512,256]{1,0:T(8,128)(2,1)S(1)}, u32[]{:S(2)}, u32[]{:S(2)}) collective-permute-start(bf16[512,256]{1,0:T(8,128)(2,1)S(1)} %constant_dynamic-update-slice_fusion.2.refs_0_), channel_id=1, source_target_pairs={{0,8},{8,16},{16,24},{1,9},{9,17},{17,25},{2,10},{10,18},{18,26},{... | collective-permute-start | bytes 786440 | tf_op jit(solution)/shard_map/ppermute | solution.py:315
  144.3 20.8 %collective-permute-start.26 = (bf16[512,256]{1,0:T(8,128)(2,1)S(1)}, bf16[512,256]{1,0:T(8,128)(2,1)S(1)}, u32[]{:S(2)}, u32[]{:S(2)}) collective-permute-start(bf16[512,256]{1,0:T(8,128)(2,1)S(1)} %constant_dynamic-update-slice_fusion.2.refs_0_), channel_id=1, source_target_pairs={{8,0},{16,8},{24,16},{9,1},{17,9},{25,17},{10,2},{18,10},{26,18},{... | collective-permute-start | bytes 786440 | tf_op jit(solution)/shard_map/ppermute | solution.py:316
  155.5 15.3 %collective-permute-start.28 = (bf16[512,256]{1,0:T(8,128)(2,1)S(1)}, bf16[512,256]{1,0:T(8,128)(2,1)S(1)}, u32[]{:S(2)}, u32[]{:S(2)}) collective-permute-start(bf16[512,256]{1,0:T(8,128)(2,1)S(1)} %collective-permute-done.27.refs_4_), channel_id=1, source_target_pairs={{8,0},{16,24},{9,1},{17,25},{10,2},{18,26},{11,3},{19,27},{12,4},{... | collective-permute-start | bytes 786440 | tf_op jit(solution)/shard_map/ppermute | solution.py:317
  156.8 15.9 %collective-permute-start.20 = (bf16[512,256]{1,0:T(8,128)(2,1)S(1)}, bf16[512,256]{1,0:T(8,128)(2,1)S(1)}, u32[]{:S(2)}, u32[]{:S(2)}) collective-permute-start(bf16[512,256]{1,0:T(8,128)(2,1)S(1)} %constant_dynamic-update-slice_fusion.refs_0_), channel_id=1, source_target_pairs={{0,8},{8,16},{16,24},{1,9},{9,17},{17,25},{2,10},{10,18},{18,26},{... | collective-permute-start | bytes 786440 | tf_op jit(solution)/shard_map/ppermute | solution.py:315
  161.4 15.0 %collective-permute-start.21 = (bf16[512,256]{1,0:T(8,128)(2,1)S(1)}, bf16[512,256]{1,0:T(8,128)(2,1)S(1)}, u32[]{:S(2)}, u32[]{:S(2)}) collective-permute-start(bf16[512,256]{1,0:T(8,128)(2,1)S(1)} %constant_dynamic-update-slice_fusion.refs_0_), channel_id=1, source_target_pairs={{8,0},{16,8},{24,16},{9,1},{17,9},{25,17},{10,2},{18,10},{26,18},{... | collective-permute-start | bytes 786440 | tf_op jit(solution)/shard_map/ppermute | solution.py:316
  162.7 17.5 %collective-permute-start.23 = (bf16[512,256]{1,0:T(8,128)(2,1)S(1)}, bf16[512,256]{1,0:T(8,128)(2,1)S(1)}, u32[]{:S(2)}, u32[]{:S(2)}) collective-permute-start(bf16[512,256]{1,0:T(8,128)(2,1)S(1)} %collective-permute-done.22.refs_4_), channel_id=1, source_target_pairs={{8,0},{16,24},{9,1},{17,25},{10,2},{18,26},{11,3},{19,27},{12,4},{... | collective-permute-start | bytes 786440 | tf_op jit(solution)/shard_map/ppermute | solution.py:317
  183.0 1.7 collective-permute-start.29
  184.8 6.3 %collective-permute-start.30 = (bf16[4,32,640]{2,1,0:T(8,128)(2,1)S(1)}, bf16[4,32,640]{2,1,0:T(8,128)(2,1)S(1)}, u32[]{:S(2)}, u32[]{:S(2)}) collective-permute-start(bf16[4,32,640]{2,1,0:T(8,128)(2,1)S(1)} %fusion.1), channel_id=1, source_target_pairs={{0,2},{1,3},{2,0},{3,1},{4,6},{5,7},{6,4},{7,5},{8,10},{9,11},{10,... | collective-permute-start | bytes 491528 | tf_op jit(solution)/shard_map/ppermute | solution.py:23
  191.4 11.6 %collective-permute-start.31 = (bf16[128,640]{1,0:T(8,128)(2,1)S(1)}, bf16[128,640]{1,0:T(8,128)(2,1)S(1)}, u32[]{:S(2)}, u32[]{:S(2)}) collective-permute-start(bf16[128,640]{1,0:T(8,128)(2,1)S(1)} %pad_maximum_fusion.3), channel_id=1, source_target_pairs={{0,0},{1,8},{2,16},{3,24},{4,4},{5,12},{6,20},{7,28},{8,1},{9,9},{... | collective-permute-start | bytes 491528 | tf_op jit(solution)/shard_map/ppermute | solution.py:500

commit v11 on v8

--- a/solution.py
+++ b/solution.py
@@ -192,7 +192,7 @@
     )(*pieces, *weights)
 
 
-def attend(here, queries, head, packed, limits, places, key_width, masked, layout):
+def attend(here, queries, heads, packed, limits, places, key_width, masked, layout):
     rows_each = queries[0].shape[0]
     rows = rows_each * len(queries)
     value_start = round_up(key_width, LANES)
@@ -208,7 +208,8 @@
         out_refs = refs[len(queries) + 3 :]
         keys = kv_ref[:, :key_width]
         values = kv_ref[:, value_start:]
-        for start in range(0, rows, tile):
+        for order, start in [(o, r) for o in range(len(heads)) for r in range(0, rows, tile)]:
+            head, lanes = heads[order], slice(order * value_width, (order + 1) * value_width)
             from_ref, at = query_refs[start // rows_each], start % rows_each
             query = from_ref[at : at + tile, head * key_width : (head + 1) * key_width]
             scores = lax.dot_general(
@@ -233,9 +234,9 @@
                 which, where = sends((start + low) // unit, here_ref[0], here_ref[1])
                 if not isinstance(where, int):
                     where = pl.multiple_of(where, unit)
-                out_refs[which][pl.ds(where, unit), :] = done[low : low + unit]
-
-    shape = jax.ShapeDtypeStruct((rows // outputs, value_width), jnp.bfloat16)
+                out_refs[which][pl.ds(where, unit), lanes] = done[low : low + unit]
+
+    shape = jax.ShapeDtypeStruct((rows // outputs, len(heads) * value_width), jnp.bfloat16)
     return pl.pallas_call(
         kernel,
         out_shape=(shape,) * outputs,
@@ -463,16 +464,16 @@
         limits = jnp.asarray(limits, jnp.int32)
 
     total = None
-    for head in range(heads_here):
+    for head in range(1 if fast else heads_here):
+        heads = tuple(range(heads_here)) if fast else (head,)
         attended = attend(
-            here, queries, head, packed, limits, places, key_width, masked, layout
+            here, queries, heads, packed, limits, places, key_width, masked, layout
         )
         if fast:
-            last = head == heads_here - 1
             block = jnp.concatenate([attended[0], swap(attended[1], "inner", 1)], axis=1)
             total = expel(
                 here, line_pieces(block, "outer"), out_weights, [] if total is None else [total],
-                head, heads_here, (heads_axis, quarter) if last else None,
+                0, 1, (heads_axis, quarter),
             )
         else:
             attended = gather_line(attended[0], "outer", 1)

time: 195 us -> 198 us (1.015)
  waiting for transfers between devices: 97.4 us -> 111 us
  starting transfers between devices: 49.8 us -> 39 us
    ppermute x20 -> x18, waiting for transfers between devices: 64.8 us -> 77.5 us  [swap(): lax.ppermute(block, axis, [(i, i ^ bit) for i in range(lax.axis_size(axis...]
    ppermute x2 -> x1, starting transfers between devices: 6.84 us -> 2.16 us  [line_pieces(): up = lax.ppermute(block, axis, [(i, i + 1) for i in range(3)])]
    ppermute x20 -> x18, starting transfers between devices: 17.3 us -> 14.4 us  [swap(): lax.ppermute(block, axis, [(i, i ^ bit) for i in range(lax.axis_size(axis...]
    pallas_call x2 -> x1, Pallas kernels: 8.37 us -> 7.41 us  [attend(): pl.pallas_call(kernel, out_shape=(shape,) * outputs, in_specs=[pl.BlockSp...]
    ppermute x2 -> x1, waiting for transfers between devices: 4.73 us -> 5.58 us  [line_pieces(): down = lax.ppermute(block, axis, [(i + 1, i) for i in range(3)])]
    ppermute x2 -> x1, waiting for transfers between devices: 9.37 us -> 10 us  [line_pieces(): passed = lax.ppermute(far, axis, [(1, 0), (2, 3)])]
    pallas_call x2 -> x1, Pallas kernels: 4.78 us -> 4.81 us  [expel(): pl.pallas_call(kernel, out_shape=out_shape, in_specs=[pl.BlockSpec(memory...]
  transfers between devices with their start and end apart: 34 -> 29, of which waited for: 16 -> 15; matrix products, arithmetic and copies ran while one was open for 4% -> 4% of each run, Pallas kernels for 8% -> 7%
where the time goes in v11:
time: 198 us
  waiting for transfers between devices  111 us (56%)
  starting transfers between devices  39 us (20%)
  Pallas kernels  33.8 us (17%)
  local copies, waits for them, and re-layouts  9.25 us (5%)
  other arithmetic  3.49 us (2%)
    ppermute x18, waiting for transfers between devices, swap(): lax.ppermute(block, axis, [(i, i ^ bit) for i in range(lax.axis_size(axis...  77.5 us
    ppermute x18, starting transfers between devices, swap(): lax.ppermute(block, axis, [(i, i ^ bit) for i in range(lax.axis_size(axis...  14.4 us
    ppermute x1, waiting for transfers between devices, line_pieces(): passed = lax.ppermute(far, axis, [(1, 0), (2, 3)])  10 us
    ppermute x1, waiting for transfers between devices, shards(): return lax.ppermute(result, ('outer', 'inner', 'head'), route)  9.67 us
    pallas_call x1, Pallas kernels, compress(): pl.pallas_call(compress_kernel, out_shape=jax.ShapeDtypeStruct((G, blocks...  8.41 us
    all_to_all x2, starting transfers between devices, exchange(): lax.all_to_all(block, seq_axes, split_axis=0, concat_axis=0, tiled=True)  8.35 us
    pallas_call x1, Pallas kernels, project(): pl.pallas_call(kernel, out_shape=jax.ShapeDtypeStruct((rows, columns), jn...  7.46 us
    pallas_call x1, Pallas kernels, attend(): pl.pallas_call(kernel, out_shape=(shape,) * outputs, in_specs=[pl.BlockSp...  7.41 us
  transfers between devices with their start and end apart: 29, of which 15 were waited for; matrix products, arithmetic and copies ran while one was open for 4% of the time, Pallas kernels for 7%

profile of v11, /device:TPU:2, one launch (start us, length us, event | category | flops | bytes accessed | tf_op | source)
XLA Modules:
  0.0 197.7 jit_solution(9172927738210819133)
XLA Ops:
  0.0 0.8 slice.19
  0.8 0.7 slice.18
  1.5 1.9 collective-permute-start.3
  3.5 1.6 collective-permute-start
  5.1 2.2 %collective-permute-start.1 = (bf16[32,2560]{1,0:T(8,128)(2,1)S(1)}, bf16[32,2560]{1,0:T(8,128)(2,1)S(1)}, u32[]{:S(2)}, u32[]{:S(2)}) collective-permute-start(bf16[32,2560]{1,0:T(8,128)(2,1)S(1)} %constant_dynamic-slice_fusion), channel_id=1, source_target_pairs={{8,0},{16,8},{24,16},{0,24},{9,1},{17,9},{25,17},{1,25},{10,2},{18... | collective-permute-start | bytes 491528 | tf_op jit(solution)/shard_map/ppermute | solution.py:324
  7.4 0.8 collective-permute-start.2
  8.2 1.5 collective-permute-start.7
  9.7 5.7 %cut.1 = (bf16[8,160,384]{2,1,0:T(8,128)(2,1)}, bf16[8,160,384]{2,1,0:T(8,128)(2,1)}) custom-call(bf16[320,3072]{1,0:T(8,128)(2,1)} %in_ref.1), custom_call_target="tpu_custom_call" | custom-call | tf_op jit(solution)/shard_map/cut/pallas_call | solution.py:129
  15.4 7.2 %collective-permute-done.2 = bf16[32,2560]{1,0:T(8,128)(2,1)S(1)} collective-permute-done((bf16[32,2560]{1,0:T(8,128)(2,1)S(1)}, bf16[32,2560]{1,0:T(8,128)(2,1)S(1)}, u32[]{:S(2)}, u32[]{:S(2)}) %collective-permute-start.2) | collective-permute-done | bytes 163872 | tf_op jit(solution)/shard_map/ppermute | solution.py:23
  22.5 3.9 %all-to-all-start = ((bf16[8,160,384]{2,1,0:T(8,128)(2,1)}), bf16[8,160,384]{2,1,0:T(8,128)(2,1)S(1)}, u32[]{:S(2)}, u32[]{:S(2)}) async-start(bf16[8,160,384]{2,1,0:T(8,128)(2,1)} %get-tuple-element.37), calls=%async_computation | async-start | bytes 1966080 | tf_op jit(solution)/shard_map/all_to_all | solution.py:381
  26.4 0.9 copy.15.key_reduce
  27.3 0.6 slice.20.edge_keys
  28.5 8.4 %compress.1 = bf16[4,64,384]{2,1,0:T(8,128)(2,1)} custom-call(bf16[1024,768]{1,0:T(8,128)(2,1)} %raw_keys.1, bf16[1024,512]{1,0:T(8,128)(2,1)} %raw_values.1, bf16[16,768]{1,0:T(8,128)(2,1)} %slice.20.edge_keys, bf16[16,512]{1,0:T(8,128)(2,1)} %slice.21.edge_values, bf16[192,768]{1,0:T(8,128)(2,1)} %key_expand.1, f32[32,768]{1,0:T(8,128)} %key_mix.1, ...), custom_call_target="tpu_custom_call" | custom-call | flops 2013265920 | bytes 1572864 | tf_op jit(solution)/shard_map/compress/pallas_call | solution.py:105
  37.0 0.9 dynamic-slice_bitcast_fusion.3
  37.9 1.4 collective-permute-start.5
  39.8 2.1 %collective-permute-start.11 = (bf16[128,2560]{1,0:T(8,128)(2,1)S(1)}, bf16[128,2560]{1,0:T(8,128)(2,1)S(1)}, u32[]{:S(2)}, u32[]{:S(2)}) collective-permute-start(bf16[128,2560]{1,0:T(8,128)(2,1)S(1)} %pad_maximum_fusion.1.refs_0_), channel_id=1, source_target_pairs={{0,4},{4,0},{1,5},{5,1},{2,6},{6,2},{3,7},{7,3},{8,12},{12,8},{9,1... | collective-permute-start | bytes 1966088 | tf_op jit(solution)/shard_map/ppermute | solution.py:23
  42.9 3.5 %collective-permute-done.7.refs_6_ = bf16[320,2048]{1,0:T(8,128)(2,1)} collective-permute-done((bf16[320,2048]{1,0:T(8,128)(2,1)}, bf16[320,2048]{1,0:T(8,128)(2,1)}, u32[]{:S(2)}, u32[]{:S(2)}) %collective-permute-start.7) | collective-permute-done | bytes 1310752 | tf_op jit(solution)/shard_map/ppermute | solution.py:23
  46.5 1.5 collective-permute-start.8
  47.9 2.3 %collective-permute-start.9 = (bf16[256,384]{1,0:T(8,128)(2,1)S(1)}, bf16[256,384]{1,0:T(8,128)(2,1)S(1)}, u32[]{:S(2)}, u32[]{:S(2)}) collective-permute-start(bf16[256,384]{1,0:T(8,128)(2,1)S(1)} %pad_maximum_fusion.2), channel_id=1, source_target_pairs={{8,0},{16,8},{24,16},{0,24},{9,1},{17,9},{25,17},{1,25},{10,2},{18... | collective-permute-start | bytes 589832 | tf_op jit(solution)/shard_map/ppermute | solution.py:324
  50.3 1.8 collective-permute-start.10
  52.2 1.8 collective-permute-done.8
  54.1 6.1 %collective-permute-done.9 = bf16[256,384]{1,0:T(8,128)(2,1)S(1)} collective-permute-done((bf16[256,384]{1,0:T(8,128)(2,1)S(1)}, bf16[256,384]{1,0:T(8,128)(2,1)S(1)}, u32[]{:S(2)}, u32[]{:S(2)}) %collective-permute-start.9) | collective-permute-done | bytes 196640 | tf_op jit(solution)/shard_map/ppermute | solution.py:324
  60.3 8.4 %collective-permute-done.10 = bf16[256,384]{1,0:T(8,128)(2,1)S(1)} collective-permute-done((bf16[256,384]{1,0:T(8,128)(2,1)S(1)}, bf16[256,384]{1,0:T(8,128)(2,1)S(1)}, u32[]{:S(2)}, u32[]{:S(2)}) %collective-permute-start.10) | collective-permute-done | bytes 196640 | tf_op jit(solution)/shard_map/ppermute | solution.py:23
  68.7 0.9 copy-done.6
  69.8 4.5 %all-to-all-start.1 = ((bf16[8,160,384]{2,1,0:T(8,128)(2,1)}), bf16[8,160,384]{2,1,0:T(8,128)(2,1)S(1)}, u32[]{:S(2)}, u32[]{:S(2)}) async-start(bf16[8,160,384]{2,1,0:T(8,128)(2,1)} %get-tuple-element.38), calls=%async_computation.1 | async-start | bytes 1966080 | tf_op jit(solution)/shard_map/all_to_all | solution.py:381
  75.5 0.9 collective-permute-start.18
  77.2 13.7 %collective-permute-done.13.refs_3_ = bf16[128,2560]{1,0:T(8,128)(2,1)} collective-permute-done((bf16[128,2560]{1,0:T(8,128)(2,1)}, bf16[128,2560]{1,0:T(8,128)(2,1)}, u32[]{:S(2)}, u32[]{:S(2)}) %collective-permute-start.13) | collective-permute-done | bytes 655392 | tf_op jit(solution)/shard_map/ppermute | solution.py:23
  91.0 1.3 add.630.refs_3_
  92.4 11.8 %collective-permute-done.18 = bf16[1024,384]{1,0:T(8,128)(2,1)} collective-permute-done((bf16[1024,384]{1,0:T(8,128)(2,1)}, bf16[1024,384]{1,0:T(8,128)(2,1)}, u32[]{:S(2)}, u32[]{:S(2)}) %collective-permute-start.18) | collective-permute-done | bytes 786464 | tf_op jit(solution)/shard_map/ppermute | solution.py:23
  104.2 1.5 select_bitcast_fusion.1
  105.7 1.4 pad_maximum_fusion
  107.1 1.1 copy-done.4
  108.2 7.5 %project.1.refs_0_ = bf16[1024,384]{1,0:T(8,128)(2,1)S(1)} custom-call(bf16[128,2560]{1,0:T(8,128)(2,1)S(1)} %pad_maximum_fusion.1.refs_0_, bf16[128,2560]{1,0:T(8,128)(2,1)S(1)} %copy-done.4, bf16[128,2560]{1,0:T(8,128)(2,1)} %collective-permute-done.12.refs_2_, bf16[128,2560]{1,0:T(8,128)(2,1)} %collective-permute-done.13.refs_3_, ...), custom_call_target="tpu_custom_call" | custom-call | flops 2013265920 | bytes 5242880 | tf_op jit(solution)/shard_map/project/pallas_call | solution.py:178
  115.7 7.4 %attend.1 = (bf16[512,256]{1,0:T(8,128)(2,1)S(1)}, bf16[512,256]{1,0:T(8,128)(2,1)S(1)}) custom-call(s32[3]{0:T(128)S(1)} %pad_add_fusion.here_ref.place_ref, bf16[1024,384]{1,0:T(8,128)(2,1)S(1)} %project.1.refs_0_, bf16[2048,384]{1,0:T(8,128)(2,1)S(1)} %bitcast.58, s32[1,2048]{1,0:T(1,128)S(1)} %sub.145.refs_2_, s32[1024,1]{1,0:T(8,128)S(1)} %copy-done.5), custom_call_target="tpu_custom_call" | custom-call | flops 1342177280 | bytes 1572864 | tf_op jit(solution)/shard_map/attend/pallas_call | solution.py:240
  123.5 6.6 %collective-permute-done.19 = bf16[512,256]{1,0:T(8,128)(2,1)S(1)} collective-permute-done((bf16[512,256]{1,0:T(8,128)(2,1)S(1)}, bf16[512,256]{1,0:T(8,128)(2,1)S(1)}, u32[]{:S(2)}, u32[]{:S(2)}) %collective-permute-start.19) | collective-permute-done | bytes 262176 | tf_op jit(solution)/shard_map/ppermute | solution.py:23
  130.1 3.7 %collective-permute-start.22 = (bf16[512,512]{1,0:T(8,128)(2,1)S(1)}, bf16[512,512]{1,0:T(8,128)(2,1)S(1)}, u32[]{:S(2)}, u32[]{:S(2)}) collective-permute-start(bf16[512,512]{1,0:T(8,128)(2,1)S(1)} %constant_dynamic-update-slice_fusion.refs_0_), channel_id=1, source_target_pairs={{0,16},{8,24},{16,0},{24,8},{1,17},{9,25},{17,1},{25,9},{2,18},{10... | collective-permute-start | bytes 1572872 | tf_op jit(solution)/shard_map/ppermute | solution.py:23
  133.9 2.2 %collective-permute-start.20 = (bf16[512,512]{1,0:T(8,128)(2,1)S(1)}, bf16[512,512]{1,0:T(8,128)(2,1)S(1)}, u32[]{:S(2)}, u32[]{:S(2)}) collective-permute-start(bf16[512,512]{1,0:T(8,128)(2,1)S(1)} %constant_dynamic-update-slice_fusion.refs_0_), channel_id=1, source_target_pairs={{0,8},{8,16},{16,24},{1,9},{9,17},{17,25},{2,10},{10,18},{18,26},{... | collective-permute-start | bytes 1572872 | tf_op jit(solution)/shard_map/ppermute | solution.py:316
  136.0 1.3 collective-permute-start.21
  137.3 17.9 %collective-permute-done.22.refs_4_ = bf16[512,512]{1,0:T(8,128)(2,1)S(1)} collective-permute-done((bf16[512,512]{1,0:T(8,128)(2,1)S(1)}, bf16[512,512]{1,0:T(8,128)(2,1)S(1)}, u32[]{:S(2)}, u32[]{:S(2)}) %collective-permute-start.22) | collective-permute-done | bytes 524320 | tf_op jit(solution)/shard_map/ppermute | solution.py:23
  155.2 1.3 collective-permute-start.23
  156.5 5.6 %collective-permute-done.21.refs_2_ = bf16[512,512]{1,0:T(8,128)(2,1)S(1)} collective-permute-done((bf16[512,512]{1,0:T(8,128)(2,1)S(1)}, bf16[512,512]{1,0:T(8,128)(2,1)S(1)}, u32[]{:S(2)}, u32[]{:S(2)}) %collective-permute-start.21) | collective-permute-done | bytes 524320 | tf_op jit(solution)/shard_map/ppermute | solution.py:317
  162.1 10.0 %collective-permute-done.23.refs_3_ = bf16[512,512]{1,0:T(8,128)(2,1)S(1)} collective-permute-done((bf16[512,512]{1,0:T(8,128)(2,1)S(1)}, bf16[512,512]{1,0:T(8,128)(2,1)S(1)}, u32[]{:S(2)}, u32[]{:S(2)}) %collective-permute-start.23) | collective-permute-done | bytes 524320 | tf_op jit(solution)/shard_map/ppermute | solution.py:318
  172.1 4.8 %expel.1 = (f32[4,2,32,640]{3,2,1,0:T(8,128)S(1)}, bf16[4,2,32,640]{3,2,1,0:T(8,128)(2,1)}) custom-call(s32[3]{0:T(128)S(1)} %pad_add_fusion.here_ref.place_ref, bf16[512,512]{1,0:T(8,128)(2,1)S(1)} %constant_dynamic-update-slice_fusion.refs_0_, bf16[512,512]{1,0:T(8,128)(2,1)S(1)} %collective-permute-done.20.refs_1_, ...), custom_call_target="tpu_custom_call" | custom-call | flops 1342177280 | bytes 2621440 | tf_op jit(solution)/shard_map/expel/pallas_call | solution.py:300
  177.0 1.8 collective-permute-done.24
  179.0 6.2 %collective-permute-done.25 = bf16[4,32,640]{2,1,0:T(8,128)(2,1)S(1)} collective-permute-done((bf16[4,32,640]{2,1,0:T(8,128)(2,1)S(1)}, bf16[4,32,640]{2,1,0:T(8,128)(2,1)S(1)}, u32[]{:S(2)}, u32[]{:S(2)}) %collective-permute-start.25) | collective-permute-done | bytes 163872 | tf_op jit(solution)/shard_map/ppermute | solution.py:23
  185.4 1.9 collective-permute-start.26
  187.4 9.7 %collective-permute-done.26 = bf16[128,640]{1,0:T(8,128)(2,1)S(1)} collective-permute-done((bf16[128,640]{1,0:T(8,128)(2,1)S(1)}, bf16[128,640]{1,0:T(8,128)(2,1)S(1)}, u32[]{:S(2)}, u32[]{:S(2)}) %collective-permute-start.26) | collective-permute-done | bytes 163872 | tf_op jit(solution)/shard_map/ppermute | solution.py:503
  197.0 0.7 copy.23
  (67 shorter events, 4.5 us)
Async XLA Ops:
  0.0 3.5 %copy-start = (bf16[128,2560]{1,0:T(8,128)(2,1)S(1)}, bf16[128,2560]{1,0:T(8,128)(2,1)}, u32[]{:S(2)}) copy-start(bf16[128,2560]{1,0:T(8,128)(2,1)} %param.13) | copy-start | bytes 1966084
  1.5 6.6 %collective-permute-start.3 = (bf16[16,1280]{1,0:T(8,128)(2,1)S(1)}, bf16[16,1280]{1,0:T(8,128)(2,1)S(1)}, u32[]{:S(2)}, u32[]{:S(2)}) collective-permute-start(bf16[16,1280]{1,0:T(8,128)(2,1)S(1)} %pad_maximum_fusion.4), channel_id=1, source_target_pairs={{1,0},{2,1},{3,2},{4,3},{5,4},{6,5},{7,6},{8,7},{9,8},{10,9},{11,1... | collective-permute-start | bytes 122888 | tf_op jit(solution)/shard_map/ppermute | solution.py:366
  3.5 11.9 %collective-permute-start = (bf16[32,2560]{1,0:T(8,128)(2,1)S(1)}, bf16[32,2560]{1,0:T(8,128)(2,1)S(1)}, u32[]{:S(2)}, u32[]{:S(2)}) collective-permute-start(bf16[32,2560]{1,0:T(8,128)(2,1)S(1)} %constant_dynamic-slice_fusion), channel_id=1, source_target_pairs={{0,8},{8,16},{16,24},{24,0},{1,9},{9,17},{17,25},{25,1},{2,10},{10... | collective-permute-start | bytes 491528 | tf_op jit(solution)/shard_map/ppermute | solution.py:323
  5.1 10.2 %collective-permute-start.1 = (bf16[32,2560]{1,0:T(8,128)(2,1)S(1)}, bf16[32,2560]{1,0:T(8,128)(2,1)S(1)}, u32[]{:S(2)}, u32[]{:S(2)}) collective-permute-start(bf16[32,2560]{1,0:T(8,128)(2,1)S(1)} %constant_dynamic-slice_fusion), channel_id=1, source_target_pairs={{8,0},{16,8},{24,16},{0,24},{9,1},{17,9},{25,17},{1,25},{10,2},{18... | collective-permute-start | bytes 491528 | tf_op jit(solution)/shard_map/ppermute | solution.py:324
  7.4 15.2 %collective-permute-start.2 = (bf16[32,2560]{1,0:T(8,128)(2,1)S(1)}, bf16[32,2560]{1,0:T(8,128)(2,1)S(1)}, u32[]{:S(2)}, u32[]{:S(2)}) collective-permute-start(bf16[32,2560]{1,0:T(8,128)(2,1)S(1)} %constant_dynamic-slice_fusion), channel_id=1, source_target_pairs={{0,16},{8,24},{16,0},{24,8},{1,17},{9,25},{17,1},{25,9},{2,18},{10... | collective-permute-start | bytes 491528 | tf_op jit(solution)/shard_map/ppermute | solution.py:23
  8.2 38.3 %collective-permute-start.7 = (bf16[320,2048]{1,0:T(8,128)(2,1)}, bf16[320,2048]{1,0:T(8,128)(2,1)}, u32[]{:S(2)}, u32[]{:S(2)}) collective-permute-start(bf16[320,2048]{1,0:T(8,128)(2,1)} %bitcast.59), channel_id=1, source_target_pairs={{0,4},{4,0},{1,5},{5,1},{2,6},{6,2},{3,7},{7,3},{8,12},{12,8},{9,1... | collective-permute-start | bytes 3932168 | tf_op jit(solution)/shard_map/ppermute | solution.py:23
  15.4 11.1 %copy-start.7 = (bf16[768,192]{0,1:T(8,128)(2,1)S(1)}, bf16[768,192]{0,1:T(8,128)(2,1)}, u32[]{:S(2)}) copy-start(bf16[768,192]{0,1:T(8,128)(2,1)} %param.20) | copy-start | bytes 884740
  22.5 47.1 %all-to-all-start = ((bf16[8,160,384]{2,1,0:T(8,128)(2,1)}), bf16[8,160,384]{2,1,0:T(8,128)(2,1)S(1)}, u32[]{:S(2)}, u32[]{:S(2)}) async-start(bf16[8,160,384]{2,1,0:T(8,128)(2,1)} %get-tuple-element.37), calls=%async_computation | async-start | bytes 1966080 | tf_op jit(solution)/shard_map/all_to_all | solution.py:381
  37.9 4.1 %collective-permute-start.6 = (bf16[64,384]{1,0:T(8,128)(2,1)S(1)}, bf16[64,384]{1,0:T(8,128)(2,1)S(1)}, u32[]{:S(2)}, u32[]{:S(2)}) collective-permute-start(bf16[64,384]{1,0:T(8,128)(2,1)S(1)} %get-tuple-element.48), channel_id=1, source_target_pairs={{0,3},{1,2},{2,1},{3,0},{4,7},{5,6},{6,5},{7,4},{8,11},{9,10},{10,... | collective-permute-start | bytes 147464 | tf_op jit(solution)/shard_map/ppermute | solution.py:23
  37.9 5.0 %collective-permute-start.5 = (bf16[64,384]{1,0:T(8,128)(2,1)S(1)}, bf16[64,384]{1,0:T(8,128)(2,1)S(1)}, u32[]{:S(2)}, u32[]{:S(2)}) collective-permute-start(bf16[64,384]{1,0:T(8,128)(2,1)S(1)} %get-tuple-element.49), channel_id=1, source_target_pairs={{0,2},{1,3},{2,0},{3,1},{4,6},{5,7},{6,4},{7,5},{8,10},{9,11},{10,... | collective-permute-start | bytes 147464 | tf_op jit(solution)/shard_map/ppermute | solution.py:23
  39.3 3.6 %collective-permute-start.4 = (bf16[64,384]{1,0:T(8,128)(2,1)S(1)}, bf16[64,384]{1,0:T(8,128)(2,1)S(1)}, u32[]{:S(2)}, u32[]{:S(2)}) collective-permute-start(bf16[64,384]{1,0:T(8,128)(2,1)S(1)} %get-tuple-element.50), channel_id=1, source_target_pairs={{0,1},{1,0},{2,3},{3,2},{4,5},{5,4},{6,7},{7,6},{8,9},{9,8},{10,11... | collective-permute-start | bytes 147464 | tf_op jit(solution)/shard_map/ppermute | solution.py:23
  39.8 28.9 %collective-permute-start.11 = (bf16[128,2560]{1,0:T(8,128)(2,1)S(1)}, bf16[128,2560]{1,0:T(8,128)(2,1)S(1)}, u32[]{:S(2)}, u32[]{:S(2)}) collective-permute-start(bf16[128,2560]{1,0:T(8,128)(2,1)S(1)} %pad_maximum_fusion.1.refs_0_), channel_id=1, source_target_pairs={{0,4},{4,0},{1,5},{5,1},{2,6},{6,2},{3,7},{7,3},{8,12},{12,8},{9,1... | collective-permute-start | bytes 1966088 | tf_op jit(solution)/shard_map/ppermute | solution.py:23
  42.0 26.8 %collective-permute-start.12 = (bf16[128,2560]{1,0:T(8,128)(2,1)S(1)}, bf16[128,2560]{1,0:T(8,128)(2,1)}, u32[]{:S(2)}, u32[]{:S(2)}) collective-permute-start(bf16[128,2560]{1,0:T(8,128)(2,1)S(1)} %pad_maximum_fusion.1.refs_0_), channel_id=1, source_target_pairs={{0,2},{1,3},{2,0},{3,1},{4,6},{5,7},{6,4},{7,5},{8,10},{9,11},{10,... | collective-permute-start | bytes 1966088 | tf_op jit(solution)/shard_map/ppermute | solution.py:23
  46.5 7.6 %collective-permute-start.8 = (bf16[256,384]{1,0:T(8,128)(2,1)S(1)}, bf16[256,384]{1,0:T(8,128)(2,1)S(1)}, u32[]{:S(2)}, u32[]{:S(2)}) collective-permute-start(bf16[256,384]{1,0:T(8,128)(2,1)S(1)} %pad_maximum_fusion.2), channel_id=1, source_target_pairs={{0,8},{8,16},{16,24},{24,0},{1,9},{9,17},{17,25},{25,1},{2,10},{10... | collective-permute-start | bytes 589832 | tf_op jit(solution)/shard_map/ppermute | solution.py:323
  47.9 12.3 %collective-permute-start.9 = (bf16[256,384]{1,0:T(8,128)(2,1)S(1)}, bf16[256,384]{1,0:T(8,128)(2,1)S(1)}, u32[]{:S(2)}, u32[]{:S(2)}) collective-permute-start(bf16[256,384]{1,0:T(8,128)(2,1)S(1)} %pad_maximum_fusion.2), channel_id=1, source_target_pairs={{8,0},{16,8},{24,16},{0,24},{9,1},{17,9},{25,17},{1,25},{10,2},{18... | collective-permute-start | bytes 589832 | tf_op jit(solution)/shard_map/ppermute | solution.py:324
  50.3 18.4 %collective-permute-start.10 = (bf16[256,384]{1,0:T(8,128)(2,1)S(1)}, bf16[256,384]{1,0:T(8,128)(2,1)S(1)}, u32[]{:S(2)}, u32[]{:S(2)}) collective-permute-start(bf16[256,384]{1,0:T(8,128)(2,1)S(1)} %pad_maximum_fusion.2), channel_id=1, source_target_pairs={{0,16},{8,24},{16,0},{24,8},{1,17},{9,25},{17,1},{25,9},{2,18},{10... | collective-permute-start | bytes 589832 | tf_op jit(solution)/shard_map/ppermute | solution.py:23
  68.7 0.9 copy-start.6
  68.7 1.1 copy-start.3
  69.6 6.9 %copy-start.9 = (s32[1,1,4,1]{2,3,1,0:T(1,128)S(1)}, s32[1,1,4,1]{2,3,1,0:T(1,128)}, u32[]{:S(2)}) copy-start(s32[1,1,4,1]{2,3,1,0:T(1,128)} %constant.475.clone) | copy-start | bytes 52
  69.6 6.9 %copy-start.8 = (s32[2,4,64]{2,1,0:T(4,128)S(1)}, s32[2,4,64]{2,1,0:T(4,128)}, u32[]{:S(2)}) copy-start(s32[2,4,64]{2,1,0:T(4,128)} %constant.478) | copy-start | bytes 6148
  69.8 37.3 %all-to-all-start.1 = ((bf16[8,160,384]{2,1,0:T(8,128)(2,1)}), bf16[8,160,384]{2,1,0:T(8,128)(2,1)S(1)}, u32[]{:S(2)}, u32[]{:S(2)}) async-start(bf16[8,160,384]{2,1,0:T(8,128)(2,1)} %get-tuple-element.38), calls=%async_computation.1 | async-start | bytes 1966080 | tf_op jit(solution)/shard_map/all_to_all | solution.py:381
  74.3 16.5 %collective-permute-start.13 = (bf16[128,2560]{1,0:T(8,128)(2,1)}, bf16[128,2560]{1,0:T(8,128)(2,1)}, u32[]{:S(2)}, u32[]{:S(2)}) collective-permute-start(bf16[128,2560]{1,0:T(8,128)(2,1)} %copy-done.3), channel_id=1, source_target_pairs={{0,2},{1,3},{2,0},{3,1},{4,6},{5,7},{6,4},{7,5},{8,10},{9,11},{10,... | collective-permute-start | bytes 1966088 | tf_op jit(solution)/shard_map/ppermute | solution.py:23
  75.5 28.7 %collective-permute-start.18 = (bf16[1024,384]{1,0:T(8,128)(2,1)}, bf16[1024,384]{1,0:T(8,128)(2,1)}, u32[]{:S(2)}, u32[]{:S(2)}) collective-permute-start(bf16[1024,384]{1,0:T(8,128)(2,1)} %copy-done.6), channel_id=1, source_target_pairs={{0,4},{4,0},{1,5},{5,1},{2,6},{6,2},{3,7},{7,3},{8,12},{12,8},{9,1... | collective-permute-start | bytes 2359304 | tf_op jit(solution)/shard_map/ppermute | solution.py:23
  76.6 30.5 %collective-permute-start.15 = (bf16[128,2560]{1,0:T(8,128)(2,1)}, bf16[128,2560]{1,0:T(8,128)(2,1)}, u32[]{:S(2)}, u32[]{:S(2)}) collective-permute-start(bf16[128,2560]{1,0:T(8,128)(2,1)} %copy-done.3), channel_id=1, source_target_pairs={{0,1},{1,0},{2,3},{3,2},{4,5},{5,4},{6,7},{7,6},{8,9},{9,8},{10,11... | collective-permute-start | bytes 1966088 | tf_op jit(solution)/shard_map/ppermute | solution.py:23
  76.6 30.5 %collective-permute-start.14 = (bf16[128,2560]{1,0:T(8,128)(2,1)S(1)}, bf16[128,2560]{1,0:T(8,128)(2,1)}, u32[]{:S(2)}, u32[]{:S(2)}) collective-permute-start(bf16[128,2560]{1,0:T(8,128)(2,1)S(1)} %pad_maximum_fusion.1.refs_0_), channel_id=1, source_target_pairs={{0,1},{1,0},{2,3},{3,2},{4,5},{5,4},{6,7},{7,6},{8,9},{9,8},{10,11... | collective-permute-start | bytes 1966088 | tf_op jit(solution)/shard_map/ppermute | solution.py:23
  77.1 30.0 %collective-permute-start.16 = (bf16[128,2560]{1,0:T(8,128)(2,1)}, bf16[128,2560]{1,0:T(8,128)(2,1)}, u32[]{:S(2)}, u32[]{:S(2)}) collective-permute-start(bf16[128,2560]{1,0:T(8,128)(2,1)} %collective-permute-done.12.refs_2_), channel_id=1, source_target_pairs={{0,1},{1,0},{2,3},{3,2},{4,5},{5,4},{6,7},{7,6},{8,9},{9,8},{10,11... | collective-permute-start | bytes 1966088 | tf_op jit(solution)/shard_map/ppermute | solution.py:23
  90.9 16.2 %collective-permute-start.17 = (bf16[128,2560]{1,0:T(8,128)(2,1)}, bf16[128,2560]{1,0:T(8,128)(2,1)}, u32[]{:S(2)}, u32[]{:S(2)}) collective-permute-start(bf16[128,2560]{1,0:T(8,128)(2,1)} %collective-permute-done.13.refs_3_), channel_id=1, source_target_pairs={{0,1},{1,0},{2,3},{3,2},{4,5},{5,4},{6,7},{7,6},{8,9},{9,8},{10,11... | collective-permute-start | bytes 1966088 | tf_op jit(solution)/shard_map/ppermute | solution.py:23
  107.1 1.1 copy-start.4
  108.2 7.5 %copy-start.1 = (bf16[2,1024,384]{2,1,0:T(8,128)(2,1)S(1)}, bf16[2,1024,384]{2,1,0:T(8,128)(2,1)}, u32[]{:S(2)}) copy-start(bf16[2,1024,384]{2,1,0:T(8,128)(2,1)} %pad_maximum_fusion) | copy-start | bytes 4718596
  108.2 7.5 %copy-start.5 = (s32[1024,1]{1,0:T(8,128)S(1)}, s32[1024,1]{1,0:T(8,128)}, u32[]{:S(2)}) copy-start(s32[1024,1]{1,0:T(8,128)} %add.630.refs_3_) | copy-start | bytes 12292
  115.7 56.4 %copy-start.2 = (bf16[2048,320]{0,1:T(8,128)(2,1)S(1)}, bf16[2048,320]{0,1:T(8,128)(2,1)}, u32[]{:S(2)}) copy-start(bf16[2048,320]{0,1:T(8,128)(2,1)} %param.17) | copy-start | bytes 3932164
  123.1 7.0 %collective-permute-start.19 = (bf16[512,256]{1,0:T(8,128)(2,1)S(1)}, bf16[512,256]{1,0:T(8,128)(2,1)S(1)}, u32[]{:S(2)}, u32[]{:S(2)}) collective-permute-start(bf16[512,256]{1,0:T(8,128)(2,1)S(1)} %get-tuple-element.41), channel_id=1, source_target_pairs={{0,4},{4,0},{1,5},{5,1},{2,6},{6,2},{3,7},{7,3},{8,12},{12,8},{9,1... | collective-permute-start | bytes 786440 | tf_op jit(solution)/shard_map/ppermute | solution.py:23
  130.1 25.1 %collective-permute-start.22 = (bf16[512,512]{1,0:T(8,128)(2,1)S(1)}, bf16[512,512]{1,0:T(8,128)(2,1)S(1)}, u32[]{:S(2)}, u32[]{:S(2)}) collective-permute-start(bf16[512,512]{1,0:T(8,128)(2,1)S(1)} %constant_dynamic-update-slice_fusion.refs_0_), channel_id=1, source_target_pairs={{0,16},{8,24},{16,0},{24,8},{1,17},{9,25},{17,1},{25,9},{2,18},{10... | collective-permute-start | bytes 1572872 | tf_op jit(solution)/shard_map/ppermute | solution.py:23
  133.9 22.7 %collective-permute-start.20 = (bf16[512,512]{1,0:T(8,128)(2,1)S(1)}, bf16[512,512]{1,0:T(8,128)(2,1)S(1)}, u32[]{:S(2)}, u32[]{:S(2)}) collective-permute-start(bf16[512,512]{1,0:T(8,128)(2,1)S(1)} %constant_dynamic-update-slice_fusion.refs_0_), channel_id=1, source_target_pairs={{0,8},{8,16},{16,24},{1,9},{9,17},{17,25},{2,10},{10,18},{18,26},{... | collective-permute-start | bytes 1572872 | tf_op jit(solution)/shard_map/ppermute | solution.py:316
  136.0 26.1 %collective-permute-start.21 = (bf16[512,512]{1,0:T(8,128)(2,1)S(1)}, bf16[512,512]{1,0:T(8,128)(2,1)S(1)}, u32[]{:S(2)}, u32[]{:S(2)}) collective-permute-start(bf16[512,512]{1,0:T(8,128)(2,1)S(1)} %constant_dynamic-update-slice_fusion.refs_0_), channel_id=1, source_target_pairs={{8,0},{16,8},{24,16},{9,1},{17,9},{25,17},{10,2},{18,10},{26,18},{... | collective-permute-start | bytes 1572872 | tf_op jit(solution)/shard_map/ppermute | solution.py:317
  155.2 16.9 %collective-permute-start.23 = (bf16[512,512]{1,0:T(8,128)(2,1)S(1)}, bf16[512,512]{1,0:T(8,128)(2,1)S(1)}, u32[]{:S(2)}, u32[]{:S(2)}) collective-permute-start(bf16[512,512]{1,0:T(8,128)(2,1)S(1)} %collective-permute-done.22.refs_4_), channel_id=1, source_target_pairs={{8,0},{16,24},{9,1},{17,25},{10,2},{18,26},{11,3},{19,27},{12,4},{... | collective-permute-start | bytes 1572872 | tf_op jit(solution)/shard_map/ppermute | solution.py:318
  176.9 1.8 collective-permute-start.24
  178.9 6.3 %collective-permute-start.25 = (bf16[4,32,640]{2,1,0:T(8,128)(2,1)S(1)}, bf16[4,32,640]{2,1,0:T(8,128)(2,1)S(1)}, u32[]{:S(2)}, u32[]{:S(2)}) collective-permute-start(bf16[4,32,640]{2,1,0:T(8,128)(2,1)S(1)} %fusion.1), channel_id=1, source_target_pairs={{0,2},{1,3},{2,0},{3,1},{4,6},{5,7},{6,4},{7,5},{8,10},{9,11},{10,... | collective-permute-start | bytes 491528 | tf_op jit(solution)/shard_map/ppermute | solution.py:23
  185.4 11.6 %collective-permute-start.26 = (bf16[128,640]{1,0:T(8,128)(2,1)S(1)}, bf16[128,640]{1,0:T(8,128)(2,1)S(1)}, u32[]{:S(2)}, u32[]{:S(2)}) collective-permute-start(bf16[128,640]{1,0:T(8,128)(2,1)S(1)} %pad_maximum_fusion.3), channel_id=1, source_target_pairs={{0,0},{1,8},{2,16},{3,24},{4,4},{5,12},{6,20},{7,28},{8,1},{9,9},{... | collective-permute-start | bytes 491528 | tf_op jit(solution)/shard_map/ppermute | solution.py:503
